TPU v7x, 32 devices: a whole 2x2x4 slice. The times are simulated.
32 devices in a mesh: groups: 2 (over y), gx: 4 (over x, core), gy: 4 (over z).
Axes of the slice: x: 2, y: 2, z: 4, core: 2. Of those that a mesh axis runs over, the one named last changes fastest.
Arguments:
- cell_index: int32 [32, 32768], P(('groups', 'gx', 'gy')), parts along dimension 0, may hold values from 0 to 32767, each once within a row
- offset_code: int32 [32, 32768], P(('groups', 'gx', 'gy')), parts along dimension 0, may hold values from 0 to 63
- particle_state: float32 [32, 12, 32768], P(('groups', 'gx', 'gy')), parts along dimension 0, may hold values from -6 to 6
- fluid_flags: int32 [128, 32, 256], P(('groups', 'gx'), 'gy'), parts along dimension 0, may hold values 0 or 1
Outputs:
- pressure: float32 [128, 32, 256], P(('groups', 'gx'), 'gy'), parts along dimension 0
- new_velocity: float32 [32, 3, 32768], P(('groups', 'gx', 'gy')), parts along dimension 0
There are 2 independent parts, one for each index of `groups`. A program takes and returns all parts, laid end to end along the dimension named above; each array names one. Nothing has to cross between parts.
Inputs may be any that keep to these rules, and one draw needn't show every extreme that they name: `cell_index`: each row of a brick lists every cell of the brick exactly once.
All inputs are finite; a program needn't handle non-finite values. No bound on the sum of `fluid_flags` on one device may be relied on, other than what follows from the above.
Results may differ from a plain program's by a relative error of at most 0.0001.
Values sent between devices are 32-bit elements; how exact they have to be, the bound alone decides.
No kernel may reach another device: no remote copies, remote signals or barrier semaphores. Data moves between devices by JAX's collectives and lax.ppermute only.
A program may use at most 128 MiB of HBM per device.

v0:
```python
import jax
import jax.numpy as jnp
from jax import lax
from jax.sharding import PartitionSpec as P

ITERS = 3


CORNERS = [(0, 0, 0), (0, 0, 1), (0, 1, 0), (0, 1, 1), (1, 0, 0), (1, 0, 1), (1, 1, 0), (1, 1, 1)]


def padded_2(block, sides, width):
    for axis, dim in sides:
        count = lax.axis_size(axis)
        forward = [(i, i + 1) for i in range(count - 1)]
        backward = [(target, source) for source, target in forward]
        low = lax.ppermute(
            lax.slice_in_dim(block, block.shape[dim] - width, None, axis=dim), axis, forward
        )
        high = lax.ppermute(lax.slice_in_dim(block, 0, width, axis=dim), axis, backward)
        block = jnp.concatenate([low, block, high], axis=dim)
    return block


def shifted(value, axis, steps):
    count = lax.axis_size(axis)
    leading, last = (max(0, -steps), min(count, count - steps))
    return lax.ppermute(value, axis, [(source, source + steps) for source in range(leading, last)])


def ahead(field, axis):
    widths = [(0, 0)] * field.ndim
    widths[axis] = (0, 1)
    return lax.slice_in_dim(jnp.pad(field, widths), 1, field.shape[axis] + 1, axis=axis)


def behind(field, axis):
    widths = [(0, 0)] * field.ndim
    widths[axis] = (1, 0)
    return lax.slice_in_dim(jnp.pad(field, widths), 0, field.shape[axis], axis=axis)


def fractions(offset_code):
    frac_x = ((offset_code % 4).astype(jnp.float32) + 0.5) * 0.25
    frac_y = ((offset_code // 4 % 4).astype(jnp.float32) + 0.5) * 0.25
    frac_z = ((offset_code // 16).astype(jnp.float32) + 0.5) * 0.25
    return (frac_x, frac_y, frac_z)


def corner_terms(state, frac_x, frac_y, frac_z, corner):
    step_x, step_y, step_z = corner
    weight_x = frac_x if step_x else 1.0 - frac_x
    weight_y = frac_y if step_y else 1.0 - frac_y
    weight_z = frac_z if step_z else 1.0 - frac_z
    weight = weight_x * weight_y * weight_z
    delta_x = step_x - frac_x
    delta_y = step_y - frac_y
    delta_z = step_z - frac_z
    moments = [
        weight
        * (
            state[comp]
            + state[3 + 3 * comp] * delta_x
            + state[4 + 3 * comp] * delta_y
            + state[5 + 3 * comp] * delta_z
        )
        for comp in range(3)
    ]
    return (weight, jnp.stack([weight] + moments))


def operate(field, fluid):
    masked = fluid * field
    padded = padded_2(masked, (("gx", 0), ("gy", 1)), 1)
    beside = (
        padded[2:, 1:-1]
        + padded[:-2, 1:-1]
        + padded[1:-1, 2:]
        + padded[1:-1, :-2]
        + ahead(masked, 2)
        + behind(masked, 2)
    )
    return fluid * (6.0 * field - beside) + (1.0 - fluid) * field


def precond_total(residual, precond):
    return lax.psum(jnp.sum(residual * precond), ("gx", "gy"))


def local(cell_index, offset_code, particle_state, fluid_flags):
    width_x, width_y, depth = fluid_flags.shape
    cells = cell_index[0]
    count = cells.shape[0]
    shape_cells = (width_x, width_y, depth)
    state_cells = (
        jnp.zeros((12, count), jnp.float32)
        .at[:, cells]
        .set(particle_state[0])
        .reshape((12,) + shape_cells)
    )
    code_cells = jnp.zeros((count,), jnp.int32).at[cells].set(offset_code[0]).reshape(shape_cells)
    frac_x, frac_y, frac_z = fractions(code_cells)
    grid = jnp.zeros((4, width_x + 1, width_y + 1, depth + 1), jnp.float32)
    weights = []
    for corner in CORNERS:
        weight, terms = corner_terms(state_cells, frac_x, frac_y, frac_z, corner)
        weights.append(weight)
        grid = grid + jnp.pad(
            terms,
            (
                (0, 0),
                (corner[0], 1 - corner[0]),
                (corner[1], 1 - corner[1]),
                (corner[2], 1 - corner[2]),
            ),
        )
    arrived_x = shifted(grid[:, width_x], "gx", 1)
    grid = grid[:, :width_x].at[:, 0].add(arrived_x)
    arrived_y = shifted(grid[:, :, width_y], "gy", 1)
    grid = grid[:, :, :width_y].at[:, :, 0].add(arrived_y)
    grid = grid[..., :depth]
    velocity = grid[1:] / jnp.maximum(grid[0], 0.5)
    fluid = fluid_flags.astype(jnp.float32)
    framed = padded_2(velocity, (("gx", 1), ("gy", 2)), 1)
    divergence = (
        0.5 * (framed[0, 2:, 1:-1] - framed[0, :-2, 1:-1])
        + 0.5 * (framed[1, 1:-1, 2:] - framed[1, 1:-1, :-2])
        + 0.5 * (ahead(velocity[2], 2) - behind(velocity[2], 2))
    )
    rhs = -fluid * divergence
    inv_diag = 1.0 / (6.0 * fluid + (1.0 - fluid))
    pressure = jnp.zeros_like(rhs)
    residual = rhs
    precond = residual * inv_diag
    direction = precond
    norm_now = precond_total(residual, precond)
    for step in range(ITERS):
        image = operate(direction, fluid)
        alpha = norm_now / lax.psum(jnp.sum(direction * image), ("gx", "gy"))
        pressure = pressure + alpha * direction
        residual = residual - alpha * image
        if step + 1 < ITERS:
            precond = residual * inv_diag
            norm_next = precond_total(residual, precond)
            direction = precond + norm_next / norm_now * direction
            norm_now = norm_next
    framed_p = padded_2(pressure, (("gx", 0), ("gy", 1)), 1)
    slope_x = framed_p[2:, 1:-1] - framed_p[:-2, 1:-1]
    slope_y = framed_p[1:-1, 2:] - framed_p[1:-1, :-2]
    slope_z = ahead(pressure, 2) - behind(pressure, 2)
    projected = jnp.stack(
        [
            fluid * (velocity[0] - 0.5 * slope_x),
            fluid * (velocity[1] - 0.5 * slope_y),
            fluid * (velocity[2] - 0.5 * slope_z),
        ]
    )
    upper_x = shifted(projected[:, 0:1], "gx", -1)
    extended = jnp.concatenate([projected, upper_x], axis=1)
    upper_y = shifted(extended[:, :, 0:1], "gy", -1)
    extended = jnp.concatenate([extended, upper_y], axis=2)
    extended = jnp.concatenate(
        [extended, jnp.zeros(extended.shape[:3] + (1,), jnp.float32)], axis=3
    )
    result_cells = jnp.zeros((3,) + shape_cells, jnp.float32)
    for corner, weight in zip(CORNERS, weights):
        window = extended[
            :,
            corner[0] : corner[0] + width_x,
            corner[1] : corner[1] + width_y,
            corner[2] : corner[2] + depth,
        ]
        result_cells = result_cells + weight * window
    result = result_cells.reshape(3, count)[:, cells]
    return (pressure, result[None])


def solution(mesh):
    return jax.shard_map(
        local,
        mesh=mesh,
        in_specs=(
            P(("groups", "gx", "gy"), None),
            P(("groups", "gx", "gy"), None),
            P(("groups", "gx", "gy"), None, None),
            P(("groups", "gx"), "gy", None),
        ),
        out_specs=(P(("groups", "gx"), "gy", None), P(("groups", "gx", "gy"), None, None)),
        check_vma=False,
    )
```

profile of v0, /device:TPU:0, one launch (start us, length us, event | category | flops | bytes accessed | tf_op | source)
XLA Modules:
  0.0 770.8 jit_solution(8922711065402307797)
XLA Ops:
  0.6 1.0 compare_select_fusion
  1.7 10.9 %copy.24 = f32[1,12,32768]{1,2,0:T(8,128)} copy(f32[1,12,32768]{2,0,1:T(1,128)} %param.10) | data formatting | bytes 3145728 | tf_op jit(solution)/shard_map/squeeze | solution.py:98
  12.6 88.2 %scatter_custom_fusion.1 = f32[12,32768]{0,1:T(8,128)} fusion(s32[32768]{0:T(1024)S(1)} %bitcast.62, f32[1,12,32768]{1,2,0:T(8,128)} %copy.24, f32[]{:T(128)} %constant.110.clone.1), kind=kCustom, calls=%fused_computation.15 | custom fusion | bytes 3145732 | tf_op jit(solution)/shard_map/scatter | solution.py:98
  100.8 141.4 %slice_reduce_fusion.9 = (f32[32768]{0:T(1024)S(1)}, f32[32768]{0:T(1024)S(1)}, f32[32768]{0:T(1024)S(1)}, f32[32768]{0:T(1024)S(1)}, f32[32768]{0:T(1024)S(1)},...) fusion(f32[12,32768]{0,1:T(8,128)} %scatter_custom_fusion.1), kind=kLoop, calls=%fused_computation.12 | loop fusion | bytes 3145728 | tf_op jit(solution)/shard_map/slice | solution.py:64
  242.3 120.6 %scatter_custom_fusion = s32[32768]{0:T(1024)S(1)} fusion(s32[32768]{0:T(1024)S(1)} %bitcast.63, s32[32768]{0:T(1024)} %bitcast.66, s32[]{:T(128)} %constant.100.clone.1), kind=kCustom, calls=%fused_computation.321 | custom fusion | bytes 131584 | tf_op jit(solution)/shard_map/scatter | solution.py:101
  363.3 0.3 add_multiply_fusion.23
  363.6 0.2 add_multiply_fusion.17
  363.9 0.4 add_multiply_fusion.14
  364.2 0.3 add_multiply_fusion.10
  364.7 8.9 %fusion.3 = f32[4,17,9,257]{3,2,1,0:T(8,128)S(1)} fusion(f32[1,16,8,256]{3,2,1,0:T(8,128)S(1)} %get-tuple-element.130, f32[1,16,8,256]{3,2,1,0:T(8,128)S(1)} %get-tuple-element.133, f32[1,16,8,256]{3,2,1,0:T(8,128)S(1)} %get-tuple-element.105, f32[1,16,8,256]{3,2,1,0:T(8,128)S(1)} %get-tuple-element.106, f32[1,16,8,256]{3,2,1,0:T(8,128)S(1)} %get-tuple-element.135, ...), kind=kLoop, calls=%fused_computation.19 | loop fusion | flops 22806180 | bytes 4823440 | tf_op jit(solution)/shard_map/add | solution.py:108
  373.6 2.4 collective-permute-start
  376.1 0.8 collective-permute-done
  377.1 4.3 collective-permute-start.1
  381.5 2.1 collective-permute-done.1
  383.7 0.9 scatter-add.9
  384.7 1.3 collective-permute-start.2
  386.0 4.1 collective-permute-start.3
  390.2 0.8 collective-permute-done.3
  391.1 1.3 collective-permute-start.4
  392.4 4.6 collective-permute-start.5
  397.2 1.6 collective-permute-done.5
  399.0 1.3 collective-permute-start.6
  400.3 5.3 collective-permute-start.7
  405.6 0.8 collective-permute-done.7
  406.5 1.3 collective-permute-start.8
  407.8 4.6 collective-permute-start.9
  412.4 1.4 collective-permute-done.9
  413.8 0.8 multiply_reduce_fusion.3
  414.6 37.3 %all-reduce.19 = (f32[]{:T(128)}, f32[]{:T(128)}) all-reduce(f32[]{:T(128)} %get-tuple-element.43, f32[]{:T(128)} %get-tuple-element.42), channel_id=1, replica_groups=mesh['groups'=2,'gx'=4,'gy'=4] {'gx','gy'}, use_global_device_ids=true, to_apply=%region_3.4 | all-reduce | flops 2 | bytes 16 | tf_op jit(solution)/shard_map/psum | solution.py:87
  453.2 0.7 multiply_reduce_fusion.2
  453.8 30.3 %psum.44 = f32[]{:T(128)} all-reduce(f32[]{:T(128)} %get-tuple-element.52), channel_id=1, replica_groups=mesh['groups'=2,'gx'=4,'gy'=4] {'gx','gy'}, use_global_device_ids=true, to_apply=%region_7.8 | all-reduce | flops 1 | bytes 8 | tf_op jit(solution)/shard_map/psum | solution.py:87
  485.5 1.3 collective-permute-start.10
  486.8 3.0 collective-permute-start.11
  489.9 0.8 collective-permute-done.11
  490.7 1.3 collective-permute-start.12
  492.0 4.8 collective-permute-start.13
  496.8 1.4 collective-permute-done.13
  498.2 0.8 multiply_reduce_fusion.1
  499.0 33.0 %psum.45 = f32[]{:T(128)} all-reduce(f32[]{:T(128)} %get-tuple-element.48), channel_id=1, replica_groups=mesh['groups'=2,'gx'=4,'gy'=4] {'gx','gy'}, use_global_device_ids=true, to_apply=%region_9.10 | all-reduce | flops 1 | bytes 8 | tf_op jit(solution)/shard_map/psum | solution.py:139
  533.4 0.7 multiply_reduce_fusion
  534.0 30.3 %psum.46 = f32[]{:T(128)} all-reduce(f32[]{:T(128)} %multiply_reduce_fusion), channel_id=1, replica_groups=mesh['groups'=2,'gx'=4,'gy'=4] {'gx','gy'}, use_global_device_ids=true, to_apply=%region_11.12 | all-reduce | flops 1 | bytes 8 | tf_op jit(solution)/shard_map/psum | solution.py:87
  565.7 1.3 collective-permute-start.14
  567.0 3.0 collective-permute-start.15
  570.1 0.8 collective-permute-done.15
  570.9 1.3 collective-permute-start.16
  572.2 4.8 collective-permute-start.17
  577.0 1.4 collective-permute-done.17
  578.4 0.8 fusion.95
  579.2 34.2 %psum.47 = f32[]{:T(128)} all-reduce(f32[]{:T(128)} %fusion.95), channel_id=1, replica_groups=mesh['groups'=2,'gx'=4,'gy'=4] {'gx','gy'}, use_global_device_ids=true, to_apply=%region_13.14 | all-reduce | flops 1 | bytes 8 | tf_op jit(solution)/shard_map/psum | solution.py:139
  614.8 1.3 collective-permute-start.18
  616.1 3.0 collective-permute-start.19
  619.2 0.8 collective-permute-done.19
  620.0 1.3 collective-permute-start.20
  621.3 4.5 collective-permute-start.21
  625.9 1.4 collective-permute-done.21
  627.5 1.3 collective-permute-start.22
  628.9 2.3 collective-permute-done.22
  631.2 1.3 collective-permute-start.23
  632.5 0.3 subtract_multiply_fusion.12
  632.8 4.4 collective-permute-done.23
  637.3 0.5 fusion.17
  637.8 8.6 %copy.18 = f32[3,16,8,256]{0,3,2,1:T(8,128)} copy(f32[3,16,8,256]{3,2,1,0:T(8,128)S(1)} %fusion.17) | data formatting | bytes 786432 | tf_op jit(solution)/shard_map/add | solution.py:173
  646.5 113.9 %gather_fusion = f32[32768,3]{1,0:T(8,128)} fusion(f32[3,32768]{0,1:T(8,128)} %bitcast.60, s32[32768]{0:T(1024)S(1)} %broadcast_clamp_fusion), kind=kCustom, calls=%fused_computation | custom fusion | bytes 917504 | tf_op jit(solution)/shard_map/gather | solution.py:174
  760.4 10.4 %copy.19 = f32[1,3,32768]{2,0,1:T(1,128)} copy(f32[1,3,32768]{1,2,0:T(8,128)} %bitcast.61) | data formatting | bytes 786432
  (60 shorter events, 2.2 us)
Async XLA Ops:
  373.6 3.3 collective-permute-start
  377.1 6.5 collective-permute-start.1
  381.4 17.4 %copy-start = (s32[16,8,256]{2,1,0:T(8,128)S(1)}, s32[16,8,256]{2,1,0:T(8,128)}, u32[]{:S(2)}) copy-start(s32[16,8,256]{2,1,0:T(8,128)} %param.11) | copy-start | bytes 393220
  384.7 5.5 collective-permute-start.2
  386.0 5.0 collective-permute-start.3
  391.1 6.1 collective-permute-start.4
  392.4 6.4 collective-permute-start.5
  399.0 6.6 collective-permute-start.6
  400.3 6.1 collective-permute-start.7
  406.5 5.9 collective-permute-start.8
  407.8 6.0 collective-permute-start.9
  485.5 4.3 collective-permute-start.10
  486.8 3.8 collective-permute-start.11
  490.7 6.1 collective-permute-start.12
  492.0 6.2 collective-permute-start.13
  565.7 4.3 collective-permute-start.14
  567.0 3.8 collective-permute-start.15
  570.9 6.1 collective-permute-start.16
  572.2 6.2 collective-permute-start.17
  614.8 18.0 %copy-start.1 = (f32[16,8,256]{2,1,0:T(8,128)}, f32[16,8,256]{2,1,0:T(8,128)S(1)}, u32[]{:S(2)}) copy-start(f32[16,8,256]{2,1,0:T(8,128)S(1)} %multiply_add_fusion) | copy-start | bytes 393220
  614.8 4.3 collective-permute-start.18
  616.1 3.8 collective-permute-start.19
  620.0 5.9 collective-permute-start.20
  621.3 6.0 collective-permute-start.21
  627.5 3.7 collective-permute-start.22
  631.2 6.0 collective-permute-start.23
where the time goes:
time: 775 us; the launch traced here: 771 us
  local copies, waits for them, and re-layouts  496 us (64%)
  blocking collectives  165 us (21%)
  starting transfers between devices  64.1 us (8%)
  waiting for transfers between devices  21.1 us (3%)
  other arithmetic  16.6 us (2%)
  between operations  8 us (1%)
    slice x1, local copies, waits for them, and re-layouts, corner_terms(): state[4 + 3 * comp] * delta_y  141 us
    scatter x1, local copies, waits for them, and re-layouts, local(): jnp.zeros((count,), jnp.int32).at[cells].set(offset_code[0])  121 us
    gather x1, local copies, waits for them, and re-layouts, local(): result = result_cells.reshape(3, count)[:, cells]  114 us
    psum x3, blocking collectives, precond_total(): return lax.psum(jnp.sum(residual * precond), ('gx', 'gy'))  97.8 us
    scatter x1, local copies, waits for them, and re-layouts, local(): state_cells = jnp.zeros((12, count), jnp.float32).at[:, cells].set(partic...  88.2 us
    psum x2, blocking collectives, local(): alpha = norm_now / lax.psum(jnp.sum(direction * image), ('gx', 'gy'))  67.3 us
    ppermute x10, starting transfers between devices, padded_2(): lax.ppermute(lax.slice_in_dim(block, block.shape[dim] - width, None, axis...  41.9 us
  transfers between devices with their start and end apart: 24, of which 15 were waited for; matrix products, arithmetic and copies ran while one was open for 0% of the time, Pallas kernels for 0%

commit v1 on v0

--- a/solution.py
+++ b/solution.py
@@ -1,7 +1,218 @@
+import functools
+
 import jax
 import jax.numpy as jnp
 from jax import lax
+from jax.experimental import pallas as pl
+from jax.experimental.pallas import tpu as pltpu
 from jax.sharding import PartitionSpec as P
+
+F32, I32 = jnp.float32, jnp.int32
+CX, CY, CELLS = 16, 8, 32768
+TILES = CELLS // 1024
+LANE_RUNS, SUB_RUNS, SWAPS = 9, 8, 15 * 16
+VMEM = 48 * 2**20
+
+
+def take(x, index, axis):
+    other = tuple(d for d in range(x.ndim) if d != axis)
+    dims = lax.GatherDimensionNumbers(
+        offset_dims=(),
+        collapsed_slice_dims=(axis,),
+        start_index_map=(axis,),
+        operand_batching_dims=other,
+        start_indices_batching_dims=other,
+    )
+    return lax.gather(
+        x, index[..., None], dims, (1,) * x.ndim, mode=lax.GatherScatterMode.PROMISE_IN_BOUNDS
+    )
+
+
+def iota(shape, dim):
+    return lax.broadcasted_iota(I32, shape, dim)
+
+
+def sort_plan(key, lane_ref, sub_ref, swap_ref):
+    lanes, subs = iota((64, 128), 1), iota((8, 128), 0)
+    zero = jnp.zeros((8, 128), I32)
+
+    def flip(phase, tile):
+        if phase < 7:
+            return jnp.where(iota((8, 128), 1) & (1 << phase) != 0, 0x7FFF, zero)
+        if phase < 10:
+            return jnp.where(subs & (1 << (phase - 7)) != 0, 0x7FFF, zero)
+        if phase < 15 and tile >> (phase - 10) & 1:
+            return zero + 0x7FFF
+        return zero
+
+    def lane_steps(groups, top):
+        stride = top
+        while stride:
+            low = lanes & stride == 0
+            other = [take(g, lanes ^ stride, 1) for g in groups]
+            groups = [
+                jnp.where(low, jnp.minimum(g, o), jnp.maximum(g, o)) for g, o in zip(groups, other)
+            ]
+            stride //= 2
+        return groups
+
+    def grouped(tiles):
+        return [jnp.concatenate(tiles[8 * i : 8 * i + 8], axis=0) for i in range(4)]
+
+    def lane_run(run, tiles, phases):
+        groups = [(g << 7) | lanes for g in grouped(tiles)]
+        for phase in phases:
+            if len(phases) > 1:
+                turn = jnp.concatenate([flip(phase, 0) << 7] * 8, axis=0)
+                groups = [g ^ turn for g in groups]
+            groups = lane_steps(groups, 1 << min(phase - 1, 6))
+            if len(phases) > 1:
+                groups = [g ^ turn for g in groups]
+        for i, g in enumerate(groups):
+            lane_ref[run, 64 * i : 64 * i + 64] = g & 127
+        return [groups[i // 8][8 * (i % 8) : 8 * (i % 8) + 8] >> 7 for i in range(TILES)]
+
+    def sub_run(run, tiles, top):
+        tiles = [(t << 3) | subs for t in tiles]
+        stride = top
+        while stride:
+            low = subs & stride == 0
+            other = [take(t, subs ^ stride, 0) for t in tiles]
+            tiles = [jnp.where(low, jnp.minimum(t, o), jnp.maximum(t, o)) for t, o in zip(tiles, other)]
+            stride //= 2
+        for i, t in enumerate(tiles):
+            sub_ref[run, 8 * i : 8 * i + 8] = t & 7
+        return [t >> 3 for t in tiles]
+
+    odd = jnp.where(subs & 1 != 0, 0x7FFF, zero)
+    tiles = lane_run(0, key, range(1, 7))
+    tiles = [t ^ odd for t in tiles]
+    first = [lane_ref[0, 8 * i : 8 * i + 8] for i in range(TILES)]
+    groups = [(g << 7) | f for g, f in zip(grouped(tiles), grouped(first))]
+    groups = lane_steps(groups, 64)
+    for i, g in enumerate(groups):
+        lane_ref[0, 64 * i : 64 * i + 64] = g & 127
+    tiles = [(groups[i // 8][8 * (i % 8) : 8 * (i % 8) + 8] >> 7) ^ odd for i in range(TILES)]
+
+    swap = 0
+    for phase in range(8, 16):
+        turns = [flip(phase, i) for i in range(TILES)]
+        tiles = [t ^ f for t, f in zip(tiles, turns)]
+        stride = 1 << (phase - 1)
+        while stride >= 1024:
+            hop = stride // 1024
+            for i in range(TILES):
+                if i & hop == 0:
+                    a, b = tiles[i], tiles[i + hop]
+                    swap_ref[8 * swap : 8 * swap + 8] = jnp.where(a > b, 1, zero)
+                    swap += 1
+                    tiles[i], tiles[i + hop] = jnp.minimum(a, b), jnp.maximum(a, b)
+            stride //= 2
+        tiles = sub_run(phase - 8, tiles, min(stride, 512) // 128)
+        tiles = lane_run(phase - 7, tiles, [phase])
+        tiles = [t ^ f for t, f in zip(tiles, turns)]
+    return tiles
+
+
+def follow_plan(tiles, lane_ref, sub_ref, swap_ref):
+    tiles = [take(t, lane_ref[0, 8 * i : 8 * i + 8], 1) for i, t in enumerate(tiles)]
+    swap = 0
+    for phase in range(8, 16):
+        stride = 1 << (phase - 1)
+        while stride >= 1024:
+            hop = stride // 1024
+            for i in range(TILES):
+                if i & hop == 0:
+                    a, b = tiles[i], tiles[i + hop]
+                    crossed = swap_ref[8 * swap : 8 * swap + 8] != 0
+                    swap += 1
+                    tiles[i], tiles[i + hop] = jnp.where(crossed, b, a), jnp.where(crossed, a, b)
+            stride //= 2
+        tiles = [take(t, sub_ref[phase - 8, 8 * i : 8 * i + 8], 0) for i, t in enumerate(tiles)]
+        tiles = [take(t, lane_ref[phase - 7, 8 * i : 8 * i + 8], 1) for i, t in enumerate(tiles)]
+    return tiles
+
+
+def plan_scratch():
+    return [
+        pltpu.VMEM((LANE_RUNS, CELLS // 128, 128), I32),
+        pltpu.VMEM((SUB_RUNS, CELLS // 128, 128), I32),
+        pltpu.VMEM((8 * SWAPS, 128), I32),
+    ]
+
+
+def split_tiles(array):
+    return [array[8 * i : 8 * i + 8] for i in range(TILES)]
+
+
+def to_cells_kernel(cell_ref, code_ref, state_ref, cells_ref, tag_ref, rows, lane_ref, sub_ref, swap_ref):
+    def unpack(t, carry):
+        low = pl.multiple_of(t * 128, 128)
+        at = pl.multiple_of(t * 8, 8)
+        rows[0, pl.ds(at, 8), :] = state_ref[0, 0:8, pl.ds(low, 128)]
+        rows[1, pl.ds(at, 4), :] = state_ref[0, 8:12, pl.ds(low, 128)]
+        return carry
+
+    lax.fori_loop(0, CELLS // 128, unpack, 0, unroll=8)
+    cell = cell_ref[...]
+    key = (cell & ~0x780) | ((cell & 0x80) << 3) | ((cell & 0x700) >> 1)
+    sort_plan(split_tiles(key), lane_ref, sub_ref, swap_ref)
+    tag = (code_ref[...] << 15) | (iota((256, 128), 0) * 128 + iota((256, 128), 1))
+    for i, t in enumerate(follow_plan(split_tiles(tag), lane_ref, sub_ref, swap_ref)):
+        tag_ref[8 * i : 8 * i + 8] = t
+
+    def move(c, carry):
+        half, place = c >> 3, c & 7
+        tiles = [rows[half, pl.ds(place + 64 * i, 8, stride=8), :] for i in range(TILES)]
+        for i, t in enumerate(follow_plan(tiles, lane_ref, sub_ref, swap_ref)):
+            cells_ref[c, 8 * i : 8 * i + 8] = t
+        return carry
+
+    lax.fori_loop(0, 12, move, 0)
+
+
+def to_cells(cell, code, state):
+    return pl.pallas_call(
+        to_cells_kernel,
+        out_shape=(
+            jax.ShapeDtypeStruct((12, 256, 128), F32),
+            jax.ShapeDtypeStruct((256, 128), I32),
+        ),
+        scratch_shapes=[pltpu.VMEM((2, 2048, 128), F32)] + plan_scratch(),
+        compiler_params=pltpu.CompilerParams(vmem_limit_bytes=VMEM),
+        name="to_cells",
+    )(cell, code, state)
+
+
+def to_particles_kernel(tag_ref, value_ref, out_ref, rows, lane_ref, sub_ref, swap_ref):
+    sort_plan(split_tiles(tag_ref[...] & 0x7FFF), lane_ref, sub_ref, swap_ref)
+
+    def move(c, carry):
+        tiles = [value_ref[c, 8 * i : 8 * i + 8] for i in range(TILES)]
+        for i, t in enumerate(follow_plan(tiles, lane_ref, sub_ref, swap_ref)):
+            rows[pl.ds(c + 64 * i, 8, stride=8), :] = t
+        return carry
+
+    lax.fori_loop(0, 3, move, 0)
+
+    def pack(t, carry):
+        low = pl.multiple_of(t * 128, 128)
+        at = pl.multiple_of(t * 8, 8)
+        out_ref[0, :, pl.ds(low, 128)] = rows[pl.ds(at, 3), :]
+        return carry
+
+    lax.fori_loop(0, CELLS // 128, pack, 0, unroll=8)
+
+
+def to_particles(tag, values):
+    return pl.pallas_call(
+        to_particles_kernel,
+        out_shape=jax.ShapeDtypeStruct((1, 3, CELLS), F32),
+        scratch_shapes=[pltpu.VMEM((2048, 128), F32)] + plan_scratch(),
+        compiler_params=pltpu.CompilerParams(vmem_limit_bytes=VMEM),
+        name="to_particles",
+    )(tag, values)
+
 
 ITERS = 3
 
@@ -89,16 +300,18 @@
 
 def local(cell_index, offset_code, particle_state, fluid_flags):
     width_x, width_y, depth = fluid_flags.shape
-    cells = cell_index[0]
-    count = cells.shape[0]
     shape_cells = (width_x, width_y, depth)
-    state_cells = (
-        jnp.zeros((12, count), jnp.float32)
-        .at[:, cells]
-        .set(particle_state[0])
-        .reshape((12,) + shape_cells)
-    )
-    code_cells = jnp.zeros((count,), jnp.int32).at[cells].set(offset_code[0]).reshape(shape_cells)
+    moved, tag = to_cells(
+        cell_index.reshape(256, 128), offset_code.reshape(256, 128), particle_state
+    )
+
+    def unfold(tiles):
+        return jnp.moveaxis(tiles.reshape(tiles.shape[:-2] + (CX, 2, CY, 128)), -3, -2).reshape(
+            tiles.shape[:-2] + shape_cells
+        )
+
+    state_cells = unfold(moved)
+    code_cells = unfold(tag) >> 15
     frac_x, frac_y, frac_z = fractions(code_cells)
     grid = jnp.zeros((4, width_x + 1, width_y + 1, depth + 1), jnp.float32)
     weights = []
@@ -171,8 +384,8 @@
             corner[2] : corner[2] + depth,
         ]
         result_cells = result_cells + weight * window
-    result = result_cells.reshape(3, count)[:, cells]
-    return (pressure, result[None])
+    folded = jnp.moveaxis(result_cells.reshape(3, CX, CY, 2, 128), 3, 2).reshape(3, 256, 128)
+    return (pressure, to_particles(tag, folded))
 
 
 def solution(mesh):

time: 775 us -> 312 us (0.40)
  local copies, waits for them, and re-layouts: 496 us -> 4.96 us
  Pallas kernels: 0 us -> 29.1 us
    scatter x2 -> x0, local copies, waits for them, and re-layouts: 209 us -> none  [the longest x1 121 us: local(): jnp.zeros((count,), jnp.int32).at[cells].set(offset_code[0])]
    slice x1 -> x0, local copies, waits for them, and re-layouts: 141 us -> none  [corner_terms(): state[4 + 3 * comp] * delta_y]
    gather x1 -> x0, local copies, waits for them, and re-layouts: 114 us -> none  [local(): result = result_cells.reshape(3, count)[:, cells]]
    pallas_call x0 -> x2, Pallas kernels: none -> 29.1 us  [the longest x1 19.1 us: to_cells(): pl.pallas_call(to_cells_kernel, out_shape=(jax.ShapeDtypeStruct((12, 256,...]
    squeeze x13 -> x0, local copies, waits for them, and re-layouts: 11.4 us -> none  [the longest x1 10.9 us: local(): particle_state[0]]
    add x1 -> x0, local copies, waits for them, and re-layouts: 8.63 us -> none  [local(): result_cells = result_cells + weight * window]
where the time goes in v1:
time: 312 us; the launch traced here: 308 us
  blocking collectives  165 us (53%)
  starting transfers between devices  64.3 us (21%)
  Pallas kernels  29.1 us (9%)
  waiting for transfers between devices  21 us (7%)
  other arithmetic  15.5 us (5%)
  between operations  7.91 us (3%)
  local copies, waits for them, and re-layouts  4.96 us (2%)
    psum x3, blocking collectives, precond_total(): return lax.psum(jnp.sum(residual * precond), ('gx', 'gy'))  97.8 us
    psum x2, blocking collectives, local(): alpha = norm_now / lax.psum(jnp.sum(direction * image), ('gx', 'gy'))  67.3 us
    ppermute x10, starting transfers between devices, padded_2(): lax.ppermute(lax.slice_in_dim(block, block.shape[dim] - width, None, axis...  42.1 us
    pallas_call x1, Pallas kernels, to_cells(): pl.pallas_call(to_cells_kernel, out_shape=(jax.ShapeDtypeStruct((12, 256,...  19.1 us
    ppermute x10, starting transfers between devices, padded_2(): lax.ppermute(lax.slice_in_dim(block, 0, width, axis=dim), axis, backward)  12.9 us
    ppermute x10, waiting for transfers between devices, padded_2(): lax.ppermute(lax.slice_in_dim(block, block.shape[dim] - width, None, axis...  11.2 us
    pallas_call x1, Pallas kernels, to_particles(): pl.pallas_call(to_particles_kernel, out_shape=jax.ShapeDtypeStruct((1, 3,...  9.98 us
    ppermute x4, waiting for transfers between devices, shifted(): lax.ppermute(value, axis, [(source, source + steps) for source in range(l...  9.63 us
  transfers between devices with their start and end apart: 24, of which 15 were waited for; matrix products, arithmetic and copies ran while one was open for 0% of the time, Pallas kernels for 0%

profile of v1, /device:TPU:0, one launch (start us, length us, event | category | flops | bytes accessed | tf_op | source)
XLA Modules:
  0.0 307.9 jit_solution(16660191252246313806)
XLA Ops:
  0.6 2.4 copy.6.state_ref
  3.1 19.1 %to_cells.1 = (f32[12,256,128]{2,1,0:T(8,128)S(1)}, s32[256,128]{1,0:T(8,128)S(1)}) custom-call(s32[256,128]{1,0:T(8,128)S(1)} %bitcast.163, s32[256,128]{1,0:T(8,128)S(1)} %bitcast.164, f32[1,12,32768]{2,1,0:T(8,128)S(1)} %copy.6.state_ref), custom_call_target="tpu_custom_call" | custom-call | tf_op jit(solution)/shard_map/to_cells/pallas_call | solution.py:175
  22.2 0.3 add_multiply_fusion.23
  22.5 0.4 add_multiply_fusion.22
  22.9 0.2 add_multiply_fusion.14
  23.1 0.3 add_multiply_fusion.10
  23.4 0.2 add_multiply_fusion.12
  23.6 8.9 %fusion = f32[4,17,9,257]{3,2,1,0:T(8,128)S(1)} fusion(f32[1,16,8,256]{3,2,1,0:T(8,128)S(1)} %get-tuple-element.141, f32[1,16,8,256]{3,2,1,0:T(8,128)S(1)} %get-tuple-element.144, f32[1,16,8,256]{3,2,1,0:T(8,128)S(1)} %get-tuple-element.126, f32[1,16,8,256]{3,2,1,0:T(8,128)S(1)} %get-tuple-element.127, f32[1,16,8,256]{3,2,1,0:T(8,128)S(1)} %get-tuple-element.146, ...), kind=kLoop, calls=%fused_computation.1 | loop fusion | flops 22806180 | bytes 4823440 | tf_op jit(solution)/shard_map/add | solution.py:321
  32.5 2.4 collective-permute-start
  35.0 0.8 collective-permute-done
  36.0 4.3 %collective-permute-start.1 = (f32[4,16,257]{2,1,0:T(8,128)S(1)}, f32[4,16,257]{2,1,0:T(8,128)S(1)}, u32[]{:S(2)}, u32[]{:S(2)}) collective-permute-start(f32[4,16,257]{2,1,0:T(8,128)S(1)} %bitcast.170), channel_id=1, source_target_pairs={{0,1},{1,2},{2,3},{4,5},{5,6},{6,7},{8,9},{9,10},{10,11},{12,13},{... | collective-permute-start | bytes 197384 | tf_op jit(solution)/shard_map/ppermute | solution.py:239
  40.4 2.1 collective-permute-done.1
  42.6 0.9 scatter-add.9
  43.6 1.3 collective-permute-start.2
  44.9 4.1 %collective-permute-start.3 = (f32[3,1,8,256]{3,2,1,0:T(8,128)S(1)}, f32[3,1,8,256]{3,2,1,0:T(8,128)S(1)}, u32[]{:S(2)}, u32[]{:S(2)}) collective-permute-start(f32[3,1,8,256]{3,2,1,0:T(8,128)S(1)} %get-tuple-element.134), channel_id=1, source_target_pairs={{0,4},{4,8},{8,12},{1,5},{5,9},{9,13},{2,6},{6,10},{10,14},{3,7},{... | collective-permute-start | bytes 73736 | tf_op jit(solution)/shard_map/ppermute | solution.py:228
  49.1 0.8 collective-permute-done.3
  50.0 1.3 collective-permute-start.4
  51.3 4.6 %collective-permute-start.5 = (f32[3,18,1,256]{3,2,1,0:T(1,128)S(1)}, f32[3,18,1,256]{3,2,1,0:T(1,128)S(1)}, u32[]{:S(2)}, u32[]{:S(2)}) collective-permute-start(f32[3,18,1,256]{3,2,1,0:T(1,128)S(1)} %get-tuple-element.133), channel_id=1, source_target_pairs={{0,1},{1,2},{2,3},{4,5},{5,6},{6,7},{8,9},{9,10},{10,11},{12,13},{... | collective-permute-start | bytes 165896 | tf_op jit(solution)/shard_map/ppermute | solution.py:228
  56.0 0.2 collective-permute-done.4
  56.1 1.6 collective-permute-done.5
  57.7 0.1 convert_multiply_fusion.2
  57.9 1.3 collective-permute-start.6
  59.2 5.3 %collective-permute-start.7 = (f32[1,8,256]{2,1,0:T(8,128)S(1)}, f32[1,8,256]{2,1,0:T(8,128)S(1)}, u32[]{:S(2)}, u32[]{:S(2)}) collective-permute-start(f32[1,8,256]{2,1,0:T(8,128)S(1)} %get-tuple-element.170), channel_id=1, source_target_pairs={{0,4},{4,8},{8,12},{1,5},{5,9},{9,13},{2,6},{6,10},{10,14},{3,7},{... | collective-permute-start | bytes 24584 | tf_op jit(solution)/shard_map/ppermute | solution.py:228
  64.5 0.8 collective-permute-done.7
  65.4 1.3 collective-permute-start.8
  66.7 4.8 %collective-permute-start.9 = (f32[18,1,256]{2,1,0:T(1,128)S(1)}, f32[18,1,256]{2,1,0:T(1,128)S(1)}, u32[]{:S(2)}, u32[]{:S(2)}) collective-permute-start(f32[18,1,256]{2,1,0:T(1,128)S(1)} %get-tuple-element.155), channel_id=1, source_target_pairs={{0,1},{1,2},{2,3},{4,5},{5,6},{6,7},{8,9},{9,10},{10,11},{12,13},{... | collective-permute-start | bytes 55304 | tf_op jit(solution)/shard_map/ppermute | solution.py:228
  71.4 1.3 collective-permute-done.9
  72.7 0.8 multiply_reduce_fusion.3
  73.5 37.3 %all-reduce.19 = (f32[]{:T(128)}, f32[]{:T(128)}) all-reduce(f32[]{:T(128)} %get-tuple-element.33, f32[]{:T(128)} %get-tuple-element.32), channel_id=1, replica_groups=mesh['groups'=2,'gx'=4,'gy'=4] {'gx','gy'}, use_global_device_ids=true, to_apply=%region_1.2 | all-reduce | flops 2 | bytes 16 | tf_op jit(solution)/shard_map/psum | solution.py:298
  112.1 0.7 multiply_reduce_fusion.2
  112.7 30.3 %psum.44 = f32[]{:T(128)} all-reduce(f32[]{:T(128)} %get-tuple-element.42), channel_id=1, replica_groups=mesh['groups'=2,'gx'=4,'gy'=4] {'gx','gy'}, use_global_device_ids=true, to_apply=%region_5.6 | all-reduce | flops 1 | bytes 8 | tf_op jit(solution)/shard_map/psum | solution.py:298
  144.4 1.3 collective-permute-start.10
  145.7 3.0 collective-permute-start.11
  148.8 0.8 collective-permute-done.11
  149.6 1.3 collective-permute-start.12
  150.9 4.8 %collective-permute-start.13 = (f32[18,1,256]{2,1,0:T(1,128)S(1)}, f32[18,1,256]{2,1,0:T(1,128)S(1)}, u32[]{:S(2)}, u32[]{:S(2)}) collective-permute-start(f32[18,1,256]{2,1,0:T(1,128)S(1)} %get-tuple-element.153), channel_id=1, source_target_pairs={{0,1},{1,2},{2,3},{4,5},{5,6},{6,7},{8,9},{9,10},{10,11},{12,13},{... | collective-permute-start | bytes 55304 | tf_op jit(solution)/shard_map/ppermute | solution.py:228
  155.7 1.4 collective-permute-done.13
  157.1 0.8 multiply_reduce_fusion.1
  157.9 33.0 %psum.45 = f32[]{:T(128)} all-reduce(f32[]{:T(128)} %get-tuple-element.38), channel_id=1, replica_groups=mesh['groups'=2,'gx'=4,'gy'=4] {'gx','gy'}, use_global_device_ids=true, to_apply=%region_7.8 | all-reduce | flops 1 | bytes 8 | tf_op jit(solution)/shard_map/psum | solution.py:352
  192.3 0.7 multiply_reduce_fusion
  192.9 30.3 %psum.46 = f32[]{:T(128)} all-reduce(f32[]{:T(128)} %multiply_reduce_fusion), channel_id=1, replica_groups=mesh['groups'=2,'gx'=4,'gy'=4] {'gx','gy'}, use_global_device_ids=true, to_apply=%region_9.10 | all-reduce | flops 1 | bytes 8 | tf_op jit(solution)/shard_map/psum | solution.py:298
  224.6 1.3 collective-permute-start.14
  225.9 3.0 collective-permute-start.15
  229.0 0.8 collective-permute-done.15
  229.8 1.3 collective-permute-start.16
  231.1 4.8 %collective-permute-start.17 = (f32[18,1,256]{2,1,0:T(1,128)S(1)}, f32[18,1,256]{2,1,0:T(1,128)S(1)}, u32[]{:S(2)}, u32[]{:S(2)}) collective-permute-start(f32[18,1,256]{2,1,0:T(1,128)S(1)} %get-tuple-element.151), channel_id=1, source_target_pairs={{0,1},{1,2},{2,3},{4,5},{5,6},{6,7},{8,9},{9,10},{10,11},{12,13},{... | collective-permute-start | bytes 55304 | tf_op jit(solution)/shard_map/ppermute | solution.py:228
  235.9 1.4 collective-permute-done.17
  237.3 0.8 fusion.92
  238.1 34.2 %psum.47 = f32[]{:T(128)} all-reduce(f32[]{:T(128)} %fusion.92), channel_id=1, replica_groups=mesh['groups'=2,'gx'=4,'gy'=4] {'gx','gy'}, use_global_device_ids=true, to_apply=%region_11.12 | all-reduce | flops 1 | bytes 8 | tf_op jit(solution)/shard_map/psum | solution.py:352
  273.7 1.3 collective-permute-start.18
  275.0 3.0 collective-permute-start.19
  278.1 0.8 collective-permute-done.19
  278.9 1.3 collective-permute-start.20
  280.2 4.5 %collective-permute-start.21 = (f32[18,1,256]{2,1,0:T(1,128)S(1)}, f32[18,1,256]{2,1,0:T(1,128)S(1)}, u32[]{:S(2)}, u32[]{:S(2)}) collective-permute-start(f32[18,1,256]{2,1,0:T(1,128)S(1)} %get-tuple-element.149), channel_id=1, source_target_pairs={{0,1},{1,2},{2,3},{4,5},{5,6},{6,7},{8,9},{9,10},{10,11},{12,13},{... | collective-permute-start | bytes 55304 | tf_op jit(solution)/shard_map/ppermute | solution.py:228
  284.8 1.4 collective-permute-done.21
  286.2 0.1 fusion.75
  286.4 1.3 collective-permute-start.22
  287.7 2.4 collective-permute-done.22
  290.1 1.3 collective-permute-start.23
  291.4 0.3 subtract_multiply_fusion.6
  291.8 4.4 %collective-permute-done.23 = f32[3,17,1,256]{3,2,1,0:T(1,128)S(1)} collective-permute-done((f32[3,17,1,256]{3,2,1,0:T(1,128)S(1)}, f32[3,17,1,256]{3,2,1,0:T(1,128)S(1)}, u32[]{:S(2)}, u32[]{:S(2)}) %collective-permute-start.23) | collective-permute-done | bytes 52256 | tf_op jit(solution)/shard_map/ppermute | solution.py:239
  296.2 0.5 fusion.14
  296.7 10.0 %to_particles.1 = f32[1,3,32768]{2,1,0:T(4,128)S(1)} custom-call(s32[256,128]{1,0:T(8,128)S(1)} %get-tuple-element.28.tag_ref, f32[3,256,128]{2,1,0:T(8,128)S(1)} %bitcast.162), custom_call_target="tpu_custom_call" | custom-call | tf_op jit(solution)/shard_map/to_particles/pallas_call | solution.py:208
  306.7 1.2 copy.11
  (46 shorter events, 1.1 us)
Async XLA Ops:
  0.6 2.4 copy-start
  0.6 2.4 copy-start.1
  32.5 3.3 %collective-permute-start = (f32[4,9,257]{2,1,0:T(8,128)S(1)}, f32[4,9,257]{2,1,0:T(8,128)S(1)}, u32[]{:S(2)}, u32[]{:S(2)}) collective-permute-start(f32[4,9,257]{2,1,0:T(8,128)S(1)} %slice_bitcast_fusion.15), channel_id=1, source_target_pairs={{0,4},{4,8},{8,12},{1,5},{5,9},{9,13},{2,6},{6,10},{10,14},{3,7},{... | collective-permute-start | bytes 111032 | tf_op jit(solution)/shard_map/ppermute | solution.py:239
  36.0 6.5 %collective-permute-start.1 = (f32[4,16,257]{2,1,0:T(8,128)S(1)}, f32[4,16,257]{2,1,0:T(8,128)S(1)}, u32[]{:S(2)}, u32[]{:S(2)}) collective-permute-start(f32[4,16,257]{2,1,0:T(8,128)S(1)} %bitcast.170), channel_id=1, source_target_pairs={{0,1},{1,2},{2,3},{4,5},{5,6},{6,7},{8,9},{9,10},{10,11},{12,13},{... | collective-permute-start | bytes 197384 | tf_op jit(solution)/shard_map/ppermute | solution.py:239
  40.3 17.4 %copy-start.2 = (s32[16,8,256]{2,1,0:T(8,128)S(1)}, s32[16,8,256]{2,1,0:T(8,128)}, u32[]{:S(2)}) copy-start(s32[16,8,256]{2,1,0:T(8,128)} %param.11) | copy-start | bytes 393220
  43.6 5.5 %collective-permute-start.2 = (f32[3,1,8,256]{3,2,1,0:T(8,128)S(1)}, f32[3,1,8,256]{3,2,1,0:T(8,128)S(1)}, u32[]{:S(2)}, u32[]{:S(2)}) collective-permute-start(f32[3,1,8,256]{3,2,1,0:T(8,128)S(1)} %get-tuple-element.135), channel_id=1, source_target_pairs={{4,0},{8,4},{12,8},{5,1},{9,5},{13,9},{6,2},{10,6},{14,10},{7,3},{... | collective-permute-start | bytes 73736 | tf_op jit(solution)/shard_map/ppermute | solution.py:231
  44.9 5.0 %collective-permute-start.3 = (f32[3,1,8,256]{3,2,1,0:T(8,128)S(1)}, f32[3,1,8,256]{3,2,1,0:T(8,128)S(1)}, u32[]{:S(2)}, u32[]{:S(2)}) collective-permute-start(f32[3,1,8,256]{3,2,1,0:T(8,128)S(1)} %get-tuple-element.134), channel_id=1, source_target_pairs={{0,4},{4,8},{8,12},{1,5},{5,9},{9,13},{2,6},{6,10},{10,14},{3,7},{... | collective-permute-start | bytes 73736 | tf_op jit(solution)/shard_map/ppermute | solution.py:228
  50.0 6.1 %collective-permute-start.4 = (f32[3,18,1,256]{3,2,1,0:T(1,128)S(1)}, f32[3,18,1,256]{3,2,1,0:T(1,128)S(1)}, u32[]{:S(2)}, u32[]{:S(2)}) collective-permute-start(f32[3,18,1,256]{3,2,1,0:T(1,128)S(1)} %get-tuple-element.132), channel_id=1, source_target_pairs={{1,0},{2,1},{3,2},{5,4},{6,5},{7,6},{9,8},{10,9},{11,10},{13,12},{... | collective-permute-start | bytes 165896 | tf_op jit(solution)/shard_map/ppermute | solution.py:231
  51.3 6.4 %collective-permute-start.5 = (f32[3,18,1,256]{3,2,1,0:T(1,128)S(1)}, f32[3,18,1,256]{3,2,1,0:T(1,128)S(1)}, u32[]{:S(2)}, u32[]{:S(2)}) collective-permute-start(f32[3,18,1,256]{3,2,1,0:T(1,128)S(1)} %get-tuple-element.133), channel_id=1, source_target_pairs={{0,1},{1,2},{2,3},{4,5},{5,6},{6,7},{8,9},{9,10},{10,11},{12,13},{... | collective-permute-start | bytes 165896 | tf_op jit(solution)/shard_map/ppermute | solution.py:228
  57.9 6.6 %collective-permute-start.6 = (f32[1,8,256]{2,1,0:T(8,128)S(1)}, f32[1,8,256]{2,1,0:T(8,128)S(1)}, u32[]{:S(2)}, u32[]{:S(2)}) collective-permute-start(f32[1,8,256]{2,1,0:T(8,128)S(1)} %get-tuple-element.171), channel_id=1, source_target_pairs={{4,0},{8,4},{12,8},{5,1},{9,5},{13,9},{6,2},{10,6},{14,10},{7,3},{... | collective-permute-start | bytes 24584 | tf_op jit(solution)/shard_map/ppermute | solution.py:231
  59.2 6.1 %collective-permute-start.7 = (f32[1,8,256]{2,1,0:T(8,128)S(1)}, f32[1,8,256]{2,1,0:T(8,128)S(1)}, u32[]{:S(2)}, u32[]{:S(2)}) collective-permute-start(f32[1,8,256]{2,1,0:T(8,128)S(1)} %get-tuple-element.170), channel_id=1, source_target_pairs={{0,4},{4,8},{8,12},{1,5},{5,9},{9,13},{2,6},{6,10},{10,14},{3,7},{... | collective-permute-start | bytes 24584 | tf_op jit(solution)/shard_map/ppermute | solution.py:228
  65.4 6.1 %collective-permute-start.8 = (f32[18,1,256]{2,1,0:T(1,128)S(1)}, f32[18,1,256]{2,1,0:T(1,128)S(1)}, u32[]{:S(2)}, u32[]{:S(2)}) collective-permute-start(f32[18,1,256]{2,1,0:T(1,128)S(1)} %get-tuple-element.154), channel_id=1, source_target_pairs={{1,0},{2,1},{3,2},{5,4},{6,5},{7,6},{9,8},{10,9},{11,10},{13,12},{... | collective-permute-start | bytes 55304 | tf_op jit(solution)/shard_map/ppermute | solution.py:231
  66.7 6.0 %collective-permute-start.9 = (f32[18,1,256]{2,1,0:T(1,128)S(1)}, f32[18,1,256]{2,1,0:T(1,128)S(1)}, u32[]{:S(2)}, u32[]{:S(2)}) collective-permute-start(f32[18,1,256]{2,1,0:T(1,128)S(1)} %get-tuple-element.155), channel_id=1, source_target_pairs={{0,1},{1,2},{2,3},{4,5},{5,6},{6,7},{8,9},{9,10},{10,11},{12,13},{... | collective-permute-start | bytes 55304 | tf_op jit(solution)/shard_map/ppermute | solution.py:228
  144.4 4.3 %collective-permute-start.10 = (f32[1,8,256]{2,1,0:T(8,128)S(1)}, f32[1,8,256]{2,1,0:T(8,128)S(1)}, u32[]{:S(2)}, u32[]{:S(2)}) collective-permute-start(f32[1,8,256]{2,1,0:T(8,128)S(1)} %get-tuple-element.169), channel_id=1, source_target_pairs={{4,0},{8,4},{12,8},{5,1},{9,5},{13,9},{6,2},{10,6},{14,10},{7,3},{... | collective-permute-start | bytes 24584 | tf_op jit(solution)/shard_map/ppermute | solution.py:231
  145.7 3.8 %collective-permute-start.11 = (f32[1,8,256]{2,1,0:T(8,128)S(1)}, f32[1,8,256]{2,1,0:T(8,128)S(1)}, u32[]{:S(2)}, u32[]{:S(2)}) collective-permute-start(f32[1,8,256]{2,1,0:T(8,128)S(1)} %get-tuple-element.168), channel_id=1, source_target_pairs={{0,4},{4,8},{8,12},{1,5},{5,9},{9,13},{2,6},{6,10},{10,14},{3,7},{... | collective-permute-start | bytes 24584 | tf_op jit(solution)/shard_map/ppermute | solution.py:228
  149.6 6.1 %collective-permute-start.12 = (f32[18,1,256]{2,1,0:T(1,128)S(1)}, f32[18,1,256]{2,1,0:T(1,128)S(1)}, u32[]{:S(2)}, u32[]{:S(2)}) collective-permute-start(f32[18,1,256]{2,1,0:T(1,128)S(1)} %get-tuple-element.152), channel_id=1, source_target_pairs={{1,0},{2,1},{3,2},{5,4},{6,5},{7,6},{9,8},{10,9},{11,10},{13,12},{... | collective-permute-start | bytes 55304 | tf_op jit(solution)/shard_map/ppermute | solution.py:231
  150.9 6.2 %collective-permute-start.13 = (f32[18,1,256]{2,1,0:T(1,128)S(1)}, f32[18,1,256]{2,1,0:T(1,128)S(1)}, u32[]{:S(2)}, u32[]{:S(2)}) collective-permute-start(f32[18,1,256]{2,1,0:T(1,128)S(1)} %get-tuple-element.153), channel_id=1, source_target_pairs={{0,1},{1,2},{2,3},{4,5},{5,6},{6,7},{8,9},{9,10},{10,11},{12,13},{... | collective-permute-start | bytes 55304 | tf_op jit(solution)/shard_map/ppermute | solution.py:228
  224.6 4.3 %collective-permute-start.14 = (f32[1,8,256]{2,1,0:T(8,128)S(1)}, f32[1,8,256]{2,1,0:T(8,128)S(1)}, u32[]{:S(2)}, u32[]{:S(2)}) collective-permute-start(f32[1,8,256]{2,1,0:T(8,128)S(1)} %get-tuple-element.167), channel_id=1, source_target_pairs={{4,0},{8,4},{12,8},{5,1},{9,5},{13,9},{6,2},{10,6},{14,10},{7,3},{... | collective-permute-start | bytes 24584 | tf_op jit(solution)/shard_map/ppermute | solution.py:231
  225.9 3.8 %collective-permute-start.15 = (f32[1,8,256]{2,1,0:T(8,128)S(1)}, f32[1,8,256]{2,1,0:T(8,128)S(1)}, u32[]{:S(2)}, u32[]{:S(2)}) collective-permute-start(f32[1,8,256]{2,1,0:T(8,128)S(1)} %get-tuple-element.166), channel_id=1, source_target_pairs={{0,4},{4,8},{8,12},{1,5},{5,9},{9,13},{2,6},{6,10},{10,14},{3,7},{... | collective-permute-start | bytes 24584 | tf_op jit(solution)/shard_map/ppermute | solution.py:228
  229.8 6.1 %collective-permute-start.16 = (f32[18,1,256]{2,1,0:T(1,128)S(1)}, f32[18,1,256]{2,1,0:T(1,128)S(1)}, u32[]{:S(2)}, u32[]{:S(2)}) collective-permute-start(f32[18,1,256]{2,1,0:T(1,128)S(1)} %get-tuple-element.150), channel_id=1, source_target_pairs={{1,0},{2,1},{3,2},{5,4},{6,5},{7,6},{9,8},{10,9},{11,10},{13,12},{... | collective-permute-start | bytes 55304 | tf_op jit(solution)/shard_map/ppermute | solution.py:231
  231.1 6.2 %collective-permute-start.17 = (f32[18,1,256]{2,1,0:T(1,128)S(1)}, f32[18,1,256]{2,1,0:T(1,128)S(1)}, u32[]{:S(2)}, u32[]{:S(2)}) collective-permute-start(f32[18,1,256]{2,1,0:T(1,128)S(1)} %get-tuple-element.151), channel_id=1, source_target_pairs={{0,1},{1,2},{2,3},{4,5},{5,6},{6,7},{8,9},{9,10},{10,11},{12,13},{... | collective-permute-start | bytes 55304 | tf_op jit(solution)/shard_map/ppermute | solution.py:228
  273.7 18.0 %copy-start.3 = (f32[16,8,256]{2,1,0:T(8,128)}, f32[16,8,256]{2,1,0:T(8,128)S(1)}, u32[]{:S(2)}) copy-start(f32[16,8,256]{2,1,0:T(8,128)S(1)} %multiply_add_fusion) | copy-start | bytes 393220
  273.7 4.3 %collective-permute-start.18 = (f32[1,8,256]{2,1,0:T(8,128)S(1)}, f32[1,8,256]{2,1,0:T(8,128)S(1)}, u32[]{:S(2)}, u32[]{:S(2)}) collective-permute-start(f32[1,8,256]{2,1,0:T(8,128)S(1)} %get-tuple-element.165), channel_id=1, source_target_pairs={{4,0},{8,4},{12,8},{5,1},{9,5},{13,9},{6,2},{10,6},{14,10},{7,3},{... | collective-permute-start | bytes 24584 | tf_op jit(solution)/shard_map/ppermute | solution.py:231
  275.0 3.8 %collective-permute-start.19 = (f32[1,8,256]{2,1,0:T(8,128)S(1)}, f32[1,8,256]{2,1,0:T(8,128)S(1)}, u32[]{:S(2)}, u32[]{:S(2)}) collective-permute-start(f32[1,8,256]{2,1,0:T(8,128)S(1)} %get-tuple-element.164), channel_id=1, source_target_pairs={{0,4},{4,8},{8,12},{1,5},{5,9},{9,13},{2,6},{6,10},{10,14},{3,7},{... | collective-permute-start | bytes 24584 | tf_op jit(solution)/shard_map/ppermute | solution.py:228
  278.9 5.9 %collective-permute-start.20 = (f32[18,1,256]{2,1,0:T(1,128)S(1)}, f32[18,1,256]{2,1,0:T(1,128)S(1)}, u32[]{:S(2)}, u32[]{:S(2)}) collective-permute-start(f32[18,1,256]{2,1,0:T(1,128)S(1)} %get-tuple-element.148), channel_id=1, source_target_pairs={{1,0},{2,1},{3,2},{5,4},{6,5},{7,6},{9,8},{10,9},{11,10},{13,12},{... | collective-permute-start | bytes 55304 | tf_op jit(solution)/shard_map/ppermute | solution.py:231
  280.2 6.0 %collective-permute-start.21 = (f32[18,1,256]{2,1,0:T(1,128)S(1)}, f32[18,1,256]{2,1,0:T(1,128)S(1)}, u32[]{:S(2)}, u32[]{:S(2)}) collective-permute-start(f32[18,1,256]{2,1,0:T(1,128)S(1)} %get-tuple-element.149), channel_id=1, source_target_pairs={{0,1},{1,2},{2,3},{4,5},{5,6},{6,7},{8,9},{9,10},{10,11},{12,13},{... | collective-permute-start | bytes 55304 | tf_op jit(solution)/shard_map/ppermute | solution.py:228
  286.4 3.7 %collective-permute-start.22 = (f32[3,1,8,256]{3,2,1,0:T(8,128)S(1)}, f32[3,1,8,256]{3,2,1,0:T(8,128)S(1)}, u32[]{:S(2)}, u32[]{:S(2)}) collective-permute-start(f32[3,1,8,256]{3,2,1,0:T(8,128)S(1)} %slice.532), channel_id=1, source_target_pairs={{4,0},{8,4},{12,8},{5,1},{9,5},{13,9},{6,2},{10,6},{14,10},{7,3},{... | collective-permute-start | bytes 73736 | tf_op jit(solution)/shard_map/ppermute | solution.py:239
  290.1 6.0 %collective-permute-start.23 = (f32[3,17,1,256]{3,2,1,0:T(1,128)S(1)}, f32[3,17,1,256]{3,2,1,0:T(1,128)S(1)}, u32[]{:S(2)}, u32[]{:S(2)}) collective-permute-start(f32[3,17,1,256]{3,2,1,0:T(1,128)S(1)} %pad_maximum_fusion.48), channel_id=1, source_target_pairs={{1,0},{2,1},{3,2},{5,4},{6,5},{7,6},{9,8},{10,9},{11,10},{13,12},{... | collective-permute-start | bytes 156680 | tf_op jit(solution)/shard_map/ppermute | solution.py:239

commit v2 on v0

v2 whole, which is shorter than its diff:
```python
import functools

import jax
import jax.numpy as jnp
from jax import lax
from jax.experimental import pallas as pl
from jax.experimental.pallas import tpu as pltpu
from jax.sharding import PartitionSpec as P

F32, I32 = jnp.float32, jnp.int32
CX, CY, CELLS = 16, 8, 32768
TILES = CELLS // 1024
LANE_RUNS, SUB_RUNS, SWAPS = 9, 3, 30 * 16
VMEM = 48 * 2**20


def take(x, index, axis):
    other = tuple(d for d in range(x.ndim) if d != axis)
    dims = lax.GatherDimensionNumbers(
        offset_dims=(),
        collapsed_slice_dims=(axis,),
        start_index_map=(axis,),
        operand_batching_dims=other,
        start_indices_batching_dims=other,
    )
    return lax.gather(
        x, index[..., None], dims, (1,) * x.ndim, mode=lax.GatherScatterMode.PROMISE_IN_BOUNDS
    )


def iota(shape, dim):
    return lax.broadcasted_iota(I32, shape, dim)


def sort_plan(tiles, lane_ref, sub_ref, swap_ref):
    lanes, subs = iota((64, 128), 1), iota((8, 128), 0)
    top = 0x7FFF

    def grouped(tiles):
        return [jnp.concatenate(tiles[8 * i : 8 * i + 8], axis=0) for i in range(4)]

    def lane_steps(groups, stride):
        while stride:
            low = lanes & stride == 0
            other = [take(g, lanes ^ stride, 1) for g in groups]
            groups = [
                jnp.where(low, jnp.minimum(g, o), jnp.maximum(g, o)) for g, o in zip(groups, other)
            ]
            stride //= 2
        return groups

    def record(run, groups):
        for i, g in enumerate(groups):
            lane_ref[run, 64 * i : 64 * i + 64] = g & 127
        return [groups[i // 8][8 * (i % 8) : 8 * (i % 8) + 8] >> 7 for i in range(TILES)]

    groups = [(g << 7) | lanes for g in grouped(tiles)]
    for phase in range(1, 7):
        turn = jnp.where(lanes & (1 << phase) != 0, top << 7, 0)
        groups = [g ^ turn for g in groups]
        groups = lane_steps(groups, 1 << (phase - 1))
        groups = [g ^ turn for g in groups]
    turn = jnp.where(iota((64, 128), 0) & 8 != 0, top << 7, 0)
    groups = lane_steps([g ^ turn for g in groups], 64)
    tiles = record(0, groups)
    tiles = [t ^ top if i & 1 else t for i, t in enumerate(tiles)]

    swap = 0
    for phase in range(8, 16):
        if phase < 12:
            turns = [top if i >> (phase - 7) & 1 else 0 for i in range(TILES)]
        elif phase < 15:
            turns = [jnp.where(subs & (1 << (phase - 12)) != 0, top, 0)] * TILES
        else:
            turns = [0] * TILES
        tiles = [t ^ f for t, f in zip(tiles, turns)]
        if phase > 12:
            tiles = [(t << 3) | subs for t in tiles]
            stride = 1 << (phase - 13)
            while stride:
                low = subs & stride == 0
                other = [take(t, subs ^ stride, 0) for t in tiles]
                tiles = [
                    jnp.where(low, jnp.minimum(t, o), jnp.maximum(t, o)) for t, o in zip(tiles, other)
                ]
                stride //= 2
            for i, t in enumerate(tiles):
                sub_ref[phase - 13, 8 * i : 8 * i + 8] = t & 7
            tiles = [t >> 3 for t in tiles]
        hop = 1 << (min(phase, 12) - 8)
        while hop:
            for i in range(TILES):
                if i & hop == 0:
                    a, b = tiles[i], tiles[i + hop]
                    swap_ref[8 * swap : 8 * swap + 8] = jnp.where(a > b, 1, 0)
                    swap += 1
                    tiles[i], tiles[i + hop] = jnp.minimum(a, b), jnp.maximum(a, b)
            hop //= 2
        groups = [(g << 7) | lanes for g in grouped(tiles)]
        tiles = record(phase - 7, lane_steps(groups, 64))
        tiles = [t ^ f for t, f in zip(tiles, turns)]
    return tiles


def follow_plan(tiles, lane_ref, sub_ref, swap_ref):
    tiles = [take(t, lane_ref[0, 8 * i : 8 * i + 8], 1) for i, t in enumerate(tiles)]
    swap = 0
    for phase in range(8, 16):
        if phase > 12:
            tiles = [take(t, sub_ref[phase - 13, 8 * i : 8 * i + 8], 0) for i, t in enumerate(tiles)]
        hop = 1 << (min(phase, 12) - 8)
        while hop:
            for i in range(TILES):
                if i & hop == 0:
                    a, b = tiles[i], tiles[i + hop]
                    crossed = swap_ref[8 * swap : 8 * swap + 8] != 0
                    swap += 1
                    tiles[i], tiles[i + hop] = jnp.where(crossed, b, a), jnp.where(crossed, a, b)
            hop //= 2
        tiles = [take(t, lane_ref[phase - 7, 8 * i : 8 * i + 8], 1) for i, t in enumerate(tiles)]
    return tiles


def plan_shapes():
    return [(LANE_RUNS, 256, 128), (SUB_RUNS, 256, 128), (8 * SWAPS, 128)]


def plan_scratch():
    return [pltpu.VMEM(shape, I32) for shape in plan_shapes()]


def split_tiles(array):
    return [array[8 * i : 8 * i + 8] for i in range(TILES)]


def z_behind(a):
    r = pltpu.roll(a, 1, 2)
    fill = jnp.concatenate([jnp.zeros_like(r[:1]), r[:1]], axis=0)
    return jnp.where(iota(a.shape, 2) == 0, fill, r)


def z_ahead(a):
    r = pltpu.roll(a, 127, 2)
    fill = jnp.concatenate([r[1:], jnp.zeros_like(r[:1])], axis=0)
    return jnp.where(iota(a.shape, 2) == 127, fill, r)


def y_shift(a, steps):
    return jnp.stack([pltpu.roll(a[h], steps % a.shape[1], 0) for h in range(2)])


def fractions(code):
    return [((code >> shift & 3).astype(F32) + 0.5) * 0.25 for shift in (0, 2, 4)]


Y_UP = ((0, 4, 5), (1, 5, 4), (2, 4, 5), (3, 5, 4), (4, 5, 3))
Y_DOWN = ((0, 0, 5), (1, 0, 4), (2, 0, 5), (3, 0, 4), (4, 0, 4))
X_UP = ((0, 12, 5), (1, 12, 5), (2, 13, 4), (3, 13, 4), (4, 13, 3))
X_DOWN = ((0, 0, 5), (1, 0, 5), (2, 0, 4), (3, 0, 4), (4, 0, 4))
UP_ROWS, DOWN_ROWS = 720, 752


def y_pieces(table):
    at, out = 0, []
    for x in range(CX + 1):
        for field, first, count in table:
            if field == 4 and x == CX:
                continue
            for half in range(2):
                out.append((field, x, half, first, count, at))
                at += count
    return out


def x_pieces(table):
    at, out = 0, []
    for field, first, count in table:
        for plane in range(first, first + count):
            for half in range(2):
                out.append((field, plane, half, at))
                at += 17
    return out


def deposit_kernel(
    cell_ref, code_ref, state_ref, flag_ref, grid_ref, up_ref, down_ref, tag_ref, cells, lane_ref, sub_ref, swap_ref
):
    cell = cell_ref[...]
    key = ((cell & 0x700) << 4) | ((cell & 0x7800) >> 3) | (cell & 0xFF)
    sort_plan(split_tiles(key), lane_ref, sub_ref, swap_ref)
    tag = (code_ref[...] << 15) | (iota((256, 128), 0) * 128 + iota((256, 128), 1))
    for i, t in enumerate(follow_plan(split_tiles(tag), lane_ref, sub_ref, swap_ref)):
        tag_ref[8 * i : 8 * i + 8] = t

    def move(c, carry):
        tiles = [state_ref[c, 8 * i : 8 * i + 8] for i in range(TILES)]
        for i, t in enumerate(follow_plan(tiles, lane_ref, sub_ref, swap_ref)):
            cells[c, i] = t
        return carry

    lax.fori_loop(0, 12, move, 0)

    up_at = {(f, x, h): (first, count, at) for f, x, h, first, count, at in y_pieces(Y_UP)}
    down_at = {(f, x, h): (first, count, at) for f, x, h, first, count, at in y_pieces(Y_DOWN)}
    first_row = iota((2, 8, 128), 1) == 0
    before = None
    for x in range(CX + 1):
        here = []
        if x < CX:
            code = jnp.stack([tag_ref[16 * x + 8 * h : 16 * x + 8 * h + 8] >> 15 for h in range(2)])
            fx, fy, fz = fractions(code)
            wx, wy, wz = (1.0 - fx, fx), (1.0 - fy, fy), (1.0 - fz, fz)
            w = {(i, j, k): wx[i] * wy[j] * wz[k] for i in (0, 1) for j in (0, 1) for k in (0, 1)}
            here.append(w)
            for comp in range(3):
                v = cells[comp, 2 * x : 2 * x + 2]
                c0, c1, c2 = [cells[3 + 3 * comp + e, 2 * x : 2 * x + 2] for e in range(3)]
                base = v - c0 * fx - c1 * fy - c2 * fz
                terms = {}
                for i in (0, 1):
                    a = base + c0 if i else base
                    for j in (0, 1):
                        b = a + c1 if j else a
                        for k in (0, 1):
                            terms[i, j, k] = w[i, j, k] * (b + c2 if k else b)
                here.append(terms)
        for f in range(4):
            s = {}
            for j in (0, 1):
                for k in (0, 1):
                    parts = []
                    if x < CX:
                        parts.append(here[f][0, j, k])
                    if x > 0:
                        parts.append(before[f][1, j, k])
                    s[j, k] = sum(parts[1:], parts[0])
            near, far = [s[j, 0] + z_behind(s[j, 1]) for j in (0, 1)]
            turned = y_shift(far, 1)
            main = near + jnp.where(first_row, 0.0, turned)
            grid_ref[f, x] = main
            for h in range(2):
                first, count, at = up_at[f, x, h]
                up_ref[at : at + 8 - first] = main[h, first:8]
                up_ref[at + 8 - first : at + 9 - first] = turned[h, 0:1]
                first, count, at = down_at[f, x, h]
                down_ref[at : at + count] = main[h, :count]
        if x < CX:
            for h in range(2):
                flags = flag_ref[x, :, 128 * h : 128 * h + 128].astype(F32)
                for table, ref in ((up_at, up_ref), (down_at, down_ref)):
                    first, count, at = table[4, x, h]
                    ref[at : at + count] = flags[first : first + count]
        before = here


def kernel_call(body, name, outs, scratch, in_specs=None):
    return pl.pallas_call(
        body,
        out_shape=outs,
        **({} if in_specs is None else dict(in_specs=in_specs)),
        scratch_shapes=scratch,
        compiler_params=pltpu.CompilerParams(vmem_limit_bytes=VMEM),
        name=name,
    )


def of(shape, kind=F32):
    return jax.ShapeDtypeStruct(shape, kind)


def deposit(cell, code, state, flags):
    return kernel_call(
        deposit_kernel,
        "deposit",
        (of((4, CX + 1, 2, 8, 128)), of((UP_ROWS, 128)), of((DOWN_ROWS, 128)), of((256, 128), I32)),
        [pltpu.VMEM((12, TILES, 8, 128), F32)] + plan_scratch(),
    )(cell, code, state, flags)


def widen_kernel(keep_ref, grid_ref, own_ref, low_ref, high_ref, flag_ref, wide_ref, up_ref, down_ref):
    keep = keep_ref[1]
    zero = jnp.zeros((2, 8, 128), F32)
    for f in range(5):
        for x in range(CX + 1):
            wide_ref[f, x, :, 0:8] = zero
            wide_ref[f, x, :, 16:24] = zero
            if f < 4:
                wide_ref[f, x, :, 8:16] = grid_ref[f, x]
            elif x < CX:
                for h in range(2):
                    wide_ref[f, x, h, 8:16] = flag_ref[x, :, 128 * h : 128 * h + 128].astype(F32)
            else:
                wide_ref[f, x, :, 8:16] = zero
    for f, x, h, first, count, at in y_pieces(Y_DOWN):
        wide_ref[f, x, h, 16 : 16 + count] = high_ref[at : at + count]
    for f, x, h, first, count, at in y_pieces(Y_UP):
        below = 8 - first
        wide_ref[f, x, h, first:8] = low_ref[at : at + below]
        if f < 4:
            rim = at + below
            wide_ref[f, x, h, 8:9] = wide_ref[f, x, h, 8:9] + low_ref[rim : rim + 1]
            wide_ref[f, x, h, 16:17] = wide_ref[f, x, h, 16:17] + keep * own_ref[rim : rim + 1]
    for table, ref in ((X_UP, up_ref), (X_DOWN, down_ref)):
        for f, plane, h, at in x_pieces(table):
            ref[at : at + 17] = wide_ref[f, plane, h, 4:21]


def smem():
    return pl.BlockSpec(memory_space=pltpu.SMEM)


def vmem():
    return pl.BlockSpec(memory_space=pltpu.VMEM)


def widen(keep, grid, own, low, high, flags):
    return kernel_call(
        widen_kernel,
        "widen",
        (of((5, CX + 1, 2, 24, 128)), of((UP_ROWS, 128)), of((DOWN_ROWS, 128))),
        [],
        [smem()] + [vmem()] * 5,
    )(keep, grid, own, low, high, flags)


def krylov_kernel(keep_ref, wide_ref, low_ref, high_ref, vel_ref, fluid_ref, k0_ref, k1_ref, k2_ref, sums_ref, ext):
    keep = keep_ref[0]
    zero = jnp.zeros((2, 24, 128), F32)
    for f in range(5):
        for plane in (0, 1, 2, 3, 21, 22, 23, 24):
            ext[f, plane] = zero
        for x in range(CX):
            ext[f, x + 4] = wide_ref[f, x]
        ext[f, 20] = keep * wide_ref[f, CX]
    for f, plane, h, at in x_pieces(X_UP):
        rows = low_ref[at : at + 17]
        if plane == CX:
            ext[f, 4, h, 4:21] = ext[f, 4, h, 4:21] + rows
        else:
            ext[f, plane - 12, h, 4:21] = rows
    for f, plane, h, at in x_pieces(X_DOWN):
        rows = high_ref[at : at + 17]
        if plane == 0 and f < 4:
            ext[f, 20, h, 4:21] = ext[f, 20, h, 4:21] + rows
        else:
            ext[f, plane + 20, h, 4:21] = rows
    for plane in range(25):
        mass = jnp.maximum(ext[0, plane], 0.5)
        for d in range(3):
            vel_ref[d, plane] = ext[1 + d, plane] / mass
        fluid_ref[plane] = ext[4, plane]
    for plane in range(1, 24):
        vy, vz = vel_ref[1, plane], vel_ref[2, plane]
        divergence = (
            0.5 * (vel_ref[0, plane + 1] - vel_ref[0, plane - 1])
            + 0.5 * (y_shift(vy, -1) - y_shift(vy, 1))
            + 0.5 * (z_ahead(vz) - z_behind(vz))
        )
        k0_ref[plane] = -fluid_ref[plane] * divergence

    def applied(ref, plane):
        a = ref[plane]
        beside = (
            ref[plane + 1] + ref[plane - 1] + y_shift(a, 1) + y_shift(a, -1) + z_ahead(a) + z_behind(a)
        )
        return fluid_ref[plane] * (a - beside * (1.0 / 6.0))

    for plane in range(2, 23):
        k1_ref[plane] = applied(k0_ref, plane)
    for plane in range(3, 22):
        k2_ref[plane] = applied(k1_ref, plane)
    totals = [jnp.zeros((2, 8, 128), F32)] * 14
    for plane in range(4, 20):
        k0, k1, k2 = [ref[plane, :, 8:16] for ref in (k0_ref, k1_ref, k2_ref)]
        k3 = applied(k2_ref, plane)[:, 8:16]
        u1, w1 = k0 - k1, k1 - k2
        u2 = u1 - w1
        w2 = w1 - (k2 - k3)
        pairs = (
            (k0, k0), (k0, k1), (k1, k1), (k1, k2), (k2, k2), (k2, k3),
            (k0, u1), (u1, u1), (u1, u2), (u2, u2), (k0, w1), (u1, w1), (u1, w2), (u2, w2),
        )
        totals = [t + a * b for t, (a, b) in zip(totals, pairs)]
    for i, t in enumerate(totals):
        sums_ref[i : i + 1] = jnp.sum(t[0] + t[1], axis=0, keepdims=True)
    sums_ref[14:16] = jnp.zeros((2, 128), F32)


def krylov(keep, wide, low, high):
    return kernel_call(
        krylov_kernel,
        "krylov",
        (of((3, 25, 2, 24, 128)),) + (of((25, 2, 24, 128)),) * 4 + (of((16, 128)),),
        [pltpu.VMEM((5, 25, 2, 24, 128), F32)],
        [smem()] + [vmem()] * 3,
    )(keep, wide, low, high)


def steps_from(gram, energy, apply_once):
    def form(a, table):
        total = None
        for i, p in enumerate(a):
            for j, q in enumerate(a):
                if p is not None and q is not None:
                    term = p * q * table[i + j]
                    total = term if total is None else total + term
        return total

    def ratio(a, b):
        return jnp.where(b > 0.0, a / jnp.where(b > 0.0, b, 1.0), 0.0)

    one, zero = jnp.ones_like(gram[0]), jnp.zeros_like(gram[0])
    residual, direction, answer = [one], [one], [zero] * 3
    norm = gram[0]
    for step in range(3):
        alpha = ratio(norm, form(direction, energy))
        for i, p in enumerate(direction):
            answer[i] = answer[i] + alpha * p
        if step == 2:
            return answer
        image = apply_once(direction, zero)
        residual = [a - alpha * b for a, b in zip(residual + [zero], image)]
        norm_next = form(residual, gram)
        direction = [a + ratio(norm_next, norm) * b for a, b in zip(residual, direction + [zero])]
        norm = norm_next


def coefficients(m):
    power = steps_from(m[0:5], m[1:6], lambda a, zero: [zero] + a)
    shifted = steps_from(
        [m[0]] + m[6:10],
        [m[1]] + m[10:14],
        lambda a, zero: [p - q for p, q in zip(a + [zero], [zero] + a)],
    )
    turned = [shifted[0] + shifted[1] + shifted[2], -shifted[1] - 2.0 * shifted[2], shifted[2]]
    smooth = m[1] < 0.3 * m[0]
    return [jnp.where(smooth, a, b) * (1.0 / 6.0) for a, b in zip(power, turned)]


def plan_kernel(tag_ref, lane_ref, sub_ref, swap_ref):
    place = tag_ref[...] & 0x7FFF
    key = ((place & 0x380) << 5) | ((place & 0x7C00) >> 3) | (place & 0x7F)
    sort_plan(split_tiles(key), lane_ref, sub_ref, swap_ref)


def return_plan(tag):
    return kernel_call(plan_kernel, "return_plan", [of(shape, I32) for shape in plan_shapes()], [])(tag)


def project_kernel(
    sums_ref, vel_ref, fluid_ref, k0_ref, k1_ref, k2_ref, tag_ref, lane_ref, sub_ref, swap_ref,
    pressure_ref, out_ref, press, proj, value,
):
    total = jnp.sum(sums_ref[...].reshape(-1, 16, 128), axis=0)
    total = jnp.sum(total, axis=1, keepdims=True)
    c = coefficients([jnp.broadcast_to(total[i : i + 1], (8, 128)) for i in range(14)])
    c = [jnp.concatenate([a, a, a], axis=0)[None] for a in c]
    for plane in range(3, 22):
        press[plane] = c[0] * k0_ref[plane] + c[1] * k1_ref[plane] + c[2] * k2_ref[plane]
    for x in range(CX):
        for h in range(2):
            pressure_ref[x, :, 128 * h : 128 * h + 128] = press[x + 4, h, 8:16]
    for x in range(CX + 1):
        p = press[x + 4]
        slopes = (
            press[x + 5] - press[x + 3],
            y_shift(p, -1) - y_shift(p, 1),
            z_ahead(p) - z_behind(p),
        )
        for d in range(3):
            field = fluid_ref[x + 4] * (vel_ref[d, x + 4] - 0.5 * slopes[d])
            proj[x, d, 0] = field
            proj[x, d, 1] = z_ahead(field)
    for x in range(CX):
        code = jnp.stack([tag_ref[16 * x + 8 * h : 16 * x + 8 * h + 8] >> 15 for h in range(2)])
        fx, fy, fz = fractions(code)
        wx, wy, wz = (1.0 - fx, fx), (1.0 - fy, fy), (1.0 - fz, fz)
        w = {(i, j, k): wx[i] * wy[j] * wz[k] for i in (0, 1) for j in (0, 1) for k in (0, 1)}
        for d in range(3):
            result = None
            for (i, j, k), weight in w.items():
                term = weight * proj[x + i, d, k, :, 8 + j : 16 + j]
                result = term if result is None else result + term
            value[d, 2 * x : 2 * x + 2] = result

    def move(d, carry):
        tiles = [value[d, i] for i in range(TILES)]
        for i, t in enumerate(follow_plan(tiles, lane_ref, sub_ref, swap_ref)):
            out_ref[d, 8 * i : 8 * i + 8] = t
        return carry

    lax.fori_loop(0, 3, move, 0)


def project(*args):
    return kernel_call(
        project_kernel,
        "project",
        (of((CX, CY, 256)), of((3, 256, 128))),
        [
            pltpu.VMEM((25, 2, 24, 128), F32),
            pltpu.VMEM((CX + 1, 3, 2, 2, 24, 128), F32),
            pltpu.VMEM((3, TILES, 8, 128), F32),
        ],
    )(*args)


def neighbours(up, down, axis):
    pairs = [(i, i + 1) for i in range(lax.axis_size(axis) - 1)]
    return lax.ppermute(up, axis, pairs), lax.ppermute(down, axis, [(b, a) for a, b in pairs])


def everywhere(sums):
    for axis in ("gx", "gy"):
        count = lax.axis_size(axis)
        parts = [sums]
        for shift in range(1, count):
            parts.append(lax.ppermute(sums, axis, [(i, (i + shift) % count) for i in range(count)]))
        sums = functools.reduce(jnp.add, parts)
    return sums


def local(cell_index, offset_code, particle_state, fluid_flags):
    places = [(axis, lax.axis_index(axis), lax.axis_size(axis)) for axis in ("gx", "gy")]
    keep = jnp.stack([(at + 1 < size).astype(F32) for _, at, size in places])
    grid, up, down, tag = deposit(
        cell_index.reshape(256, 128),
        offset_code.reshape(256, 128),
        particle_state.reshape(12, 256, 128),
        fluid_flags,
    )
    low, high = neighbours(up, down, "gy")
    plan = return_plan(tag)
    wide, up_x, down_x = widen(keep, grid, up, low, high, fluid_flags)
    low, high = neighbours(up_x, down_x, "gx")
    vel, fluid, k0, k1, k2, sums = krylov(keep, wide, low, high)
    sums = everywhere(sums)
    pressure, result = project(sums, vel, fluid, k0, k1, k2, tag, *plan)
    return pressure, result.reshape(1, 3, CELLS)


def solution(mesh):
    return jax.shard_map(
        local,
        mesh=mesh,
        in_specs=(
            P(("groups", "gx", "gy"), None),
            P(("groups", "gx", "gy"), None),
            P(("groups", "gx", "gy"), None, None),
            P(("groups", "gx"), "gy", None),
        ),
        out_specs=(P(("groups", "gx"), "gy", None), P(("groups", "gx", "gy"), None, None)),
        check_vma=False,
    )
```

time: 775 us -> 83.3 us (0.11)
  local copies, waits for them, and re-layouts: 496 us -> 6.72 us
  blocking collectives: 165 us -> 0 us
  starting transfers between devices: 64.1 us -> 23.8 us
  Pallas kernels: 0 us -> 39.7 us
  other arithmetic: 16.6 us -> 0.09 us
  waiting for transfers between devices: 21.1 us -> 11.9 us
    scatter x2 -> x0, local copies, waits for them, and re-layouts: 209 us -> none  [the longest x1 121 us: local(): jnp.zeros((count,), jnp.int32).at[cells].set(offset_code[0])]
    psum x5 -> x0, blocking collectives: 165 us -> none  [the longest x3 97.8 us: precond_total(): return lax.psum(jnp.sum(residual * precond), ('gx', 'gy'))]
    slice x10 -> x0, local copies, waits for them, and re-layouts: 142 us -> none  [the longest x1 141 us: corner_terms(): state[4 + 3 * comp] * delta_y]
    gather x1 -> x0, local copies, waits for them, and re-layouts: 114 us -> none  [local(): result = result_cells.reshape(3, count)[:, cells]]
    ppermute x24 -> x10, starting transfers between devices: 64.1 us -> 23.8 us  [the longest x6 12.6 us: everywhere(): lax.ppermute(sums, axis, [(i, (i + shift) % count) for i in range(count)])]
    pallas_call x0 -> x5, Pallas kernels: none -> 39.7 us  [the longest x1 22 us: deposit(): kernel_call(deposit_kernel, 'deposit', (of((4, CX + 1, 2, 8, 128)), of((U...]
    squeeze x15 -> x0, local copies, waits for them, and re-layouts: 11.4 us -> none  [the longest x1 10.9 us: local(): particle_state[0]]
    add x4 -> x2, other arithmetic: 9.55 us -> 0.01 us  [everywhere(): sums = functools.reduce(jnp.add, parts)]
  transfers between devices with their start and end apart: 24 -> 10, of which waited for: 15 -> 4; matrix products, arithmetic and copies ran while one was open for 0% -> 0% of each run, Pallas kernels for 0% -> 8%
where the time goes in v2:
time: 83.3 us; the launch traced here: 82.9 us
  Pallas kernels  39.7 us (48%)
  starting transfers between devices  23.8 us (29%)
  waiting for transfers between devices  11.9 us (14%)
  local copies, waits for them, and re-layouts  6.72 us (8%)
    pallas_call x1, Pallas kernels, deposit(): kernel_call(deposit_kernel, 'deposit', (of((4, CX + 1, 2, 8, 128)), of((U...  22 us
    ppermute x6, starting transfers between devices, everywhere(): lax.ppermute(sums, axis, [(i, (i + shift) % count) for i in range(count)])  12.6 us
    ppermute x2, waiting for transfers between devices, neighbours(): lax.ppermute(up, axis, pairs)  8.99 us
    ppermute x2, starting transfers between devices, neighbours(): lax.ppermute(up, axis, pairs)  8.63 us
    pallas_call x1, Pallas kernels, project(): kernel_call(project_kernel, 'project', (of((CX, CY, 256)), of((3, 256, 12...  7.17 us
    unnamed x14, local copies, waits for them, and re-layouts  6.72 us
    pallas_call x1, Pallas kernels, return_plan(): kernel_call(plan_kernel, 'return_plan', [of(shape, I32) for shape in plan...  6.45 us
    pallas_call x1, Pallas kernels, krylov(): kernel_call(krylov_kernel, 'krylov', (of((3, 25, 2, 24, 128)),) + (of((25...  3.03 us
  transfers between devices with their start and end apart: 10, of which 4 were waited for; matrix products, arithmetic and copies ran while one was open for 0% of the time, Pallas kernels for 8%

profile of v2, /device:TPU:0, one launch (start us, length us, event | category | flops | bytes accessed | tf_op | source)
XLA Modules:
  0.0 82.9 jit_solution(821007386129628115)
XLA Ops:
  0.6 0.0 copy-start.2
  0.6 1.4 %copy-done.2 = f32[1,12,32768]{2,0,1:T(1,128)S(1)} copy-done((f32[1,12,32768]{2,0,1:T(1,128)S(1)}, f32[1,12,32768]{2,0,1:T(1,128)}, u32[]{:S(2)}) %copy-start.2) | copy-done | bytes 1572888
  2.0 0.0 copy-start.3
  2.0 0.9 %copy-done.3 = s32[16,8,256]{2,1,0:T(8,128)S(1)} copy-done((s32[16,8,256]{2,1,0:T(8,128)S(1)}, s32[16,8,256]{2,1,0:T(8,128)}, u32[]{:S(2)}) %copy-start.3) | copy-done | bytes 131096
  2.9 0.0 copy-start.5
  2.9 0.9 %copy-done.5 = s32[1,32768]{1,0:T(1,128)S(1)} copy-done((s32[1,32768]{1,0:T(1,128)S(1)}, s32[1,32768]{1,0:T(1,128)}, u32[]{:S(2)}) %copy-start.5) | copy-done | bytes 131096
  3.8 0.0 copy-start.6
  3.9 0.9 %copy-done.6 = s32[1,32768]{1,0:T(1,128)S(1)} copy-done((s32[1,32768]{1,0:T(1,128)S(1)}, s32[1,32768]{1,0:T(1,128)}, u32[]{:S(2)}) %copy-start.6) | copy-done | bytes 131096
  4.8 0.0 copy-start.4
  4.8 22.0 %deposit.1 = (f32[4,17,2,8,128]{4,3,2,1,0:T(8,128)S(1)}, f32[720,128]{1,0:T(8,128)S(1)}, f32[752,128]{1,0:T(8,128)S(1)}, s32[256,128]{1,0:T(8,128)S(1)}) custom-call(s32[256,128]{1,0:T(8,128)S(1)} %bitcast.7, s32[256,128]{1,0:T(8,128)S(1)} %bitcast.8, f32[12,256,128]{2,1,0:T(8,128)S(1)} %bitcast.6, s32[16,8,256]{2,1,0:T(8,128)S(1)} %copy-done.3), custom_call_target="tpu_custom_call" | custom-call | tf_op jit(solution)/shard_map/deposit/pallas_call | solution.py:272
  26.8 1.3 %collective-permute-start.1 = (f32[752,128]{1,0:T(8,128)S(1)}, f32[752,128]{1,0:T(8,128)S(1)}, u32[]{:S(2)}, u32[]{:S(2)}) collective-permute-start(f32[752,128]{1,0:T(8,128)S(1)} %get-tuple-element.22), channel_id=1, source_target_pairs={{1,0},{2,1},{3,2},{5,4},{6,5},{7,6},{9,8},{10,9},{11,10},{13,12},{... | collective-permute-start | bytes 1155080 | tf_op jit(solution)/shard_map/ppermute | solution.py:510
  28.1 5.6 %collective-permute-start = (f32[720,128]{1,0:T(8,128)S(1)}, f32[720,128]{1,0:T(8,128)S(1)}, u32[]{:S(2)}, u32[]{:S(2)}) collective-permute-start(f32[720,128]{1,0:T(8,128)S(1)} %get-tuple-element.21.own_ref), channel_id=1, source_target_pairs={{0,1},{1,2},{2,3},{4,5},{5,6},{6,7},{8,9},{9,10},{10,11},{12,13},{... | collective-permute-start | bytes 1105928 | tf_op jit(solution)/shard_map/ppermute | solution.py:510
  33.7 0.1 add_convert_fusion.keep_ref
  33.7 7.7 %collective-permute-done.low_ref = f32[720,128]{1,0:T(8,128)S(1)} collective-permute-done((f32[720,128]{1,0:T(8,128)S(1)}, f32[720,128]{1,0:T(8,128)S(1)}, u32[]{:S(2)}, u32[]{:S(2)}) %collective-permute-start) | collective-permute-done | bytes 368672 | tf_op jit(solution)/shard_map/ppermute | solution.py:510
  41.5 0.0 collective-permute-done.1.high_ref
  41.5 0.0 copy-done.4
  41.5 1.0 %widen.1 = (f32[5,17,2,24,128]{4,3,2,1,0:T(8,128)S(1)}, f32[720,128]{1,0:T(8,128)S(1)}, f32[752,128]{1,0:T(8,128)S(1)}) custom-call(f32[2]{0:T(128)S(1)} %add_convert_fusion.keep_ref, f32[4,17,2,8,128]{4,3,2,1,0:T(8,128)S(1)} %get-tuple-element.20.grid_ref, f32[720,128]{1,0:T(8,128)S(1)} %get-tuple-element.21.own_ref, ...), custom_call_target="tpu_custom_call" | custom-call | tf_op jit(solution)/shard_map/widen/pallas_call | solution.py:317
  42.5 0.0 copy-start
  42.5 1.3 %copy-done = f32[5,17,2,24,128]{4,3,2,1,0:T(8,128)} copy-done((f32[5,17,2,24,128]{4,3,2,1,0:T(8,128)}, f32[5,17,2,24,128]{4,3,2,1,0:T(8,128)S(1)}, u32[]{:S(2)}) %copy-start) | copy-done | bytes 2088984
  43.8 1.3 %collective-permute-start.3 = (f32[752,128]{1,0:T(8,128)S(1)}, f32[752,128]{1,0:T(8,128)S(1)}, u32[]{:S(2)}, u32[]{:S(2)}) collective-permute-start(f32[752,128]{1,0:T(8,128)S(1)} %get-tuple-element.25), channel_id=1, source_target_pairs={{4,0},{8,4},{12,8},{5,1},{9,5},{13,9},{6,2},{10,6},{14,10},{7,3},{... | collective-permute-start | bytes 1155080 | tf_op jit(solution)/shard_map/ppermute | solution.py:510
  45.1 3.1 %collective-permute-start.2 = (f32[720,128]{1,0:T(8,128)S(1)}, f32[720,128]{1,0:T(8,128)S(1)}, u32[]{:S(2)}, u32[]{:S(2)}) collective-permute-start(f32[720,128]{1,0:T(8,128)S(1)} %get-tuple-element.24), channel_id=1, source_target_pairs={{0,4},{4,8},{8,12},{1,5},{5,9},{9,13},{2,6},{6,10},{10,14},{3,7},{... | collective-permute-start | bytes 1105928 | tf_op jit(solution)/shard_map/ppermute | solution.py:510
  48.2 1.3 %collective-permute-done.2.low_ref = f32[720,128]{1,0:T(8,128)S(1)} collective-permute-done((f32[720,128]{1,0:T(8,128)S(1)}, f32[720,128]{1,0:T(8,128)S(1)}, u32[]{:S(2)}, u32[]{:S(2)}) %collective-permute-start.2) | collective-permute-done | bytes 368672 | tf_op jit(solution)/shard_map/ppermute | solution.py:510
  49.4 0.0 collective-permute-done.3.high_ref
  49.4 3.0 %krylov.1 = (f32[3,25,2,24,128]{4,3,2,1,0:T(8,128)S(1)}, f32[25,2,24,128]{3,2,1,0:T(8,128)S(1)}, f32[25,2,24,128]{3,2,1,0:T(8,128)S(1)}, f32[25,2,24,128]{3,2,1,...) custom-call(f32[2]{0:T(128)S(1)} %add_convert_fusion.keep_ref, f32[5,17,2,24,128]{4,3,2,1,0:T(8,128)} %copy-done, ...), custom_call_target="tpu_custom_call" | custom-call | tf_op jit(solution)/shard_map/krylov/pallas_call | solution.py:390
  52.5 1.7 %collective-permute-start.6 = (f32[16,128]{1,0:T(8,128)S(1)}, f32[16,128]{1,0:T(8,128)S(1)}, u32[]{:S(2)}, u32[]{:S(2)}) collective-permute-start(f32[16,128]{1,0:T(8,128)S(1)} %get-tuple-element.26), channel_id=1, source_target_pairs={{0,12},{4,0},{8,4},{12,8},{1,13},{5,1},{9,5},{13,9},{2,14},{6,2},{... | collective-permute-start | bytes 24584 | tf_op jit(solution)/shard_map/ppermute | solution.py:518
  54.2 5.2 %collective-permute-start.5 = (f32[16,128]{1,0:T(8,128)S(1)}, f32[16,128]{1,0:T(8,128)S(1)}, u32[]{:S(2)}, u32[]{:S(2)}) collective-permute-start(f32[16,128]{1,0:T(8,128)S(1)} %get-tuple-element.26), channel_id=1, source_target_pairs={{0,8},{4,12},{8,0},{12,4},{1,9},{5,13},{9,1},{13,5},{2,10},{6,14},... | collective-permute-start | bytes 24584 | tf_op jit(solution)/shard_map/ppermute | solution.py:518
  59.4 0.2 collective-permute-start.4
  59.5 0.0 collective-permute-done.6
  59.6 1.5 %collective-permute-done.5 = f32[16,128]{1,0:T(8,128)S(1)} collective-permute-done((f32[16,128]{1,0:T(8,128)S(1)}, f32[16,128]{1,0:T(8,128)S(1)}, u32[]{:S(2)}, u32[]{:S(2)}) %collective-permute-start.5) | collective-permute-done | bytes 8224 | tf_op jit(solution)/shard_map/ppermute | solution.py:518
  61.0 1.4 %collective-permute-done.4 = f32[16,128]{1,0:T(8,128)S(1)} collective-permute-done((f32[16,128]{1,0:T(8,128)S(1)}, f32[16,128]{1,0:T(8,128)S(1)}, u32[]{:S(2)}, u32[]{:S(2)}) %collective-permute-start.4) | collective-permute-done | bytes 8224 | tf_op jit(solution)/shard_map/ppermute | solution.py:518
  62.5 4.5 %collective-permute-start.9 = (f32[16,128]{1,0:T(8,128)S(1)}, f32[16,128]{1,0:T(8,128)S(1)}, u32[]{:S(2)}, u32[]{:S(2)}) collective-permute-start(f32[16,128]{1,0:T(8,128)S(1)} %add_add_fusion.1), channel_id=1, source_target_pairs={{0,3},{1,0},{2,1},{3,2},{4,7},{5,4},{6,5},{7,6},{8,11},{9,8},{10,9... | collective-permute-start | bytes 24584 | tf_op jit(solution)/shard_map/ppermute | solution.py:518
  67.0 0.0 collective-permute-start.8
  67.0 1.0 %collective-permute-start.7 = (f32[16,128]{1,0:T(8,128)S(1)}, f32[16,128]{1,0:T(8,128)S(1)}, u32[]{:S(2)}, u32[]{:S(2)}) collective-permute-start(f32[16,128]{1,0:T(8,128)S(1)} %add_add_fusion.1), channel_id=1, source_target_pairs={{0,1},{1,2},{2,3},{3,0},{4,5},{5,6},{6,7},{7,4},{8,9},{9,10},{10,1... | collective-permute-start | bytes 24584 | tf_op jit(solution)/shard_map/ppermute | solution.py:518
  68.0 6.4 %return_plan.1 = (s32[9,256,128]{2,1,0:T(8,128)S(1)}, s32[3,256,128]{2,1,0:T(8,128)S(1)}, s32[3840,128]{1,0:T(8,128)S(1)}) custom-call(s32[256,128]{1,0:T(8,128)S(1)} %get-tuple-element.32.tag_ref), custom_call_target="tpu_custom_call" | custom-call | tf_op jit(solution)/shard_map/return_plan/pallas_call | solution.py:447
  74.4 0.0 copy-start.1
  74.5 1.3 %copy-done.1 = s32[3840,128]{1,0:T(8,128)} copy-done((s32[3840,128]{1,0:T(8,128)}, s32[3840,128]{1,0:T(8,128)S(1)}, u32[]{:S(2)}) %copy-start.1) | copy-done | bytes 1966104
  75.7 0.0 collective-permute-done.9
  75.7 0.0 collective-permute-done.8
  75.7 0.0 collective-permute-done.7
  75.8 7.2 %project.1 = (f32[16,8,256]{2,1,0:T(8,128)}, f32[3,256,128]{2,1,0:T(8,128)}) custom-call(f32[16,128]{1,0:T(8,128)S(1)} %add_add_fusion.sums_ref, f32[3,25,2,24,128]{4,3,2,1,0:T(8,128)S(1)} %get-tuple-element.27.vel_ref, f32[25,2,24,128]{3,2,1,0:T(8,128)S(1)} %get-tuple-element.28.fluid_ref, f32[25,2,24,128]{3,2,1,0:T(8,128)S(1)} %get-tuple-element.29.k0_ref, ...), custom_call_target="tpu_custom_call" | custom-call | tf_op jit(solution)/shard_map/project/pallas_call | solution.py:496
  (2 shorter events, 0.0 us)
Async XLA Ops:
  0.6 1.4 %copy-start.2 = (f32[1,12,32768]{2,0,1:T(1,128)S(1)}, f32[1,12,32768]{2,0,1:T(1,128)}, u32[]{:S(2)}) copy-start(f32[1,12,32768]{2,0,1:T(1,128)} %param.6) | copy-start | bytes 4718596
  2.0 0.9 %copy-start.3 = (s32[16,8,256]{2,1,0:T(8,128)S(1)}, s32[16,8,256]{2,1,0:T(8,128)}, u32[]{:S(2)}) copy-start(s32[16,8,256]{2,1,0:T(8,128)} %flag_ref.3) | copy-start | bytes 393220
  2.9 0.9 %copy-start.5 = (s32[1,32768]{1,0:T(1,128)S(1)}, s32[1,32768]{1,0:T(1,128)}, u32[]{:S(2)}) copy-start(s32[1,32768]{1,0:T(1,128)} %param.4) | copy-start | bytes 393220
  3.8 0.9 %copy-start.6 = (s32[1,32768]{1,0:T(1,128)S(1)}, s32[1,32768]{1,0:T(1,128)}, u32[]{:S(2)}) copy-start(s32[1,32768]{1,0:T(1,128)} %param.5) | copy-start | bytes 393220
  4.8 36.7 %copy-start.4 = (s32[16,8,256]{2,1,0:T(8,128)S(1)}, s32[16,8,256]{2,1,0:T(8,128)}, u32[]{:S(2)}) copy-start(s32[16,8,256]{2,1,0:T(8,128)} %flag_ref.3) | copy-start | bytes 393220
  26.8 14.7 %collective-permute-start.1 = (f32[752,128]{1,0:T(8,128)S(1)}, f32[752,128]{1,0:T(8,128)S(1)}, u32[]{:S(2)}, u32[]{:S(2)}) collective-permute-start(f32[752,128]{1,0:T(8,128)S(1)} %get-tuple-element.22), channel_id=1, source_target_pairs={{1,0},{2,1},{3,2},{5,4},{6,5},{7,6},{9,8},{10,9},{11,10},{13,12},{... | collective-permute-start | bytes 1155080 | tf_op jit(solution)/shard_map/ppermute | solution.py:510
  28.1 13.4 %collective-permute-start = (f32[720,128]{1,0:T(8,128)S(1)}, f32[720,128]{1,0:T(8,128)S(1)}, u32[]{:S(2)}, u32[]{:S(2)}) collective-permute-start(f32[720,128]{1,0:T(8,128)S(1)} %get-tuple-element.21.own_ref), channel_id=1, source_target_pairs={{0,1},{1,2},{2,3},{4,5},{5,6},{6,7},{8,9},{9,10},{10,11},{12,13},{... | collective-permute-start | bytes 1105928 | tf_op jit(solution)/shard_map/ppermute | solution.py:510
  42.5 1.3 %copy-start = (f32[5,17,2,24,128]{4,3,2,1,0:T(8,128)}, f32[5,17,2,24,128]{4,3,2,1,0:T(8,128)S(1)}, u32[]{:S(2)}) copy-start(f32[5,17,2,24,128]{4,3,2,1,0:T(8,128)S(1)} %get-tuple-element.23.wide_ref) | copy-start | bytes 6266884
  43.8 5.6 %collective-permute-start.3 = (f32[752,128]{1,0:T(8,128)S(1)}, f32[752,128]{1,0:T(8,128)S(1)}, u32[]{:S(2)}, u32[]{:S(2)}) collective-permute-start(f32[752,128]{1,0:T(8,128)S(1)} %get-tuple-element.25), channel_id=1, source_target_pairs={{4,0},{8,4},{12,8},{5,1},{9,5},{13,9},{6,2},{10,6},{14,10},{7,3},{... | collective-permute-start | bytes 1155080 | tf_op jit(solution)/shard_map/ppermute | solution.py:510
  45.1 4.3 %collective-permute-start.2 = (f32[720,128]{1,0:T(8,128)S(1)}, f32[720,128]{1,0:T(8,128)S(1)}, u32[]{:S(2)}, u32[]{:S(2)}) collective-permute-start(f32[720,128]{1,0:T(8,128)S(1)} %get-tuple-element.24), channel_id=1, source_target_pairs={{0,4},{4,8},{8,12},{1,5},{5,9},{9,13},{2,6},{6,10},{10,14},{3,7},{... | collective-permute-start | bytes 1105928 | tf_op jit(solution)/shard_map/ppermute | solution.py:510
  52.5 7.1 %collective-permute-start.6 = (f32[16,128]{1,0:T(8,128)S(1)}, f32[16,128]{1,0:T(8,128)S(1)}, u32[]{:S(2)}, u32[]{:S(2)}) collective-permute-start(f32[16,128]{1,0:T(8,128)S(1)} %get-tuple-element.26), channel_id=1, source_target_pairs={{0,12},{4,0},{8,4},{12,8},{1,13},{5,1},{9,5},{13,9},{2,14},{6,2},{... | collective-permute-start | bytes 24584 | tf_op jit(solution)/shard_map/ppermute | solution.py:518
  54.2 6.8 %collective-permute-start.5 = (f32[16,128]{1,0:T(8,128)S(1)}, f32[16,128]{1,0:T(8,128)S(1)}, u32[]{:S(2)}, u32[]{:S(2)}) collective-permute-start(f32[16,128]{1,0:T(8,128)S(1)} %get-tuple-element.26), channel_id=1, source_target_pairs={{0,8},{4,12},{8,0},{12,4},{1,9},{5,13},{9,1},{13,5},{2,10},{6,14},... | collective-permute-start | bytes 24584 | tf_op jit(solution)/shard_map/ppermute | solution.py:518
  59.4 3.1 %collective-permute-start.4 = (f32[16,128]{1,0:T(8,128)S(1)}, f32[16,128]{1,0:T(8,128)S(1)}, u32[]{:S(2)}, u32[]{:S(2)}) collective-permute-start(f32[16,128]{1,0:T(8,128)S(1)} %get-tuple-element.26), channel_id=1, source_target_pairs={{0,4},{4,8},{8,12},{12,0},{1,5},{5,9},{9,13},{13,1},{2,6},{6,10},{... | collective-permute-start | bytes 24584 | tf_op jit(solution)/shard_map/ppermute | solution.py:518
  62.5 13.3 %collective-permute-start.9 = (f32[16,128]{1,0:T(8,128)S(1)}, f32[16,128]{1,0:T(8,128)S(1)}, u32[]{:S(2)}, u32[]{:S(2)}) collective-permute-start(f32[16,128]{1,0:T(8,128)S(1)} %add_add_fusion.1), channel_id=1, source_target_pairs={{0,3},{1,0},{2,1},{3,2},{4,7},{5,4},{6,5},{7,6},{8,11},{9,8},{10,9... | collective-permute-start | bytes 24584 | tf_op jit(solution)/shard_map/ppermute | solution.py:518
  67.0 8.7 %collective-permute-start.8 = (f32[16,128]{1,0:T(8,128)S(1)}, f32[16,128]{1,0:T(8,128)S(1)}, u32[]{:S(2)}, u32[]{:S(2)}) collective-permute-start(f32[16,128]{1,0:T(8,128)S(1)} %add_add_fusion.1), channel_id=1, source_target_pairs={{0,2},{1,3},{2,0},{3,1},{4,6},{5,7},{6,4},{7,5},{8,10},{9,11},{10,... | collective-permute-start | bytes 24584 | tf_op jit(solution)/shard_map/ppermute | solution.py:518
  67.0 8.7 %collective-permute-start.7 = (f32[16,128]{1,0:T(8,128)S(1)}, f32[16,128]{1,0:T(8,128)S(1)}, u32[]{:S(2)}, u32[]{:S(2)}) collective-permute-start(f32[16,128]{1,0:T(8,128)S(1)} %add_add_fusion.1), channel_id=1, source_target_pairs={{0,1},{1,2},{2,3},{3,0},{4,5},{5,6},{6,7},{7,4},{8,9},{9,10},{10,1... | collective-permute-start | bytes 24584 | tf_op jit(solution)/shard_map/ppermute | solution.py:518
  74.4 1.3 %copy-start.1 = (s32[3840,128]{1,0:T(8,128)}, s32[3840,128]{1,0:T(8,128)S(1)}, u32[]{:S(2)}) copy-start(s32[3840,128]{1,0:T(8,128)S(1)} %get-tuple-element.35.swap_ref) | copy-start | bytes 5898244

commit v3 on v2

--- a/solution.py
+++ b/solution.py
@@ -1,4 +1,5 @@
 import functools
+import math
 
 import jax
 import jax.numpy as jnp
@@ -11,7 +12,6 @@
 CX, CY, CELLS = 16, 8, 32768
 TILES = CELLS // 1024
 LANE_RUNS, SUB_RUNS, SWAPS = 9, 3, 30 * 16
-VMEM = 48 * 2**20
 
 
 def take(x, index, axis):
@@ -102,23 +102,30 @@
     return tiles
 
 
-def follow_plan(tiles, lane_ref, sub_ref, swap_ref):
-    tiles = [take(t, lane_ref[0, 8 * i : 8 * i + 8], 1) for i, t in enumerate(tiles)]
+def follow_plan(channels, lane_ref, sub_ref, swap_ref):
+    def gathered(ref, run, axis):
+        for i in range(TILES):
+            index = ref[run, 8 * i : 8 * i + 8]
+            for tiles in channels:
+                tiles[i] = take(tiles[i], index, axis)
+
+    gathered(lane_ref, 0, 1)
     swap = 0
     for phase in range(8, 16):
         if phase > 12:
-            tiles = [take(t, sub_ref[phase - 13, 8 * i : 8 * i + 8], 0) for i, t in enumerate(tiles)]
+            gathered(sub_ref, phase - 13, 0)
         hop = 1 << (min(phase, 12) - 8)
         while hop:
             for i in range(TILES):
                 if i & hop == 0:
-                    a, b = tiles[i], tiles[i + hop]
                     crossed = swap_ref[8 * swap : 8 * swap + 8] != 0
                     swap += 1
-                    tiles[i], tiles[i + hop] = jnp.where(crossed, b, a), jnp.where(crossed, a, b)
+                    for tiles in channels:
+                        a, b = tiles[i], tiles[i + hop]
+                        tiles[i], tiles[i + hop] = jnp.where(crossed, b, a), jnp.where(crossed, a, b)
             hop //= 2
-        tiles = [take(t, lane_ref[phase - 7, 8 * i : 8 * i + 8], 1) for i, t in enumerate(tiles)]
-    return tiles
+        gathered(lane_ref, phase - 7, 1)
+    return channels
 
 
 def plan_shapes():
@@ -182,24 +189,57 @@
     return out
 
 
-def deposit_kernel(
-    cell_ref, code_ref, state_ref, flag_ref, grid_ref, up_ref, down_ref, tag_ref, cells, lane_ref, sub_ref, swap_ref
-):
-    cell = cell_ref[...]
-    key = ((cell & 0x700) << 4) | ((cell & 0x7800) >> 3) | (cell & 0xFF)
+def plan_kernel(source, key_ref, lane_ref, sub_ref, swap_ref):
+    k = key_ref[...]
+    if source:
+        key = ((k & 0x700) << 4) | ((k & 0x7800) >> 3) | (k & 0xFF)
+    else:
+        key = ((k & 0x380) << 5) | ((k & 0x7C00) >> 3) | (k & 0x7F)
     sort_plan(split_tiles(key), lane_ref, sub_ref, swap_ref)
+
+
+def make_plan(key, source):
+    return kernel_call(
+        functools.partial(plan_kernel, source),
+        "cell_plan" if source else "particle_plan",
+        [of(shape, I32) for shape in plan_shapes()],
+        [],
+        (key,),
+        flops=10**7,
+    )
+
+
+def move_kernel(value_ref, lane_ref, sub_ref, swap_ref, out_ref):
+    def move(pair, carry):
+        at = (2 * pair, 2 * pair + 1)
+        channels = [[value_ref[c, 8 * i : 8 * i + 8] for i in range(TILES)] for c in at]
+        follow_plan(channels, lane_ref, sub_ref, swap_ref)
+        for c, tiles in zip(at, channels):
+            for i, t in enumerate(tiles):
+                out_ref[c, 8 * i : 8 * i + 8] = t
+        return carry
+
+    lax.fori_loop(0, value_ref.shape[0] // 2, move, 0)
+
+
+def move_tag_kernel(code_ref, state_ref, lane_ref, sub_ref, swap_ref, out_ref, tag_ref):
     tag = (code_ref[...] << 15) | (iota((256, 128), 0) * 128 + iota((256, 128), 1))
-    for i, t in enumerate(follow_plan(split_tiles(tag), lane_ref, sub_ref, swap_ref)):
+    for i, t in enumerate(follow_plan([split_tiles(tag)], lane_ref, sub_ref, swap_ref)[0]):
         tag_ref[8 * i : 8 * i + 8] = t
-
-    def move(c, carry):
-        tiles = [state_ref[c, 8 * i : 8 * i + 8] for i in range(TILES)]
-        for i, t in enumerate(follow_plan(tiles, lane_ref, sub_ref, swap_ref)):
-            cells[c, i] = t
-        return carry
-
-    lax.fori_loop(0, 12, move, 0)
-
+    move_kernel(state_ref, lane_ref, sub_ref, swap_ref, out_ref)
+
+
+def move_to_cells(code, state, plan):
+    return kernel_call(
+        move_tag_kernel, "to_cells", (of(state.shape), of(code.shape, I32)), [], (code, state, *plan), flops=10**7
+    )
+
+
+def move_to_particles(values, plan):
+    return kernel_call(move_kernel, "to_particles", (of(values.shape),), [], (values, *plan), flops=10**7)[0]
+
+
+def deposit_kernel(cells_ref, tag_ref, flag_ref, grid_ref, up_ref, down_ref):
     up_at = {(f, x, h): (first, count, at) for f, x, h, first, count, at in y_pieces(Y_UP)}
     down_at = {(f, x, h): (first, count, at) for f, x, h, first, count, at in y_pieces(Y_DOWN)}
     first_row = iota((2, 8, 128), 1) == 0
@@ -207,14 +247,16 @@
     for x in range(CX + 1):
         here = []
         if x < CX:
-            code = jnp.stack([tag_ref[16 * x + 8 * h : 16 * x + 8 * h + 8] >> 15 for h in range(2)])
+            code = tag_ref[16 * x : 16 * x + 16].reshape(2, 8, 128) >> 15
             fx, fy, fz = fractions(code)
             wx, wy, wz = (1.0 - fx, fx), (1.0 - fy, fy), (1.0 - fz, fz)
             w = {(i, j, k): wx[i] * wy[j] * wz[k] for i in (0, 1) for j in (0, 1) for k in (0, 1)}
             here.append(w)
             for comp in range(3):
-                v = cells[comp, 2 * x : 2 * x + 2]
-                c0, c1, c2 = [cells[3 + 3 * comp + e, 2 * x : 2 * x + 2] for e in range(3)]
+                v, c0, c1, c2 = [
+                    cells_ref[c, 16 * x : 16 * x + 16].reshape(2, 8, 128)
+                    for c in (comp, 3 + 3 * comp, 4 + 3 * comp, 5 + 3 * comp)
+                ]
                 base = v - c0 * fx - c1 * fy - c2 * fz
                 terms = {}
                 for i in (0, 1):
@@ -253,31 +295,40 @@
         before = here
 
 
-def kernel_call(body, name, outs, scratch, in_specs=None):
+def tiled_bytes(shape):
+    *outer, rows, columns = shape
+    return 4 * math.prod(outer) * (-(-rows // 8) * 8) * (-(-columns // 128) * 128)
+
+
+def kernel_call(body, name, outs, scratch, args, in_specs=None, flops=0):
+    held = [x.shape for x in (*args, *outs) if len(x.shape) > 1] + list(scratch)
+    size = sum(tiled_bytes(shape) for shape in held)
     return pl.pallas_call(
         body,
         out_shape=outs,
         **({} if in_specs is None else dict(in_specs=in_specs)),
-        scratch_shapes=scratch,
-        compiler_params=pltpu.CompilerParams(vmem_limit_bytes=VMEM),
+        scratch_shapes=[pltpu.VMEM(shape, F32) for shape in scratch],
+        compiler_params=pltpu.CompilerParams(vmem_limit_bytes=size + 4 * 2**20),
+        cost_estimate=pl.CostEstimate(flops=flops, bytes_accessed=size, transcendentals=0),
         name=name,
-    )
+    )(*args)
 
 
 def of(shape, kind=F32):
     return jax.ShapeDtypeStruct(shape, kind)
 
 
-def deposit(cell, code, state, flags):
+def deposit(cells, tag, flags):
     return kernel_call(
         deposit_kernel,
         "deposit",
-        (of((4, CX + 1, 2, 8, 128)), of((UP_ROWS, 128)), of((DOWN_ROWS, 128)), of((256, 128), I32)),
-        [pltpu.VMEM((12, TILES, 8, 128), F32)] + plan_scratch(),
-    )(cell, code, state, flags)
-
-
-def widen_kernel(keep_ref, grid_ref, own_ref, low_ref, high_ref, flag_ref, wide_ref, up_ref, down_ref):
+        (of((4, CX + 1, 2, 8, 128)), of((UP_ROWS, 128)), of((DOWN_ROWS, 128))),
+        [],
+        (cells, tag, flags),
+    )
+
+
+def widen_kernel(keep_ref, grid_ref, own_ref, low_ref, high_ref, flag_ref, after_ref, wide_ref, up_ref, down_ref):
     keep = keep_ref[1]
     zero = jnp.zeros((2, 8, 128), F32)
     for f in range(5):
@@ -313,14 +364,15 @@
     return pl.BlockSpec(memory_space=pltpu.VMEM)
 
 
-def widen(keep, grid, own, low, high, flags):
+def widen(keep, grid, own, low, high, flags, after):
     return kernel_call(
         widen_kernel,
         "widen",
         (of((5, CX + 1, 2, 24, 128)), of((UP_ROWS, 128)), of((DOWN_ROWS, 128))),
         [],
-        [smem()] + [vmem()] * 5,
-    )(keep, grid, own, low, high, flags)
+        (keep, grid, own, low, high, flags, after),
+        [smem()] + [vmem()] * 5 + [pl.BlockSpec(memory_space=pl.ANY)],
+    )
 
 
 def krylov_kernel(keep_ref, wide_ref, low_ref, high_ref, vel_ref, fluid_ref, k0_ref, k1_ref, k2_ref, sums_ref, ext):
@@ -345,9 +397,9 @@
         else:
             ext[f, plane + 20, h, 4:21] = rows
     for plane in range(25):
-        mass = jnp.maximum(ext[0, plane], 0.5)
+        inverse = 1.0 / jnp.maximum(ext[0, plane], 0.5)
         for d in range(3):
-            vel_ref[d, plane] = ext[1 + d, plane] / mass
+            vel_ref[d, plane] = ext[1 + d, plane] * inverse
         fluid_ref[plane] = ext[4, plane]
     for plane in range(1, 24):
         vy, vz = vel_ref[1, plane], vel_ref[2, plane]
@@ -391,9 +443,10 @@
         krylov_kernel,
         "krylov",
         (of((3, 25, 2, 24, 128)),) + (of((25, 2, 24, 128)),) * 4 + (of((16, 128)),),
-        [pltpu.VMEM((5, 25, 2, 24, 128), F32)],
+        [(5, 25, 2, 24, 128)],
+        (keep, wide, low, high),
         [smem()] + [vmem()] * 3,
-    )(keep, wide, low, high)
+    )
 
 
 def steps_from(gram, energy, apply_once):
@@ -437,72 +490,62 @@
     return [jnp.where(smooth, a, b) * (1.0 / 6.0) for a, b in zip(power, turned)]
 
 
-def plan_kernel(tag_ref, lane_ref, sub_ref, swap_ref):
-    place = tag_ref[...] & 0x7FFF
-    key = ((place & 0x380) << 5) | ((place & 0x7C00) >> 3) | (place & 0x7F)
-    sort_plan(split_tiles(key), lane_ref, sub_ref, swap_ref)
-
-
-def return_plan(tag):
-    return kernel_call(plan_kernel, "return_plan", [of(shape, I32) for shape in plan_shapes()], [])(tag)
-
-
-def project_kernel(
-    sums_ref, vel_ref, fluid_ref, k0_ref, k1_ref, k2_ref, tag_ref, lane_ref, sub_ref, swap_ref,
-    pressure_ref, out_ref, press, proj, value,
-):
-    total = jnp.sum(sums_ref[...].reshape(-1, 16, 128), axis=0)
-    total = jnp.sum(total, axis=1, keepdims=True)
-    c = coefficients([jnp.broadcast_to(total[i : i + 1], (8, 128)) for i in range(14)])
-    c = [jnp.concatenate([a, a, a], axis=0)[None] for a in c]
-    for plane in range(3, 22):
-        press[plane] = c[0] * k0_ref[plane] + c[1] * k1_ref[plane] + c[2] * k2_ref[plane]
+def blend_kernel(vel_ref, fluid_ref, k0_ref, k1_ref, k2_ref, tag_ref, out_ref, proj):
+    for x in range(CX + 1):
+        fluid = fluid_ref[x + 4, :, 8:24]
+        for b, ref in enumerate((None, k0_ref, k1_ref, k2_ref)):
+            if ref is None:
+                fields = [fluid * vel_ref[d, x + 4, :, 8:24] for d in range(3)]
+            else:
+                p, scale = ref[x + 4], -0.5 * fluid
+                inner = p[:, 8:24]
+                fields = [
+                    scale * (ref[x + 5, :, 8:24] - ref[x + 3, :, 8:24]),
+                    scale * (y_shift(p, -1) - y_shift(p, 1))[:, 8:24],
+                    scale * (z_ahead(inner) - z_behind(inner)),
+                ]
+            for d, field in enumerate(fields):
+                proj[x, 3 * b + d, 0] = field
+                proj[x, 3 * b + d, 1] = z_ahead(field)
     for x in range(CX):
-        for h in range(2):
-            pressure_ref[x, :, 128 * h : 128 * h + 128] = press[x + 4, h, 8:16]
-    for x in range(CX + 1):
-        p = press[x + 4]
-        slopes = (
-            press[x + 5] - press[x + 3],
-            y_shift(p, -1) - y_shift(p, 1),
-            z_ahead(p) - z_behind(p),
-        )
-        for d in range(3):
-            field = fluid_ref[x + 4] * (vel_ref[d, x + 4] - 0.5 * slopes[d])
-            proj[x, d, 0] = field
-            proj[x, d, 1] = z_ahead(field)
-    for x in range(CX):
-        code = jnp.stack([tag_ref[16 * x + 8 * h : 16 * x + 8 * h + 8] >> 15 for h in range(2)])
+        code = tag_ref[16 * x : 16 * x + 16].reshape(2, 8, 128) >> 15
         fx, fy, fz = fractions(code)
         wx, wy, wz = (1.0 - fx, fx), (1.0 - fy, fy), (1.0 - fz, fz)
         w = {(i, j, k): wx[i] * wy[j] * wz[k] for i in (0, 1) for j in (0, 1) for k in (0, 1)}
-        for d in range(3):
+        for c in range(12):
             result = None
             for (i, j, k), weight in w.items():
-                term = weight * proj[x + i, d, k, :, 8 + j : 16 + j]
+                term = weight * proj[x + i, c, k, :, j : 8 + j]
                 result = term if result is None else result + term
-            value[d, 2 * x : 2 * x + 2] = result
-
-    def move(d, carry):
-        tiles = [value[d, i] for i in range(TILES)]
-        for i, t in enumerate(follow_plan(tiles, lane_ref, sub_ref, swap_ref)):
-            out_ref[d, 8 * i : 8 * i + 8] = t
-        return carry
-
-    lax.fori_loop(0, 3, move, 0)
-
-
-def project(*args):
+            out_ref[c, 16 * x : 16 * x + 16] = result.reshape(16, 128)
+
+
+def blend(*args):
     return kernel_call(
-        project_kernel,
-        "project",
-        (of((CX, CY, 256)), of((3, 256, 128))),
-        [
-            pltpu.VMEM((25, 2, 24, 128), F32),
-            pltpu.VMEM((CX + 1, 3, 2, 2, 24, 128), F32),
-            pltpu.VMEM((3, TILES, 8, 128), F32),
-        ],
-    )(*args)
+        blend_kernel, "blend", (of((12, 256, 128)),), [(CX + 1, 12, 2, 2, 16, 128)], args, flops=10**7
+    )[0]
+
+
+def finish_kernel(sums_ref, k0_ref, k1_ref, k2_ref, parts_ref, pressure_ref, out_ref):
+    total = jnp.sum(sums_ref[...], axis=1, keepdims=True)
+    c = coefficients([jnp.broadcast_to(total[i : i + 1], (8, 128)) for i in range(14)])
+    for x in range(CX):
+        for h in range(2):
+            k0, k1, k2 = [ref[x + 4, h, 8:16] for ref in (k0_ref, k1_ref, k2_ref)]
+            pressure_ref[x, :, 128 * h : 128 * h + 128] = c[0] * k0 + c[1] * k1 + c[2] * k2
+    for i in range(TILES):
+        rows = slice(8 * i, 8 * i + 8)
+        for d in range(3):
+            out_ref[d, rows] = (
+                parts_ref[d, rows]
+                + c[0] * parts_ref[3 + d, rows]
+                + c[1] * parts_ref[6 + d, rows]
+                + c[2] * parts_ref[9 + d, rows]
+            )
+
+
+def finish(*args):
+    return kernel_call(finish_kernel, "finish", (of((CX, CY, 256)), of((3, 256, 128))), [], args)
 
 
 def neighbours(up, down, axis):
@@ -510,32 +553,30 @@
     return lax.ppermute(up, axis, pairs), lax.ppermute(down, axis, [(b, a) for a, b in pairs])
 
 
-def everywhere(sums):
-    for axis in ("gx", "gy"):
-        count = lax.axis_size(axis)
-        parts = [sums]
-        for shift in range(1, count):
-            parts.append(lax.ppermute(sums, axis, [(i, (i + shift) % count) for i in range(count)]))
-        sums = functools.reduce(jnp.add, parts)
-    return sums
+def summed(sums, axis):
+    count = lax.axis_size(axis)
+    parts = [sums]
+    for shift in range(1, count):
+        parts.append(lax.ppermute(sums, axis, [(i, (i + shift) % count) for i in range(count)]))
+    return functools.reduce(jnp.add, parts)
 
 
 def local(cell_index, offset_code, particle_state, fluid_flags):
     places = [(axis, lax.axis_index(axis), lax.axis_size(axis)) for axis in ("gx", "gy")]
     keep = jnp.stack([(at + 1 < size).astype(F32) for _, at, size in places])
-    grid, up, down, tag = deposit(
-        cell_index.reshape(256, 128),
-        offset_code.reshape(256, 128),
-        particle_state.reshape(12, 256, 128),
-        fluid_flags,
-    )
+    plan = make_plan(cell_index.reshape(256, 128), True)
+    cells, tag = move_to_cells(offset_code.reshape(256, 128), particle_state.reshape(12, 256, 128), plan)
+    grid, up, down = deposit(cells, tag, fluid_flags)
     low, high = neighbours(up, down, "gy")
-    plan = return_plan(tag)
-    wide, up_x, down_x = widen(keep, grid, up, low, high, fluid_flags)
+    plan = make_plan(tag & 0x7FFF, False)
+    wide, up_x, down_x = widen(keep, grid, up, low, high, fluid_flags, plan[1])
     low, high = neighbours(up_x, down_x, "gx")
     vel, fluid, k0, k1, k2, sums = krylov(keep, wide, low, high)
-    sums = everywhere(sums)
-    pressure, result = project(sums, vel, fluid, k0, k1, k2, tag, *plan)
+    parts = blend(vel, fluid, k0, k1, k2, tag)
+    sums, parts = lax.optimization_barrier((summed(sums, "gx"), parts))
+    parts = move_to_particles(parts, plan)
+    sums = summed(sums, "gy")
+    pressure, result = finish(sums, k0, k1, k2, parts)
     return pressure, result.reshape(1, 3, CELLS)
 
 

time: 83.3 us -> 75.5 us (0.906)
  waiting for transfers between devices: 11.9 us -> 2.35 us
  Pallas kernels: 39.7 us -> 44.7 us
  local copies, waits for them, and re-layouts: 6.72 us -> 3.21 us
    ppermute x2, waiting for transfers between devices: 8.99 us -> 2.33 us  [neighbours(): lax.ppermute(up, axis, pairs)]
    pallas_call x5 -> x9, Pallas kernels: 39.7 us -> 44.7 us  [kernel_call(): pl.pallas_call(body, out_shape=outs, **{} if in_specs is None else dict(i...]
    unnamed x14 -> x8, local copies, waits for them, and re-layouts: 6.72 us -> 3.21 us
    ppermute x6, waiting for transfers between devices: 2.92 us -> 0.02 us  [summed(): lax.ppermute(sums, axis, [(i, (i + shift) % count) for i in range(count)])]
  transfers between devices with their start and end apart: 10 -> 10, of which waited for: 4 -> 2; matrix products, arithmetic and copies ran while one was open for 0% -> 0% of each run, Pallas kernels for 8% -> 29%
where the time goes in v3:
time: 75.5 us; the launch traced here: 75.3 us
  Pallas kernels  44.7 us (59%)
  starting transfers between devices  24 us (32%)
  local copies, waits for them, and re-layouts  3.21 us (4%)
  waiting for transfers between devices  2.35 us (3%)
  between operations  0.8 us (1%)
    pallas_call x9, Pallas kernels, kernel_call(): pl.pallas_call(body, out_shape=outs, **{} if in_specs is None else dict(i...  44.7 us
    ppermute x6, starting transfers between devices, summed(): lax.ppermute(sums, axis, [(i, (i + shift) % count) for i in range(count)])  12.6 us
    ppermute x2, starting transfers between devices, neighbours(): lax.ppermute(up, axis, pairs)  8.81 us
    unnamed x8, local copies, waits for them, and re-layouts  3.21 us
    ppermute x2, starting transfers between devices, neighbours(): lax.ppermute(down, axis, [(b, a) for a, b in pairs])  2.58 us
    ppermute x2, waiting for transfers between devices, neighbours(): lax.ppermute(up, axis, pairs)  2.33 us
  transfers between devices with their start and end apart: 10, of which 2 were waited for; matrix products, arithmetic and copies ran while one was open for 0% of the time, Pallas kernels for 29%

profile of v3, /device:TPU:0, one launch (start us, length us, event | category | flops | bytes accessed | tf_op | source)
XLA Modules:
  0.0 75.3 jit_solution(1385787686110332803)
XLA Ops:
  0.6 0.0 copy-start.3
  0.6 0.9 %copy-done.3 = s32[1,32768]{1,0:T(1,128)S(1)} copy-done((s32[1,32768]{1,0:T(1,128)S(1)}, s32[1,32768]{1,0:T(1,128)}, u32[]{:S(2)}) %copy-start.3) | copy-done | bytes 131096
  1.5 6.4 %cell_plan.1 = (s32[9,256,128]{2,1,0:T(8,128)S(1)}, s32[3,256,128]{2,1,0:T(8,128)S(1)}, s32[3840,128]{1,0:T(8,128)S(1)}) custom-call(s32[256,128]{1,0:T(8,128)S(1)} %bitcast.8), custom_call_target="tpu_custom_call" | custom-call | flops 10000000 | bytes 3670016 | tf_op jit(solution)/shard_map/cell_plan/pallas_call | solution.py:306
  8.0 0.0 copy-start
  8.0 1.4 %copy-done = f32[1,12,32768]{2,0,1:T(1,128)S(1)} copy-done((f32[1,12,32768]{2,0,1:T(1,128)S(1)}, f32[1,12,32768]{2,0,1:T(1,128)}, u32[]{:S(2)}) %copy-start) | copy-done | bytes 1572888
  9.4 0.0 copy-start.2
  9.4 0.9 %copy-done.2 = s32[1,32768]{1,0:T(1,128)S(1)} copy-done((s32[1,32768]{1,0:T(1,128)S(1)}, s32[1,32768]{1,0:T(1,128)}, u32[]{:S(2)}) %copy-start.2) | copy-done | bytes 131096
  10.3 0.0 copy-start.1
  10.3 11.9 %to_cells.1 = (f32[12,256,128]{2,1,0:T(8,128)S(1)}, s32[256,128]{1,0:T(8,128)S(1)}) custom-call(s32[256,128]{1,0:T(8,128)S(1)} %bitcast.7, f32[12,256,128]{2,1,0:T(8,128)S(1)} %bitcast.6, s32[9,256,128]{2,1,0:T(8,128)S(1)} %get-tuple-element.26.lane_ref, s32[3,256,128]{2,1,0:T(8,128)S(1)} %get-tuple-element.27.sub_ref, ...), custom_call_target="tpu_custom_call" | custom-call | flops 10000000 | bytes 6946816 | tf_op jit(solution)/shard_map/to_cells/pallas_call | solution.py:306
  22.2 0.0 copy-done.1
  22.2 0.7 deposit.1
  22.9 1.3 %collective-permute-start.1 = (f32[752,128]{1,0:T(8,128)S(1)}, f32[752,128]{1,0:T(8,128)S(1)}, u32[]{:S(2)}, u32[]{:S(2)}) collective-permute-start(f32[752,128]{1,0:T(8,128)S(1)} %get-tuple-element.33), channel_id=1, source_target_pairs={{1,0},{2,1},{3,2},{5,4},{6,5},{7,6},{9,8},{10,9},{11,10},{13,12},{... | collective-permute-start | bytes 1155080 | tf_op jit(solution)/shard_map/ppermute | solution.py:553
  24.2 5.8 %collective-permute-start = (f32[720,128]{1,0:T(8,128)S(1)}, f32[720,128]{1,0:T(8,128)S(1)}, u32[]{:S(2)}, u32[]{:S(2)}) collective-permute-start(f32[720,128]{1,0:T(8,128)S(1)} %get-tuple-element.32.own_ref), channel_id=1, source_target_pairs={{0,1},{1,2},{2,3},{4,5},{5,6},{6,7},{8,9},{9,10},{10,11},{12,13},{... | collective-permute-start | bytes 1105928 | tf_op jit(solution)/shard_map/ppermute | solution.py:553
  30.0 6.4 %particle_plan.1 = (s32[9,256,128]{2,1,0:T(8,128)S(1)}, s32[3,256,128]{2,1,0:T(8,128)S(1)}, s32[3840,128]{1,0:T(8,128)S(1)}) custom-call(s32[256,128]{1,0:T(8,128)S(1)} %broadcast_and_fusion.key_ref), custom_call_target="tpu_custom_call" | custom-call | flops 10000000 | bytes 3670016 | tf_op jit(solution)/shard_map/particle_plan/pallas_call | solution.py:306
  36.5 0.1 add_convert_fusion.keep_ref
  36.6 1.1 %collective-permute-done.low_ref = f32[720,128]{1,0:T(8,128)S(1)} collective-permute-done((f32[720,128]{1,0:T(8,128)S(1)}, f32[720,128]{1,0:T(8,128)S(1)}, u32[]{:S(2)}, u32[]{:S(2)}) %collective-permute-start) | collective-permute-done | bytes 368672 | tf_op jit(solution)/shard_map/ppermute | solution.py:553
  37.6 0.0 collective-permute-done.1.high_ref
  37.6 1.0 %widen.1 = (f32[5,17,2,24,128]{4,3,2,1,0:T(8,128)S(1)}, f32[720,128]{1,0:T(8,128)S(1)}, f32[752,128]{1,0:T(8,128)S(1)}) custom-call(f32[2]{0:T(128)S(1)} %add_convert_fusion.keep_ref, f32[4,17,2,8,128]{4,3,2,1,0:T(8,128)S(1)} %get-tuple-element.31.grid_ref, f32[720,128]{1,0:T(8,128)S(1)} %get-tuple-element.32.own_ref, ...), custom_call_target="tpu_custom_call" | custom-call | bytes 5046272 | tf_op jit(solution)/shard_map/widen/pallas_call | solution.py:306
  38.6 1.3 %collective-permute-start.3 = (f32[752,128]{1,0:T(8,128)S(1)}, f32[752,128]{1,0:T(8,128)S(1)}, u32[]{:S(2)}, u32[]{:S(2)}) collective-permute-start(f32[752,128]{1,0:T(8,128)S(1)} %get-tuple-element.37), channel_id=1, source_target_pairs={{4,0},{8,4},{12,8},{5,1},{9,5},{13,9},{6,2},{10,6},{14,10},{7,3},{... | collective-permute-start | bytes 1155080 | tf_op jit(solution)/shard_map/ppermute | solution.py:553
  39.9 3.1 %collective-permute-start.2 = (f32[720,128]{1,0:T(8,128)S(1)}, f32[720,128]{1,0:T(8,128)S(1)}, u32[]{:S(2)}, u32[]{:S(2)}) collective-permute-start(f32[720,128]{1,0:T(8,128)S(1)} %get-tuple-element.36), channel_id=1, source_target_pairs={{0,4},{4,8},{8,12},{1,5},{5,9},{9,13},{2,6},{6,10},{10,14},{3,7},{... | collective-permute-start | bytes 1105928 | tf_op jit(solution)/shard_map/ppermute | solution.py:553
  43.0 1.3 %collective-permute-done.2.low_ref = f32[720,128]{1,0:T(8,128)S(1)} collective-permute-done((f32[720,128]{1,0:T(8,128)S(1)}, f32[720,128]{1,0:T(8,128)S(1)}, u32[]{:S(2)}, u32[]{:S(2)}) %collective-permute-start.2) | collective-permute-done | bytes 368672 | tf_op jit(solution)/shard_map/ppermute | solution.py:553
  44.3 0.0 collective-permute-done.3.high_ref
  44.3 2.0 %krylov.1 = (f32[3,25,2,24,128]{4,3,2,1,0:T(8,128)S(1)}, f32[25,2,24,128]{3,2,1,0:T(8,128)S(1)}, f32[25,2,24,128]{3,2,1,0:T(8,128)S(1)}, f32[25,2,24,128]{3,2,1,...) custom-call(f32[2]{0:T(128)S(1)} %add_convert_fusion.keep_ref, ...), custom_call_target="tpu_custom_call" | custom-call | bytes 10223616 | tf_op jit(solution)/shard_map/krylov/pallas_call | solution.py:306
  46.3 1.7 %collective-permute-start.6 = (f32[16,128]{1,0:T(8,128)S(1)}, f32[16,128]{1,0:T(8,128)S(1)}, u32[]{:S(2)}, u32[]{:S(2)}) collective-permute-start(f32[16,128]{1,0:T(8,128)S(1)} %get-tuple-element.38), channel_id=1, source_target_pairs={{0,12},{4,0},{8,4},{12,8},{1,13},{5,1},{9,5},{13,9},{2,14},{6,2},{... | collective-permute-start | bytes 24584 | tf_op jit(solution)/shard_map/ppermute | solution.py:560
  48.0 5.2 %collective-permute-start.5 = (f32[16,128]{1,0:T(8,128)S(1)}, f32[16,128]{1,0:T(8,128)S(1)}, u32[]{:S(2)}, u32[]{:S(2)}) collective-permute-start(f32[16,128]{1,0:T(8,128)S(1)} %get-tuple-element.38), channel_id=1, source_target_pairs={{0,8},{4,12},{8,0},{12,4},{1,9},{5,13},{9,1},{13,5},{2,10},{6,14},... | collective-permute-start | bytes 24584 | tf_op jit(solution)/shard_map/ppermute | solution.py:560
  53.2 0.2 collective-permute-start.4
  53.4 4.3 %blend.1.value_ref = f32[12,256,128]{2,1,0:T(8,128)S(1)} custom-call(f32[3,25,2,24,128]{4,3,2,1,0:T(8,128)S(1)} %get-tuple-element.39.vel_ref, f32[25,2,24,128]{3,2,1,0:T(8,128)S(1)} %get-tuple-element.40.fluid_ref, f32[25,2,24,128]{3,2,1,0:T(8,128)S(1)} %get-tuple-element.41.k0_ref, f32[25,2,24,128]{3,2,1,0:T(8,128)S(1)} %get-tuple-element.42.k1_ref, ...), custom_call_target="tpu_custom_call" | custom-call | flops 10000000 | bytes 12689408 | tf_op jit(solution)/shard_map/blend/pallas_call | solution.py:306
  57.6 0.0 collective-permute-done.6
  57.6 0.0 collective-permute-done.5
  57.7 0.0 collective-permute-done.4
  57.7 4.6 %collective-permute-start.9 = (f32[16,128]{1,0:T(8,128)S(1)}, f32[16,128]{1,0:T(8,128)S(1)}, u32[]{:S(2)}, u32[]{:S(2)}) collective-permute-start(f32[16,128]{1,0:T(8,128)S(1)} %add_add_fusion.1), channel_id=1, source_target_pairs={{0,3},{1,0},{2,1},{3,2},{4,7},{5,4},{6,5},{7,6},{8,11},{9,8},{10,9... | collective-permute-start | bytes 24584 | tf_op jit(solution)/shard_map/ppermute | solution.py:560
  62.3 0.0 collective-permute-start.8
  62.3 1.0 %collective-permute-start.7 = (f32[16,128]{1,0:T(8,128)S(1)}, f32[16,128]{1,0:T(8,128)S(1)}, u32[]{:S(2)}, u32[]{:S(2)}) collective-permute-start(f32[16,128]{1,0:T(8,128)S(1)} %add_add_fusion.1), channel_id=1, source_target_pairs={{0,1},{1,2},{2,3},{3,0},{4,5},{5,6},{6,7},{7,4},{8,9},{9,10},{10,1... | collective-permute-start | bytes 24584 | tf_op jit(solution)/shard_map/ppermute | solution.py:560
  63.3 10.9 %to_particles.1.parts_ref = f32[12,256,128]{2,1,0:T(8,128)S(1)} custom-call(f32[12,256,128]{2,1,0:T(8,128)S(1)} %blend.1.value_ref, s32[9,256,128]{2,1,0:T(8,128)S(1)} %get-tuple-element.46.lane_ref, s32[3,256,128]{2,1,0:T(8,128)S(1)} %get-tuple-element.34.after_ref.sub_ref, s32[3840,128]{1,0:T(8,128)S(1)} %get-tuple-element.47.swap_ref), custom_call_target="tpu_custom_call" | custom-call | flops 10000000 | bytes 6684672 | tf_op jit(solution)/shard_map/to_particles/pallas_call | solution.py:306
  74.2 0.0 collective-permute-done.9
  74.2 0.0 collective-permute-done.8
  74.2 0.0 collective-permute-done.7
  74.2 1.0 %finish.1 = (f32[16,8,256]{2,1,0:T(8,128)}, f32[3,256,128]{2,1,0:T(8,128)}) custom-call(f32[16,128]{1,0:T(8,128)S(1)} %add_add_fusion.sums_ref, f32[25,2,24,128]{3,2,1,0:T(8,128)S(1)} %get-tuple-element.41.k0_ref, f32[25,2,24,128]{3,2,1,0:T(8,128)S(1)} %get-tuple-element.42.k1_ref, f32[25,2,24,128]{3,2,1,0:T(8,128)S(1)} %get-tuple-element.43.k2_ref, ...), custom_call_target="tpu_custom_call" | custom-call | bytes 3948544 | tf_op jit(solution)/shard_map/finish/pallas_call | solution.py:306
  (3 shorter events, 0.0 us)
Async XLA Ops:
  0.6 0.9 %copy-start.3 = (s32[1,32768]{1,0:T(1,128)S(1)}, s32[1,32768]{1,0:T(1,128)}, u32[]{:S(2)}) copy-start(s32[1,32768]{1,0:T(1,128)} %param.4) | copy-start | bytes 393220
  8.0 1.4 %copy-start = (f32[1,12,32768]{2,0,1:T(1,128)S(1)}, f32[1,12,32768]{2,0,1:T(1,128)}, u32[]{:S(2)}) copy-start(f32[1,12,32768]{2,0,1:T(1,128)} %param.6) | copy-start | bytes 4718596
  9.4 0.9 %copy-start.2 = (s32[1,32768]{1,0:T(1,128)S(1)}, s32[1,32768]{1,0:T(1,128)}, u32[]{:S(2)}) copy-start(s32[1,32768]{1,0:T(1,128)} %param.5) | copy-start | bytes 393220
  10.3 11.9 %copy-start.1 = (s32[16,8,256]{2,1,0:T(8,128)S(1)}, s32[16,8,256]{2,1,0:T(8,128)}, u32[]{:S(2)}) copy-start(s32[16,8,256]{2,1,0:T(8,128)} %flag_ref.3) | copy-start | bytes 393220
  22.9 14.7 %collective-permute-start.1 = (f32[752,128]{1,0:T(8,128)S(1)}, f32[752,128]{1,0:T(8,128)S(1)}, u32[]{:S(2)}, u32[]{:S(2)}) collective-permute-start(f32[752,128]{1,0:T(8,128)S(1)} %get-tuple-element.33), channel_id=1, source_target_pairs={{1,0},{2,1},{3,2},{5,4},{6,5},{7,6},{9,8},{10,9},{11,10},{13,12},{... | collective-permute-start | bytes 1155080 | tf_op jit(solution)/shard_map/ppermute | solution.py:553
  24.2 13.4 %collective-permute-start = (f32[720,128]{1,0:T(8,128)S(1)}, f32[720,128]{1,0:T(8,128)S(1)}, u32[]{:S(2)}, u32[]{:S(2)}) collective-permute-start(f32[720,128]{1,0:T(8,128)S(1)} %get-tuple-element.32.own_ref), channel_id=1, source_target_pairs={{0,1},{1,2},{2,3},{4,5},{5,6},{6,7},{8,9},{9,10},{10,11},{12,13},{... | collective-permute-start | bytes 1105928 | tf_op jit(solution)/shard_map/ppermute | solution.py:553
  38.6 5.6 %collective-permute-start.3 = (f32[752,128]{1,0:T(8,128)S(1)}, f32[752,128]{1,0:T(8,128)S(1)}, u32[]{:S(2)}, u32[]{:S(2)}) collective-permute-start(f32[752,128]{1,0:T(8,128)S(1)} %get-tuple-element.37), channel_id=1, source_target_pairs={{4,0},{8,4},{12,8},{5,1},{9,5},{13,9},{6,2},{10,6},{14,10},{7,3},{... | collective-permute-start | bytes 1155080 | tf_op jit(solution)/shard_map/ppermute | solution.py:553
  39.9 4.3 %collective-permute-start.2 = (f32[720,128]{1,0:T(8,128)S(1)}, f32[720,128]{1,0:T(8,128)S(1)}, u32[]{:S(2)}, u32[]{:S(2)}) collective-permute-start(f32[720,128]{1,0:T(8,128)S(1)} %get-tuple-element.36), channel_id=1, source_target_pairs={{0,4},{4,8},{8,12},{1,5},{5,9},{9,13},{2,6},{6,10},{10,14},{3,7},{... | collective-permute-start | bytes 1105928 | tf_op jit(solution)/shard_map/ppermute | solution.py:553
  46.3 11.3 %collective-permute-start.6 = (f32[16,128]{1,0:T(8,128)S(1)}, f32[16,128]{1,0:T(8,128)S(1)}, u32[]{:S(2)}, u32[]{:S(2)}) collective-permute-start(f32[16,128]{1,0:T(8,128)S(1)} %get-tuple-element.38), channel_id=1, source_target_pairs={{0,12},{4,0},{8,4},{12,8},{1,13},{5,1},{9,5},{13,9},{2,14},{6,2},{... | collective-permute-start | bytes 24584 | tf_op jit(solution)/shard_map/ppermute | solution.py:560
  48.0 9.7 %collective-permute-start.5 = (f32[16,128]{1,0:T(8,128)S(1)}, f32[16,128]{1,0:T(8,128)S(1)}, u32[]{:S(2)}, u32[]{:S(2)}) collective-permute-start(f32[16,128]{1,0:T(8,128)S(1)} %get-tuple-element.38), channel_id=1, source_target_pairs={{0,8},{4,12},{8,0},{12,4},{1,9},{5,13},{9,1},{13,5},{2,10},{6,14},... | collective-permute-start | bytes 24584 | tf_op jit(solution)/shard_map/ppermute | solution.py:560
  53.2 4.5 %collective-permute-start.4 = (f32[16,128]{1,0:T(8,128)S(1)}, f32[16,128]{1,0:T(8,128)S(1)}, u32[]{:S(2)}, u32[]{:S(2)}) collective-permute-start(f32[16,128]{1,0:T(8,128)S(1)} %get-tuple-element.38), channel_id=1, source_target_pairs={{0,4},{4,8},{8,12},{12,0},{1,5},{5,9},{9,13},{13,1},{2,6},{6,10},{... | collective-permute-start | bytes 24584 | tf_op jit(solution)/shard_map/ppermute | solution.py:560
  57.7 16.5 %collective-permute-start.9 = (f32[16,128]{1,0:T(8,128)S(1)}, f32[16,128]{1,0:T(8,128)S(1)}, u32[]{:S(2)}, u32[]{:S(2)}) collective-permute-start(f32[16,128]{1,0:T(8,128)S(1)} %add_add_fusion.1), channel_id=1, source_target_pairs={{0,3},{1,0},{2,1},{3,2},{4,7},{5,4},{6,5},{7,6},{8,11},{9,8},{10,9... | collective-permute-start | bytes 24584 | tf_op jit(solution)/shard_map/ppermute | solution.py:560
  62.3 12.0 %collective-permute-start.8 = (f32[16,128]{1,0:T(8,128)S(1)}, f32[16,128]{1,0:T(8,128)S(1)}, u32[]{:S(2)}, u32[]{:S(2)}) collective-permute-start(f32[16,128]{1,0:T(8,128)S(1)} %add_add_fusion.1), channel_id=1, source_target_pairs={{0,2},{1,3},{2,0},{3,1},{4,6},{5,7},{6,4},{7,5},{8,10},{9,11},{10,... | collective-permute-start | bytes 24584 | tf_op jit(solution)/shard_map/ppermute | solution.py:560
  62.3 12.0 %collective-permute-start.7 = (f32[16,128]{1,0:T(8,128)S(1)}, f32[16,128]{1,0:T(8,128)S(1)}, u32[]{:S(2)}, u32[]{:S(2)}) collective-permute-start(f32[16,128]{1,0:T(8,128)S(1)} %add_add_fusion.1), channel_id=1, source_target_pairs={{0,1},{1,2},{2,3},{3,0},{4,5},{5,6},{6,7},{7,4},{8,9},{9,10},{10,1... | collective-permute-start | bytes 24584 | tf_op jit(solution)/shard_map/ppermute | solution.py:560

commit v4 on v3

--- a/solution.py
+++ b/solution.py
@@ -40,13 +40,23 @@
         return [jnp.concatenate(tiles[8 * i : 8 * i + 8], axis=0) for i in range(4)]
 
     def lane_steps(groups, stride):
+        def ordered(low, a, b):
+            return jnp.where(low, jnp.minimum(a, b), jnp.maximum(a, b))
+
         while stride:
-            low = lanes & stride == 0
-            other = [take(g, lanes ^ stride, 1) for g in groups]
-            groups = [
-                jnp.where(low, jnp.minimum(g, o), jnp.maximum(g, o)) for g, o in zip(groups, other)
-            ]
-            stride //= 2
+            half = stride // 2
+            low, low_half = lanes & stride == 0, lanes & half == 0
+            across = [take(g, lanes ^ stride, 1) for g in groups]
+            if half:
+                beside = [take(g, lanes ^ half, 1) for g in groups]
+                both = [take(g, lanes ^ (stride | half), 1) for g in groups]
+                groups = [
+                    ordered(low_half, ordered(low, g, a), ordered(low, b, c))
+                    for g, a, b, c in zip(groups, across, beside, both)
+                ]
+            else:
+                groups = [ordered(low, g, a) for g, a in zip(groups, across)]
+            stride //= 4
         return groups
 
     def record(run, groups):
@@ -102,30 +112,69 @@
     return tiles
 
 
-def follow_plan(channels, lane_ref, sub_ref, swap_ref):
-    def gathered(ref, run, axis):
-        for i in range(TILES):
-            index = ref[run, 8 * i : 8 * i + 8]
-            for tiles in channels:
-                tiles[i] = take(tiles[i], index, axis)
-
-    gathered(lane_ref, 0, 1)
-    swap = 0
-    for phase in range(8, 16):
-        if phase > 12:
-            gathered(sub_ref, phase - 13, 0)
-        hop = 1 << (min(phase, 12) - 8)
-        while hop:
+def follow_plan(stages, lane_ref, sub_ref, swap_ref):
+    def crossings(hops, before):
+        out = {}
+        for hop in hops:
             for i in range(TILES):
                 if i & hop == 0:
-                    crossed = swap_ref[8 * swap : 8 * swap + 8] != 0
-                    swap += 1
-                    for tiles in channels:
+                    out[hop, i] = before
+                    before += 1
+        return out, before
+
+    def pass_over(sets, work):
+        for members in sets:
+            moved = [{i: ref[c, i] for i in members} for ref, c in stages]
+            work(members, moved)
+            for (ref, c), tiles in zip(stages, moved):
+                for i, t in tiles.items():
+                    ref[c, i] = t
+
+    def gathered(ref, run, axis, members, moved):
+        for i in members:
+            index = ref[run, 8 * i : 8 * i + 8]
+            for tiles in moved:
+                tiles[i] = take(tiles[i], index, axis)
+
+    def exchanged(hops, number, members, moved):
+        for hop in hops:
+            for i in members:
+                if i & hop == 0:
+                    at = 8 * number[hop, i]
+                    crossed = swap_ref[at : at + 8] != 0
+                    for tiles in moved:
                         a, b = tiles[i], tiles[i + hop]
                         tiles[i], tiles[i + hop] = jnp.where(crossed, b, a), jnp.where(crossed, a, b)
-            hop //= 2
-        gathered(lane_ref, phase - 7, 1)
-    return channels
+
+    eights = [range(8 * g, 8 * g + 8) for g in range(4)]
+    numbers, before = {}, 0
+    for phase in range(8, 16):
+        hops = [1 << k for k in reversed(range(min(phase, 12) - 7))]
+        numbers[phase], before = crossings(hops, before)
+
+    def first(members, moved):
+        gathered(lane_ref, 0, 1, members, moved)
+        for phase in (8, 9, 10):
+            exchanged([4, 2, 1][10 - phase :], numbers[phase], members, moved)
+            gathered(lane_ref, phase - 7, 1, members, moved)
+
+    pass_over(eights, first)
+    for phase in range(11, 16):
+        wide = [16, 8] if phase > 11 else [8]
+        reach = 32 if phase > 11 else 16
+        sets = [range(low + k, low + reach, 8) for low in range(0, 32, reach) for k in range(8)]
+
+        def across(members, moved):
+            if phase > 12:
+                gathered(sub_ref, phase - 13, 0, members, moved)
+            exchanged(wide, numbers[phase], members, moved)
+
+        def within(members, moved):
+            exchanged([4, 2, 1], numbers[phase], members, moved)
+            gathered(lane_ref, phase - 7, 1, members, moved)
+
+        pass_over(sets, across)
+        pass_over(eights, within)
 
 
 def plan_shapes():
@@ -189,54 +238,48 @@
     return out
 
 
-def plan_kernel(source, key_ref, lane_ref, sub_ref, swap_ref):
-    k = key_ref[...]
-    if source:
-        key = ((k & 0x700) << 4) | ((k & 0x7800) >> 3) | (k & 0xFF)
-    else:
-        key = ((k & 0x380) << 5) | ((k & 0x7C00) >> 3) | (k & 0x7F)
+def particle_plan_kernel(tag_ref, lane_ref, sub_ref, swap_ref):
+    k = tag_ref[...] & 0x7FFF
+    key = ((k & 0x380) << 5) | ((k & 0x7C00) >> 3) | (k & 0x7F)
     sort_plan(split_tiles(key), lane_ref, sub_ref, swap_ref)
 
 
-def make_plan(key, source):
+def particle_plan(tag):
+    outs = [of(shape, I32) for shape in plan_shapes()]
+    return kernel_call(particle_plan_kernel, "particle_plan", outs, [], (tag,), flops=10**7)
+
+
+def to_cells_kernel(cell_ref, code_ref, state_ref, cells_ref, tag_ref, code, lane_ref, sub_ref, swap_ref, done):
+    arrivals = [
+        pltpu.make_async_copy(code_ref, code, done.at[0]),
+        pltpu.make_async_copy(state_ref, cells_ref, done.at[1]),
+    ]
+    for arrival in arrivals:
+        arrival.start()
+    k = cell_ref[...]
+    key = ((k & 0x700) << 4) | ((k & 0x7800) >> 3) | (k & 0xFF)
+    sort_plan(split_tiles(key), lane_ref, sub_ref, swap_ref)
+    for arrival in arrivals:
+        arrival.wait()
+    tag_ref[0] = (code[...] << 15) | (iota((TILES, 8, 128), 0) * 8 + iota((TILES, 8, 128), 1)) * 128 + iota(
+        (TILES, 8, 128), 2
+    )
+    for quad in range(3):
+        stages = [(cells_ref, 4 * quad + c) for c in range(4)]
+        follow_plan(stages + [(tag_ref, 0)] * (quad == 0), lane_ref, sub_ref, swap_ref)
+
+
+def to_cells(cell, code, state):
+    anywhere = pl.BlockSpec(memory_space=pltpu.HBM)
     return kernel_call(
-        functools.partial(plan_kernel, source),
-        "cell_plan" if source else "particle_plan",
-        [of(shape, I32) for shape in plan_shapes()],
-        [],
-        (key,),
+        to_cells_kernel,
+        "to_cells",
+        (of((12, TILES, 8, 128)), of((1, TILES, 8, 128), I32)),
+        [pltpu.VMEM(shape, I32) for shape in [(TILES, 8, 128)] + plan_shapes()] + [pltpu.SemaphoreType.DMA((2,))],
+        (cell, code.reshape(TILES, 8, 128), state.reshape(12, TILES, 8, 128)),
+        [vmem(), anywhere, anywhere],
         flops=10**7,
     )
-
-
-def move_kernel(value_ref, lane_ref, sub_ref, swap_ref, out_ref):
-    def move(pair, carry):
-        at = (2 * pair, 2 * pair + 1)
-        channels = [[value_ref[c, 8 * i : 8 * i + 8] for i in range(TILES)] for c in at]
-        follow_plan(channels, lane_ref, sub_ref, swap_ref)
-        for c, tiles in zip(at, channels):
-            for i, t in enumerate(tiles):
-                out_ref[c, 8 * i : 8 * i + 8] = t
-        return carry
-
-    lax.fori_loop(0, value_ref.shape[0] // 2, move, 0)
-
-
-def move_tag_kernel(code_ref, state_ref, lane_ref, sub_ref, swap_ref, out_ref, tag_ref):
-    tag = (code_ref[...] << 15) | (iota((256, 128), 0) * 128 + iota((256, 128), 1))
-    for i, t in enumerate(follow_plan([split_tiles(tag)], lane_ref, sub_ref, swap_ref)[0]):
-        tag_ref[8 * i : 8 * i + 8] = t
-    move_kernel(state_ref, lane_ref, sub_ref, swap_ref, out_ref)
-
-
-def move_to_cells(code, state, plan):
-    return kernel_call(
-        move_tag_kernel, "to_cells", (of(state.shape), of(code.shape, I32)), [], (code, state, *plan), flops=10**7
-    )
-
-
-def move_to_particles(values, plan):
-    return kernel_call(move_kernel, "to_particles", (of(values.shape),), [], (values, *plan), flops=10**7)[0]
 
 
 def deposit_kernel(cells_ref, tag_ref, flag_ref, grid_ref, up_ref, down_ref):
@@ -247,14 +290,14 @@
     for x in range(CX + 1):
         here = []
         if x < CX:
-            code = tag_ref[16 * x : 16 * x + 16].reshape(2, 8, 128) >> 15
+            code = tag_ref[0, 2 * x : 2 * x + 2] >> 15
             fx, fy, fz = fractions(code)
             wx, wy, wz = (1.0 - fx, fx), (1.0 - fy, fy), (1.0 - fz, fz)
             w = {(i, j, k): wx[i] * wy[j] * wz[k] for i in (0, 1) for j in (0, 1) for k in (0, 1)}
             here.append(w)
             for comp in range(3):
                 v, c0, c1, c2 = [
-                    cells_ref[c, 16 * x : 16 * x + 16].reshape(2, 8, 128)
+                    cells_ref[c, 2 * x : 2 * x + 2]
                     for c in (comp, 3 + 3 * comp, 4 + 3 * comp, 5 + 3 * comp)
                 ]
                 base = v - c0 * fx - c1 * fy - c2 * fz
@@ -301,13 +344,13 @@
 
 
 def kernel_call(body, name, outs, scratch, args, in_specs=None, flops=0):
-    held = [x.shape for x in (*args, *outs) if len(x.shape) > 1] + list(scratch)
-    size = sum(tiled_bytes(shape) for shape in held)
+    scratch = [x if hasattr(x, "dtype") else pltpu.VMEM(x, F32) for x in scratch]
+    size = sum(tiled_bytes(x.shape) for x in (*args, *outs, *scratch) if len(x.shape) > 1)
     return pl.pallas_call(
         body,
         out_shape=outs,
         **({} if in_specs is None else dict(in_specs=in_specs)),
-        scratch_shapes=[pltpu.VMEM(shape, F32) for shape in scratch],
+        scratch_shapes=scratch,
         compiler_params=pltpu.CompilerParams(vmem_limit_bytes=size + 4 * 2**20),
         cost_estimate=pl.CostEstimate(flops=flops, bytes_accessed=size, transcendentals=0),
         name=name,
@@ -490,62 +533,54 @@
     return [jnp.where(smooth, a, b) * (1.0 / 6.0) for a, b in zip(power, turned)]
 
 
-def blend_kernel(vel_ref, fluid_ref, k0_ref, k1_ref, k2_ref, tag_ref, out_ref, proj):
+def project_kernel(
+    sums_ref, vel_ref, fluid_ref, k0_ref, k1_ref, k2_ref, tag_ref, lane_ref, sub_ref, swap_ref,
+    pressure_ref, out_ref, press, proj,
+):
+    total = jnp.sum(jnp.sum(sums_ref[...], axis=0), axis=1, keepdims=True)
+    c = coefficients([jnp.broadcast_to(total[i : i + 1], (8, 128)) for i in range(14)])
+    c = [jnp.concatenate([a, a, a], axis=0)[None] for a in c]
+    for plane in range(3, 22):
+        press[plane] = c[0] * k0_ref[plane] + c[1] * k1_ref[plane] + c[2] * k2_ref[plane]
+    for x in range(CX):
+        for h in range(2):
+            pressure_ref[x, :, 128 * h : 128 * h + 128] = press[x + 4, h, 8:16]
     for x in range(CX + 1):
+        p = press[x + 4]
+        inner = p[:, 8:24]
+        slopes = (
+            press[x + 5, :, 8:24] - press[x + 3, :, 8:24],
+            (y_shift(p, -1) - y_shift(p, 1))[:, 8:24],
+            z_ahead(inner) - z_behind(inner),
+        )
         fluid = fluid_ref[x + 4, :, 8:24]
-        for b, ref in enumerate((None, k0_ref, k1_ref, k2_ref)):
-            if ref is None:
-                fields = [fluid * vel_ref[d, x + 4, :, 8:24] for d in range(3)]
-            else:
-                p, scale = ref[x + 4], -0.5 * fluid
-                inner = p[:, 8:24]
-                fields = [
-                    scale * (ref[x + 5, :, 8:24] - ref[x + 3, :, 8:24]),
-                    scale * (y_shift(p, -1) - y_shift(p, 1))[:, 8:24],
-                    scale * (z_ahead(inner) - z_behind(inner)),
-                ]
-            for d, field in enumerate(fields):
-                proj[x, 3 * b + d, 0] = field
-                proj[x, 3 * b + d, 1] = z_ahead(field)
+        for d in range(3):
+            field = fluid * (vel_ref[d, x + 4, :, 8:24] - 0.5 * slopes[d])
+            for j, rows in enumerate((field[:, 0:8], y_shift(field, -1)[:, 0:8])):
+                proj[x, d, j, 0] = rows
+                proj[x, d, j, 1] = z_ahead(rows)
     for x in range(CX):
-        code = tag_ref[16 * x : 16 * x + 16].reshape(2, 8, 128) >> 15
+        code = tag_ref[0, 2 * x : 2 * x + 2] >> 15
         fx, fy, fz = fractions(code)
         wx, wy, wz = (1.0 - fx, fx), (1.0 - fy, fy), (1.0 - fz, fz)
         w = {(i, j, k): wx[i] * wy[j] * wz[k] for i in (0, 1) for j in (0, 1) for k in (0, 1)}
-        for c in range(12):
+        for d in range(3):
             result = None
             for (i, j, k), weight in w.items():
-                term = weight * proj[x + i, c, k, :, j : 8 + j]
+                term = weight * proj[x + i, d, j, k]
                 result = term if result is None else result + term
-            out_ref[c, 16 * x : 16 * x + 16] = result.reshape(16, 128)
-
-
-def blend(*args):
+            out_ref[d, 2 * x : 2 * x + 2] = result
+    follow_plan([(out_ref, d) for d in range(3)], lane_ref, sub_ref, swap_ref)
+
+
+def project(*args):
     return kernel_call(
-        blend_kernel, "blend", (of((12, 256, 128)),), [(CX + 1, 12, 2, 2, 16, 128)], args, flops=10**7
-    )[0]
-
-
-def finish_kernel(sums_ref, k0_ref, k1_ref, k2_ref, parts_ref, pressure_ref, out_ref):
-    total = jnp.sum(sums_ref[...], axis=1, keepdims=True)
-    c = coefficients([jnp.broadcast_to(total[i : i + 1], (8, 128)) for i in range(14)])
-    for x in range(CX):
-        for h in range(2):
-            k0, k1, k2 = [ref[x + 4, h, 8:16] for ref in (k0_ref, k1_ref, k2_ref)]
-            pressure_ref[x, :, 128 * h : 128 * h + 128] = c[0] * k0 + c[1] * k1 + c[2] * k2
-    for i in range(TILES):
-        rows = slice(8 * i, 8 * i + 8)
-        for d in range(3):
-            out_ref[d, rows] = (
-                parts_ref[d, rows]
-                + c[0] * parts_ref[3 + d, rows]
-                + c[1] * parts_ref[6 + d, rows]
-                + c[2] * parts_ref[9 + d, rows]
-            )
-
-
-def finish(*args):
-    return kernel_call(finish_kernel, "finish", (of((CX, CY, 256)), of((3, 256, 128))), [], args)
+        project_kernel,
+        "project",
+        (of((CX, CY, 256)), of((3, TILES, 8, 128))),
+        [(25, 2, 24, 128), (CX + 1, 3, 2, 2, 2, 8, 128)],
+        args,
+    )
 
 
 def neighbours(up, down, axis):
@@ -553,30 +588,23 @@
     return lax.ppermute(up, axis, pairs), lax.ppermute(down, axis, [(b, a) for a, b in pairs])
 
 
-def summed(sums, axis):
-    count = lax.axis_size(axis)
-    parts = [sums]
-    for shift in range(1, count):
-        parts.append(lax.ppermute(sums, axis, [(i, (i + shift) % count) for i in range(count)]))
-    return functools.reduce(jnp.add, parts)
+def everywhere(sums):
+    count = lax.axis_size("gx") * lax.axis_size("gy")
+    spread = jnp.broadcast_to(sums[None], (count,) + sums.shape)
+    return lax.all_to_all(spread, ("gx", "gy"), 0, 0)
 
 
 def local(cell_index, offset_code, particle_state, fluid_flags):
     places = [(axis, lax.axis_index(axis), lax.axis_size(axis)) for axis in ("gx", "gy")]
     keep = jnp.stack([(at + 1 < size).astype(F32) for _, at, size in places])
-    plan = make_plan(cell_index.reshape(256, 128), True)
-    cells, tag = move_to_cells(offset_code.reshape(256, 128), particle_state.reshape(12, 256, 128), plan)
+    cells, tag = to_cells(cell_index.reshape(256, 128), offset_code, particle_state)
     grid, up, down = deposit(cells, tag, fluid_flags)
     low, high = neighbours(up, down, "gy")
-    plan = make_plan(tag & 0x7FFF, False)
+    plan = particle_plan(tag.reshape(256, 128))
     wide, up_x, down_x = widen(keep, grid, up, low, high, fluid_flags, plan[1])
     low, high = neighbours(up_x, down_x, "gx")
     vel, fluid, k0, k1, k2, sums = krylov(keep, wide, low, high)
-    parts = blend(vel, fluid, k0, k1, k2, tag)
-    sums, parts = lax.optimization_barrier((summed(sums, "gx"), parts))
-    parts = move_to_particles(parts, plan)
-    sums = summed(sums, "gy")
-    pressure, result = finish(sums, k0, k1, k2, parts)
+    pressure, result = project(everywhere(sums), vel, fluid, k0, k1, k2, tag, *plan)
     return pressure, result.reshape(1, 3, CELLS)
 
 

time: 75.5 us -> 69.2 us (0.917)
  blocking collectives: 0 us -> 19.3 us
  starting transfers between devices: 24 us -> 11.2 us
  Pallas kernels: 44.7 us -> 32.5 us
    all_to_all x0 -> x1, blocking collectives: none -> 19.3 us  [everywhere(): return lax.all_to_all(spread, ('gx', 'gy'), 0, 0)]
    ppermute x6 -> x0, starting transfers between devices: 12.6 us -> none  [summed(): lax.ppermute(sums, axis, [(i, (i + shift) % count) for i in range(count)])]
    pallas_call x9 -> x6, Pallas kernels: 44.7 us -> 32.5 us  [kernel_call(): pl.pallas_call(body, out_shape=outs, **{} if in_specs is None else dict(i...]
  transfers between devices with their start and end apart: 10 -> 4, of which waited for: 2 -> 2; matrix products, arithmetic and copies ran while one was open for 0% -> 0% of each run, Pallas kernels for 29% -> 10%
where the time goes in v4:
time: 69.2 us; the launch traced here: 68.9 us
  Pallas kernels  32.5 us (47%)
  blocking collectives  19.3 us (28%)
  starting transfers between devices  11.2 us (16%)
  local copies, waits for them, and re-layouts  3.22 us (5%)
  waiting for transfers between devices  1.94 us (3%)
  between operations  0.74 us (1%)
    pallas_call x6, Pallas kernels, kernel_call(): pl.pallas_call(body, out_shape=outs, **{} if in_specs is None else dict(i...  32.5 us
    all_to_all x1, blocking collectives, everywhere(): return lax.all_to_all(spread, ('gx', 'gy'), 0, 0)  19.3 us
    ppermute x2, starting transfers between devices, neighbours(): lax.ppermute(up, axis, pairs)  8.63 us
    unnamed x8, local copies, waits for them, and re-layouts  3.21 us
    ppermute x2, starting transfers between devices, neighbours(): lax.ppermute(down, axis, [(b, a) for a, b in pairs])  2.58 us
    ppermute x2, waiting for transfers between devices, neighbours(): lax.ppermute(up, axis, pairs)  1.94 us
  transfers between devices with their start and end apart: 4, of which 2 were waited for; matrix products, arithmetic and copies ran while one was open for 0% of the time, Pallas kernels for 10%

profile of v4, /device:TPU:0, one launch (start us, length us, event | category | flops | bytes accessed | tf_op | source)
XLA Modules:
  0.0 68.9 jit_solution(10112990864579036718)
XLA Ops:
  0.6 0.0 copy-start
  0.6 1.4 %copy-done = f32[1,12,32768]{2,0,1:T(1,128)S(1)} copy-done((f32[1,12,32768]{2,0,1:T(1,128)S(1)}, f32[1,12,32768]{2,0,1:T(1,128)}, u32[]{:S(2)}) %copy-start) | copy-done | bytes 1572888
  2.0 0.0 copy-start.2
  2.0 0.9 %copy-done.2 = s32[1,32768]{1,0:T(1,128)S(1)} copy-done((s32[1,32768]{1,0:T(1,128)S(1)}, s32[1,32768]{1,0:T(1,128)}, u32[]{:S(2)}) %copy-start.2) | copy-done | bytes 131096
  2.9 0.0 copy-start.3
  2.9 0.9 %copy-done.3 = s32[1,32768]{1,0:T(1,128)S(1)} copy-done((s32[1,32768]{1,0:T(1,128)S(1)}, s32[1,32768]{1,0:T(1,128)}, u32[]{:S(2)}) %copy-start.3) | copy-done | bytes 131096
  3.8 0.0 copy-start.1
  3.9 17.1 %to_cells.1 = (f32[12,32,8,128]{3,2,1,0:T(8,128)S(1)}, s32[1,32,8,128]{3,2,1,0:T(8,128)S(1)}) custom-call(s32[256,128]{1,0:T(8,128)S(1)} %bitcast.9, s32[32,8,128]{2,1,0:T(8,128)S(1)} %bitcast.10, f32[12,32,8,128]{3,2,1,0:T(8,128)S(1)} %bitcast.7), custom_call_target="tpu_custom_call" | custom-call | flops 10000000 | bytes 7208960 | tf_op jit(solution)/shard_map/to_cells/pallas_call | solution.py:349
  20.9 0.0 copy-done.1
  20.9 0.7 deposit.1
  21.6 1.3 %collective-permute-start.1 = (f32[752,128]{1,0:T(8,128)S(1)}, f32[752,128]{1,0:T(8,128)S(1)}, u32[]{:S(2)}, u32[]{:S(2)}) collective-permute-start(f32[752,128]{1,0:T(8,128)S(1)} %get-tuple-element.25), channel_id=1, source_target_pairs={{1,0},{2,1},{3,2},{5,4},{6,5},{7,6},{9,8},{10,9},{11,10},{13,12},{... | collective-permute-start | bytes 1155080 | tf_op jit(solution)/shard_map/ppermute | solution.py:588
  22.9 5.6 %collective-permute-start = (f32[720,128]{1,0:T(8,128)S(1)}, f32[720,128]{1,0:T(8,128)S(1)}, u32[]{:S(2)}, u32[]{:S(2)}) collective-permute-start(f32[720,128]{1,0:T(8,128)S(1)} %get-tuple-element.24.own_ref), channel_id=1, source_target_pairs={{0,1},{1,2},{2,3},{4,5},{5,6},{6,7},{8,9},{9,10},{10,11},{12,13},{... | collective-permute-start | bytes 1105928 | tf_op jit(solution)/shard_map/ppermute | solution.py:588
  28.5 7.0 %particle_plan.1 = (s32[9,256,128]{2,1,0:T(8,128)S(1)}, s32[3,256,128]{2,1,0:T(8,128)S(1)}, s32[3840,128]{1,0:T(8,128)S(1)}) custom-call(s32[256,128]{1,0:T(8,128)S(1)} %bitcast.8), custom_call_target="tpu_custom_call" | custom-call | flops 10000000 | bytes 3670016 | tf_op jit(solution)/shard_map/particle_plan/pallas_call | solution.py:349
  35.6 0.1 add_convert_fusion.keep_ref
  35.6 0.7 collective-permute-done.low_ref
  36.3 0.0 collective-permute-done.1.high_ref
  36.3 1.0 %widen.1 = (f32[5,17,2,24,128]{4,3,2,1,0:T(8,128)S(1)}, f32[720,128]{1,0:T(8,128)S(1)}, f32[752,128]{1,0:T(8,128)S(1)}) custom-call(f32[2]{0:T(128)S(1)} %add_convert_fusion.keep_ref, f32[4,17,2,8,128]{4,3,2,1,0:T(8,128)S(1)} %get-tuple-element.23.grid_ref, f32[720,128]{1,0:T(8,128)S(1)} %get-tuple-element.24.own_ref, ...), custom_call_target="tpu_custom_call" | custom-call | bytes 5046272 | tf_op jit(solution)/shard_map/widen/pallas_call | solution.py:349
  37.3 1.3 %collective-permute-start.3 = (f32[752,128]{1,0:T(8,128)S(1)}, f32[752,128]{1,0:T(8,128)S(1)}, u32[]{:S(2)}, u32[]{:S(2)}) collective-permute-start(f32[752,128]{1,0:T(8,128)S(1)} %get-tuple-element.29), channel_id=1, source_target_pairs={{4,0},{8,4},{12,8},{5,1},{9,5},{13,9},{6,2},{10,6},{14,10},{7,3},{... | collective-permute-start | bytes 1155080 | tf_op jit(solution)/shard_map/ppermute | solution.py:588
  38.6 3.1 %collective-permute-start.2 = (f32[720,128]{1,0:T(8,128)S(1)}, f32[720,128]{1,0:T(8,128)S(1)}, u32[]{:S(2)}, u32[]{:S(2)}) collective-permute-start(f32[720,128]{1,0:T(8,128)S(1)} %get-tuple-element.28), channel_id=1, source_target_pairs={{0,4},{4,8},{8,12},{1,5},{5,9},{9,13},{2,6},{6,10},{10,14},{3,7},{... | collective-permute-start | bytes 1105928 | tf_op jit(solution)/shard_map/ppermute | solution.py:588
  41.7 1.3 %collective-permute-done.2.low_ref = f32[720,128]{1,0:T(8,128)S(1)} collective-permute-done((f32[720,128]{1,0:T(8,128)S(1)}, f32[720,128]{1,0:T(8,128)S(1)}, u32[]{:S(2)}, u32[]{:S(2)}) %collective-permute-start.2) | collective-permute-done | bytes 368672 | tf_op jit(solution)/shard_map/ppermute | solution.py:588
  42.9 0.0 collective-permute-done.3.high_ref
  42.9 2.0 %krylov.1 = (f32[3,25,2,24,128]{4,3,2,1,0:T(8,128)S(1)}, f32[25,2,24,128]{3,2,1,0:T(8,128)S(1)}, f32[25,2,24,128]{3,2,1,0:T(8,128)S(1)}, f32[25,2,24,128]{3,2,1,...) custom-call(f32[2]{0:T(128)S(1)} %add_convert_fusion.keep_ref, ...), custom_call_target="tpu_custom_call" | custom-call | bytes 10223616 | tf_op jit(solution)/shard_map/krylov/pallas_call | solution.py:349
  45.0 19.3 %all_to_all.5.sums_ref = f32[16,16,128]{2,1,0:T(8,128)S(1)} all-to-all(f32[16,16,128]{2,1,0:T(8,128)S(1)} %broadcast_in_dim.2), channel_id=1, replica_groups=mesh['groups'=2,'gx'=4,'gy'=4] {'gx','gy'}, dimensions={0} | all-to-all | bytes 262144 | tf_op jit(solution)/shard_map/all_to_all | solution.py:594
  64.3 4.7 %project.1 = (f32[16,8,256]{2,1,0:T(8,128)}, f32[3,32,8,128]{3,2,1,0:T(8,128)}) custom-call(f32[16,16,128]{2,1,0:T(8,128)S(1)} %all_to_all.5.sums_ref, f32[3,25,2,24,128]{4,3,2,1,0:T(8,128)S(1)} %get-tuple-element.31.vel_ref, f32[25,2,24,128]{3,2,1,0:T(8,128)S(1)} %get-tuple-element.32.fluid_ref, f32[25,2,24,128]{3,2,1,0:T(8,128)S(1)} %get-tuple-element.33.k0_ref, ...), custom_call_target="tpu_custom_call" | custom-call | bytes 10911744 | tf_op jit(solution)/shard_map/project/pallas_call | solution.py:349
  (1 shorter events, 0.0 us)
Async XLA Ops:
  0.6 1.4 %copy-start = (f32[1,12,32768]{2,0,1:T(1,128)S(1)}, f32[1,12,32768]{2,0,1:T(1,128)}, u32[]{:S(2)}) copy-start(f32[1,12,32768]{2,0,1:T(1,128)} %param.6) | copy-start | bytes 4718596
  2.0 0.9 %copy-start.2 = (s32[1,32768]{1,0:T(1,128)S(1)}, s32[1,32768]{1,0:T(1,128)}, u32[]{:S(2)}) copy-start(s32[1,32768]{1,0:T(1,128)} %param.4) | copy-start | bytes 393220
  2.9 0.9 %copy-start.3 = (s32[1,32768]{1,0:T(1,128)S(1)}, s32[1,32768]{1,0:T(1,128)}, u32[]{:S(2)}) copy-start(s32[1,32768]{1,0:T(1,128)} %param.5) | copy-start | bytes 393220
  3.8 17.1 %copy-start.1 = (s32[16,8,256]{2,1,0:T(8,128)S(1)}, s32[16,8,256]{2,1,0:T(8,128)}, u32[]{:S(2)}) copy-start(s32[16,8,256]{2,1,0:T(8,128)} %flag_ref.3) | copy-start | bytes 393220
  21.6 14.7 %collective-permute-start.1 = (f32[752,128]{1,0:T(8,128)S(1)}, f32[752,128]{1,0:T(8,128)S(1)}, u32[]{:S(2)}, u32[]{:S(2)}) collective-permute-start(f32[752,128]{1,0:T(8,128)S(1)} %get-tuple-element.25), channel_id=1, source_target_pairs={{1,0},{2,1},{3,2},{5,4},{6,5},{7,6},{9,8},{10,9},{11,10},{13,12},{... | collective-permute-start | bytes 1155080 | tf_op jit(solution)/shard_map/ppermute | solution.py:588
  22.9 13.4 %collective-permute-start = (f32[720,128]{1,0:T(8,128)S(1)}, f32[720,128]{1,0:T(8,128)S(1)}, u32[]{:S(2)}, u32[]{:S(2)}) collective-permute-start(f32[720,128]{1,0:T(8,128)S(1)} %get-tuple-element.24.own_ref), channel_id=1, source_target_pairs={{0,1},{1,2},{2,3},{4,5},{5,6},{6,7},{8,9},{9,10},{10,11},{12,13},{... | collective-permute-start | bytes 1105928 | tf_op jit(solution)/shard_map/ppermute | solution.py:588
  37.3 5.6 %collective-permute-start.3 = (f32[752,128]{1,0:T(8,128)S(1)}, f32[752,128]{1,0:T(8,128)S(1)}, u32[]{:S(2)}, u32[]{:S(2)}) collective-permute-start(f32[752,128]{1,0:T(8,128)S(1)} %get-tuple-element.29), channel_id=1, source_target_pairs={{4,0},{8,4},{12,8},{5,1},{9,5},{13,9},{6,2},{10,6},{14,10},{7,3},{... | collective-permute-start | bytes 1155080 | tf_op jit(solution)/shard_map/ppermute | solution.py:588
  38.6 4.3 %collective-permute-start.2 = (f32[720,128]{1,0:T(8,128)S(1)}, f32[720,128]{1,0:T(8,128)S(1)}, u32[]{:S(2)}, u32[]{:S(2)}) collective-permute-start(f32[720,128]{1,0:T(8,128)S(1)} %get-tuple-element.28), channel_id=1, source_target_pairs={{0,4},{4,8},{8,12},{1,5},{5,9},{9,13},{2,6},{6,10},{10,14},{3,7},{... | collective-permute-start | bytes 1105928 | tf_op jit(solution)/shard_map/ppermute | solution.py:588

commit v5 on v4

--- a/solution.py
+++ b/solution.py
@@ -39,24 +39,20 @@
     def grouped(tiles):
         return [jnp.concatenate(tiles[8 * i : 8 * i + 8], axis=0) for i in range(4)]
 
+    def partner(x, index, stride, axis):
+        if 2 * stride == (128, 8)[axis == 0]:
+            return pltpu.roll(x, stride, axis)
+        return take(x, index ^ stride, axis)
+
+    def ordered(low, a, b):
+        return jnp.where(low, jnp.minimum(a, b), jnp.maximum(a, b))
+
     def lane_steps(groups, stride):
-        def ordered(low, a, b):
-            return jnp.where(low, jnp.minimum(a, b), jnp.maximum(a, b))
-
         while stride:
-            half = stride // 2
-            low, low_half = lanes & stride == 0, lanes & half == 0
-            across = [take(g, lanes ^ stride, 1) for g in groups]
-            if half:
-                beside = [take(g, lanes ^ half, 1) for g in groups]
-                both = [take(g, lanes ^ (stride | half), 1) for g in groups]
-                groups = [
-                    ordered(low_half, ordered(low, g, a), ordered(low, b, c))
-                    for g, a, b, c in zip(groups, across, beside, both)
-                ]
-            else:
-                groups = [ordered(low, g, a) for g, a in zip(groups, across)]
-            stride //= 4
+            low = lanes & stride == 0
+            other = [partner(g, lanes, stride, 1) for g in groups]
+            groups = [ordered(low, g, o) for g, o in zip(groups, other)]
+            stride //= 2
         return groups
 
     def record(run, groups):
@@ -89,10 +85,8 @@
             stride = 1 << (phase - 13)
             while stride:
                 low = subs & stride == 0
-                other = [take(t, subs ^ stride, 0) for t in tiles]
-                tiles = [
-                    jnp.where(low, jnp.minimum(t, o), jnp.maximum(t, o)) for t, o in zip(tiles, other)
-                ]
+                other = [partner(t, subs, stride, 0) for t in tiles]
+                tiles = [ordered(low, t, o) for t, o in zip(tiles, other)]
                 stride //= 2
             for i, t in enumerate(tiles):
                 sub_ref[phase - 13, 8 * i : 8 * i + 8] = t & 7
@@ -209,33 +203,43 @@
     return [((code >> shift & 3).astype(F32) + 0.5) * 0.25 for shift in (0, 2, 4)]
 
 
-Y_UP = ((0, 4, 5), (1, 5, 4), (2, 4, 5), (3, 5, 4), (4, 5, 3))
-Y_DOWN = ((0, 0, 5), (1, 0, 4), (2, 0, 5), (3, 0, 4), (4, 0, 4))
-X_UP = ((0, 12, 5), (1, 12, 5), (2, 13, 4), (3, 13, 4), (4, 13, 3))
-X_DOWN = ((0, 0, 5), (1, 0, 5), (2, 0, 4), (3, 0, 4), (4, 0, 4))
-UP_ROWS, DOWN_ROWS = 720, 752
-
-
-def y_pieces(table):
+WAYS = [(dx, dy) for dx in (-1, 0, 1) for dy in (-1, 0, 1) if dx or dy]
+
+
+def pieces(dx, dy):
+    def reach(place, last):
+        return max(0, -place, place - last)
+
     at, out = 0, []
-    for x in range(CX + 1):
-        for field, first, count in table:
-            if field == 4 and x == CX:
-                continue
-            for half in range(2):
-                out.append((field, x, half, first, count, at))
-                at += count
-    return out
-
-
-def x_pieces(table):
-    at, out = 0, []
-    for field, first, count in table:
-        for plane in range(first, first + count):
-            for half in range(2):
-                out.append((field, plane, half, at))
-                at += 17
-    return out
+    for plane in {1: range(12, 17), 0: range(17), -1: range(5)}[dx]:
+        far_x = reach(plane - dx * CX, CX)
+        for field in range(8):
+            rows = []
+            for row in {1: range(4, 9), 0: range(9), -1: range(5)}[dy]:
+                far_y = reach(row - dy * CY, CY)
+                read = [
+                    max(far_x - 1, 0) + far_y <= 3,
+                    far_x + max(far_y - 1, 0) <= 3,
+                    far_x + far_y <= 3,
+                ]
+                shared = plane in (0, CX) or row in (0, CY)
+                if field == 7:
+                    wanted = read[2] and plane < CX and row < CY
+                elif field == 0:
+                    wanted = shared and any(read)
+                else:
+                    wanted = read[(field - 1) % 3] and shared == (field < 4)
+                if wanted:
+                    rows.append(row)
+            while rows:
+                count = 1
+                while count < len(rows) and rows[count] == rows[0] + count:
+                    count += 1
+                for half in range(2):
+                    out.append((field, plane, half, rows[0], count, at))
+                    at += count
+                rows = rows[count:]
+    return out, -(-at // 8) * 8
 
 
 def particle_plan_kernel(tag_ref, lane_ref, sub_ref, swap_ref):
@@ -246,7 +250,7 @@
 
 def particle_plan(tag):
     outs = [of(shape, I32) for shape in plan_shapes()]
-    return kernel_call(particle_plan_kernel, "particle_plan", outs, [], (tag,), flops=10**7)
+    return kernel_call(particle_plan_kernel, "particle_plan", outs, [], (tag,), flops=7 * 10**9)
 
 
 def to_cells_kernel(cell_ref, code_ref, state_ref, cells_ref, tag_ref, code, lane_ref, sub_ref, swap_ref, done):
@@ -278,13 +282,28 @@
         [pltpu.VMEM(shape, I32) for shape in [(TILES, 8, 128)] + plan_shapes()] + [pltpu.SemaphoreType.DMA((2,))],
         (cell, code.reshape(TILES, 8, 128), state.reshape(12, TILES, 8, 128)),
         [vmem(), anywhere, anywhere],
-        flops=10**7,
-    )
-
-
-def deposit_kernel(cells_ref, tag_ref, flag_ref, grid_ref, up_ref, down_ref):
-    up_at = {(f, x, h): (first, count, at) for f, x, h, first, count, at in y_pieces(Y_UP)}
-    down_at = {(f, x, h): (first, count, at) for f, x, h, first, count, at in y_pieces(Y_DOWN)}
+        flops=2 * 10**10,
+    )
+
+
+def deposit_kernel(cells_ref, tag_ref, flag_ref, grid_ref, rim_ref, *out_refs):
+    wanted = {}
+    for (dx, dy), ref in zip(WAYS, out_refs):
+        listed, rows = pieces(dx, dy)
+        used = listed[-1][4] + listed[-1][5]
+        if used < rows:
+            ref[used:rows] = jnp.zeros((rows - used, 128), F32)
+        for field, plane, half, first, count, at in listed:
+            wanted.setdefault((field, plane), []).append((ref, half, first, count, at))
+
+    def hand_out(field, plane, main, rim):
+        for ref, half, first, count, at in wanted.get((field, plane), ()):
+            inside = min(count, CY - first)
+            if inside > 0:
+                ref[at : at + inside] = main[half, first : first + inside]
+            if inside < count:
+                ref[at + count - 1 : at + count] = rim[half, 0:1]
+
     first_row = iota((2, 8, 128), 1) == 0
     before = None
     for x in range(CX + 1):
@@ -322,19 +341,16 @@
             near, far = [s[j, 0] + z_behind(s[j, 1]) for j in (0, 1)]
             turned = y_shift(far, 1)
             main = near + jnp.where(first_row, 0.0, turned)
-            grid_ref[f, x] = main
-            for h in range(2):
-                first, count, at = up_at[f, x, h]
-                up_ref[at : at + 8 - first] = main[h, first:8]
-                up_ref[at + 8 - first : at + 9 - first] = turned[h, 0:1]
-                first, count, at = down_at[f, x, h]
-                down_ref[at : at + count] = main[h, :count]
+            rim = jnp.where(first_row, turned, 0.0)
+            grid_ref[f, x], rim_ref[f, x] = main, rim
+            hand_out(f, x, main, rim)
+            if f == 0:
+                inverse = 1.0 / jnp.maximum(main, 0.5)
+            else:
+                hand_out(3 + f, x, main * inverse, None)
         if x < CX:
-            for h in range(2):
-                flags = flag_ref[x, :, 128 * h : 128 * h + 128].astype(F32)
-                for table, ref in ((up_at, up_ref), (down_at, down_ref)):
-                    first, count, at = table[4, x, h]
-                    ref[at : at + count] = flags[first : first + count]
+            flags = jnp.stack([flag_ref[x, :, 128 * h : 128 * h + 128] for h in range(2)])
+            hand_out(7, x, flags.astype(F32), None)
         before = here
 
 
@@ -362,41 +378,9 @@
 
 
 def deposit(cells, tag, flags):
-    return kernel_call(
-        deposit_kernel,
-        "deposit",
-        (of((4, CX + 1, 2, 8, 128)), of((UP_ROWS, 128)), of((DOWN_ROWS, 128))),
-        [],
-        (cells, tag, flags),
-    )
-
-
-def widen_kernel(keep_ref, grid_ref, own_ref, low_ref, high_ref, flag_ref, after_ref, wide_ref, up_ref, down_ref):
-    keep = keep_ref[1]
-    zero = jnp.zeros((2, 8, 128), F32)
-    for f in range(5):
-        for x in range(CX + 1):
-            wide_ref[f, x, :, 0:8] = zero
-            wide_ref[f, x, :, 16:24] = zero
-            if f < 4:
-                wide_ref[f, x, :, 8:16] = grid_ref[f, x]
-            elif x < CX:
-                for h in range(2):
-                    wide_ref[f, x, h, 8:16] = flag_ref[x, :, 128 * h : 128 * h + 128].astype(F32)
-            else:
-                wide_ref[f, x, :, 8:16] = zero
-    for f, x, h, first, count, at in y_pieces(Y_DOWN):
-        wide_ref[f, x, h, 16 : 16 + count] = high_ref[at : at + count]
-    for f, x, h, first, count, at in y_pieces(Y_UP):
-        below = 8 - first
-        wide_ref[f, x, h, first:8] = low_ref[at : at + below]
-        if f < 4:
-            rim = at + below
-            wide_ref[f, x, h, 8:9] = wide_ref[f, x, h, 8:9] + low_ref[rim : rim + 1]
-            wide_ref[f, x, h, 16:17] = wide_ref[f, x, h, 16:17] + keep * own_ref[rim : rim + 1]
-    for table, ref in ((X_UP, up_ref), (X_DOWN, down_ref)):
-        for f, plane, h, at in x_pieces(table):
-            ref[at : at + 17] = wide_ref[f, plane, h, 4:21]
+    slabs = [of((pieces(dx, dy)[1], 128)) for dx, dy in WAYS]
+    grid = of((4, CX + 1, 2, 8, 128))
+    return kernel_call(deposit_kernel, "deposit", [grid, grid, *slabs], [], (cells, tag, flags))
 
 
 def smem():
@@ -407,43 +391,40 @@
     return pl.BlockSpec(memory_space=pltpu.VMEM)
 
 
-def widen(keep, grid, own, low, high, flags, after):
-    return kernel_call(
-        widen_kernel,
-        "widen",
-        (of((5, CX + 1, 2, 24, 128)), of((UP_ROWS, 128)), of((DOWN_ROWS, 128))),
-        [],
-        (keep, grid, own, low, high, flags, after),
-        [smem()] + [vmem()] * 5 + [pl.BlockSpec(memory_space=pl.ANY)],
-    )
-
-
-def krylov_kernel(keep_ref, wide_ref, low_ref, high_ref, vel_ref, fluid_ref, k0_ref, k1_ref, k2_ref, sums_ref, ext):
-    keep = keep_ref[0]
-    zero = jnp.zeros((2, 24, 128), F32)
-    for f in range(5):
-        for plane in (0, 1, 2, 3, 21, 22, 23, 24):
-            ext[f, plane] = zero
-        for x in range(CX):
-            ext[f, x + 4] = wide_ref[f, x]
-        ext[f, 20] = keep * wide_ref[f, CX]
-    for f, plane, h, at in x_pieces(X_UP):
-        rows = low_ref[at : at + 17]
-        if plane == CX:
-            ext[f, 4, h, 4:21] = ext[f, 4, h, 4:21] + rows
-        else:
-            ext[f, plane - 12, h, 4:21] = rows
-    for f, plane, h, at in x_pieces(X_DOWN):
-        rows = high_ref[at : at + 17]
-        if plane == 0 and f < 4:
-            ext[f, 20, h, 4:21] = ext[f, 20, h, 4:21] + rows
-        else:
-            ext[f, plane + 20, h, 4:21] = rows
+def krylov_kernel(keep_ref, grid_ref, rim_ref, flag_ref, *refs):
+    slab_refs, after_ref = refs[: len(WAYS)], refs[len(WAYS)]
+    vel_ref, fluid_ref, k0_ref, k1_ref, k2_ref, sums_ref, ext = refs[len(WAYS) + 1 :]
+    zero = jnp.zeros((2, 8, 128), F32)
+    for plane in range(25):
+        own = 4 <= plane <= 20
+        for f in range(4):
+            ext[f, plane, :, 0:8] = zero
+            ext[f, plane, :, 8:16] = grid_ref[f, plane - 4] if own else zero
+            ext[f, plane, :, 16:24] = rim_ref[f, plane - 4] if own else zero
+        fluid_ref[plane] = jnp.zeros((2, 24, 128), F32)
+        if 4 <= plane < 20:
+            for h in range(2):
+                fluid_ref[plane, h, 8:16] = flag_ref[plane - 4, :, 128 * h : 128 * h + 128].astype(F32)
+    arrived = []
+    for (dx, dy), ref in zip(WAYS, slab_refs):
+        for field, plane, half, first, count, at in pieces(-dx, -dy)[0]:
+            arrived.append((field, plane + dx * CX + 4, half, first + dy * CY + 8, count, ref[at : at + count]))
+    for field, plane, half, row, count, rows in arrived:
+        if field < 4:
+            ext[field, plane, half, row : row + count] = ext[field, plane, half, row : row + count] + rows
+        elif field == 7:
+            fluid_ref[plane, half, row : row + count] = rows
+    for f in range(4):
+        ext[f, 20] = keep_ref[0] * ext[f, 20]
+        for plane in range(25):
+            ext[f, plane, :, 16:24] = keep_ref[1] * ext[f, plane, :, 16:24]
     for plane in range(25):
         inverse = 1.0 / jnp.maximum(ext[0, plane], 0.5)
         for d in range(3):
             vel_ref[d, plane] = ext[1 + d, plane] * inverse
-        fluid_ref[plane] = ext[4, plane]
+    for field, plane, half, row, count, rows in arrived:
+        if 4 <= field < 7:
+            vel_ref[field - 4, plane, half, row : row + count] = rows
     for plane in range(1, 24):
         vy, vz = vel_ref[1, plane], vel_ref[2, plane]
         divergence = (
@@ -481,14 +462,14 @@
     sums_ref[14:16] = jnp.zeros((2, 128), F32)
 
 
-def krylov(keep, wide, low, high):
+def krylov(keep, grid, rim, flags, slabs, after):
     return kernel_call(
         krylov_kernel,
         "krylov",
         (of((3, 25, 2, 24, 128)),) + (of((25, 2, 24, 128)),) * 4 + (of((16, 128)),),
-        [(5, 25, 2, 24, 128)],
-        (keep, wide, low, high),
-        [smem()] + [vmem()] * 3,
+        [(4, 25, 2, 24, 128)],
+        (keep, grid, rim, flags, *slabs, after),
+        [smem()] + [vmem()] * (3 + len(WAYS)) + [pl.BlockSpec(memory_space=pl.ANY)],
     )
 
 
@@ -583,28 +564,36 @@
     )
 
 
-def neighbours(up, down, axis):
-    pairs = [(i, i + 1) for i in range(lax.axis_size(axis) - 1)]
-    return lax.ppermute(up, axis, pairs), lax.ppermute(down, axis, [(b, a) for a, b in pairs])
-
-
-def everywhere(sums):
-    count = lax.axis_size("gx") * lax.axis_size("gy")
-    spread = jnp.broadcast_to(sums[None], (count,) + sums.shape)
-    return lax.all_to_all(spread, ("gx", "gy"), 0, 0)
+def to_neighbour(slab, dx, dy):
+    wide, high = lax.axis_size("gx"), lax.axis_size("gy")
+    pairs = [
+        (x * high + y, (x + dx) * high + y + dy)
+        for x in range(max(0, -dx), min(wide, wide - dx))
+        for y in range(max(0, -dy), min(high, high - dy))
+    ]
+    return lax.ppermute(slab, ("gx", "gy"), pairs)
+
+
+def summed(sums, axis):
+    count = lax.axis_size(axis)
+    parts = [sums]
+    for shift in range(1, count):
+        parts.append(lax.ppermute(sums, axis, [(i, (i + shift) % count) for i in range(count)]))
+    return functools.reduce(jnp.add, parts)
 
 
 def local(cell_index, offset_code, particle_state, fluid_flags):
     places = [(axis, lax.axis_index(axis), lax.axis_size(axis)) for axis in ("gx", "gy")]
     keep = jnp.stack([(at + 1 < size).astype(F32) for _, at, size in places])
     cells, tag = to_cells(cell_index.reshape(256, 128), offset_code, particle_state)
-    grid, up, down = deposit(cells, tag, fluid_flags)
-    low, high = neighbours(up, down, "gy")
+    grid, rim, *slabs = deposit(cells, tag, fluid_flags)
+    order = [WAYS.index(way) for way in ((0, 1), (0, -1), (1, 0), (-1, 0), (1, 1), (-1, -1), (1, -1), (-1, 1))]
+    sent = {i: to_neighbour(slabs[i], *WAYS[i]) for i in order}
+    arrived = [sent[WAYS.index((-dx, -dy))] for dx, dy in WAYS]
     plan = particle_plan(tag.reshape(256, 128))
-    wide, up_x, down_x = widen(keep, grid, up, low, high, fluid_flags, plan[1])
-    low, high = neighbours(up_x, down_x, "gx")
-    vel, fluid, k0, k1, k2, sums = krylov(keep, wide, low, high)
-    pressure, result = project(everywhere(sums), vel, fluid, k0, k1, k2, tag, *plan)
+    vel, fluid, k0, k1, k2, sums = krylov(keep, grid, rim, fluid_flags, arrived, plan[1])
+    sums = summed(summed(sums, "gx"), "gy")[None]
+    pressure, result = project(sums, vel, fluid, k0, k1, k2, tag, *plan)
     return pressure, result.reshape(1, 3, CELLS)
 
 

time: 69.2 us -> 84.8 us (1.23)
  blocking collectives: 19.3 us -> 0 us
  starting transfers between devices: 11.2 us -> 28.8 us
  waiting for transfers between devices: 1.94 us -> 14 us
  local copies, waits for them, and re-layouts: 3.22 us -> 8.48 us
    all_to_all x1 -> x0, blocking collectives: 19.3 us -> none  [everywhere(): return lax.all_to_all(spread, ('gx', 'gy'), 0, 0)]
    ppermute x4 -> x14, starting transfers between devices: 11.2 us -> 28.8 us  [the longest x8 22.2 us: to_neighbour(): return lax.ppermute(slab, ('gx', 'gy'), pairs)]
    ppermute x4 -> x14, waiting for transfers between devices: 1.94 us -> 14 us  [the longest x6 8.52 us: summed(): lax.ppermute(sums, axis, [(i, (i + shift) % count) for i in range(count)])]
    unnamed x8 -> x32, local copies, waits for them, and re-layouts: 3.21 us -> 8.48 us
    pallas_call x6 -> x5, Pallas kernels: 32.5 us -> 32 us  [kernel_call(): pl.pallas_call(body, out_shape=outs, **{} if in_specs is None else dict(i...]
  transfers between devices with their start and end apart: 4 -> 14, of which waited for: 2 -> 6; matrix products, arithmetic and copies ran while one was open for 0% -> 0% of each run, Pallas kernels for 10% -> 8%
where the time goes in v5:
time: 84.8 us; the launch traced here: 84.2 us
  Pallas kernels  32 us (38%)
  starting transfers between devices  28.8 us (34%)
  waiting for transfers between devices  14 us (17%)
  local copies, waits for them, and re-layouts  8.48 us (10%)
    pallas_call x5, Pallas kernels, kernel_call(): pl.pallas_call(body, out_shape=outs, **{} if in_specs is None else dict(i...  32 us
    ppermute x8, starting transfers between devices, to_neighbour(): return lax.ppermute(slab, ('gx', 'gy'), pairs)  22.2 us
    ppermute x6, waiting for transfers between devices, summed(): lax.ppermute(sums, axis, [(i, (i + shift) % count) for i in range(count)])  8.52 us
    unnamed x32, local copies, waits for them, and re-layouts  8.48 us
    ppermute x6, starting transfers between devices, summed(): lax.ppermute(sums, axis, [(i, (i + shift) % count) for i in range(count)])  6.56 us
    ppermute x8, waiting for transfers between devices, to_neighbour(): return lax.ppermute(slab, ('gx', 'gy'), pairs)  5.47 us
  transfers between devices with their start and end apart: 14, of which 6 were waited for; matrix products, arithmetic and copies ran while one was open for 0% of the time, Pallas kernels for 8%

profile of v5, /device:TPU:0, one launch (start us, length us, event | category | flops | bytes accessed | tf_op | source)
XLA Modules:
  0.0 84.2 jit_solution(4404170057175997108)
XLA Ops:
  0.6 0.0 copy-start.12
  0.6 1.4 %copy-done.12 = f32[1,12,32768]{2,0,1:T(1,128)S(1)} copy-done((f32[1,12,32768]{2,0,1:T(1,128)S(1)}, f32[1,12,32768]{2,0,1:T(1,128)}, u32[]{:S(2)}) %copy-start.12) | copy-done | bytes 1572888
  2.0 0.0 copy-start.13
  2.0 0.9 %copy-done.13 = s32[1,32768]{1,0:T(1,128)S(1)} copy-done((s32[1,32768]{1,0:T(1,128)S(1)}, s32[1,32768]{1,0:T(1,128)}, u32[]{:S(2)}) %copy-start.13) | copy-done | bytes 131096
  2.9 0.0 copy-start.14
  2.9 0.9 %copy-done.14 = s32[1,32768]{1,0:T(1,128)S(1)} copy-done((s32[1,32768]{1,0:T(1,128)S(1)}, s32[1,32768]{1,0:T(1,128)}, u32[]{:S(2)}) %copy-start.14) | copy-done | bytes 131096
  3.8 0.0 copy-start.6
  3.9 16.3 %to_cells.1 = (f32[12,32,8,128]{3,2,1,0:T(8,128)S(1)}, s32[1,32,8,128]{3,2,1,0:T(8,128)S(1)}) custom-call(s32[256,128]{1,0:T(8,128)S(1)} %bitcast.11, s32[32,8,128]{2,1,0:T(8,128)S(1)} %bitcast.12, f32[12,32,8,128]{3,2,1,0:T(8,128)S(1)} %bitcast.10), custom_call_target="tpu_custom_call" | custom-call | flops 20000000000 | bytes 7208960 | tf_op jit(solution)/shard_map/to_cells/pallas_call | solution.py:365
  20.1 0.0 copy-start.4
  20.1 0.0 copy-done.6
  20.2 1.7 %deposit.1 = (f32[4,17,2,8,128]{4,3,2,1,0:T(8,128)S(1)}, f32[4,17,2,8,128]{4,3,2,1,0:T(8,128)S(1)}, f32[120,128]{1,0:T(8,128)S(1)}, f32[336,128]{1,0:T(8,128)}, ...) custom-call(f32[12,32,8,128]{3,2,1,0:T(8,128)S(1)} %get-tuple-elemen, ...), custom_call_target="tpu_custom_call" | custom-call | bytes 4136960 | tf_op jit(solution)/shard_map/deposit/pallas_call | solution.py:365
  21.9 0.0 copy-start.15
  21.9 0.6 copy-done.15
  22.5 0.0 copy-start
  22.5 0.0 copy-start.2
  22.5 0.7 collective-permute-start.2
  23.1 7.3 %collective-permute-start = (f32[104,128]{1,0:T(8,128)S(1)}, f32[104,128]{1,0:T(8,128)S(1)}, u32[]{:S(2)}, u32[]{:S(2)}) collective-permute-start(f32[104,128]{1,0:T(8,128)S(1)} %get-tuple-element.29), channel_id=1, source_target_pairs={{0,5},{1,6},{2,7},{4,9},{5,10},{6,11},{8,13},{9,14},{10,15},{16,21... | collective-permute-start | bytes 159752 | tf_op jit(solution)/shard_map/ppermute | solution.py:574
  30.4 1.5 %collective-permute-start.5 = (f32[112,128]{1,0:T(8,128)}, f32[112,128]{1,0:T(8,128)}, u32[]{:S(2)}, u32[]{:S(2)}) collective-permute-start(f32[112,128]{1,0:T(8,128)} %get-tuple-element.34), channel_id=1, source_target_pairs={{4,1},{5,2},{6,3},{8,5},{9,6},{10,7},{12,9},{13,10},{14,11},{20,17... | collective-permute-start | bytes 172040 | tf_op jit(solution)/shard_map/ppermute | solution.py:574
  31.9 5.3 %collective-permute-start.1 = (f32[320,128]{1,0:T(8,128)}, f32[320,128]{1,0:T(8,128)}, u32[]{:S(2)}, u32[]{:S(2)}) collective-permute-start(f32[320,128]{1,0:T(8,128)} %get-tuple-element.30), channel_id=1, source_target_pairs={{0,4},{1,5},{2,6},{3,7},{4,8},{5,9},{6,10},{7,11},{8,12},{9,13},{1... | collective-permute-start | bytes 491528 | tf_op jit(solution)/shard_map/ppermute | solution.py:574
  37.2 1.3 %collective-permute-start.6 = (f32[336,128]{1,0:T(8,128)}, f32[336,128]{1,0:T(8,128)}, u32[]{:S(2)}, u32[]{:S(2)}) collective-permute-start(f32[336,128]{1,0:T(8,128)} %get-tuple-element.35), channel_id=1, source_target_pairs={{4,0},{5,1},{6,2},{7,3},{8,4},{9,5},{10,6},{11,7},{12,8},{13,9},{1... | collective-permute-start | bytes 516104 | tf_op jit(solution)/shard_map/ppermute | solution.py:574
  38.5 0.0 collective-permute-done.refs_0_
  38.5 0.0 copy-start.10
  38.5 3.6 %collective-permute-start.3 = (f32[592,128]{1,0:T(8,128)}, f32[592,128]{1,0:T(8,128)}, u32[]{:S(2)}, u32[]{:S(2)}) collective-permute-start(f32[592,128]{1,0:T(8,128)} %get-tuple-element.32), channel_id=1, source_target_pairs={{0,1},{1,2},{2,3},{4,5},{5,6},{6,7},{8,9},{9,10},{10,11},{12,13},{... | collective-permute-start | bytes 909320 | tf_op jit(solution)/shard_map/ppermute | solution.py:574
  42.2 0.0 collective-permute-done.2.refs_2_
  42.2 0.0 copy-start.8
  42.2 1.3 %collective-permute-start.4 = (f32[624,128]{1,0:T(8,128)}, f32[624,128]{1,0:T(8,128)}, u32[]{:S(2)}, u32[]{:S(2)}) collective-permute-start(f32[624,128]{1,0:T(8,128)} %get-tuple-element.33), channel_id=1, source_target_pairs={{1,0},{2,1},{3,2},{5,4},{6,5},{7,6},{9,8},{10,9},{11,10},{13,12},{... | collective-permute-start | bytes 958472 | tf_op jit(solution)/shard_map/ppermute | solution.py:574
  43.4 6.5 %particle_plan.1 = (s32[9,256,128]{2,1,0:T(8,128)S(1)}, s32[3,256,128]{2,1,0:T(8,128)S(1)}, s32[3840,128]{1,0:T(8,128)S(1)}) custom-call(s32[256,128]{1,0:T(8,128)S(1)} %bitcast.9), custom_call_target="tpu_custom_call" | custom-call | flops 7000000000 | bytes 3670016 | tf_op jit(solution)/shard_map/particle_plan/pallas_call | solution.py:365
  49.9 0.0 copy-done.4
  49.9 0.0 copy-done
  49.9 0.0 copy-done.2
  49.9 0.0 copy-done.10
  49.9 0.0 copy-done.8
  50.0 0.0 collective-permute-done.5.refs_5_
  50.0 1.3 %collective-permute-start.7 = (f32[120,128]{1,0:T(8,128)}, f32[120,128]{1,0:T(8,128)S(1)}, u32[]{:S(2)}, u32[]{:S(2)}) collective-permute-start(f32[120,128]{1,0:T(8,128)} %copy-done.15), channel_id=1, source_target_pairs={{5,0},{6,1},{7,2},{9,4},{10,5},{11,6},{13,8},{14,9},{15,10},{21,16... | collective-permute-start | bytes 184328 | tf_op jit(solution)/shard_map/ppermute | solution.py:574
  51.3 0.1 add_convert_fusion.keep_ref
  51.4 5.5 %collective-permute-done.7.refs_7_ = f32[120,128]{1,0:T(8,128)S(1)} collective-permute-done((f32[120,128]{1,0:T(8,128)}, f32[120,128]{1,0:T(8,128)S(1)}, u32[]{:S(2)}, u32[]{:S(2)}) %collective-permute-start.7) | collective-permute-done | bytes 61472 | tf_op jit(solution)/shard_map/ppermute | solution.py:574
  56.8 0.0 collective-permute-done.1.refs_1_
  56.8 0.0 collective-permute-done.6.refs_6_
  56.8 0.0 collective-permute-done.3.refs_3_
  56.8 0.0 collective-permute-done.4.refs_4_
  56.8 0.0 copy-start.1
  56.8 1.0 %copy-done.1 = f32[4,17,2,8,128]{4,3,2,1,0:T(8,128)S(1)} copy-done((f32[4,17,2,8,128]{4,3,2,1,0:T(8,128)S(1)}, f32[4,17,2,8,128]{4,3,2,1,0:T(8,128)}, u32[]{:S(2)}) %copy-start.1) | copy-done | bytes 557080
  57.9 0.0 copy-start.3
  57.9 1.1 %copy-done.3 = f32[4,17,2,8,128]{4,3,2,1,0:T(8,128)S(1)} copy-done((f32[4,17,2,8,128]{4,3,2,1,0:T(8,128)S(1)}, f32[4,17,2,8,128]{4,3,2,1,0:T(8,128)}, u32[]{:S(2)}) %copy-start.3) | copy-done | bytes 557080
  58.9 0.0 copy-start.7
  58.9 0.9 %copy-done.7 = s32[16,8,256]{2,1,0:T(8,128)S(1)} copy-done((s32[16,8,256]{2,1,0:T(8,128)S(1)}, s32[16,8,256]{2,1,0:T(8,128)}, u32[]{:S(2)}) %copy-start.7) | copy-done | bytes 131096
  59.8 0.0 copy-start.9
  59.9 0.8 copy-done.9
  60.7 0.8 copy-done.11
  61.5 3.0 %krylov.1 = (f32[3,25,2,24,128]{4,3,2,1,0:T(8,128)S(1)}, f32[25,2,24,128]{3,2,1,0:T(8,128)S(1)}, f32[25,2,24,128]{3,2,1,0:T(8,128)S(1)}, f32[25,2,24,128]{3,2,1,...) custom-call(f32[2]{0:T(128)S(1)} %add_convert_fusion.keep_ref, ...), custom_call_target="tpu_custom_call" | custom-call | bytes 9592832 | tf_op jit(solution)/shard_map/krylov/pallas_call | solution.py:365
  64.5 0.1 collective-permute-start.10
  64.6 3.5 %collective-permute-start.9 = (f32[16,128]{1,0:T(8,128)S(1)}, f32[16,128]{1,0:T(8,128)S(1)}, u32[]{:S(2)}, u32[]{:S(2)}) collective-permute-start(f32[16,128]{1,0:T(8,128)S(1)} %get-tuple-element.38), channel_id=1, source_target_pairs={{0,8},{4,12},{8,0},{12,4},{1,9},{5,13},{9,1},{13,5},{2,10},{6,14},... | collective-permute-start | bytes 24584 | tf_op jit(solution)/shard_map/ppermute | solution.py:581
  68.0 0.0 collective-permute-start.8
  68.1 0.0 collective-permute-done.10
  68.1 1.7 %collective-permute-done.9 = f32[16,128]{1,0:T(8,128)S(1)} collective-permute-done((f32[16,128]{1,0:T(8,128)S(1)}, f32[16,128]{1,0:T(8,128)S(1)}, u32[]{:S(2)}, u32[]{:S(2)}) %collective-permute-start.9) | collective-permute-done | bytes 8224 | tf_op jit(solution)/shard_map/ppermute | solution.py:581
  69.8 1.4 %collective-permute-done.8 = f32[16,128]{1,0:T(8,128)S(1)} collective-permute-done((f32[16,128]{1,0:T(8,128)S(1)}, f32[16,128]{1,0:T(8,128)S(1)}, u32[]{:S(2)}, u32[]{:S(2)}) %collective-permute-start.8) | collective-permute-done | bytes 8224 | tf_op jit(solution)/shard_map/ppermute | solution.py:581
  71.1 0.0 collective-permute-start.13
  71.1 3.0 %collective-permute-start.12 = (f32[16,128]{1,0:T(8,128)S(1)}, f32[16,128]{1,0:T(8,128)S(1)}, u32[]{:S(2)}, u32[]{:S(2)}) collective-permute-start(f32[16,128]{1,0:T(8,128)S(1)} %add_add_fusion), channel_id=1, source_target_pairs={{0,2},{1,3},{2,0},{3,1},{4,6},{5,7},{6,4},{7,5},{8,10},{9,11},{10,... | collective-permute-start | bytes 24584 | tf_op jit(solution)/shard_map/ppermute | solution.py:581
  74.2 0.0 collective-permute-start.11
  74.2 0.6 collective-permute-done.13
  74.8 1.1 %collective-permute-done.12 = f32[16,128]{1,0:T(8,128)S(1)} collective-permute-done((f32[16,128]{1,0:T(8,128)S(1)}, f32[16,128]{1,0:T(8,128)S(1)}, u32[]{:S(2)}, u32[]{:S(2)}) %collective-permute-start.12) | collective-permute-done | bytes 8224 | tf_op jit(solution)/shard_map/ppermute | solution.py:581
  75.9 3.7 %collective-permute-done.11 = f32[16,128]{1,0:T(8,128)S(1)} collective-permute-done((f32[16,128]{1,0:T(8,128)S(1)}, f32[16,128]{1,0:T(8,128)S(1)}, u32[]{:S(2)}, u32[]{:S(2)}) %collective-permute-start.11) | collective-permute-done | bytes 8224 | tf_op jit(solution)/shard_map/ppermute | solution.py:581
  79.6 0.0 copy-done.5
  79.6 4.6 %project.1 = (f32[16,8,256]{2,1,0:T(8,128)}, f32[3,32,8,128]{3,2,1,0:T(8,128)}) custom-call(f32[1,16,128]{2,1,0:T(8,128)S(1)} %add_bitcast_fusion.sums_ref, f32[3,25,2,24,128]{4,3,2,1,0:T(8,128)S(1)} %get-tuple-element.39.vel_ref, f32[25,2,24,128]{3,2,1,0:T(8,128)S(1)} %get-tuple-element.40.fluid_ref, f32[25,2,24,128]{3,2,1,0:T(8,128)S(1)} %get-tuple-element.41.k0_ref, ...), custom_call_target="tpu_custom_call" | custom-call | bytes 10788864 | tf_op jit(solution)/shard_map/project/pallas_call | solution.py:365
  (4 shorter events, 0.0 us)
Async XLA Ops:
  0.6 1.4 %copy-start.12 = (f32[1,12,32768]{2,0,1:T(1,128)S(1)}, f32[1,12,32768]{2,0,1:T(1,128)}, u32[]{:S(2)}) copy-start(f32[1,12,32768]{2,0,1:T(1,128)} %param.6) | copy-start | bytes 4718596
  2.0 0.9 %copy-start.13 = (s32[1,32768]{1,0:T(1,128)S(1)}, s32[1,32768]{1,0:T(1,128)}, u32[]{:S(2)}) copy-start(s32[1,32768]{1,0:T(1,128)} %param.4) | copy-start | bytes 393220
  2.9 0.9 %copy-start.14 = (s32[1,32768]{1,0:T(1,128)S(1)}, s32[1,32768]{1,0:T(1,128)}, u32[]{:S(2)}) copy-start(s32[1,32768]{1,0:T(1,128)} %param.5) | copy-start | bytes 393220
  3.8 16.3 %copy-start.6 = (s32[16,8,256]{2,1,0:T(8,128)S(1)}, s32[16,8,256]{2,1,0:T(8,128)}, u32[]{:S(2)}) copy-start(s32[16,8,256]{2,1,0:T(8,128)} %flag_ref.3) | copy-start | bytes 393220
  20.1 29.8 %copy-start.4 = (s32[1,32,8,128]{3,2,1,0:T(8,128)}, s32[1,32,8,128]{3,2,1,0:T(8,128)S(1)}, u32[]{:S(2)}) copy-start(s32[1,32,8,128]{3,2,1,0:T(8,128)S(1)} %get-tuple-element.26.tag_ref) | copy-start | bytes 393220
  21.9 0.6 copy-start.15
  22.5 27.4 %copy-start = (f32[4,17,2,8,128]{4,3,2,1,0:T(8,128)}, f32[4,17,2,8,128]{4,3,2,1,0:T(8,128)S(1)}, u32[]{:S(2)}) copy-start(f32[4,17,2,8,128]{4,3,2,1,0:T(8,128)S(1)} %get-tuple-element.27.grid_ref) | copy-start | bytes 1671172
  22.5 27.5 %copy-start.2 = (f32[4,17,2,8,128]{4,3,2,1,0:T(8,128)}, f32[4,17,2,8,128]{4,3,2,1,0:T(8,128)S(1)}, u32[]{:S(2)}) copy-start(f32[4,17,2,8,128]{4,3,2,1,0:T(8,128)S(1)} %get-tuple-element.28.rim_ref) | copy-start | bytes 1671172
  22.5 19.7 %collective-permute-start.2 = (f32[112,128]{1,0:T(8,128)S(1)}, f32[112,128]{1,0:T(8,128)S(1)}, u32[]{:S(2)}, u32[]{:S(2)}) collective-permute-start(f32[112,128]{1,0:T(8,128)S(1)} %get-tuple-element.31), channel_id=1, source_target_pairs={{1,4},{2,5},{3,6},{5,8},{6,9},{7,10},{9,12},{10,13},{11,14},{17,20... | collective-permute-start | bytes 172040 | tf_op jit(solution)/shard_map/ppermute | solution.py:574
  23.1 15.4 %collective-permute-start = (f32[104,128]{1,0:T(8,128)S(1)}, f32[104,128]{1,0:T(8,128)S(1)}, u32[]{:S(2)}, u32[]{:S(2)}) collective-permute-start(f32[104,128]{1,0:T(8,128)S(1)} %get-tuple-element.29), channel_id=1, source_target_pairs={{0,5},{1,6},{2,7},{4,9},{5,10},{6,11},{8,13},{9,14},{10,15},{16,21... | collective-permute-start | bytes 159752 | tf_op jit(solution)/shard_map/ppermute | solution.py:574
  30.4 19.6 %collective-permute-start.5 = (f32[112,128]{1,0:T(8,128)}, f32[112,128]{1,0:T(8,128)}, u32[]{:S(2)}, u32[]{:S(2)}) collective-permute-start(f32[112,128]{1,0:T(8,128)} %get-tuple-element.34), channel_id=1, source_target_pairs={{4,1},{5,2},{6,3},{8,5},{9,6},{10,7},{12,9},{13,10},{14,11},{20,17... | collective-permute-start | bytes 172040 | tf_op jit(solution)/shard_map/ppermute | solution.py:574
  31.9 24.9 %collective-permute-start.1 = (f32[320,128]{1,0:T(8,128)}, f32[320,128]{1,0:T(8,128)}, u32[]{:S(2)}, u32[]{:S(2)}) collective-permute-start(f32[320,128]{1,0:T(8,128)} %get-tuple-element.30), channel_id=1, source_target_pairs={{0,4},{1,5},{2,6},{3,7},{4,8},{5,9},{6,10},{7,11},{8,12},{9,13},{1... | collective-permute-start | bytes 491528 | tf_op jit(solution)/shard_map/ppermute | solution.py:574
  37.2 19.6 %collective-permute-start.6 = (f32[336,128]{1,0:T(8,128)}, f32[336,128]{1,0:T(8,128)}, u32[]{:S(2)}, u32[]{:S(2)}) collective-permute-start(f32[336,128]{1,0:T(8,128)} %get-tuple-element.35), channel_id=1, source_target_pairs={{4,0},{5,1},{6,2},{7,3},{8,4},{9,5},{10,6},{11,7},{12,8},{13,9},{1... | collective-permute-start | bytes 516104 | tf_op jit(solution)/shard_map/ppermute | solution.py:574
  38.5 11.4 %copy-start.10 = (f32[104,128]{1,0:T(8,128)}, f32[104,128]{1,0:T(8,128)S(1)}, u32[]{:S(2)}) copy-start(f32[104,128]{1,0:T(8,128)S(1)} %collective-permute-done.refs_0_) | copy-start | bytes 159748
  38.5 18.3 %collective-permute-start.3 = (f32[592,128]{1,0:T(8,128)}, f32[592,128]{1,0:T(8,128)}, u32[]{:S(2)}, u32[]{:S(2)}) collective-permute-start(f32[592,128]{1,0:T(8,128)} %get-tuple-element.32), channel_id=1, source_target_pairs={{0,1},{1,2},{2,3},{4,5},{5,6},{6,7},{8,9},{9,10},{10,11},{12,13},{... | collective-permute-start | bytes 909320 | tf_op jit(solution)/shard_map/ppermute | solution.py:574
  42.2 7.8 %copy-start.8 = (f32[112,128]{1,0:T(8,128)}, f32[112,128]{1,0:T(8,128)S(1)}, u32[]{:S(2)}) copy-start(f32[112,128]{1,0:T(8,128)S(1)} %collective-permute-done.2.refs_2_) | copy-start | bytes 172036
  42.2 14.7 %collective-permute-start.4 = (f32[624,128]{1,0:T(8,128)}, f32[624,128]{1,0:T(8,128)}, u32[]{:S(2)}, u32[]{:S(2)}) collective-permute-start(f32[624,128]{1,0:T(8,128)} %get-tuple-element.33), channel_id=1, source_target_pairs={{1,0},{2,1},{3,2},{5,4},{6,5},{7,6},{9,8},{10,9},{11,10},{13,12},{... | collective-permute-start | bytes 958472 | tf_op jit(solution)/shard_map/ppermute | solution.py:574
  50.0 6.8 %collective-permute-start.7 = (f32[120,128]{1,0:T(8,128)}, f32[120,128]{1,0:T(8,128)S(1)}, u32[]{:S(2)}, u32[]{:S(2)}) collective-permute-start(f32[120,128]{1,0:T(8,128)} %copy-done.15), channel_id=1, source_target_pairs={{5,0},{6,1},{7,2},{9,4},{10,5},{11,6},{13,8},{14,9},{15,10},{21,16... | collective-permute-start | bytes 184328 | tf_op jit(solution)/shard_map/ppermute | solution.py:574
  56.8 1.1 %copy-start.1 = (f32[4,17,2,8,128]{4,3,2,1,0:T(8,128)S(1)}, f32[4,17,2,8,128]{4,3,2,1,0:T(8,128)}, u32[]{:S(2)}) copy-start(f32[4,17,2,8,128]{4,3,2,1,0:T(8,128)} %copy-done) | copy-start | bytes 1671172
  57.9 1.1 %copy-start.3 = (f32[4,17,2,8,128]{4,3,2,1,0:T(8,128)S(1)}, f32[4,17,2,8,128]{4,3,2,1,0:T(8,128)}, u32[]{:S(2)}) copy-start(f32[4,17,2,8,128]{4,3,2,1,0:T(8,128)} %copy-done.2) | copy-start | bytes 1671172
  58.9 0.9 %copy-start.7 = (s32[16,8,256]{2,1,0:T(8,128)S(1)}, s32[16,8,256]{2,1,0:T(8,128)}, u32[]{:S(2)}) copy-start(s32[16,8,256]{2,1,0:T(8,128)} %flag_ref.3) | copy-start | bytes 393220
  59.8 0.8 copy-start.9
  60.7 0.8 copy-start.11
  61.5 18.1 %copy-start.5 = (s32[1,32,8,128]{3,2,1,0:T(8,128)S(1)}, s32[1,32,8,128]{3,2,1,0:T(8,128)}, u32[]{:S(2)}) copy-start(s32[1,32,8,128]{3,2,1,0:T(8,128)} %copy-done.4) | copy-start | bytes 393220
  64.5 3.5 %collective-permute-start.10 = (f32[16,128]{1,0:T(8,128)S(1)}, f32[16,128]{1,0:T(8,128)S(1)}, u32[]{:S(2)}, u32[]{:S(2)}) collective-permute-start(f32[16,128]{1,0:T(8,128)S(1)} %get-tuple-element.38), channel_id=1, source_target_pairs={{0,12},{4,0},{8,4},{12,8},{1,13},{5,1},{9,5},{13,9},{2,14},{6,2},{... | collective-permute-start | bytes 24584 | tf_op jit(solution)/shard_map/ppermute | solution.py:581
  64.6 5.2 %collective-permute-start.9 = (f32[16,128]{1,0:T(8,128)S(1)}, f32[16,128]{1,0:T(8,128)S(1)}, u32[]{:S(2)}, u32[]{:S(2)}) collective-permute-start(f32[16,128]{1,0:T(8,128)S(1)} %get-tuple-element.38), channel_id=1, source_target_pairs={{0,8},{4,12},{8,0},{12,4},{1,9},{5,13},{9,1},{13,5},{2,10},{6,14},... | collective-permute-start | bytes 24584 | tf_op jit(solution)/shard_map/ppermute | solution.py:581
  68.0 3.1 %collective-permute-start.8 = (f32[16,128]{1,0:T(8,128)S(1)}, f32[16,128]{1,0:T(8,128)S(1)}, u32[]{:S(2)}, u32[]{:S(2)}) collective-permute-start(f32[16,128]{1,0:T(8,128)S(1)} %get-tuple-element.38), channel_id=1, source_target_pairs={{0,4},{4,8},{8,12},{12,0},{1,5},{5,9},{9,13},{13,1},{2,6},{6,10},{... | collective-permute-start | bytes 24584 | tf_op jit(solution)/shard_map/ppermute | solution.py:581
  71.1 3.7 %collective-permute-start.13 = (f32[16,128]{1,0:T(8,128)S(1)}, f32[16,128]{1,0:T(8,128)S(1)}, u32[]{:S(2)}, u32[]{:S(2)}) collective-permute-start(f32[16,128]{1,0:T(8,128)S(1)} %add_add_fusion), channel_id=1, source_target_pairs={{0,3},{1,0},{2,1},{3,2},{4,7},{5,4},{6,5},{7,6},{8,11},{9,8},{10,9... | collective-permute-start | bytes 24584 | tf_op jit(solution)/shard_map/ppermute | solution.py:581
  71.1 4.7 %collective-permute-start.12 = (f32[16,128]{1,0:T(8,128)S(1)}, f32[16,128]{1,0:T(8,128)S(1)}, u32[]{:S(2)}, u32[]{:S(2)}) collective-permute-start(f32[16,128]{1,0:T(8,128)S(1)} %add_add_fusion), channel_id=1, source_target_pairs={{0,2},{1,3},{2,0},{3,1},{4,6},{5,7},{6,4},{7,5},{8,10},{9,11},{10,... | collective-permute-start | bytes 24584 | tf_op jit(solution)/shard_map/ppermute | solution.py:581
  74.2 5.4 %collective-permute-start.11 = (f32[16,128]{1,0:T(8,128)S(1)}, f32[16,128]{1,0:T(8,128)S(1)}, u32[]{:S(2)}, u32[]{:S(2)}) collective-permute-start(f32[16,128]{1,0:T(8,128)S(1)} %add_add_fusion), channel_id=1, source_target_pairs={{0,1},{1,2},{2,3},{3,0},{4,5},{5,6},{6,7},{7,4},{8,9},{9,10},{10,1... | collective-permute-start | bytes 24584 | tf_op jit(solution)/shard_map/ppermute | solution.py:581

commit v6 on v5

--- a/solution.py
+++ b/solution.py
@@ -203,28 +203,30 @@
     return [((code >> shift & 3).astype(F32) + 0.5) * 0.25 for shift in (0, 2, 4)]
 
 
-WAYS = [(dx, dy) for dx in (-1, 0, 1) for dy in (-1, 0, 1) if dx or dy]
+PLANES = {1: range(12, 17), 0: range(17), -1: range(5)}
+ROWS = {1: range(4, 9), -1: range(5)}
+
+
+def reach(place, last):
+    return max(0, -place, place - last)
 
 
 def pieces(dx, dy):
-    def reach(place, last):
-        return max(0, -place, place - last)
-
     at, out = 0, []
-    for plane in {1: range(12, 17), 0: range(17), -1: range(5)}[dx]:
+    for plane in PLANES[dx]:
         far_x = reach(plane - dx * CX, CX)
         for field in range(8):
             rows = []
-            for row in {1: range(4, 9), 0: range(9), -1: range(5)}[dy]:
+            for row in ROWS[dy] if dy else range(-4, 13):
                 far_y = reach(row - dy * CY, CY)
                 read = [
                     max(far_x - 1, 0) + far_y <= 3,
                     far_x + max(far_y - 1, 0) <= 3,
                     far_x + far_y <= 3,
                 ]
-                shared = plane in (0, CX) or row in (0, CY)
+                shared = plane in (0, CX) or (dy != 0 and row in (0, CY))
                 if field == 7:
-                    wanted = read[2] and plane < CX and row < CY
+                    wanted = read[2] and plane < CX and (row < CY or not dy)
                 elif field == 0:
                     wanted = shared and any(read)
                 else:
@@ -242,6 +244,16 @@
     return out, -(-at // 8) * 8
 
 
+def slab_shape(dx, dy):
+    return of((pieces(dx, dy)[1], 128))
+
+
+def clear_end(ref, listed):
+    used = listed[-1][4] + listed[-1][5]
+    if used < ref.shape[0]:
+        ref[used:] = jnp.zeros((ref.shape[0] - used, 128), F32)
+
+
 def particle_plan_kernel(tag_ref, lane_ref, sub_ref, swap_ref):
     k = tag_ref[...] & 0x7FFF
     key = ((k & 0x380) << 5) | ((k & 0x7C00) >> 3) | (k & 0x7F)
@@ -250,7 +262,7 @@
 
 def particle_plan(tag):
     outs = [of(shape, I32) for shape in plan_shapes()]
-    return kernel_call(particle_plan_kernel, "particle_plan", outs, [], (tag,), flops=7 * 10**9)
+    return kernel_call(particle_plan_kernel, "particle_plan", outs, [], (tag,), flops=10**7)
 
 
 def to_cells_kernel(cell_ref, code_ref, state_ref, cells_ref, tag_ref, code, lane_ref, sub_ref, swap_ref, done):
@@ -282,17 +294,15 @@
         [pltpu.VMEM(shape, I32) for shape in [(TILES, 8, 128)] + plan_shapes()] + [pltpu.SemaphoreType.DMA((2,))],
         (cell, code.reshape(TILES, 8, 128), state.reshape(12, TILES, 8, 128)),
         [vmem(), anywhere, anywhere],
-        flops=2 * 10**10,
-    )
-
-
-def deposit_kernel(cells_ref, tag_ref, flag_ref, grid_ref, rim_ref, *out_refs):
+        flops=10**7,
+    )
+
+
+def deposit_kernel(cells_ref, tag_ref, flag_ref, grid_ref, rim_ref, up_ref, down_ref):
     wanted = {}
-    for (dx, dy), ref in zip(WAYS, out_refs):
-        listed, rows = pieces(dx, dy)
-        used = listed[-1][4] + listed[-1][5]
-        if used < rows:
-            ref[used:rows] = jnp.zeros((rows - used, 128), F32)
+    for dy, ref in ((1, up_ref), (-1, down_ref)):
+        listed = pieces(0, dy)[0]
+        clear_end(ref, listed)
         for field, plane, half, first, count, at in listed:
             wanted.setdefault((field, plane), []).append((ref, half, first, count, at))
 
@@ -378,9 +388,10 @@
 
 
 def deposit(cells, tag, flags):
-    slabs = [of((pieces(dx, dy)[1], 128)) for dx, dy in WAYS]
     grid = of((4, CX + 1, 2, 8, 128))
-    return kernel_call(deposit_kernel, "deposit", [grid, grid, *slabs], [], (cells, tag, flags))
+    return kernel_call(
+        deposit_kernel, "deposit", [grid, grid, slab_shape(0, 1), slab_shape(0, -1)], [], (cells, tag, flags)
+    )
 
 
 def smem():
@@ -391,40 +402,89 @@
     return pl.BlockSpec(memory_space=pltpu.VMEM)
 
 
-def krylov_kernel(keep_ref, grid_ref, rim_ref, flag_ref, *refs):
-    slab_refs, after_ref = refs[: len(WAYS)], refs[len(WAYS)]
-    vel_ref, fluid_ref, k0_ref, k1_ref, k2_ref, sums_ref, ext = refs[len(WAYS) + 1 :]
+def add_rows(ref, place, row, rows):
+    at = (*place, slice(row, row + rows.shape[0]))
+    ref[at] = ref[at] + rows
+
+
+def widen_kernel(
+    keep_ref, grid_ref, rim_ref, low_ref, high_ref, flag_ref, after_ref, vel_ref, edge_ref, fluid_ref, up_ref, down_ref, ext
+):
     zero = jnp.zeros((2, 8, 128), F32)
+    for x in range(CX + 1):
+        for f in range(4):
+            ext[f, x, :, 0:8] = zero
+            ext[f, x, :, 8:16] = grid_ref[f, x]
+            ext[f, x, :, 16:24] = rim_ref[f, x]
+        if x < CX:
+            fluid_ref[x, :, 0:8] = zero
+            fluid_ref[x, :, 16:24] = zero
+            for h in range(2):
+                fluid_ref[x, h, 8:16] = flag_ref[x, :, 128 * h : 128 * h + 128].astype(F32)
+    arrived = []
+    for dy, ref in ((1, low_ref), (-1, high_ref)):
+        for field, x, half, first, count, at in pieces(0, dy)[0]:
+            arrived.append((field, x, half, first - dy * CY + 8, ref[at : at + count]))
+    for field, x, half, row, rows in arrived:
+        if field < 4:
+            add_rows(ext, (field, x, half), row, rows)
+        elif field == 7:
+            fluid_ref[x, half, row : row + rows.shape[0]] = rows
+    for f in range(4):
+        for x in range(CX + 1):
+            ext[f, x, :, 16:24] = keep_ref[1] * ext[f, x, :, 16:24]
+        edge_ref[f, 0], edge_ref[f, 1] = ext[f, 0], ext[f, CX]
+    for x in range(1, CX):
+        inverse = 1.0 / jnp.maximum(ext[0, x], 0.5)
+        for d in range(3):
+            vel_ref[d, x] = ext[1 + d, x] * inverse
+    for field, x, half, row, rows in arrived:
+        if 4 <= field < 7:
+            vel_ref[field - 4, x, half, row : row + rows.shape[0]] = rows
+    for dx, ref in ((1, up_ref), (-1, down_ref)):
+        listed = pieces(dx, 0)[0]
+        clear_end(ref, listed)
+        for field, x, half, first, count, at in listed:
+            source = ext.at[field] if field < 4 else fluid_ref if field == 7 else vel_ref.at[field - 4]
+            ref[at : at + count] = source[x, half, first + 8 : first + 8 + count]
+
+
+def widen(keep, *args):
+    wide = (CX, 2, 24, 128)
+    return kernel_call(
+        widen_kernel,
+        "widen",
+        (of((3, *wide)), of((4, 2, 2, 24, 128)), of(wide), slab_shape(1, 0), slab_shape(-1, 0)),
+        [(4, CX + 1, 2, 24, 128)],
+        (keep, *args),
+        [smem()] + [vmem()] * 5 + [pl.BlockSpec(memory_space=pl.ANY)],
+    )
+
+
+def krylov_kernel(
+    keep_ref, near_ref, edge_ref, flag_ref, low_ref, high_ref, vel_ref, fluid_ref, k0_ref, k1_ref, k2_ref, sums_ref, edge
+):
+    zero = jnp.zeros((2, 24, 128), F32)
     for plane in range(25):
-        own = 4 <= plane <= 20
-        for f in range(4):
-            ext[f, plane, :, 0:8] = zero
-            ext[f, plane, :, 8:16] = grid_ref[f, plane - 4] if own else zero
-            ext[f, plane, :, 16:24] = rim_ref[f, plane - 4] if own else zero
-        fluid_ref[plane] = jnp.zeros((2, 24, 128), F32)
-        if 4 <= plane < 20:
-            for h in range(2):
-                fluid_ref[plane, h, 8:16] = flag_ref[plane - 4, :, 128 * h : 128 * h + 128].astype(F32)
-    arrived = []
-    for (dx, dy), ref in zip(WAYS, slab_refs):
-        for field, plane, half, first, count, at in pieces(-dx, -dy)[0]:
-            arrived.append((field, plane + dx * CX + 4, half, first + dy * CY + 8, count, ref[at : at + count]))
-    for field, plane, half, row, count, rows in arrived:
-        if field < 4:
-            ext[field, plane, half, row : row + count] = ext[field, plane, half, row : row + count] + rows
-        elif field == 7:
-            fluid_ref[plane, half, row : row + count] = rows
+        inner = 4 < plane < 20
+        for d in range(3):
+            vel_ref[d, plane] = near_ref[d, plane - 4] if inner else zero
+        fluid_ref[plane] = flag_ref[plane - 4] if 4 <= plane < 20 else zero
     for f in range(4):
-        ext[f, 20] = keep_ref[0] * ext[f, 20]
-        for plane in range(25):
-            ext[f, plane, :, 16:24] = keep_ref[1] * ext[f, plane, :, 16:24]
-    for plane in range(25):
-        inverse = 1.0 / jnp.maximum(ext[0, plane], 0.5)
+        edge[f, 0], edge[f, 1] = edge_ref[f, 0], edge_ref[f, 1]
+    for dx, ref in ((1, low_ref), (-1, high_ref)):
+        for field, x, half, first, count, at in pieces(dx, 0)[0]:
+            rows, row, plane = ref[at : at + count], first + 8, x - dx * CX + 4
+            if field < 4:
+                add_rows(edge, (field, (plane - 4) // CX, half), row, rows)
+            elif field == 7:
+                fluid_ref[plane, half, row : row + count] = rows
+            else:
+                vel_ref[field - 4, plane, half, row : row + count] = rows
+    for side, plane, keep in ((0, 4, 1.0), (1, 20, keep_ref[0])):
+        inverse = keep / jnp.maximum(edge[0, side], 0.5)
         for d in range(3):
-            vel_ref[d, plane] = ext[1 + d, plane] * inverse
-    for field, plane, half, row, count, rows in arrived:
-        if 4 <= field < 7:
-            vel_ref[field - 4, plane, half, row : row + count] = rows
+            vel_ref[d, plane] = edge[1 + d, side] * inverse
     for plane in range(1, 24):
         vy, vz = vel_ref[1, plane], vel_ref[2, plane]
         divergence = (
@@ -462,14 +522,14 @@
     sums_ref[14:16] = jnp.zeros((2, 128), F32)
 
 
-def krylov(keep, grid, rim, flags, slabs, after):
+def krylov(keep, *args):
     return kernel_call(
         krylov_kernel,
         "krylov",
         (of((3, 25, 2, 24, 128)),) + (of((25, 2, 24, 128)),) * 4 + (of((16, 128)),),
-        [(4, 25, 2, 24, 128)],
-        (keep, grid, rim, flags, *slabs, after),
-        [smem()] + [vmem()] * (3 + len(WAYS)) + [pl.BlockSpec(memory_space=pl.ANY)],
+        [(4, 2, 2, 24, 128)],
+        (keep, *args),
+        [smem()] + [vmem()] * 5,
     )
 
 
@@ -564,14 +624,9 @@
     )
 
 
-def to_neighbour(slab, dx, dy):
-    wide, high = lax.axis_size("gx"), lax.axis_size("gy")
-    pairs = [
-        (x * high + y, (x + dx) * high + y + dy)
-        for x in range(max(0, -dx), min(wide, wide - dx))
-        for y in range(max(0, -dy), min(high, high - dy))
-    ]
-    return lax.ppermute(slab, ("gx", "gy"), pairs)
+def neighbours(up, down, axis):
+    pairs = [(i, i + 1) for i in range(lax.axis_size(axis) - 1)]
+    return lax.ppermute(up, axis, pairs), lax.ppermute(down, axis, [(b, a) for a, b in pairs])
 
 
 def summed(sums, axis):
@@ -586,12 +641,12 @@
     places = [(axis, lax.axis_index(axis), lax.axis_size(axis)) for axis in ("gx", "gy")]
     keep = jnp.stack([(at + 1 < size).astype(F32) for _, at, size in places])
     cells, tag = to_cells(cell_index.reshape(256, 128), offset_code, particle_state)
-    grid, rim, *slabs = deposit(cells, tag, fluid_flags)
-    order = [WAYS.index(way) for way in ((0, 1), (0, -1), (1, 0), (-1, 0), (1, 1), (-1, -1), (1, -1), (-1, 1))]
-    sent = {i: to_neighbour(slabs[i], *WAYS[i]) for i in order}
-    arrived = [sent[WAYS.index((-dx, -dy))] for dx, dy in WAYS]
+    grid, rim, up, down = deposit(cells, tag, fluid_flags)
+    low, high = neighbours(up, down, "gy")
     plan = particle_plan(tag.reshape(256, 128))
-    vel, fluid, k0, k1, k2, sums = krylov(keep, grid, rim, fluid_flags, arrived, plan[1])
+    near, edge, flags, up, down = widen(keep, grid, rim, low, high, fluid_flags, plan[1])
+    low, high = neighbours(up, down, "gx")
+    vel, fluid, k0, k1, k2, sums = krylov(keep, near, edge, flags, low, high)
     sums = summed(summed(sums, "gx"), "gy")[None]
     pressure, result = project(sums, vel, fluid, k0, k1, k2, tag, *plan)
     return pressure, result.reshape(1, 3, CELLS)

time: 84.8 us -> 66.2 us (0.78)
  starting transfers between devices: 28.8 us -> 22.5 us
  waiting for transfers between devices: 14 us -> 8.45 us
  local copies, waits for them, and re-layouts: 8.48 us -> 3.21 us
  Pallas kernels: 32 us -> 31 us
    ppermute x8 -> x4, starting transfers between devices: 22.2 us -> 11.4 us  [the longest x2 8.8 us: neighbours(): lax.ppermute(up, axis, pairs)]
    unnamed x32 -> x8, local copies, waits for them, and re-layouts: 8.48 us -> 3.21 us
    ppermute x6, starting transfers between devices: 6.56 us -> 11.1 us  [summed(): lax.ppermute(sums, axis, [(i, (i + shift) % count) for i in range(count)])]
    ppermute x8 -> x4, waiting for transfers between devices: 5.47 us -> 1.09 us  [the longest x2 1.08 us: neighbours(): lax.ppermute(up, axis, pairs)]
    ppermute x6, waiting for transfers between devices: 8.52 us -> 7.36 us  [summed(): lax.ppermute(sums, axis, [(i, (i + shift) % count) for i in range(count)])]
    pallas_call x5 -> x6, Pallas kernels: 32 us -> 31 us  [kernel_call(): pl.pallas_call(body, out_shape=outs, **{} if in_specs is None else dict(i...]
  transfers between devices with their start and end apart: 14 -> 10, of which waited for: 6 -> 6; matrix products, arithmetic and copies ran while one was open for 0% -> 0% of each run, Pallas kernels for 8% -> 10%
where the time goes in v6:
time: 66.2 us; the launch traced here: 66 us
  Pallas kernels  31 us (47%)
  starting transfers between devices  22.5 us (34%)
  waiting for transfers between devices  8.45 us (13%)
  local copies, waits for them, and re-layouts  3.21 us (5%)
  between operations  0.74 us (1%)
    pallas_call x6, Pallas kernels, kernel_call(): pl.pallas_call(body, out_shape=outs, **{} if in_specs is None else dict(i...  31 us
    ppermute x6, starting transfers between devices, summed(): lax.ppermute(sums, axis, [(i, (i + shift) % count) for i in range(count)])  11.1 us
    ppermute x2, starting transfers between devices, neighbours(): lax.ppermute(up, axis, pairs)  8.8 us
    ppermute x6, waiting for transfers between devices, summed(): lax.ppermute(sums, axis, [(i, (i + shift) % count) for i in range(count)])  7.36 us
    unnamed x8, local copies, waits for them, and re-layouts  3.21 us
    ppermute x2, starting transfers between devices, neighbours(): lax.ppermute(down, axis, [(b, a) for a, b in pairs])  2.58 us
  transfers between devices with their start and end apart: 10, of which 6 were waited for; matrix products, arithmetic and copies ran while one was open for 0% of the time, Pallas kernels for 10%

profile of v6, /device:TPU:0, one launch (start us, length us, event | category | flops | bytes accessed | tf_op | source)
XLA Modules:
  0.0 66.0 jit_solution(16381817262184069921)
XLA Ops:
  0.6 0.0 copy-start
  0.6 1.4 %copy-done = f32[1,12,32768]{2,0,1:T(1,128)S(1)} copy-done((f32[1,12,32768]{2,0,1:T(1,128)S(1)}, f32[1,12,32768]{2,0,1:T(1,128)}, u32[]{:S(2)}) %copy-start) | copy-done | bytes 1572888
  2.0 0.0 copy-start.2
  2.0 0.9 %copy-done.2 = s32[1,32768]{1,0:T(1,128)S(1)} copy-done((s32[1,32768]{1,0:T(1,128)S(1)}, s32[1,32768]{1,0:T(1,128)}, u32[]{:S(2)}) %copy-start.2) | copy-done | bytes 131096
  2.9 0.0 copy-start.3
  2.9 0.9 %copy-done.3 = s32[1,32768]{1,0:T(1,128)S(1)} copy-done((s32[1,32768]{1,0:T(1,128)S(1)}, s32[1,32768]{1,0:T(1,128)}, u32[]{:S(2)}) %copy-start.3) | copy-done | bytes 131096
  3.8 0.0 copy-start.1
  3.9 16.3 %to_cells.1 = (f32[12,32,8,128]{3,2,1,0:T(8,128)S(1)}, s32[1,32,8,128]{3,2,1,0:T(8,128)S(1)}) custom-call(s32[256,128]{1,0:T(8,128)S(1)} %bitcast.11, s32[32,8,128]{2,1,0:T(8,128)S(1)} %bitcast.12, f32[12,32,8,128]{3,2,1,0:T(8,128)S(1)} %bitcast.9), custom_call_target="tpu_custom_call" | custom-call | flops 10000000 | bytes 7208960 | tf_op jit(solution)/shard_map/to_cells/pallas_call | solution.py:375
  20.1 0.0 copy-done.1
  20.1 0.7 %deposit.1 = (f32[4,17,2,8,128]{4,3,2,1,0:T(8,128)S(1)}, f32[4,17,2,8,128]{4,3,2,1,0:T(8,128)S(1)}, f32[592,128]{1,0:T(8,128)S(1)}, f32[624,128]{1,0:T(8,128)S(1)}) custom-call(f32[12,32,8,128]{3,2,1,0:T(8,128)S(1)} %get-tuple-element.24.cells_ref, s32[1,32,8,128]{3,2,1,0:T(8,128)S(1)} %get-tuple-element.25.tag_ref, s32[16,8,256]{2,1,0:T(8,128)S(1)} %copy-done.1), custom_call_target="tpu_custom_call" | custom-call | bytes 3571712 | tf_op jit(solution)/shard_map/deposit/pallas_call | solution.py:375
  20.9 1.3 %collective-permute-start.1 = (f32[624,128]{1,0:T(8,128)S(1)}, f32[624,128]{1,0:T(8,128)S(1)}, u32[]{:S(2)}, u32[]{:S(2)}) collective-permute-start(f32[624,128]{1,0:T(8,128)S(1)} %get-tuple-element.29), channel_id=1, source_target_pairs={{1,0},{2,1},{3,2},{5,4},{6,5},{7,6},{9,8},{10,9},{11,10},{13,12},{... | collective-permute-start | bytes 958472 | tf_op jit(solution)/shard_map/ppermute | solution.py:629
  22.2 5.8 %collective-permute-start = (f32[592,128]{1,0:T(8,128)S(1)}, f32[592,128]{1,0:T(8,128)S(1)}, u32[]{:S(2)}, u32[]{:S(2)}) collective-permute-start(f32[592,128]{1,0:T(8,128)S(1)} %get-tuple-element.28), channel_id=1, source_target_pairs={{0,1},{1,2},{2,3},{4,5},{5,6},{6,7},{8,9},{9,10},{10,11},{12,13},{... | collective-permute-start | bytes 909320 | tf_op jit(solution)/shard_map/ppermute | solution.py:629
  28.0 6.5 %particle_plan.1 = (s32[9,256,128]{2,1,0:T(8,128)S(1)}, s32[3,256,128]{2,1,0:T(8,128)S(1)}, s32[3840,128]{1,0:T(8,128)S(1)}) custom-call(s32[256,128]{1,0:T(8,128)S(1)} %bitcast.10), custom_call_target="tpu_custom_call" | custom-call | flops 10000000 | bytes 3670016 | tf_op jit(solution)/shard_map/particle_plan/pallas_call | solution.py:375
  34.4 0.1 add_convert_fusion.keep_ref
  34.5 0.0 collective-permute-done.low_ref
  34.5 0.0 collective-permute-done.1.high_ref
  34.5 1.0 %widen.1 = (f32[3,16,2,24,128]{4,3,2,1,0:T(8,128)S(1)}, f32[4,2,2,24,128]{4,3,2,1,0:T(8,128)S(1)}, f32[16,2,24,128]{3,2,1,0:T(8,128)S(1)}, f32[440,128]{1,0:T(8,128)S(1)}, f32[464,128]{1,0:T(8,128)S(1)}) custom-call(f32[2]{0:T(128)S(1)} %add_convert_fusion.keep_ref, f32[4,17,2,8,128]{4,3,2,1,0:T(8,128)S(1)} %get-tuple-element.26.grid_ref, ...), custom_call_target="tpu_custom_call" | custom-call | bytes 6164480 | tf_op jit(solution)/shard_map/widen/pallas_call | solution.py:375
  35.6 1.3 %collective-permute-start.3 = (f32[464,128]{1,0:T(8,128)S(1)}, f32[464,128]{1,0:T(8,128)S(1)}, u32[]{:S(2)}, u32[]{:S(2)}) collective-permute-start(f32[464,128]{1,0:T(8,128)S(1)} %get-tuple-element.35), channel_id=1, source_target_pairs={{4,0},{8,4},{12,8},{5,1},{9,5},{13,9},{6,2},{10,6},{14,10},{7,3},{... | collective-permute-start | bytes 712712 | tf_op jit(solution)/shard_map/ppermute | solution.py:629
  36.9 3.0 %collective-permute-start.2 = (f32[440,128]{1,0:T(8,128)S(1)}, f32[440,128]{1,0:T(8,128)S(1)}, u32[]{:S(2)}, u32[]{:S(2)}) collective-permute-start(f32[440,128]{1,0:T(8,128)S(1)} %get-tuple-element.34), channel_id=1, source_target_pairs={{0,4},{4,8},{8,12},{1,5},{5,9},{9,13},{2,6},{6,10},{10,14},{3,7},{... | collective-permute-start | bytes 675848 | tf_op jit(solution)/shard_map/ppermute | solution.py:629
  39.9 1.1 %collective-permute-done.2.low_ref = f32[440,128]{1,0:T(8,128)S(1)} collective-permute-done((f32[440,128]{1,0:T(8,128)S(1)}, f32[440,128]{1,0:T(8,128)S(1)}, u32[]{:S(2)}, u32[]{:S(2)}) %collective-permute-start.2) | collective-permute-done | bytes 225312 | tf_op jit(solution)/shard_map/ppermute | solution.py:629
  41.0 0.0 collective-permute-done.3.high_ref
  41.0 1.8 %krylov.1 = (f32[3,25,2,24,128]{4,3,2,1,0:T(8,128)S(1)}, f32[25,2,24,128]{3,2,1,0:T(8,128)S(1)}, f32[25,2,24,128]{3,2,1,0:T(8,128)S(1)}, f32[25,2,24,128]{3,2,1,...) custom-call(f32[2]{0:T(128)S(1)} %add_convert_fusion.keep_ref, ...), custom_call_target="tpu_custom_call" | custom-call | bytes 6737920 | tf_op jit(solution)/shard_map/krylov/pallas_call | solution.py:375
  42.8 2.0 %collective-permute-start.6 = (f32[16,128]{1,0:T(8,128)S(1)}, f32[16,128]{1,0:T(8,128)S(1)}, u32[]{:S(2)}, u32[]{:S(2)}) collective-permute-start(f32[16,128]{1,0:T(8,128)S(1)} %get-tuple-element.36), channel_id=1, source_target_pairs={{0,12},{4,0},{8,4},{12,8},{1,13},{5,1},{9,5},{13,9},{2,14},{6,2},{... | collective-permute-start | bytes 24584 | tf_op jit(solution)/shard_map/ppermute | solution.py:636
  44.8 3.9 %collective-permute-start.5 = (f32[16,128]{1,0:T(8,128)S(1)}, f32[16,128]{1,0:T(8,128)S(1)}, u32[]{:S(2)}, u32[]{:S(2)}) collective-permute-start(f32[16,128]{1,0:T(8,128)S(1)} %get-tuple-element.36), channel_id=1, source_target_pairs={{0,8},{4,12},{8,0},{12,4},{1,9},{5,13},{9,1},{13,5},{2,10},{6,14},... | collective-permute-start | bytes 24584 | tf_op jit(solution)/shard_map/ppermute | solution.py:636
  48.7 0.2 collective-permute-start.4
  48.9 0.0 collective-permute-done.6
  48.9 1.5 %collective-permute-done.5 = f32[16,128]{1,0:T(8,128)S(1)} collective-permute-done((f32[16,128]{1,0:T(8,128)S(1)}, f32[16,128]{1,0:T(8,128)S(1)}, u32[]{:S(2)}, u32[]{:S(2)}) %collective-permute-start.5) | collective-permute-done | bytes 8224 | tf_op jit(solution)/shard_map/ppermute | solution.py:636
  50.3 1.4 %collective-permute-done.4 = f32[16,128]{1,0:T(8,128)S(1)} collective-permute-done((f32[16,128]{1,0:T(8,128)S(1)}, f32[16,128]{1,0:T(8,128)S(1)}, u32[]{:S(2)}, u32[]{:S(2)}) %collective-permute-start.4) | collective-permute-done | bytes 8224 | tf_op jit(solution)/shard_map/ppermute | solution.py:636
  51.8 4.1 %collective-permute-start.9 = (f32[16,128]{1,0:T(8,128)S(1)}, f32[16,128]{1,0:T(8,128)S(1)}, u32[]{:S(2)}, u32[]{:S(2)}) collective-permute-start(f32[16,128]{1,0:T(8,128)S(1)} %add_add_fusion), channel_id=1, source_target_pairs={{0,3},{1,0},{2,1},{3,2},{4,7},{5,4},{6,5},{7,6},{8,11},{9,8},{10,9... | collective-permute-start | bytes 24584 | tf_op jit(solution)/shard_map/ppermute | solution.py:636
  55.9 0.0 collective-permute-start.8
  55.9 1.0 %collective-permute-start.7 = (f32[16,128]{1,0:T(8,128)S(1)}, f32[16,128]{1,0:T(8,128)S(1)}, u32[]{:S(2)}, u32[]{:S(2)}) collective-permute-start(f32[16,128]{1,0:T(8,128)S(1)} %add_add_fusion), channel_id=1, source_target_pairs={{0,1},{1,2},{2,3},{3,0},{4,5},{5,6},{6,7},{7,4},{8,9},{9,10},{10,1... | collective-permute-start | bytes 24584 | tf_op jit(solution)/shard_map/ppermute | solution.py:636
  56.9 0.4 collective-permute-done.9
  57.2 3.2 %collective-permute-done.8 = f32[16,128]{1,0:T(8,128)S(1)} collective-permute-done((f32[16,128]{1,0:T(8,128)S(1)}, f32[16,128]{1,0:T(8,128)S(1)}, u32[]{:S(2)}, u32[]{:S(2)}) %collective-permute-start.8) | collective-permute-done | bytes 8224 | tf_op jit(solution)/shard_map/ppermute | solution.py:636
  60.4 0.9 %collective-permute-done.7 = f32[16,128]{1,0:T(8,128)S(1)} collective-permute-done((f32[16,128]{1,0:T(8,128)S(1)}, f32[16,128]{1,0:T(8,128)S(1)}, u32[]{:S(2)}, u32[]{:S(2)}) %collective-permute-start.7) | collective-permute-done | bytes 8224 | tf_op jit(solution)/shard_map/ppermute | solution.py:636
  61.3 4.6 %project.1 = (f32[16,8,256]{2,1,0:T(8,128)}, f32[3,32,8,128]{3,2,1,0:T(8,128)}) custom-call(f32[1,16,128]{2,1,0:T(8,128)S(1)} %add_bitcast_fusion.sums_ref, f32[3,25,2,24,128]{4,3,2,1,0:T(8,128)S(1)} %get-tuple-element.37.vel_ref, f32[25,2,24,128]{3,2,1,0:T(8,128)S(1)} %get-tuple-element.38.fluid_ref, f32[25,2,24,128]{3,2,1,0:T(8,128)S(1)} %get-tuple-element.39.k0_ref, ...), custom_call_target="tpu_custom_call" | custom-call | bytes 10788864 | tf_op jit(solution)/shard_map/project/pallas_call | solution.py:375
  (2 shorter events, 0.0 us)
Async XLA Ops:
  0.6 1.4 %copy-start = (f32[1,12,32768]{2,0,1:T(1,128)S(1)}, f32[1,12,32768]{2,0,1:T(1,128)}, u32[]{:S(2)}) copy-start(f32[1,12,32768]{2,0,1:T(1,128)} %param.6) | copy-start | bytes 4718596
  2.0 0.9 %copy-start.2 = (s32[1,32768]{1,0:T(1,128)S(1)}, s32[1,32768]{1,0:T(1,128)}, u32[]{:S(2)}) copy-start(s32[1,32768]{1,0:T(1,128)} %param.4) | copy-start | bytes 393220
  2.9 0.9 %copy-start.3 = (s32[1,32768]{1,0:T(1,128)S(1)}, s32[1,32768]{1,0:T(1,128)}, u32[]{:S(2)}) copy-start(s32[1,32768]{1,0:T(1,128)} %param.5) | copy-start | bytes 393220
  3.8 16.3 %copy-start.1 = (s32[16,8,256]{2,1,0:T(8,128)S(1)}, s32[16,8,256]{2,1,0:T(8,128)}, u32[]{:S(2)}) copy-start(s32[16,8,256]{2,1,0:T(8,128)} %flag_ref.3) | copy-start | bytes 393220
  20.9 13.6 %collective-permute-start.1 = (f32[624,128]{1,0:T(8,128)S(1)}, f32[624,128]{1,0:T(8,128)S(1)}, u32[]{:S(2)}, u32[]{:S(2)}) collective-permute-start(f32[624,128]{1,0:T(8,128)S(1)} %get-tuple-element.29), channel_id=1, source_target_pairs={{1,0},{2,1},{3,2},{5,4},{6,5},{7,6},{9,8},{10,9},{11,10},{13,12},{... | collective-permute-start | bytes 958472 | tf_op jit(solution)/shard_map/ppermute | solution.py:629
  22.2 12.3 %collective-permute-start = (f32[592,128]{1,0:T(8,128)S(1)}, f32[592,128]{1,0:T(8,128)S(1)}, u32[]{:S(2)}, u32[]{:S(2)}) collective-permute-start(f32[592,128]{1,0:T(8,128)S(1)} %get-tuple-element.28), channel_id=1, source_target_pairs={{0,1},{1,2},{2,3},{4,5},{5,6},{6,7},{8,9},{9,10},{10,11},{12,13},{... | collective-permute-start | bytes 909320 | tf_op jit(solution)/shard_map/ppermute | solution.py:629
  35.6 5.4 %collective-permute-start.3 = (f32[464,128]{1,0:T(8,128)S(1)}, f32[464,128]{1,0:T(8,128)S(1)}, u32[]{:S(2)}, u32[]{:S(2)}) collective-permute-start(f32[464,128]{1,0:T(8,128)S(1)} %get-tuple-element.35), channel_id=1, source_target_pairs={{4,0},{8,4},{12,8},{5,1},{9,5},{13,9},{6,2},{10,6},{14,10},{7,3},{... | collective-permute-start | bytes 712712 | tf_op jit(solution)/shard_map/ppermute | solution.py:629
  36.9 4.1 %collective-permute-start.2 = (f32[440,128]{1,0:T(8,128)S(1)}, f32[440,128]{1,0:T(8,128)S(1)}, u32[]{:S(2)}, u32[]{:S(2)}) collective-permute-start(f32[440,128]{1,0:T(8,128)S(1)} %get-tuple-element.34), channel_id=1, source_target_pairs={{0,4},{4,8},{8,12},{1,5},{5,9},{9,13},{2,6},{6,10},{10,14},{3,7},{... | collective-permute-start | bytes 675848 | tf_op jit(solution)/shard_map/ppermute | solution.py:629
  42.8 6.0 %collective-permute-start.6 = (f32[16,128]{1,0:T(8,128)S(1)}, f32[16,128]{1,0:T(8,128)S(1)}, u32[]{:S(2)}, u32[]{:S(2)}) collective-permute-start(f32[16,128]{1,0:T(8,128)S(1)} %get-tuple-element.36), channel_id=1, source_target_pairs={{0,12},{4,0},{8,4},{12,8},{1,13},{5,1},{9,5},{13,9},{2,14},{6,2},{... | collective-permute-start | bytes 24584 | tf_op jit(solution)/shard_map/ppermute | solution.py:636
  44.8 5.5 %collective-permute-start.5 = (f32[16,128]{1,0:T(8,128)S(1)}, f32[16,128]{1,0:T(8,128)S(1)}, u32[]{:S(2)}, u32[]{:S(2)}) collective-permute-start(f32[16,128]{1,0:T(8,128)S(1)} %get-tuple-element.36), channel_id=1, source_target_pairs={{0,8},{4,12},{8,0},{12,4},{1,9},{5,13},{9,1},{13,5},{2,10},{6,14},... | collective-permute-start | bytes 24584 | tf_op jit(solution)/shard_map/ppermute | solution.py:636
  48.7 3.1 %collective-permute-start.4 = (f32[16,128]{1,0:T(8,128)S(1)}, f32[16,128]{1,0:T(8,128)S(1)}, u32[]{:S(2)}, u32[]{:S(2)}) collective-permute-start(f32[16,128]{1,0:T(8,128)S(1)} %get-tuple-element.36), channel_id=1, source_target_pairs={{0,4},{4,8},{8,12},{12,0},{1,5},{5,9},{9,13},{13,1},{2,6},{6,10},{... | collective-permute-start | bytes 24584 | tf_op jit(solution)/shard_map/ppermute | solution.py:636
  51.8 5.5 %collective-permute-start.9 = (f32[16,128]{1,0:T(8,128)S(1)}, f32[16,128]{1,0:T(8,128)S(1)}, u32[]{:S(2)}, u32[]{:S(2)}) collective-permute-start(f32[16,128]{1,0:T(8,128)S(1)} %add_add_fusion), channel_id=1, source_target_pairs={{0,3},{1,0},{2,1},{3,2},{4,7},{5,4},{6,5},{7,6},{8,11},{9,8},{10,9... | collective-permute-start | bytes 24584 | tf_op jit(solution)/shard_map/ppermute | solution.py:636
  55.9 4.5 %collective-permute-start.8 = (f32[16,128]{1,0:T(8,128)S(1)}, f32[16,128]{1,0:T(8,128)S(1)}, u32[]{:S(2)}, u32[]{:S(2)}) collective-permute-start(f32[16,128]{1,0:T(8,128)S(1)} %add_add_fusion), channel_id=1, source_target_pairs={{0,2},{1,3},{2,0},{3,1},{4,6},{5,7},{6,4},{7,5},{8,10},{9,11},{10,... | collective-permute-start | bytes 24584 | tf_op jit(solution)/shard_map/ppermute | solution.py:636
  55.9 5.4 %collective-permute-start.7 = (f32[16,128]{1,0:T(8,128)S(1)}, f32[16,128]{1,0:T(8,128)S(1)}, u32[]{:S(2)}, u32[]{:S(2)}) collective-permute-start(f32[16,128]{1,0:T(8,128)S(1)} %add_add_fusion), channel_id=1, source_target_pairs={{0,1},{1,2},{2,3},{3,0},{4,5},{5,6},{6,7},{7,4},{8,9},{9,10},{10,1... | collective-permute-start | bytes 24584 | tf_op jit(solution)/shard_map/ppermute | solution.py:636

commit v7 on v6

--- a/solution.py
+++ b/solution.py
@@ -106,7 +106,7 @@
     return tiles
 
 
-def follow_plan(stages, lane_ref, sub_ref, swap_ref):
+def follow_plan(stages, lane_ref, sub_ref, swap_ref, sources=None):
     def crossings(hops, before):
         out = {}
         for hop in hops:
@@ -116,9 +116,9 @@
                     before += 1
         return out, before
 
-    def pass_over(sets, work):
+    def pass_over(sets, work, sources=stages):
         for members in sets:
-            moved = [{i: ref[c, i] for i in members} for ref, c in stages]
+            moved = [{i: ref[c, i] for i in members} for ref, c in sources]
             work(members, moved)
             for (ref, c), tiles in zip(stages, moved):
                 for i, t in tiles.items():
@@ -152,7 +152,7 @@
             exchanged([4, 2, 1][10 - phase :], numbers[phase], members, moved)
             gathered(lane_ref, phase - 7, 1, members, moved)
 
-    pass_over(eights, first)
+    pass_over(eights, first, sources or stages)
     for phase in range(11, 16):
         wide = [16, 8] if phase > 11 else [8]
         reach = 32 if phase > 11 else 16
@@ -265,35 +265,34 @@
     return kernel_call(particle_plan_kernel, "particle_plan", outs, [], (tag,), flops=10**7)
 
 
-def to_cells_kernel(cell_ref, code_ref, state_ref, cells_ref, tag_ref, code, lane_ref, sub_ref, swap_ref, done):
-    arrivals = [
-        pltpu.make_async_copy(code_ref, code, done.at[0]),
-        pltpu.make_async_copy(state_ref, cells_ref, done.at[1]),
-    ]
-    for arrival in arrivals:
-        arrival.start()
+def cell_plan_kernel(cell_ref, lane_ref, sub_ref, swap_ref):
     k = cell_ref[...]
     key = ((k & 0x700) << 4) | ((k & 0x7800) >> 3) | (k & 0xFF)
     sort_plan(split_tiles(key), lane_ref, sub_ref, swap_ref)
-    for arrival in arrivals:
-        arrival.wait()
-    tag_ref[0] = (code[...] << 15) | (iota((TILES, 8, 128), 0) * 8 + iota((TILES, 8, 128), 1)) * 128 + iota(
-        (TILES, 8, 128), 2
-    )
+
+
+def cell_plan(cell):
+    outs = [of(shape, I32) for shape in plan_shapes()]
+    return kernel_call(cell_plan_kernel, "cell_plan", outs, [], (cell,), flops=7 * 10**9)
+
+
+def to_cells_kernel(code_ref, state_ref, lane_ref, sub_ref, swap_ref, cells_ref, tag_ref):
+    shape = (TILES, 8, 128)
+    tag_ref[0] = (code_ref[...] << 15) | (iota(shape, 0) * 8 + iota(shape, 1)) * 128 + iota(shape, 2)
     for quad in range(3):
-        stages = [(cells_ref, 4 * quad + c) for c in range(4)]
-        follow_plan(stages + [(tag_ref, 0)] * (quad == 0), lane_ref, sub_ref, swap_ref)
-
-
-def to_cells(cell, code, state):
-    anywhere = pl.BlockSpec(memory_space=pltpu.HBM)
+        channels = range(4 * quad, 4 * quad + 4)
+        stages = [(cells_ref, c) for c in channels] + [(tag_ref, 0)] * (quad == 0)
+        sources = [(state_ref, c) for c in channels] + [(tag_ref, 0)] * (quad == 0)
+        follow_plan(stages, lane_ref, sub_ref, swap_ref, sources)
+
+
+def to_cells(code, state, plan):
     return kernel_call(
         to_cells_kernel,
         "to_cells",
         (of((12, TILES, 8, 128)), of((1, TILES, 8, 128), I32)),
-        [pltpu.VMEM(shape, I32) for shape in [(TILES, 8, 128)] + plan_shapes()] + [pltpu.SemaphoreType.DMA((2,))],
-        (cell, code.reshape(TILES, 8, 128), state.reshape(12, TILES, 8, 128)),
-        [vmem(), anywhere, anywhere],
+        [],
+        (code.reshape(TILES, 8, 128), state.reshape(12, TILES, 8, 128), *plan),
         flops=10**7,
     )
 
@@ -625,22 +624,32 @@
 
 
 def neighbours(up, down, axis):
-    pairs = [(i, i + 1) for i in range(lax.axis_size(axis) - 1)]
-    return lax.ppermute(up, axis, pairs), lax.ppermute(down, axis, [(b, a) for a, b in pairs])
+    count = lax.axis_size(axis)
+    odd = lax.axis_index(axis) % 2 == 1
+    high_rows, low_rows = down.shape[0], up.shape[0]
+    up = jnp.concatenate([up, jnp.zeros((high_rows - low_rows, 128), F32)])
+    arrived = []
+    for first, slab in ((0, jnp.where(odd, down, up)), (1, jnp.where(odd, up, down))):
+        pairs = [(i, i + 1) for i in range(first, count - 1, 2)]
+        arrived.append(lax.ppermute(slab, axis, pairs + [(b, a) for a, b in pairs]))
+    return jnp.where(odd, arrived[0], arrived[1]), jnp.where(odd, arrived[1], arrived[0])
 
 
 def summed(sums, axis):
     count = lax.axis_size(axis)
     parts = [sums]
     for shift in range(1, count):
-        parts.append(lax.ppermute(sums, axis, [(i, (i + shift) % count) for i in range(count)]))
+        swaps = [(i, i ^ shift) for i in range(count)]
+        if max(b for _, b in swaps) >= count:
+            swaps = [(i, (i + shift) % count) for i in range(count)]
+        parts.append(lax.ppermute(sums, axis, swaps))
     return functools.reduce(jnp.add, parts)
 
 
 def local(cell_index, offset_code, particle_state, fluid_flags):
     places = [(axis, lax.axis_index(axis), lax.axis_size(axis)) for axis in ("gx", "gy")]
     keep = jnp.stack([(at + 1 < size).astype(F32) for _, at, size in places])
-    cells, tag = to_cells(cell_index.reshape(256, 128), offset_code, particle_state)
+    cells, tag = to_cells(offset_code, particle_state, cell_plan(cell_index.reshape(256, 128)))
     grid, rim, up, down = deposit(cells, tag, fluid_flags)
     low, high = neighbours(up, down, "gy")
     plan = particle_plan(tag.reshape(256, 128))

time: 66.2 us -> 57.4 us (0.87)
  starting transfers between devices: 22.5 us -> 19.2 us
  waiting for transfers between devices: 8.45 us -> 5.91 us
  local copies, waits for them, and re-layouts: 3.21 us -> 0.91 us
  Pallas kernels: 31 us -> 30.2 us
    ppermute x10, starting transfers between devices: 22.5 us -> 19.2 us  [the longest x4 10.3 us: neighbours(): arrived.append(lax.ppermute(slab, axis, pairs + [(b, a) for a, b in pairs]))]
    ppermute x10, waiting for transfers between devices: 8.45 us -> 5.91 us  [the longest x6 4.07 us: summed(): parts.append(lax.ppermute(sums, axis, swaps))]
    unnamed x8, local copies, waits for them, and re-layouts: 3.21 us -> 0.91 us
    pallas_call x6 -> x7, Pallas kernels: 31 us -> 30.2 us  [kernel_call(): pl.pallas_call(body, out_shape=outs, **{} if in_specs is None else dict(i...]
  transfers between devices with their start and end apart: 10 -> 10, of which waited for: 6 -> 6; matrix products, arithmetic and copies ran while one was open for 0% -> 0% of each run, Pallas kernels for 10% -> 11%
where the time goes in v7:
time: 57.4 us; the launch traced here: 57.2 us
  Pallas kernels  30.2 us (53%)
  starting transfers between devices  19.2 us (33%)
  waiting for transfers between devices  5.91 us (10%)
  local copies, waits for them, and re-layouts  0.91 us (2%)
  between operations  0.77 us (1%)
    pallas_call x7, Pallas kernels, kernel_call(): pl.pallas_call(body, out_shape=outs, **{} if in_specs is None else dict(i...  30.2 us
    ppermute x4, starting transfers between devices, neighbours(): arrived.append(lax.ppermute(slab, axis, pairs + [(b, a) for a, b in pairs]))  10.3 us
    ppermute x6, starting transfers between devices, summed(): parts.append(lax.ppermute(sums, axis, swaps))  8.84 us
    ppermute x6, waiting for transfers between devices, summed(): parts.append(lax.ppermute(sums, axis, swaps))  4.07 us
    ppermute x4, waiting for transfers between devices, neighbours(): arrived.append(lax.ppermute(slab, axis, pairs + [(b, a) for a, b in pairs]))  1.84 us
  transfers between devices with their start and end apart: 10, of which 6 were waited for; matrix products, arithmetic and copies ran while one was open for 0% of the time, Pallas kernels for 11%

profile of v7, /device:TPU:0, one launch (start us, length us, event | category | flops | bytes accessed | tf_op | source)
XLA Modules:
  0.0 57.2 jit_solution(10738282431891400291)
XLA Ops:
  0.6 0.0 copy-start.3
  0.7 0.9 %copy-done.3 = s32[1,32768]{1,0:T(1,128)S(1)} copy-done((s32[1,32768]{1,0:T(1,128)S(1)}, s32[1,32768]{1,0:T(1,128)}, u32[]{:S(2)}) %copy-start.3) | copy-done | bytes 131096
  1.5 0.0 copy-start
  1.6 0.0 copy-start.2
  1.6 6.4 %cell_plan.1 = (s32[9,256,128]{2,1,0:T(8,128)S(1)}, s32[3,256,128]{2,1,0:T(8,128)S(1)}, s32[3840,128]{1,0:T(8,128)S(1)}) custom-call(s32[256,128]{1,0:T(8,128)S(1)} %bitcast.12), custom_call_target="tpu_custom_call" | custom-call | flops 7000000000 | bytes 3670016 | tf_op jit(solution)/shard_map/cell_plan/pallas_call | solution.py:374
  8.0 0.0 copy-done
  8.0 0.0 copy-done.2
  8.0 0.0 copy-start.1
  8.0 9.1 %to_cells.1 = (f32[12,32,8,128]{3,2,1,0:T(8,128)S(1)}, s32[1,32,8,128]{3,2,1,0:T(8,128)S(1)}) custom-call(s32[32,8,128]{2,1,0:T(8,128)S(1)} %bitcast.11, f32[12,32,8,128]{3,2,1,0:T(8,128)S(1)} %bitcast.9, s32[9,256,128]{2,1,0:T(8,128)S(1)} %get-tuple-element.27.lane_ref, s32[3,256,128]{2,1,0:T(8,128)S(1)} %get-tuple-element.28.sub_ref, ...), custom_call_target="tpu_custom_call" | custom-call | flops 10000000 | bytes 6946816 | tf_op jit(solution)/shard_map/to_cells/pallas_call | solution.py:374
  17.1 0.0 copy-done.1
  17.1 0.7 %deposit.1 = (f32[4,17,2,8,128]{4,3,2,1,0:T(8,128)S(1)}, f32[4,17,2,8,128]{4,3,2,1,0:T(8,128)S(1)}, f32[592,128]{1,0:T(8,128)S(1)}, f32[624,128]{1,0:T(8,128)S(1)}) custom-call(f32[12,32,8,128]{3,2,1,0:T(8,128)S(1)} %get-tuple-element.30.cells_ref, s32[1,32,8,128]{3,2,1,0:T(8,128)S(1)} %get-tuple-element.31.tag_ref, s32[16,8,256]{2,1,0:T(8,128)S(1)} %copy-done.1), custom_call_target="tpu_custom_call" | custom-call | bytes 3571712 | tf_op jit(solution)/shard_map/deposit/pallas_call | solution.py:374
  17.9 0.9 %collective-permute-start.1 = (f32[624,128]{1,0:T(8,128)S(1)}, f32[624,128]{1,0:T(8,128)S(1)}, u32[]{:S(2)}, u32[]{:S(2)}) collective-permute-start(f32[624,128]{1,0:T(8,128)S(1)} %get-tuple-element.58), channel_id=1, source_target_pairs={{1,2},{2,1},{5,6},{6,5},{9,10},{10,9},{13,14},{14,13},{17,18},{18,... | collective-permute-start | bytes 958472 | tf_op jit(solution)/shard_map/ppermute | solution.py:634
  18.8 5.9 %collective-permute-start = (f32[624,128]{1,0:T(8,128)S(1)}, f32[624,128]{1,0:T(8,128)S(1)}, u32[]{:S(2)}, u32[]{:S(2)}) collective-permute-start(f32[624,128]{1,0:T(8,128)S(1)} %get-tuple-element.59), channel_id=1, source_target_pairs={{0,1},{2,3},{1,0},{3,2},{4,5},{6,7},{5,4},{7,6},{8,9},{10,11},{9,8... | collective-permute-start | bytes 958472 | tf_op jit(solution)/shard_map/ppermute | solution.py:634
  24.7 6.5 %particle_plan.1 = (s32[9,256,128]{2,1,0:T(8,128)S(1)}, s32[3,256,128]{2,1,0:T(8,128)S(1)}, s32[3840,128]{1,0:T(8,128)S(1)}) custom-call(s32[256,128]{1,0:T(8,128)S(1)} %bitcast.10), custom_call_target="tpu_custom_call" | custom-call | flops 10000000 | bytes 3670016 | tf_op jit(solution)/shard_map/particle_plan/pallas_call | solution.py:374
  31.1 0.1 add_convert_fusion.keep_ref
  31.2 0.0 collective-permute-done.1
  31.2 0.7 %collective-permute-done = f32[624,128]{1,0:T(8,128)S(1)} collective-permute-done((f32[624,128]{1,0:T(8,128)S(1)}, f32[624,128]{1,0:T(8,128)S(1)}, u32[]{:S(2)}, u32[]{:S(2)}) %collective-permute-start) | collective-permute-done | bytes 319520 | tf_op jit(solution)/shard_map/ppermute | solution.py:634
  32.0 1.1 %widen.1 = (f32[3,16,2,24,128]{4,3,2,1,0:T(8,128)S(1)}, f32[4,2,2,24,128]{4,3,2,1,0:T(8,128)S(1)}, f32[16,2,24,128]{3,2,1,0:T(8,128)S(1)}, f32[440,128]{1,0:T(8,128)S(1)}, f32[464,128]{1,0:T(8,128)S(1)}) custom-call(f32[2]{0:T(128)S(1)} %add_convert_fusion.keep_ref, f32[4,17,2,8,128]{4,3,2,1,0:T(8,128)S(1)} %get-tuple-element.32.grid_ref, ...), custom_call_target="tpu_custom_call" | custom-call | bytes 6180864 | tf_op jit(solution)/shard_map/widen/pallas_call | solution.py:374
  33.1 0.7 %collective-permute-start.3 = (f32[464,128]{1,0:T(8,128)S(1)}, f32[464,128]{1,0:T(8,128)S(1)}, u32[]{:S(2)}, u32[]{:S(2)}) collective-permute-start(f32[464,128]{1,0:T(8,128)S(1)} %get-tuple-element.62), channel_id=1, source_target_pairs={{4,8},{8,4},{5,9},{9,5},{6,10},{10,6},{7,11},{11,7},{20,24},{24,20... | collective-permute-start | bytes 712712 | tf_op jit(solution)/shard_map/ppermute | solution.py:634
  33.8 2.9 %collective-permute-start.2 = (f32[464,128]{1,0:T(8,128)S(1)}, f32[464,128]{1,0:T(8,128)S(1)}, u32[]{:S(2)}, u32[]{:S(2)}) collective-permute-start(f32[464,128]{1,0:T(8,128)S(1)} %get-tuple-element.63), channel_id=1, source_target_pairs={{0,4},{8,12},{4,0},{12,8},{1,5},{9,13},{5,1},{13,9},{2,6},{10,14},... | collective-permute-start | bytes 712712 | tf_op jit(solution)/shard_map/ppermute | solution.py:634
  36.7 0.0 collective-permute-done.3
  36.7 1.1 %collective-permute-done.2 = f32[464,128]{1,0:T(8,128)S(1)} collective-permute-done((f32[464,128]{1,0:T(8,128)S(1)}, f32[464,128]{1,0:T(8,128)S(1)}, u32[]{:S(2)}, u32[]{:S(2)}) %collective-permute-start.2) | collective-permute-done | bytes 237600 | tf_op jit(solution)/shard_map/ppermute | solution.py:634
  37.8 1.8 %krylov.1 = (f32[3,25,2,24,128]{4,3,2,1,0:T(8,128)S(1)}, f32[25,2,24,128]{3,2,1,0:T(8,128)S(1)}, f32[25,2,24,128]{3,2,1,0:T(8,128)S(1)}, f32[25,2,24,128]{3,2,1,...) custom-call(f32[2]{0:T(128)S(1)} %add_convert_fusion.keep_ref, ...), custom_call_target="tpu_custom_call" | custom-call | bytes 6750208 | tf_op jit(solution)/shard_map/krylov/pallas_call | solution.py:374
  39.7 0.1 collective-permute-start.6
  39.8 4.3 %collective-permute-start.5 = (f32[16,128]{1,0:T(8,128)S(1)}, f32[16,128]{1,0:T(8,128)S(1)}, u32[]{:S(2)}, u32[]{:S(2)}) collective-permute-start(f32[16,128]{1,0:T(8,128)S(1)} %get-tuple-element.42), channel_id=1, source_target_pairs={{0,8},{4,12},{8,0},{12,4},{1,9},{5,13},{9,1},{13,5},{2,10},{6,14},... | collective-permute-start | bytes 24584 | tf_op jit(solution)/shard_map/ppermute | solution.py:645
  44.0 0.0 collective-permute-start.4
  44.1 0.0 collective-permute-done.6
  44.1 1.6 %collective-permute-done.5 = f32[16,128]{1,0:T(8,128)S(1)} collective-permute-done((f32[16,128]{1,0:T(8,128)S(1)}, f32[16,128]{1,0:T(8,128)S(1)}, u32[]{:S(2)}, u32[]{:S(2)}) %collective-permute-start.5) | collective-permute-done | bytes 8224 | tf_op jit(solution)/shard_map/ppermute | solution.py:645
  45.7 0.0 collective-permute-done.4
  45.7 1.4 %collective-permute-start.9 = (f32[16,128]{1,0:T(8,128)S(1)}, f32[16,128]{1,0:T(8,128)S(1)}, u32[]{:S(2)}, u32[]{:S(2)}) collective-permute-start(f32[16,128]{1,0:T(8,128)S(1)} %add_add_fusion), channel_id=1, source_target_pairs={{0,3},{1,2},{2,1},{3,0},{4,7},{5,6},{6,5},{7,4},{8,11},{9,10},{10,... | collective-permute-start | bytes 24584 | tf_op jit(solution)/shard_map/ppermute | solution.py:645
  47.1 1.9 %collective-permute-start.8 = (f32[16,128]{1,0:T(8,128)S(1)}, f32[16,128]{1,0:T(8,128)S(1)}, u32[]{:S(2)}, u32[]{:S(2)}) collective-permute-start(f32[16,128]{1,0:T(8,128)S(1)} %add_add_fusion), channel_id=1, source_target_pairs={{0,2},{1,3},{2,0},{3,1},{4,6},{5,7},{6,4},{7,5},{8,10},{9,11},{10,... | collective-permute-start | bytes 24584 | tf_op jit(solution)/shard_map/ppermute | solution.py:645
  49.0 1.2 %collective-permute-start.7 = (f32[16,128]{1,0:T(8,128)S(1)}, f32[16,128]{1,0:T(8,128)S(1)}, u32[]{:S(2)}, u32[]{:S(2)}) collective-permute-start(f32[16,128]{1,0:T(8,128)S(1)} %add_add_fusion), channel_id=1, source_target_pairs={{0,1},{1,0},{2,3},{3,2},{4,5},{5,4},{6,7},{7,6},{8,9},{9,8},{10,11... | collective-permute-start | bytes 24584 | tf_op jit(solution)/shard_map/ppermute | solution.py:645
  50.1 1.1 %collective-permute-done.9 = f32[16,128]{1,0:T(8,128)S(1)} collective-permute-done((f32[16,128]{1,0:T(8,128)S(1)}, f32[16,128]{1,0:T(8,128)S(1)}, u32[]{:S(2)}, u32[]{:S(2)}) %collective-permute-start.9) | collective-permute-done | bytes 8224 | tf_op jit(solution)/shard_map/ppermute | solution.py:645
  51.2 0.4 collective-permute-done.8
  51.7 0.9 %collective-permute-done.7 = f32[16,128]{1,0:T(8,128)S(1)} collective-permute-done((f32[16,128]{1,0:T(8,128)S(1)}, f32[16,128]{1,0:T(8,128)S(1)}, u32[]{:S(2)}, u32[]{:S(2)}) %collective-permute-start.7) | collective-permute-done | bytes 8224 | tf_op jit(solution)/shard_map/ppermute | solution.py:645
  52.6 4.6 %project.1 = (f32[16,8,256]{2,1,0:T(8,128)}, f32[3,32,8,128]{3,2,1,0:T(8,128)}) custom-call(f32[1,16,128]{2,1,0:T(8,128)S(1)} %add_bitcast_fusion.sums_ref, f32[3,25,2,24,128]{4,3,2,1,0:T(8,128)S(1)} %get-tuple-element.43.vel_ref, f32[25,2,24,128]{3,2,1,0:T(8,128)S(1)} %get-tuple-element.44.fluid_ref, f32[25,2,24,128]{3,2,1,0:T(8,128)S(1)} %get-tuple-element.45.k0_ref, ...), custom_call_target="tpu_custom_call" | custom-call | bytes 10788864 | tf_op jit(solution)/shard_map/project/pallas_call | solution.py:374
  (6 shorter events, 0.2 us)
Async XLA Ops:
  0.6 0.9 %copy-start.3 = (s32[1,32768]{1,0:T(1,128)S(1)}, s32[1,32768]{1,0:T(1,128)}, u32[]{:S(2)}) copy-start(s32[1,32768]{1,0:T(1,128)} %param.4) | copy-start | bytes 393220
  1.5 6.5 %copy-start = (f32[1,12,32768]{2,0,1:T(1,128)S(1)}, f32[1,12,32768]{2,0,1:T(1,128)}, u32[]{:S(2)}) copy-start(f32[1,12,32768]{2,0,1:T(1,128)} %param.6) | copy-start | bytes 4718596
  1.6 6.5 %copy-start.2 = (s32[1,32768]{1,0:T(1,128)S(1)}, s32[1,32768]{1,0:T(1,128)}, u32[]{:S(2)}) copy-start(s32[1,32768]{1,0:T(1,128)} %param.5) | copy-start | bytes 393220
  8.0 9.1 %copy-start.1 = (s32[16,8,256]{2,1,0:T(8,128)S(1)}, s32[16,8,256]{2,1,0:T(8,128)}, u32[]{:S(2)}) copy-start(s32[16,8,256]{2,1,0:T(8,128)} %flag_ref.3) | copy-start | bytes 393220
  17.9 13.3 %collective-permute-start.1 = (f32[624,128]{1,0:T(8,128)S(1)}, f32[624,128]{1,0:T(8,128)S(1)}, u32[]{:S(2)}, u32[]{:S(2)}) collective-permute-start(f32[624,128]{1,0:T(8,128)S(1)} %get-tuple-element.58), channel_id=1, source_target_pairs={{1,2},{2,1},{5,6},{6,5},{9,10},{10,9},{13,14},{14,13},{17,18},{18,... | collective-permute-start | bytes 958472 | tf_op jit(solution)/shard_map/ppermute | solution.py:634
  18.8 13.1 %collective-permute-start = (f32[624,128]{1,0:T(8,128)S(1)}, f32[624,128]{1,0:T(8,128)S(1)}, u32[]{:S(2)}, u32[]{:S(2)}) collective-permute-start(f32[624,128]{1,0:T(8,128)S(1)} %get-tuple-element.59), channel_id=1, source_target_pairs={{0,1},{2,3},{1,0},{3,2},{4,5},{6,7},{5,4},{7,6},{8,9},{10,11},{9,8... | collective-permute-start | bytes 958472 | tf_op jit(solution)/shard_map/ppermute | solution.py:634
  33.1 3.6 %collective-permute-start.3 = (f32[464,128]{1,0:T(8,128)S(1)}, f32[464,128]{1,0:T(8,128)S(1)}, u32[]{:S(2)}, u32[]{:S(2)}) collective-permute-start(f32[464,128]{1,0:T(8,128)S(1)} %get-tuple-element.62), channel_id=1, source_target_pairs={{4,8},{8,4},{5,9},{9,5},{6,10},{10,6},{7,11},{11,7},{20,24},{24,20... | collective-permute-start | bytes 712712 | tf_op jit(solution)/shard_map/ppermute | solution.py:634
  33.8 4.0 %collective-permute-start.2 = (f32[464,128]{1,0:T(8,128)S(1)}, f32[464,128]{1,0:T(8,128)S(1)}, u32[]{:S(2)}, u32[]{:S(2)}) collective-permute-start(f32[464,128]{1,0:T(8,128)S(1)} %get-tuple-element.63), channel_id=1, source_target_pairs={{0,4},{8,12},{4,0},{12,8},{1,5},{9,13},{5,1},{13,9},{2,6},{10,14},... | collective-permute-start | bytes 712712 | tf_op jit(solution)/shard_map/ppermute | solution.py:634
  39.7 4.4 %collective-permute-start.6 = (f32[16,128]{1,0:T(8,128)S(1)}, f32[16,128]{1,0:T(8,128)S(1)}, u32[]{:S(2)}, u32[]{:S(2)}) collective-permute-start(f32[16,128]{1,0:T(8,128)S(1)} %get-tuple-element.42), channel_id=1, source_target_pairs={{0,12},{4,8},{8,4},{12,0},{1,13},{5,9},{9,5},{13,1},{2,14},{6,10},... | collective-permute-start | bytes 24584 | tf_op jit(solution)/shard_map/ppermute | solution.py:645
  39.8 5.9 %collective-permute-start.5 = (f32[16,128]{1,0:T(8,128)S(1)}, f32[16,128]{1,0:T(8,128)S(1)}, u32[]{:S(2)}, u32[]{:S(2)}) collective-permute-start(f32[16,128]{1,0:T(8,128)S(1)} %get-tuple-element.42), channel_id=1, source_target_pairs={{0,8},{4,12},{8,0},{12,4},{1,9},{5,13},{9,1},{13,5},{2,10},{6,14},... | collective-permute-start | bytes 24584 | tf_op jit(solution)/shard_map/ppermute | solution.py:645
  44.0 1.6 %collective-permute-start.4 = (f32[16,128]{1,0:T(8,128)S(1)}, f32[16,128]{1,0:T(8,128)S(1)}, u32[]{:S(2)}, u32[]{:S(2)}) collective-permute-start(f32[16,128]{1,0:T(8,128)S(1)} %get-tuple-element.42), channel_id=1, source_target_pairs={{0,4},{4,0},{8,12},{12,8},{1,5},{5,1},{9,13},{13,9},{2,6},{6,2},{1... | collective-permute-start | bytes 24584 | tf_op jit(solution)/shard_map/ppermute | solution.py:645
  45.7 5.5 %collective-permute-start.9 = (f32[16,128]{1,0:T(8,128)S(1)}, f32[16,128]{1,0:T(8,128)S(1)}, u32[]{:S(2)}, u32[]{:S(2)}) collective-permute-start(f32[16,128]{1,0:T(8,128)S(1)} %add_add_fusion), channel_id=1, source_target_pairs={{0,3},{1,2},{2,1},{3,0},{4,7},{5,6},{6,5},{7,4},{8,11},{9,10},{10,... | collective-permute-start | bytes 24584 | tf_op jit(solution)/shard_map/ppermute | solution.py:645
  47.1 4.6 %collective-permute-start.8 = (f32[16,128]{1,0:T(8,128)S(1)}, f32[16,128]{1,0:T(8,128)S(1)}, u32[]{:S(2)}, u32[]{:S(2)}) collective-permute-start(f32[16,128]{1,0:T(8,128)S(1)} %add_add_fusion), channel_id=1, source_target_pairs={{0,2},{1,3},{2,0},{3,1},{4,6},{5,7},{6,4},{7,5},{8,10},{9,11},{10,... | collective-permute-start | bytes 24584 | tf_op jit(solution)/shard_map/ppermute | solution.py:645
  49.0 3.7 %collective-permute-start.7 = (f32[16,128]{1,0:T(8,128)S(1)}, f32[16,128]{1,0:T(8,128)S(1)}, u32[]{:S(2)}, u32[]{:S(2)}) collective-permute-start(f32[16,128]{1,0:T(8,128)S(1)} %add_add_fusion), channel_id=1, source_target_pairs={{0,1},{1,0},{2,3},{3,2},{4,5},{5,4},{6,7},{7,6},{8,9},{9,8},{10,11... | collective-permute-start | bytes 24584 | tf_op jit(solution)/shard_map/ppermute | solution.py:645

commit v8 on v7

--- a/solution.py
+++ b/solution.py
@@ -32,44 +32,97 @@
     return lax.broadcasted_iota(I32, shape, dim)
 
 
+class Lanes:
+    def __init__(self, lane_bits):
+        self.tiles = [None] * TILES
+        self.tile_bits = [7, 8, 9, 10, 11]
+        self.lane_bits = list(lane_bits)
+
+    def trade(self, slot, lane):
+        self.tile_bits[slot], self.lane_bits[lane] = self.lane_bits[lane], self.tile_bits[slot]
+        if self.tiles[0] is None:
+            return
+        stride, hop = 1 << lane, 1 << slot
+        low = iota((8, 128), 1) & stride == 0
+        for i in range(TILES):
+            if i & hop == 0:
+                a, b = self.tiles[i], self.tiles[i + hop]
+                self.tiles[i] = jnp.where(low, a, pltpu.roll(b, stride, 1))
+                self.tiles[i + hop] = jnp.where(low, pltpu.roll(a, 128 - stride, 1), b)
+
+    def bring(self, bit, out):
+        if bit not in self.tile_bits:
+            self.trade(self.tile_bits.index(out), self.lane_bits.index(bit))
+
+    def compare(self, bit):
+        if self.tiles[0] is None:
+            return
+        hop = 1 << self.tile_bits.index(bit)
+        for i in range(TILES):
+            if i & hop == 0:
+                a, b = self.tiles[i], self.tiles[i + hop]
+                self.tiles[i], self.tiles[i + hop] = jnp.minimum(a, b), jnp.maximum(a, b)
+
+    def turn(self, bit, mask):
+        if self.tiles[0] is None:
+            return
+        if bit in self.tile_bits:
+            hop = 1 << self.tile_bits.index(bit)
+            self.tiles = [t ^ mask if i & hop else t for i, t in enumerate(self.tiles)]
+        else:
+            here = iota((8, 128), 1) & (1 << self.lane_bits.index(bit)) != 0
+            self.tiles = [t ^ jnp.where(here, mask, 0) for t in self.tiles]
+
+    def sort_rows(self, mask):
+        for bit in range(5):
+            self.bring(bit, 7 + bit)
+        for phase in range(1, 8):
+            self.turn(phase, mask)
+            if phase == 6:
+                self.bring(5, 0)
+                self.compare(5)
+            if phase == 7:
+                self.bring(6, 0)
+                self.compare(6)
+                self.bring(5, 6)
+                self.compare(5)
+            for bit in reversed(range(min(phase, 5))):
+                self.bring(bit, 5)
+                self.compare(bit)
+            self.turn(phase, mask)
+        for bit in range(5):
+            self.bring(7 + bit, bit)
+
+    def merge_rows(self):
+        out = 7
+        for bit in reversed(range(7)):
+            self.bring(bit, out)
+            self.compare(bit)
+            out = bit
+        self.bring(7, 0)
+
+
+def first_layout():
+    dry = Lanes(range(7))
+    dry.sort_rows(0)
+    for _ in range(8):
+        dry.merge_rows()
+    return [dry.lane_bits.index(bit) for bit in range(7)]
+
+
 def sort_plan(tiles, lane_ref, sub_ref, swap_ref):
-    lanes, subs = iota((64, 128), 1), iota((8, 128), 0)
+    lanes, subs = iota((8, 128), 1), iota((8, 128), 0)
     top = 0x7FFF
 
-    def grouped(tiles):
-        return [jnp.concatenate(tiles[8 * i : 8 * i + 8], axis=0) for i in range(4)]
-
-    def partner(x, index, stride, axis):
-        if 2 * stride == (128, 8)[axis == 0]:
-            return pltpu.roll(x, stride, axis)
-        return take(x, index ^ stride, axis)
-
-    def ordered(low, a, b):
-        return jnp.where(low, jnp.minimum(a, b), jnp.maximum(a, b))
-
-    def lane_steps(groups, stride):
-        while stride:
-            low = lanes & stride == 0
-            other = [partner(g, lanes, stride, 1) for g in groups]
-            groups = [ordered(low, g, o) for g, o in zip(groups, other)]
-            stride //= 2
-        return groups
-
-    def record(run, groups):
-        for i, g in enumerate(groups):
-            lane_ref[run, 64 * i : 64 * i + 64] = g & 127
-        return [groups[i // 8][8 * (i % 8) : 8 * (i % 8) + 8] >> 7 for i in range(TILES)]
-
-    groups = [(g << 7) | lanes for g in grouped(tiles)]
-    for phase in range(1, 7):
-        turn = jnp.where(lanes & (1 << phase) != 0, top << 7, 0)
-        groups = [g ^ turn for g in groups]
-        groups = lane_steps(groups, 1 << (phase - 1))
-        groups = [g ^ turn for g in groups]
-    turn = jnp.where(iota((64, 128), 0) & 8 != 0, top << 7, 0)
-    groups = lane_steps([g ^ turn for g in groups], 64)
-    tiles = record(0, groups)
-    tiles = [t ^ top if i & 1 else t for i, t in enumerate(tiles)]
+    def record(run, tiles):
+        for i, t in enumerate(tiles):
+            lane_ref[run, 8 * i : 8 * i + 8] = t & 127
+        return [t >> 7 for t in tiles]
+
+    state = Lanes(first_layout())
+    state.tiles = [(t << 7) | lanes for t in tiles]
+    state.sort_rows(top << 7)
+    tiles = record(0, state.tiles)
 
     swap = 0
     for phase in range(8, 16):
@@ -85,8 +138,12 @@
             stride = 1 << (phase - 13)
             while stride:
                 low = subs & stride == 0
-                other = [partner(t, subs, stride, 0) for t in tiles]
-                tiles = [ordered(low, t, o) for t, o in zip(tiles, other)]
+                other = [
+                    pltpu.roll(t, 4, 0) if stride == 4 else take(t, subs ^ stride, 0) for t in tiles
+                ]
+                tiles = [
+                    jnp.where(low, jnp.minimum(t, o), jnp.maximum(t, o)) for t, o in zip(tiles, other)
+                ]
                 stride //= 2
             for i, t in enumerate(tiles):
                 sub_ref[phase - 13, 8 * i : 8 * i + 8] = t & 7
@@ -100,10 +157,9 @@
                     swap += 1
                     tiles[i], tiles[i + hop] = jnp.minimum(a, b), jnp.maximum(a, b)
             hop //= 2
-        groups = [(g << 7) | lanes for g in grouped(tiles)]
-        tiles = record(phase - 7, lane_steps(groups, 64))
-        tiles = [t ^ f for t, f in zip(tiles, turns)]
-    return tiles
+        state.tiles = [(t << 7) | lanes for t in tiles]
+        state.merge_rows()
+        tiles = [t ^ f for t, f in zip(record(phase - 7, state.tiles), turns)]
 
 
 def follow_plan(stages, lane_ref, sub_ref, swap_ref, sources=None):

time: 57.4 us -> 57.2 us (level)
  no operation moved by 1% of the time
where the time goes in v8:
time: 57.2 us; the launch traced here: 57 us
  Pallas kernels  29.8 us (52%)
  starting transfers between devices  19.2 us (34%)
  waiting for transfers between devices  6.11 us (11%)
  local copies, waits for them, and re-layouts  0.91 us (2%)
  between operations  0.76 us (1%)
    pallas_call x7, Pallas kernels, kernel_call(): pl.pallas_call(body, out_shape=outs, **{} if in_specs is None else dict(i...  29.8 us
    ppermute x4, starting transfers between devices, neighbours(): arrived.append(lax.ppermute(slab, axis, pairs + [(b, a) for a, b in pairs]))  10.3 us
    ppermute x6, starting transfers between devices, summed(): parts.append(lax.ppermute(sums, axis, swaps))  8.84 us
    ppermute x6, waiting for transfers between devices, summed(): parts.append(lax.ppermute(sums, axis, swaps))  4.07 us
    ppermute x4, waiting for transfers between devices, neighbours(): arrived.append(lax.ppermute(slab, axis, pairs + [(b, a) for a, b in pairs]))  2.04 us
  transfers between devices with their start and end apart: 10, of which 6 were waited for; matrix products, arithmetic and copies ran while one was open for 0% of the time, Pallas kernels for 11%

profile of v8, /device:TPU:0, one launch (start us, length us, event | category | flops | bytes accessed | tf_op | source)
XLA Modules:
  0.0 57.0 jit_solution(126637107430119375)
XLA Ops:
  0.6 0.0 copy-start.3
  0.7 0.9 %copy-done.3 = s32[1,32768]{1,0:T(1,128)S(1)} copy-done((s32[1,32768]{1,0:T(1,128)S(1)}, s32[1,32768]{1,0:T(1,128)}, u32[]{:S(2)}) %copy-start.3) | copy-done | bytes 131096
  1.5 0.0 copy-start
  1.6 0.0 copy-start.2
  1.6 6.3 %cell_plan.1 = (s32[9,256,128]{2,1,0:T(8,128)S(1)}, s32[3,256,128]{2,1,0:T(8,128)S(1)}, s32[3840,128]{1,0:T(8,128)S(1)}) custom-call(s32[256,128]{1,0:T(8,128)S(1)} %bitcast.12), custom_call_target="tpu_custom_call" | custom-call | flops 7000000000 | bytes 3670016 | tf_op jit(solution)/shard_map/cell_plan/pallas_call | solution.py:430
  7.8 0.0 copy-done
  7.8 0.0 copy-done.2
  7.8 0.0 copy-start.1
  7.8 9.1 %to_cells.1 = (f32[12,32,8,128]{3,2,1,0:T(8,128)S(1)}, s32[1,32,8,128]{3,2,1,0:T(8,128)S(1)}) custom-call(s32[32,8,128]{2,1,0:T(8,128)S(1)} %bitcast.11, f32[12,32,8,128]{3,2,1,0:T(8,128)S(1)} %bitcast.9, s32[9,256,128]{2,1,0:T(8,128)S(1)} %get-tuple-element.27.lane_ref, s32[3,256,128]{2,1,0:T(8,128)S(1)} %get-tuple-element.28.sub_ref, ...), custom_call_target="tpu_custom_call" | custom-call | flops 10000000 | bytes 6946816 | tf_op jit(solution)/shard_map/to_cells/pallas_call | solution.py:430
  16.9 0.0 copy-done.1
  16.9 0.7 %deposit.1 = (f32[4,17,2,8,128]{4,3,2,1,0:T(8,128)S(1)}, f32[4,17,2,8,128]{4,3,2,1,0:T(8,128)S(1)}, f32[592,128]{1,0:T(8,128)S(1)}, f32[624,128]{1,0:T(8,128)S(1)}) custom-call(f32[12,32,8,128]{3,2,1,0:T(8,128)S(1)} %get-tuple-element.30.cells_ref, s32[1,32,8,128]{3,2,1,0:T(8,128)S(1)} %get-tuple-element.31.tag_ref, s32[16,8,256]{2,1,0:T(8,128)S(1)} %copy-done.1), custom_call_target="tpu_custom_call" | custom-call | bytes 3571712 | tf_op jit(solution)/shard_map/deposit/pallas_call | solution.py:430
  17.7 0.9 %collective-permute-start.1 = (f32[624,128]{1,0:T(8,128)S(1)}, f32[624,128]{1,0:T(8,128)S(1)}, u32[]{:S(2)}, u32[]{:S(2)}) collective-permute-start(f32[624,128]{1,0:T(8,128)S(1)} %get-tuple-element.58), channel_id=1, source_target_pairs={{1,2},{2,1},{5,6},{6,5},{9,10},{10,9},{13,14},{14,13},{17,18},{18,... | collective-permute-start | bytes 958472 | tf_op jit(solution)/shard_map/ppermute | solution.py:690
  18.6 5.9 %collective-permute-start = (f32[624,128]{1,0:T(8,128)S(1)}, f32[624,128]{1,0:T(8,128)S(1)}, u32[]{:S(2)}, u32[]{:S(2)}) collective-permute-start(f32[624,128]{1,0:T(8,128)S(1)} %get-tuple-element.59), channel_id=1, source_target_pairs={{0,1},{2,3},{1,0},{3,2},{4,5},{6,7},{5,4},{7,6},{8,9},{10,11},{9,8... | collective-permute-start | bytes 958472 | tf_op jit(solution)/shard_map/ppermute | solution.py:690
  24.5 6.3 %particle_plan.1 = (s32[9,256,128]{2,1,0:T(8,128)S(1)}, s32[3,256,128]{2,1,0:T(8,128)S(1)}, s32[3840,128]{1,0:T(8,128)S(1)}) custom-call(s32[256,128]{1,0:T(8,128)S(1)} %bitcast.10), custom_call_target="tpu_custom_call" | custom-call | flops 10000000 | bytes 3670016 | tf_op jit(solution)/shard_map/particle_plan/pallas_call | solution.py:430
  30.7 0.1 add_convert_fusion.keep_ref
  30.8 0.0 collective-permute-done.1
  30.8 0.9 %collective-permute-done = f32[624,128]{1,0:T(8,128)S(1)} collective-permute-done((f32[624,128]{1,0:T(8,128)S(1)}, f32[624,128]{1,0:T(8,128)S(1)}, u32[]{:S(2)}, u32[]{:S(2)}) %collective-permute-start) | collective-permute-done | bytes 319520 | tf_op jit(solution)/shard_map/ppermute | solution.py:690
  31.8 1.1 %widen.1 = (f32[3,16,2,24,128]{4,3,2,1,0:T(8,128)S(1)}, f32[4,2,2,24,128]{4,3,2,1,0:T(8,128)S(1)}, f32[16,2,24,128]{3,2,1,0:T(8,128)S(1)}, f32[440,128]{1,0:T(8,128)S(1)}, f32[464,128]{1,0:T(8,128)S(1)}) custom-call(f32[2]{0:T(128)S(1)} %add_convert_fusion.keep_ref, f32[4,17,2,8,128]{4,3,2,1,0:T(8,128)S(1)} %get-tuple-element.32.grid_ref, ...), custom_call_target="tpu_custom_call" | custom-call | bytes 6180864 | tf_op jit(solution)/shard_map/widen/pallas_call | solution.py:430
  32.9 0.7 %collective-permute-start.3 = (f32[464,128]{1,0:T(8,128)S(1)}, f32[464,128]{1,0:T(8,128)S(1)}, u32[]{:S(2)}, u32[]{:S(2)}) collective-permute-start(f32[464,128]{1,0:T(8,128)S(1)} %get-tuple-element.62), channel_id=1, source_target_pairs={{4,8},{8,4},{5,9},{9,5},{6,10},{10,6},{7,11},{11,7},{20,24},{24,20... | collective-permute-start | bytes 712712 | tf_op jit(solution)/shard_map/ppermute | solution.py:690
  33.6 2.9 %collective-permute-start.2 = (f32[464,128]{1,0:T(8,128)S(1)}, f32[464,128]{1,0:T(8,128)S(1)}, u32[]{:S(2)}, u32[]{:S(2)}) collective-permute-start(f32[464,128]{1,0:T(8,128)S(1)} %get-tuple-element.63), channel_id=1, source_target_pairs={{0,4},{8,12},{4,0},{12,8},{1,5},{9,13},{5,1},{13,9},{2,6},{10,14},... | collective-permute-start | bytes 712712 | tf_op jit(solution)/shard_map/ppermute | solution.py:690
  36.5 0.0 collective-permute-done.3
  36.5 1.1 %collective-permute-done.2 = f32[464,128]{1,0:T(8,128)S(1)} collective-permute-done((f32[464,128]{1,0:T(8,128)S(1)}, f32[464,128]{1,0:T(8,128)S(1)}, u32[]{:S(2)}, u32[]{:S(2)}) %collective-permute-start.2) | collective-permute-done | bytes 237600 | tf_op jit(solution)/shard_map/ppermute | solution.py:690
  37.6 1.8 %krylov.1 = (f32[3,25,2,24,128]{4,3,2,1,0:T(8,128)S(1)}, f32[25,2,24,128]{3,2,1,0:T(8,128)S(1)}, f32[25,2,24,128]{3,2,1,0:T(8,128)S(1)}, f32[25,2,24,128]{3,2,1,...) custom-call(f32[2]{0:T(128)S(1)} %add_convert_fusion.keep_ref, ...), custom_call_target="tpu_custom_call" | custom-call | bytes 6750208 | tf_op jit(solution)/shard_map/krylov/pallas_call | solution.py:430
  39.5 0.1 collective-permute-start.6
  39.6 4.3 %collective-permute-start.5 = (f32[16,128]{1,0:T(8,128)S(1)}, f32[16,128]{1,0:T(8,128)S(1)}, u32[]{:S(2)}, u32[]{:S(2)}) collective-permute-start(f32[16,128]{1,0:T(8,128)S(1)} %get-tuple-element.42), channel_id=1, source_target_pairs={{0,8},{4,12},{8,0},{12,4},{1,9},{5,13},{9,1},{13,5},{2,10},{6,14},... | collective-permute-start | bytes 24584 | tf_op jit(solution)/shard_map/ppermute | solution.py:701
  43.8 0.0 collective-permute-start.4
  43.9 0.0 collective-permute-done.6
  43.9 1.6 %collective-permute-done.5 = f32[16,128]{1,0:T(8,128)S(1)} collective-permute-done((f32[16,128]{1,0:T(8,128)S(1)}, f32[16,128]{1,0:T(8,128)S(1)}, u32[]{:S(2)}, u32[]{:S(2)}) %collective-permute-start.5) | collective-permute-done | bytes 8224 | tf_op jit(solution)/shard_map/ppermute | solution.py:701
  45.5 0.0 collective-permute-done.4
  45.5 1.4 %collective-permute-start.9 = (f32[16,128]{1,0:T(8,128)S(1)}, f32[16,128]{1,0:T(8,128)S(1)}, u32[]{:S(2)}, u32[]{:S(2)}) collective-permute-start(f32[16,128]{1,0:T(8,128)S(1)} %add_add_fusion), channel_id=1, source_target_pairs={{0,3},{1,2},{2,1},{3,0},{4,7},{5,6},{6,5},{7,4},{8,11},{9,10},{10,... | collective-permute-start | bytes 24584 | tf_op jit(solution)/shard_map/ppermute | solution.py:701
  46.9 1.9 %collective-permute-start.8 = (f32[16,128]{1,0:T(8,128)S(1)}, f32[16,128]{1,0:T(8,128)S(1)}, u32[]{:S(2)}, u32[]{:S(2)}) collective-permute-start(f32[16,128]{1,0:T(8,128)S(1)} %add_add_fusion), channel_id=1, source_target_pairs={{0,2},{1,3},{2,0},{3,1},{4,6},{5,7},{6,4},{7,5},{8,10},{9,11},{10,... | collective-permute-start | bytes 24584 | tf_op jit(solution)/shard_map/ppermute | solution.py:701
  48.8 1.2 %collective-permute-start.7 = (f32[16,128]{1,0:T(8,128)S(1)}, f32[16,128]{1,0:T(8,128)S(1)}, u32[]{:S(2)}, u32[]{:S(2)}) collective-permute-start(f32[16,128]{1,0:T(8,128)S(1)} %add_add_fusion), channel_id=1, source_target_pairs={{0,1},{1,0},{2,3},{3,2},{4,5},{5,4},{6,7},{7,6},{8,9},{9,8},{10,11... | collective-permute-start | bytes 24584 | tf_op jit(solution)/shard_map/ppermute | solution.py:701
  49.9 1.1 %collective-permute-done.9 = f32[16,128]{1,0:T(8,128)S(1)} collective-permute-done((f32[16,128]{1,0:T(8,128)S(1)}, f32[16,128]{1,0:T(8,128)S(1)}, u32[]{:S(2)}, u32[]{:S(2)}) %collective-permute-start.9) | collective-permute-done | bytes 8224 | tf_op jit(solution)/shard_map/ppermute | solution.py:701
  51.0 0.4 collective-permute-done.8
  51.5 0.9 %collective-permute-done.7 = f32[16,128]{1,0:T(8,128)S(1)} collective-permute-done((f32[16,128]{1,0:T(8,128)S(1)}, f32[16,128]{1,0:T(8,128)S(1)}, u32[]{:S(2)}, u32[]{:S(2)}) %collective-permute-start.7) | collective-permute-done | bytes 8224 | tf_op jit(solution)/shard_map/ppermute | solution.py:701
  52.4 4.6 %project.1 = (f32[16,8,256]{2,1,0:T(8,128)}, f32[3,32,8,128]{3,2,1,0:T(8,128)}) custom-call(f32[1,16,128]{2,1,0:T(8,128)S(1)} %add_bitcast_fusion.sums_ref, f32[3,25,2,24,128]{4,3,2,1,0:T(8,128)S(1)} %get-tuple-element.43.vel_ref, f32[25,2,24,128]{3,2,1,0:T(8,128)S(1)} %get-tuple-element.44.fluid_ref, f32[25,2,24,128]{3,2,1,0:T(8,128)S(1)} %get-tuple-element.45.k0_ref, ...), custom_call_target="tpu_custom_call" | custom-call | bytes 10788864 | tf_op jit(solution)/shard_map/project/pallas_call | solution.py:430
  (6 shorter events, 0.2 us)
Async XLA Ops:
  0.6 0.9 %copy-start.3 = (s32[1,32768]{1,0:T(1,128)S(1)}, s32[1,32768]{1,0:T(1,128)}, u32[]{:S(2)}) copy-start(s32[1,32768]{1,0:T(1,128)} %param.4) | copy-start | bytes 393220
  1.5 6.3 %copy-start = (f32[1,12,32768]{2,0,1:T(1,128)S(1)}, f32[1,12,32768]{2,0,1:T(1,128)}, u32[]{:S(2)}) copy-start(f32[1,12,32768]{2,0,1:T(1,128)} %param.6) | copy-start | bytes 4718596
  1.6 6.3 %copy-start.2 = (s32[1,32768]{1,0:T(1,128)S(1)}, s32[1,32768]{1,0:T(1,128)}, u32[]{:S(2)}) copy-start(s32[1,32768]{1,0:T(1,128)} %param.5) | copy-start | bytes 393220
  7.8 9.1 %copy-start.1 = (s32[16,8,256]{2,1,0:T(8,128)S(1)}, s32[16,8,256]{2,1,0:T(8,128)}, u32[]{:S(2)}) copy-start(s32[16,8,256]{2,1,0:T(8,128)} %flag_ref.3) | copy-start | bytes 393220
  17.7 13.1 %collective-permute-start.1 = (f32[624,128]{1,0:T(8,128)S(1)}, f32[624,128]{1,0:T(8,128)S(1)}, u32[]{:S(2)}, u32[]{:S(2)}) collective-permute-start(f32[624,128]{1,0:T(8,128)S(1)} %get-tuple-element.58), channel_id=1, source_target_pairs={{1,2},{2,1},{5,6},{6,5},{9,10},{10,9},{13,14},{14,13},{17,18},{18,... | collective-permute-start | bytes 958472 | tf_op jit(solution)/shard_map/ppermute | solution.py:690
  18.6 13.1 %collective-permute-start = (f32[624,128]{1,0:T(8,128)S(1)}, f32[624,128]{1,0:T(8,128)S(1)}, u32[]{:S(2)}, u32[]{:S(2)}) collective-permute-start(f32[624,128]{1,0:T(8,128)S(1)} %get-tuple-element.59), channel_id=1, source_target_pairs={{0,1},{2,3},{1,0},{3,2},{4,5},{6,7},{5,4},{7,6},{8,9},{10,11},{9,8... | collective-permute-start | bytes 958472 | tf_op jit(solution)/shard_map/ppermute | solution.py:690
  32.9 3.6 %collective-permute-start.3 = (f32[464,128]{1,0:T(8,128)S(1)}, f32[464,128]{1,0:T(8,128)S(1)}, u32[]{:S(2)}, u32[]{:S(2)}) collective-permute-start(f32[464,128]{1,0:T(8,128)S(1)} %get-tuple-element.62), channel_id=1, source_target_pairs={{4,8},{8,4},{5,9},{9,5},{6,10},{10,6},{7,11},{11,7},{20,24},{24,20... | collective-permute-start | bytes 712712 | tf_op jit(solution)/shard_map/ppermute | solution.py:690
  33.6 4.0 %collective-permute-start.2 = (f32[464,128]{1,0:T(8,128)S(1)}, f32[464,128]{1,0:T(8,128)S(1)}, u32[]{:S(2)}, u32[]{:S(2)}) collective-permute-start(f32[464,128]{1,0:T(8,128)S(1)} %get-tuple-element.63), channel_id=1, source_target_pairs={{0,4},{8,12},{4,0},{12,8},{1,5},{9,13},{5,1},{13,9},{2,6},{10,14},... | collective-permute-start | bytes 712712 | tf_op jit(solution)/shard_map/ppermute | solution.py:690
  39.5 4.4 %collective-permute-start.6 = (f32[16,128]{1,0:T(8,128)S(1)}, f32[16,128]{1,0:T(8,128)S(1)}, u32[]{:S(2)}, u32[]{:S(2)}) collective-permute-start(f32[16,128]{1,0:T(8,128)S(1)} %get-tuple-element.42), channel_id=1, source_target_pairs={{0,12},{4,8},{8,4},{12,0},{1,13},{5,9},{9,5},{13,1},{2,14},{6,10},... | collective-permute-start | bytes 24584 | tf_op jit(solution)/shard_map/ppermute | solution.py:701
  39.6 5.9 %collective-permute-start.5 = (f32[16,128]{1,0:T(8,128)S(1)}, f32[16,128]{1,0:T(8,128)S(1)}, u32[]{:S(2)}, u32[]{:S(2)}) collective-permute-start(f32[16,128]{1,0:T(8,128)S(1)} %get-tuple-element.42), channel_id=1, source_target_pairs={{0,8},{4,12},{8,0},{12,4},{1,9},{5,13},{9,1},{13,5},{2,10},{6,14},... | collective-permute-start | bytes 24584 | tf_op jit(solution)/shard_map/ppermute | solution.py:701
  43.8 1.6 %collective-permute-start.4 = (f32[16,128]{1,0:T(8,128)S(1)}, f32[16,128]{1,0:T(8,128)S(1)}, u32[]{:S(2)}, u32[]{:S(2)}) collective-permute-start(f32[16,128]{1,0:T(8,128)S(1)} %get-tuple-element.42), channel_id=1, source_target_pairs={{0,4},{4,0},{8,12},{12,8},{1,5},{5,1},{9,13},{13,9},{2,6},{6,2},{1... | collective-permute-start | bytes 24584 | tf_op jit(solution)/shard_map/ppermute | solution.py:701
  45.5 5.5 %collective-permute-start.9 = (f32[16,128]{1,0:T(8,128)S(1)}, f32[16,128]{1,0:T(8,128)S(1)}, u32[]{:S(2)}, u32[]{:S(2)}) collective-permute-start(f32[16,128]{1,0:T(8,128)S(1)} %add_add_fusion), channel_id=1, source_target_pairs={{0,3},{1,2},{2,1},{3,0},{4,7},{5,6},{6,5},{7,4},{8,11},{9,10},{10,... | collective-permute-start | bytes 24584 | tf_op jit(solution)/shard_map/ppermute | solution.py:701
  46.9 4.6 %collective-permute-start.8 = (f32[16,128]{1,0:T(8,128)S(1)}, f32[16,128]{1,0:T(8,128)S(1)}, u32[]{:S(2)}, u32[]{:S(2)}) collective-permute-start(f32[16,128]{1,0:T(8,128)S(1)} %add_add_fusion), channel_id=1, source_target_pairs={{0,2},{1,3},{2,0},{3,1},{4,6},{5,7},{6,4},{7,5},{8,10},{9,11},{10,... | collective-permute-start | bytes 24584 | tf_op jit(solution)/shard_map/ppermute | solution.py:701
  48.8 3.7 %collective-permute-start.7 = (f32[16,128]{1,0:T(8,128)S(1)}, f32[16,128]{1,0:T(8,128)S(1)}, u32[]{:S(2)}, u32[]{:S(2)}) collective-permute-start(f32[16,128]{1,0:T(8,128)S(1)} %add_add_fusion), channel_id=1, source_target_pairs={{0,1},{1,0},{2,3},{3,2},{4,5},{5,4},{6,7},{7,6},{8,9},{9,8},{10,11... | collective-permute-start | bytes 24584 | tf_op jit(solution)/shard_map/ppermute | solution.py:701

commit v9 on v8

--- a/solution.py
+++ b/solution.py
@@ -12,6 +12,7 @@
 CX, CY, CELLS = 16, 8, 32768
 TILES = CELLS // 1024
 LANE_RUNS, SUB_RUNS, SWAPS = 9, 3, 30 * 16
+GROUP = 2
 
 
 def take(x, index, axis):
@@ -93,13 +94,15 @@
         for bit in range(5):
             self.bring(7 + bit, bit)
 
-    def merge_rows(self):
+    def merge_rows(self, tick=lambda: None):
         out = 7
         for bit in reversed(range(7)):
             self.bring(bit, out)
             self.compare(bit)
             out = bit
+            tick()
         self.bring(7, 0)
+        tick()
 
 
 def first_layout():
@@ -110,22 +113,32 @@
     return [dry.lane_bits.index(bit) for bit in range(7)]
 
 
+def record_run(run, tiles, lane_ref):
+    for i, t in enumerate(tiles):
+        lane_ref[run, 8 * i : 8 * i + 8] = t & 127
+    return [t >> 7 for t in tiles]
+
+
+def plan_rows(tiles, lane_ref):
+    state = Lanes(first_layout())
+    state.tiles = [(t << 7) | iota((8, 128), 1) for t in tiles]
+    state.sort_rows(0x7FFF << 7)
+    return record_run(0, state.tiles, lane_ref)
+
+
 def sort_plan(tiles, lane_ref, sub_ref, swap_ref):
+    plan_rest(plan_rows(tiles, lane_ref), lane_ref, sub_ref, swap_ref)
+
+
+def plan_rest(tiles, lane_ref, sub_ref, swap_ref, begin=lambda phase: None, tick=lambda: None):
     lanes, subs = iota((8, 128), 1), iota((8, 128), 0)
     top = 0x7FFF
 
-    def record(run, tiles):
-        for i, t in enumerate(tiles):
-            lane_ref[run, 8 * i : 8 * i + 8] = t & 127
-        return [t >> 7 for t in tiles]
-
     state = Lanes(first_layout())
-    state.tiles = [(t << 7) | lanes for t in tiles]
-    state.sort_rows(top << 7)
-    tiles = record(0, state.tiles)
-
+    state.sort_rows(0)
     swap = 0
     for phase in range(8, 16):
+        begin(phase)
         if phase < 12:
             turns = [top if i >> (phase - 7) & 1 else 0 for i in range(TILES)]
         elif phase < 15:
@@ -158,8 +171,8 @@
                     tiles[i], tiles[i + hop] = jnp.minimum(a, b), jnp.maximum(a, b)
             hop //= 2
         state.tiles = [(t << 7) | lanes for t in tiles]
-        state.merge_rows()
-        tiles = [t ^ f for t, f in zip(record(phase - 7, state.tiles), turns)]
+        state.merge_rows(tick)
+        tiles = [t ^ f for t, f in zip(record_run(phase - 7, state.tiles, lane_ref), turns)]
 
 
 def follow_plan(stages, lane_ref, sub_ref, swap_ref, sources=None):
@@ -225,6 +238,69 @@
 
         pass_over(sets, across)
         pass_over(eights, within)
+
+
+def crossings(phase):
+    before, numbers = 0, {}
+    for p in range(8, phase + 1):
+        for k in reversed(range(min(p, 12) - 7)):
+            for i in range(TILES):
+                if i & (1 << k) == 0:
+                    if p == phase:
+                        numbers[1 << k, i] = before
+                    before += 1
+    return numbers
+
+
+def move_items(phase, stages, sources, lane_ref, sub_ref, swap_ref):
+    numbers = crossings(phase)
+
+    def item(members, sources, steps):
+        def work():
+            moved = [{i: ref[c, i] for i in members} for ref, c in sources]
+            for step in steps:
+                step(members, moved)
+            for (ref, c), tiles in zip(stages, moved):
+                for i, t in tiles.items():
+                    ref[c, i] = t
+
+        return work
+
+    def gathered(ref, run, axis):
+        def step(members, moved):
+            for i in members:
+                index = ref[run, 8 * i : 8 * i + 8]
+                for tiles in moved:
+                    tiles[i] = take(tiles[i], index, axis)
+
+        return step
+
+    def exchanged(*hops):
+        def step(members, moved):
+            for hop in hops:
+                for i in members:
+                    if i & hop == 0:
+                        at = 8 * numbers[hop, i]
+                        crossed = swap_ref[at : at + 8] != 0
+                        for tiles in moved:
+                            a, b = tiles[i], tiles[i + hop]
+                            tiles[i], tiles[i + hop] = jnp.where(crossed, b, a), jnp.where(crossed, a, b)
+
+        return step
+
+    items = []
+    if phase > 10:
+        spread = 32 if phase > 11 else 16
+        steps = [gathered(sub_ref, phase - 13, 0)] if phase > 12 else []
+        steps.append(exchanged(16, 8) if phase > 11 else exchanged(8))
+        for low in range(0, 32, spread):
+            items += [item(range(low + k, low + spread, 8), stages, steps) for k in range(8)]
+    steps = [gathered(lane_ref, 0, 1)] if phase == 8 else []
+    steps.append(exchanged(*[4, 2, 1][max(0, 10 - phase) :]))
+    steps.append(gathered(lane_ref, phase - 7, 1))
+    return items + [
+        item(range(8 * g, 8 * g + 8), sources if phase == 8 else stages, steps) for g in range(4)
+    ]
 
 
 def plan_shapes():
@@ -321,34 +397,54 @@
     return kernel_call(particle_plan_kernel, "particle_plan", outs, [], (tag,), flops=10**7)
 
 
-def cell_plan_kernel(cell_ref, lane_ref, sub_ref, swap_ref):
+def cell_rows_kernel(cell_ref, key_ref, lane_ref):
     k = cell_ref[...]
     key = ((k & 0x700) << 4) | ((k & 0x7800) >> 3) | (k & 0xFF)
-    sort_plan(split_tiles(key), lane_ref, sub_ref, swap_ref)
-
-
-def cell_plan(cell):
-    outs = [of(shape, I32) for shape in plan_shapes()]
-    return kernel_call(cell_plan_kernel, "cell_plan", outs, [], (cell,), flops=7 * 10**9)
-
-
-def to_cells_kernel(code_ref, state_ref, lane_ref, sub_ref, swap_ref, cells_ref, tag_ref):
+    for i, t in enumerate(plan_rows(split_tiles(key), lane_ref)):
+        key_ref[8 * i : 8 * i + 8] = t
+
+
+def cell_rows(cell):
+    outs = [of((256, 128), I32), of((1, 256, 128), I32)]
+    return kernel_call(cell_rows_kernel, "cell_rows", outs, [], (cell,), flops=3 * 10**9)
+
+
+def to_cells_kernel(code_ref, state_ref, key_ref, rows_ref, cells_ref, tag_ref, lane_ref, sub_ref, swap_ref):
     shape = (TILES, 8, 128)
     tag_ref[0] = (code_ref[...] << 15) | (iota(shape, 0) * 8 + iota(shape, 1)) * 128 + iota(shape, 2)
-    for quad in range(3):
-        channels = range(4 * quad, 4 * quad + 4)
-        stages = [(cells_ref, c) for c in channels] + [(tag_ref, 0)] * (quad == 0)
-        sources = [(state_ref, c) for c in channels] + [(tag_ref, 0)] * (quad == 0)
-        follow_plan(stages, lane_ref, sub_ref, swap_ref, sources)
-
-
-def to_cells(code, state, plan):
+    lane_ref[0] = rows_ref[0]
+    stages = [(tag_ref, 0)] + [(cells_ref, c) for c in range(12)]
+    sources = [(tag_ref, 0)] + [(state_ref, c) for c in range(12)]
+    waiting, pace = [], [0]
+
+    def begin(phase):
+        while waiting:
+            waiting.pop(0)()
+        if phase > 8:
+            for low in range(0, 13, GROUP):
+                chosen = slice(low, low + GROUP)
+                waiting.extend(
+                    move_items(phase - 1, stages[chosen], sources[chosen], lane_ref, sub_ref, swap_ref)
+                )
+        pace[0] = -(-len(waiting) // 8)
+
+    def tick():
+        for _ in range(min(pace[0], len(waiting))):
+            waiting.pop(0)()
+
+    plan_rest(split_tiles(key_ref[...]), lane_ref, sub_ref, swap_ref, begin, tick)
+    begin(16)
+    while waiting:
+        waiting.pop(0)()
+
+
+def to_cells(code, state, key, rows):
     return kernel_call(
         to_cells_kernel,
         "to_cells",
         (of((12, TILES, 8, 128)), of((1, TILES, 8, 128), I32)),
-        [],
-        (code.reshape(TILES, 8, 128), state.reshape(12, TILES, 8, 128), *plan),
+        plan_scratch(),
+        (code.reshape(TILES, 8, 128), state.reshape(12, TILES, 8, 128), key, rows),
         flops=10**7,
     )
 
@@ -705,7 +801,7 @@
 def local(cell_index, offset_code, particle_state, fluid_flags):
     places = [(axis, lax.axis_index(axis), lax.axis_size(axis)) for axis in ("gx", "gy")]
     keep = jnp.stack([(at + 1 < size).astype(F32) for _, at, size in places])
-    cells, tag = to_cells(offset_code, particle_state, cell_plan(cell_index.reshape(256, 128)))
+    cells, tag = to_cells(offset_code, particle_state, *cell_rows(cell_index.reshape(256, 128)))
     grid, rim, up, down = deposit(cells, tag, fluid_flags)
     low, high = neighbours(up, down, "gy")
     plan = particle_plan(tag.reshape(256, 128))

time: 57.2 us -> 56.9 us (level)
  no operation moved by 1% of the time
where the time goes in v9:
time: 56.9 us; the launch traced here: 56.7 us
  Pallas kernels  29.4 us (52%)
  starting transfers between devices  19.2 us (34%)
  waiting for transfers between devices  6.11 us (11%)
  local copies, waits for them, and re-layouts  0.98 us (2%)
  between operations  0.74 us (1%)
    pallas_call x7, Pallas kernels, kernel_call(): pl.pallas_call(body, out_shape=outs, **{} if in_specs is None else dict(i...  29.4 us
    ppermute x4, starting transfers between devices, neighbours(): arrived.append(lax.ppermute(slab, axis, pairs + [(b, a) for a, b in pairs]))  10.3 us
    ppermute x6, starting transfers between devices, summed(): parts.append(lax.ppermute(sums, axis, swaps))  8.84 us
    ppermute x6, waiting for transfers between devices, summed(): parts.append(lax.ppermute(sums, axis, swaps))  4.07 us
    ppermute x4, waiting for transfers between devices, neighbours(): arrived.append(lax.ppermute(slab, axis, pairs + [(b, a) for a, b in pairs]))  2.04 us
  transfers between devices with their start and end apart: 10, of which 6 were waited for; matrix products, arithmetic and copies ran while one was open for 0% of the time, Pallas kernels for 11%

profile of v9, /device:TPU:0, one launch (start us, length us, event | category | flops | bytes accessed | tf_op | source)
XLA Modules:
  0.0 56.7 jit_solution(3328998760181338318)
XLA Ops:
  0.6 0.0 copy-start.3
  0.7 0.9 %copy-done.3 = s32[1,32768]{1,0:T(1,128)S(1)} copy-done((s32[1,32768]{1,0:T(1,128)S(1)}, s32[1,32768]{1,0:T(1,128)}, u32[]{:S(2)}) %copy-start.3) | copy-done | bytes 131096
  1.5 0.0 copy-start
  1.6 0.0 copy-start.2
  1.6 1.3 %cell_rows.1 = (s32[256,128]{1,0:T(8,128)S(1)}, s32[1,256,128]{2,1,0:T(8,128)S(1)}) custom-call(s32[256,128]{1,0:T(8,128)S(1)} %bitcast.12), custom_call_target="tpu_custom_call" | custom-call | flops 3000000000 | bytes 393216 | tf_op jit(solution)/shard_map/cell_rows/pallas_call | solution.py:526
  2.9 0.0 copy-start.1
  2.9 0.1 copy-done
  3.0 0.0 copy-done.2
  3.0 13.6 %to_cells.1 = (f32[12,32,8,128]{3,2,1,0:T(8,128)S(1)}, s32[1,32,8,128]{3,2,1,0:T(8,128)S(1)}) custom-call(s32[32,8,128]{2,1,0:T(8,128)S(1)} %bitcast.11, f32[12,32,8,128]{3,2,1,0:T(8,128)S(1)} %bitcast.9, s32[256,128]{1,0:T(8,128)S(1)} %get-tuple-element.26.key_ref, s32[1,256,128]{2,1,0:T(8,128)S(1)} %get-tuple-element.27.rows_ref), custom_call_target="tpu_custom_call" | custom-call | flops 10000000 | bytes 7208960 | tf_op jit(solution)/shard_map/to_cells/pallas_call | solution.py:526
  16.6 0.0 copy-done.1
  16.6 0.7 %deposit.1 = (f32[4,17,2,8,128]{4,3,2,1,0:T(8,128)S(1)}, f32[4,17,2,8,128]{4,3,2,1,0:T(8,128)S(1)}, f32[592,128]{1,0:T(8,128)S(1)}, f32[624,128]{1,0:T(8,128)S(1)}) custom-call(f32[12,32,8,128]{3,2,1,0:T(8,128)S(1)} %get-tuple-element.28.cells_ref, s32[1,32,8,128]{3,2,1,0:T(8,128)S(1)} %get-tuple-element.29.tag_ref, s32[16,8,256]{2,1,0:T(8,128)S(1)} %copy-done.1), custom_call_target="tpu_custom_call" | custom-call | bytes 3571712 | tf_op jit(solution)/shard_map/deposit/pallas_call | solution.py:526
  17.4 0.9 %collective-permute-start.1 = (f32[624,128]{1,0:T(8,128)S(1)}, f32[624,128]{1,0:T(8,128)S(1)}, u32[]{:S(2)}, u32[]{:S(2)}) collective-permute-start(f32[624,128]{1,0:T(8,128)S(1)} %get-tuple-element.56), channel_id=1, source_target_pairs={{1,2},{2,1},{5,6},{6,5},{9,10},{10,9},{13,14},{14,13},{17,18},{18,... | collective-permute-start | bytes 958472 | tf_op jit(solution)/shard_map/ppermute | solution.py:786
  18.3 5.9 %collective-permute-start = (f32[624,128]{1,0:T(8,128)S(1)}, f32[624,128]{1,0:T(8,128)S(1)}, u32[]{:S(2)}, u32[]{:S(2)}) collective-permute-start(f32[624,128]{1,0:T(8,128)S(1)} %get-tuple-element.57), channel_id=1, source_target_pairs={{0,1},{2,3},{1,0},{3,2},{4,5},{6,7},{5,4},{7,6},{8,9},{10,11},{9,8... | collective-permute-start | bytes 958472 | tf_op jit(solution)/shard_map/ppermute | solution.py:786
  24.1 6.3 %particle_plan.1 = (s32[9,256,128]{2,1,0:T(8,128)S(1)}, s32[3,256,128]{2,1,0:T(8,128)S(1)}, s32[3840,128]{1,0:T(8,128)S(1)}) custom-call(s32[256,128]{1,0:T(8,128)S(1)} %bitcast.10), custom_call_target="tpu_custom_call" | custom-call | flops 10000000 | bytes 3670016 | tf_op jit(solution)/shard_map/particle_plan/pallas_call | solution.py:526
  30.4 0.1 add_convert_fusion.keep_ref
  30.5 0.0 collective-permute-done.1
  30.5 0.9 %collective-permute-done = f32[624,128]{1,0:T(8,128)S(1)} collective-permute-done((f32[624,128]{1,0:T(8,128)S(1)}, f32[624,128]{1,0:T(8,128)S(1)}, u32[]{:S(2)}, u32[]{:S(2)}) %collective-permute-start) | collective-permute-done | bytes 319520 | tf_op jit(solution)/shard_map/ppermute | solution.py:786
  31.4 1.1 %widen.1 = (f32[3,16,2,24,128]{4,3,2,1,0:T(8,128)S(1)}, f32[4,2,2,24,128]{4,3,2,1,0:T(8,128)S(1)}, f32[16,2,24,128]{3,2,1,0:T(8,128)S(1)}, f32[440,128]{1,0:T(8,128)S(1)}, f32[464,128]{1,0:T(8,128)S(1)}) custom-call(f32[2]{0:T(128)S(1)} %add_convert_fusion.keep_ref, f32[4,17,2,8,128]{4,3,2,1,0:T(8,128)S(1)} %get-tuple-element.30.grid_ref, ...), custom_call_target="tpu_custom_call" | custom-call | bytes 6180864 | tf_op jit(solution)/shard_map/widen/pallas_call | solution.py:526
  32.6 0.7 %collective-permute-start.3 = (f32[464,128]{1,0:T(8,128)S(1)}, f32[464,128]{1,0:T(8,128)S(1)}, u32[]{:S(2)}, u32[]{:S(2)}) collective-permute-start(f32[464,128]{1,0:T(8,128)S(1)} %get-tuple-element.60), channel_id=1, source_target_pairs={{4,8},{8,4},{5,9},{9,5},{6,10},{10,6},{7,11},{11,7},{20,24},{24,20... | collective-permute-start | bytes 712712 | tf_op jit(solution)/shard_map/ppermute | solution.py:786
  33.2 2.9 %collective-permute-start.2 = (f32[464,128]{1,0:T(8,128)S(1)}, f32[464,128]{1,0:T(8,128)S(1)}, u32[]{:S(2)}, u32[]{:S(2)}) collective-permute-start(f32[464,128]{1,0:T(8,128)S(1)} %get-tuple-element.61), channel_id=1, source_target_pairs={{0,4},{8,12},{4,0},{12,8},{1,5},{9,13},{5,1},{13,9},{2,6},{10,14},... | collective-permute-start | bytes 712712 | tf_op jit(solution)/shard_map/ppermute | solution.py:786
  36.1 0.0 collective-permute-done.3
  36.1 1.1 %collective-permute-done.2 = f32[464,128]{1,0:T(8,128)S(1)} collective-permute-done((f32[464,128]{1,0:T(8,128)S(1)}, f32[464,128]{1,0:T(8,128)S(1)}, u32[]{:S(2)}, u32[]{:S(2)}) %collective-permute-start.2) | collective-permute-done | bytes 237600 | tf_op jit(solution)/shard_map/ppermute | solution.py:786
  37.3 1.8 %krylov.1 = (f32[3,25,2,24,128]{4,3,2,1,0:T(8,128)S(1)}, f32[25,2,24,128]{3,2,1,0:T(8,128)S(1)}, f32[25,2,24,128]{3,2,1,0:T(8,128)S(1)}, f32[25,2,24,128]{3,2,1,...) custom-call(f32[2]{0:T(128)S(1)} %add_convert_fusion.keep_ref, ...), custom_call_target="tpu_custom_call" | custom-call | bytes 6750208 | tf_op jit(solution)/shard_map/krylov/pallas_call | solution.py:526
  39.1 0.1 collective-permute-start.6
  39.2 4.3 %collective-permute-start.5 = (f32[16,128]{1,0:T(8,128)S(1)}, f32[16,128]{1,0:T(8,128)S(1)}, u32[]{:S(2)}, u32[]{:S(2)}) collective-permute-start(f32[16,128]{1,0:T(8,128)S(1)} %get-tuple-element.40), channel_id=1, source_target_pairs={{0,8},{4,12},{8,0},{12,4},{1,9},{5,13},{9,1},{13,5},{2,10},{6,14},... | collective-permute-start | bytes 24584 | tf_op jit(solution)/shard_map/ppermute | solution.py:797
  43.5 0.0 collective-permute-start.4
  43.5 0.0 collective-permute-done.6
  43.5 1.6 %collective-permute-done.5 = f32[16,128]{1,0:T(8,128)S(1)} collective-permute-done((f32[16,128]{1,0:T(8,128)S(1)}, f32[16,128]{1,0:T(8,128)S(1)}, u32[]{:S(2)}, u32[]{:S(2)}) %collective-permute-start.5) | collective-permute-done | bytes 8224 | tf_op jit(solution)/shard_map/ppermute | solution.py:797
  45.1 0.0 collective-permute-done.4
  45.2 1.4 %collective-permute-start.9 = (f32[16,128]{1,0:T(8,128)S(1)}, f32[16,128]{1,0:T(8,128)S(1)}, u32[]{:S(2)}, u32[]{:S(2)}) collective-permute-start(f32[16,128]{1,0:T(8,128)S(1)} %add_add_fusion), channel_id=1, source_target_pairs={{0,3},{1,2},{2,1},{3,0},{4,7},{5,6},{6,5},{7,4},{8,11},{9,10},{10,... | collective-permute-start | bytes 24584 | tf_op jit(solution)/shard_map/ppermute | solution.py:797
  46.6 1.9 %collective-permute-start.8 = (f32[16,128]{1,0:T(8,128)S(1)}, f32[16,128]{1,0:T(8,128)S(1)}, u32[]{:S(2)}, u32[]{:S(2)}) collective-permute-start(f32[16,128]{1,0:T(8,128)S(1)} %add_add_fusion), channel_id=1, source_target_pairs={{0,2},{1,3},{2,0},{3,1},{4,6},{5,7},{6,4},{7,5},{8,10},{9,11},{10,... | collective-permute-start | bytes 24584 | tf_op jit(solution)/shard_map/ppermute | solution.py:797
  48.4 1.2 %collective-permute-start.7 = (f32[16,128]{1,0:T(8,128)S(1)}, f32[16,128]{1,0:T(8,128)S(1)}, u32[]{:S(2)}, u32[]{:S(2)}) collective-permute-start(f32[16,128]{1,0:T(8,128)S(1)} %add_add_fusion), channel_id=1, source_target_pairs={{0,1},{1,0},{2,3},{3,2},{4,5},{5,4},{6,7},{7,6},{8,9},{9,8},{10,11... | collective-permute-start | bytes 24584 | tf_op jit(solution)/shard_map/ppermute | solution.py:797
  49.6 1.1 %collective-permute-done.9 = f32[16,128]{1,0:T(8,128)S(1)} collective-permute-done((f32[16,128]{1,0:T(8,128)S(1)}, f32[16,128]{1,0:T(8,128)S(1)}, u32[]{:S(2)}, u32[]{:S(2)}) %collective-permute-start.9) | collective-permute-done | bytes 8224 | tf_op jit(solution)/shard_map/ppermute | solution.py:797
  50.7 0.4 collective-permute-done.8
  51.1 0.9 %collective-permute-done.7 = f32[16,128]{1,0:T(8,128)S(1)} collective-permute-done((f32[16,128]{1,0:T(8,128)S(1)}, f32[16,128]{1,0:T(8,128)S(1)}, u32[]{:S(2)}, u32[]{:S(2)}) %collective-permute-start.7) | collective-permute-done | bytes 8224 | tf_op jit(solution)/shard_map/ppermute | solution.py:797
  52.1 4.6 %project.1 = (f32[16,8,256]{2,1,0:T(8,128)}, f32[3,32,8,128]{3,2,1,0:T(8,128)}) custom-call(f32[1,16,128]{2,1,0:T(8,128)S(1)} %add_bitcast_fusion.sums_ref, f32[3,25,2,24,128]{4,3,2,1,0:T(8,128)S(1)} %get-tuple-element.41.vel_ref, f32[25,2,24,128]{3,2,1,0:T(8,128)S(1)} %get-tuple-element.42.fluid_ref, f32[25,2,24,128]{3,2,1,0:T(8,128)S(1)} %get-tuple-element.43.k0_ref, ...), custom_call_target="tpu_custom_call" | custom-call | bytes 10788864 | tf_op jit(solution)/shard_map/project/pallas_call | solution.py:526
  (6 shorter events, 0.2 us)
Async XLA Ops:
  0.6 0.9 %copy-start.3 = (s32[1,32768]{1,0:T(1,128)S(1)}, s32[1,32768]{1,0:T(1,128)}, u32[]{:S(2)}) copy-start(s32[1,32768]{1,0:T(1,128)} %param.4) | copy-start | bytes 393220
  1.5 1.4 %copy-start = (f32[1,12,32768]{2,0,1:T(1,128)S(1)}, f32[1,12,32768]{2,0,1:T(1,128)}, u32[]{:S(2)}) copy-start(f32[1,12,32768]{2,0,1:T(1,128)} %param.6) | copy-start | bytes 4718596
  1.6 1.4 %copy-start.2 = (s32[1,32768]{1,0:T(1,128)S(1)}, s32[1,32768]{1,0:T(1,128)}, u32[]{:S(2)}) copy-start(s32[1,32768]{1,0:T(1,128)} %param.5) | copy-start | bytes 393220
  2.9 13.7 %copy-start.1 = (s32[16,8,256]{2,1,0:T(8,128)S(1)}, s32[16,8,256]{2,1,0:T(8,128)}, u32[]{:S(2)}) copy-start(s32[16,8,256]{2,1,0:T(8,128)} %flag_ref.3) | copy-start | bytes 393220
  17.4 13.1 %collective-permute-start.1 = (f32[624,128]{1,0:T(8,128)S(1)}, f32[624,128]{1,0:T(8,128)S(1)}, u32[]{:S(2)}, u32[]{:S(2)}) collective-permute-start(f32[624,128]{1,0:T(8,128)S(1)} %get-tuple-element.56), channel_id=1, source_target_pairs={{1,2},{2,1},{5,6},{6,5},{9,10},{10,9},{13,14},{14,13},{17,18},{18,... | collective-permute-start | bytes 958472 | tf_op jit(solution)/shard_map/ppermute | solution.py:786
  18.3 13.1 %collective-permute-start = (f32[624,128]{1,0:T(8,128)S(1)}, f32[624,128]{1,0:T(8,128)S(1)}, u32[]{:S(2)}, u32[]{:S(2)}) collective-permute-start(f32[624,128]{1,0:T(8,128)S(1)} %get-tuple-element.57), channel_id=1, source_target_pairs={{0,1},{2,3},{1,0},{3,2},{4,5},{6,7},{5,4},{7,6},{8,9},{10,11},{9,8... | collective-permute-start | bytes 958472 | tf_op jit(solution)/shard_map/ppermute | solution.py:786
  32.6 3.6 %collective-permute-start.3 = (f32[464,128]{1,0:T(8,128)S(1)}, f32[464,128]{1,0:T(8,128)S(1)}, u32[]{:S(2)}, u32[]{:S(2)}) collective-permute-start(f32[464,128]{1,0:T(8,128)S(1)} %get-tuple-element.60), channel_id=1, source_target_pairs={{4,8},{8,4},{5,9},{9,5},{6,10},{10,6},{7,11},{11,7},{20,24},{24,20... | collective-permute-start | bytes 712712 | tf_op jit(solution)/shard_map/ppermute | solution.py:786
  33.2 4.0 %collective-permute-start.2 = (f32[464,128]{1,0:T(8,128)S(1)}, f32[464,128]{1,0:T(8,128)S(1)}, u32[]{:S(2)}, u32[]{:S(2)}) collective-permute-start(f32[464,128]{1,0:T(8,128)S(1)} %get-tuple-element.61), channel_id=1, source_target_pairs={{0,4},{8,12},{4,0},{12,8},{1,5},{9,13},{5,1},{13,9},{2,6},{10,14},... | collective-permute-start | bytes 712712 | tf_op jit(solution)/shard_map/ppermute | solution.py:786
  39.1 4.4 %collective-permute-start.6 = (f32[16,128]{1,0:T(8,128)S(1)}, f32[16,128]{1,0:T(8,128)S(1)}, u32[]{:S(2)}, u32[]{:S(2)}) collective-permute-start(f32[16,128]{1,0:T(8,128)S(1)} %get-tuple-element.40), channel_id=1, source_target_pairs={{0,12},{4,8},{8,4},{12,0},{1,13},{5,9},{9,5},{13,1},{2,14},{6,10},... | collective-permute-start | bytes 24584 | tf_op jit(solution)/shard_map/ppermute | solution.py:797
  39.2 5.9 %collective-permute-start.5 = (f32[16,128]{1,0:T(8,128)S(1)}, f32[16,128]{1,0:T(8,128)S(1)}, u32[]{:S(2)}, u32[]{:S(2)}) collective-permute-start(f32[16,128]{1,0:T(8,128)S(1)} %get-tuple-element.40), channel_id=1, source_target_pairs={{0,8},{4,12},{8,0},{12,4},{1,9},{5,13},{9,1},{13,5},{2,10},{6,14},... | collective-permute-start | bytes 24584 | tf_op jit(solution)/shard_map/ppermute | solution.py:797
  43.5 1.6 %collective-permute-start.4 = (f32[16,128]{1,0:T(8,128)S(1)}, f32[16,128]{1,0:T(8,128)S(1)}, u32[]{:S(2)}, u32[]{:S(2)}) collective-permute-start(f32[16,128]{1,0:T(8,128)S(1)} %get-tuple-element.40), channel_id=1, source_target_pairs={{0,4},{4,0},{8,12},{12,8},{1,5},{5,1},{9,13},{13,9},{2,6},{6,2},{1... | collective-permute-start | bytes 24584 | tf_op jit(solution)/shard_map/ppermute | solution.py:797
  45.2 5.5 %collective-permute-start.9 = (f32[16,128]{1,0:T(8,128)S(1)}, f32[16,128]{1,0:T(8,128)S(1)}, u32[]{:S(2)}, u32[]{:S(2)}) collective-permute-start(f32[16,128]{1,0:T(8,128)S(1)} %add_add_fusion), channel_id=1, source_target_pairs={{0,3},{1,2},{2,1},{3,0},{4,7},{5,6},{6,5},{7,4},{8,11},{9,10},{10,... | collective-permute-start | bytes 24584 | tf_op jit(solution)/shard_map/ppermute | solution.py:797
  46.6 4.6 %collective-permute-start.8 = (f32[16,128]{1,0:T(8,128)S(1)}, f32[16,128]{1,0:T(8,128)S(1)}, u32[]{:S(2)}, u32[]{:S(2)}) collective-permute-start(f32[16,128]{1,0:T(8,128)S(1)} %add_add_fusion), channel_id=1, source_target_pairs={{0,2},{1,3},{2,0},{3,1},{4,6},{5,7},{6,4},{7,5},{8,10},{9,11},{10,... | collective-permute-start | bytes 24584 | tf_op jit(solution)/shard_map/ppermute | solution.py:797
  48.4 3.7 %collective-permute-start.7 = (f32[16,128]{1,0:T(8,128)S(1)}, f32[16,128]{1,0:T(8,128)S(1)}, u32[]{:S(2)}, u32[]{:S(2)}) collective-permute-start(f32[16,128]{1,0:T(8,128)S(1)} %add_add_fusion), channel_id=1, source_target_pairs={{0,1},{1,0},{2,3},{3,2},{4,5},{5,4},{6,7},{7,6},{8,9},{9,8},{10,11... | collective-permute-start | bytes 24584 | tf_op jit(solution)/shard_map/ppermute | solution.py:797

commit v10 on v9

--- a/solution.py
+++ b/solution.py
@@ -12,7 +12,7 @@
 CX, CY, CELLS = 16, 8, 32768
 TILES = CELLS // 1024
 LANE_RUNS, SUB_RUNS, SWAPS = 9, 3, 30 * 16
-GROUP = 2
+GROUP = 3
 
 
 def take(x, index, axis):
@@ -725,54 +725,73 @@
     return [jnp.where(smooth, a, b) * (1.0 / 6.0) for a, b in zip(power, turned)]
 
 
-def project_kernel(
-    sums_ref, vel_ref, fluid_ref, k0_ref, k1_ref, k2_ref, tag_ref, lane_ref, sub_ref, swap_ref,
-    pressure_ref, out_ref, press, proj,
-):
-    total = jnp.sum(jnp.sum(sums_ref[...], axis=0), axis=1, keepdims=True)
-    c = coefficients([jnp.broadcast_to(total[i : i + 1], (8, 128)) for i in range(14)])
-    c = [jnp.concatenate([a, a, a], axis=0)[None] for a in c]
-    for plane in range(3, 22):
-        press[plane] = c[0] * k0_ref[plane] + c[1] * k1_ref[plane] + c[2] * k2_ref[plane]
-    for x in range(CX):
-        for h in range(2):
-            pressure_ref[x, :, 128 * h : 128 * h + 128] = press[x + 4, h, 8:16]
+def interpolate_kernel(tag_ref, fluid_ref, *refs):
+    *fields, out_ref, proj = refs
     for x in range(CX + 1):
-        p = press[x + 4]
-        inner = p[:, 8:24]
-        slopes = (
-            press[x + 5, :, 8:24] - press[x + 3, :, 8:24],
-            (y_shift(p, -1) - y_shift(p, 1))[:, 8:24],
-            z_ahead(inner) - z_behind(inner),
-        )
         fluid = fluid_ref[x + 4, :, 8:24]
-        for d in range(3):
-            field = fluid * (vel_ref[d, x + 4, :, 8:24] - 0.5 * slopes[d])
-            for j, rows in enumerate((field[:, 0:8], y_shift(field, -1)[:, 0:8])):
-                proj[x, d, j, 0] = rows
-                proj[x, d, j, 1] = z_ahead(rows)
+        channel = 0
+        for ref in fields:
+            if len(ref.shape) == 5:
+                parts = [fluid * ref[d, x + 4, :, 8:24] for d in range(3)]
+            else:
+                p, scale = ref[x + 4], -0.5 * fluid
+                inner = p[:, 8:24]
+                parts = [
+                    scale * (ref[x + 5, :, 8:24] - ref[x + 3, :, 8:24]),
+                    scale * (y_shift(p, -1) - y_shift(p, 1))[:, 8:24],
+                    scale * (z_ahead(inner) - z_behind(inner)),
+                ]
+            for part in parts:
+                for j, rows in enumerate((part[:, 0:8], y_shift(part, -1)[:, 0:8])):
+                    proj[x, channel, j, 0] = rows
+                    proj[x, channel, j, 1] = z_ahead(rows)
+                channel += 1
     for x in range(CX):
         code = tag_ref[0, 2 * x : 2 * x + 2] >> 15
         fx, fy, fz = fractions(code)
         wx, wy, wz = (1.0 - fx, fx), (1.0 - fy, fy), (1.0 - fz, fz)
         w = {(i, j, k): wx[i] * wy[j] * wz[k] for i in (0, 1) for j in (0, 1) for k in (0, 1)}
-        for d in range(3):
+        for c in range(6):
             result = None
             for (i, j, k), weight in w.items():
-                term = weight * proj[x + i, d, j, k]
+                term = weight * proj[x + i, c, j, k]
                 result = term if result is None else result + term
-            out_ref[d, 2 * x : 2 * x + 2] = result
+            out_ref[c, 2 * x : 2 * x + 2] = result
+
+
+def interpolate(*args):
+    return kernel_call(
+        interpolate_kernel,
+        "interpolate",
+        (of((6, TILES, 8, 128)),),
+        [(CX + 1, 6, 2, 2, 2, 8, 128)],
+        args,
+        flops=10**7,
+    )[0]
+
+
+def finish_kernel(
+    sums_ref, k0_ref, k1_ref, k2_ref, first_ref, second_ref, lane_ref, sub_ref, swap_ref, pressure_ref, out_ref
+):
+    total = jnp.sum(sums_ref[...], axis=1, keepdims=True)
+    c = coefficients([jnp.broadcast_to(total[i : i + 1], (8, 128)) for i in range(14)])
+    for i in range(TILES):
+        for d in range(3):
+            out_ref[d, i] = (
+                first_ref[d, i]
+                + c[0] * first_ref[3 + d, i]
+                + c[1] * second_ref[d, i]
+                + c[2] * second_ref[3 + d, i]
+            )
     follow_plan([(out_ref, d) for d in range(3)], lane_ref, sub_ref, swap_ref)
-
-
-def project(*args):
-    return kernel_call(
-        project_kernel,
-        "project",
-        (of((CX, CY, 256)), of((3, TILES, 8, 128))),
-        [(25, 2, 24, 128), (CX + 1, 3, 2, 2, 2, 8, 128)],
-        args,
-    )
+    for x in range(CX):
+        for h in range(2):
+            k0, k1, k2 = [ref[x + 4, h, 8:16] for ref in (k0_ref, k1_ref, k2_ref)]
+            pressure_ref[x, :, 128 * h : 128 * h + 128] = c[0] * k0 + c[1] * k1 + c[2] * k2
+
+
+def finish(*args):
+    return kernel_call(finish_kernel, "finish", (of((CX, CY, 256)), of((3, TILES, 8, 128))), [], args)
 
 
 def neighbours(up, down, axis):
@@ -808,8 +827,10 @@
     near, edge, flags, up, down = widen(keep, grid, rim, low, high, fluid_flags, plan[1])
     low, high = neighbours(up, down, "gx")
     vel, fluid, k0, k1, k2, sums = krylov(keep, near, edge, flags, low, high)
-    sums = summed(summed(sums, "gx"), "gy")[None]
-    pressure, result = project(sums, vel, fluid, k0, k1, k2, tag, *plan)
+    first = interpolate(tag, fluid, vel, k0)
+    sums, first, tag = lax.optimization_barrier((summed(sums, "gx"), first, tag))
+    second = interpolate(tag, fluid, k1, k2)
+    pressure, result = finish(summed(sums, "gy"), k0, k1, k2, first, second, *plan)
     return pressure, result.reshape(1, 3, CELLS)
 
 

time: 56.9 us -> 54.3 us (0.954)
  waiting for transfers between devices: 6.11 us -> 2.16 us
  Pallas kernels: 29.4 us -> 30.8 us
    ppermute x6, waiting for transfers between devices: 4.07 us -> 0.12 us  [summed(): parts.append(lax.ppermute(sums, axis, swaps))]
    pallas_call x7 -> x9, Pallas kernels: 29.4 us -> 30.8 us  [kernel_call(): pl.pallas_call(body, out_shape=outs, **{} if in_specs is None else dict(i...]
  transfers between devices with their start and end apart: 10 -> 10, of which waited for: 6 -> 3; matrix products, arithmetic and copies ran while one was open for 0% -> 0% of each run, Pallas kernels for 11% -> 19%
where the time goes in v10:
time: 54.3 us; the launch traced here: 54.2 us
  Pallas kernels  30.8 us (57%)
  starting transfers between devices  19.2 us (35%)
  waiting for transfers between devices  2.16 us (4%)
  local copies, waits for them, and re-layouts  0.98 us (2%)
  between operations  0.79 us (1%)
    pallas_call x9, Pallas kernels, kernel_call(): pl.pallas_call(body, out_shape=outs, **{} if in_specs is None else dict(i...  30.8 us
    ppermute x4, starting transfers between devices, neighbours(): arrived.append(lax.ppermute(slab, axis, pairs + [(b, a) for a, b in pairs]))  10.3 us
    ppermute x6, starting transfers between devices, summed(): parts.append(lax.ppermute(sums, axis, swaps))  8.84 us
    ppermute x4, waiting for transfers between devices, neighbours(): arrived.append(lax.ppermute(slab, axis, pairs + [(b, a) for a, b in pairs]))  2.04 us
  transfers between devices with their start and end apart: 10, of which 3 were waited for; matrix products, arithmetic and copies ran while one was open for 0% of the time, Pallas kernels for 19%

profile of v10, /device:TPU:0, one launch (start us, length us, event | category | flops | bytes accessed | tf_op | source)
XLA Modules:
  0.0 54.2 jit_solution(16173948718598790249)
XLA Ops:
  0.6 0.0 copy-start.3
  0.7 0.9 %copy-done.3 = s32[1,32768]{1,0:T(1,128)S(1)} copy-done((s32[1,32768]{1,0:T(1,128)S(1)}, s32[1,32768]{1,0:T(1,128)}, u32[]{:S(2)}) %copy-start.3) | copy-done | bytes 131096
  1.5 0.0 copy-start
  1.6 0.0 copy-start.2
  1.6 1.3 %cell_rows.1 = (s32[256,128]{1,0:T(8,128)S(1)}, s32[1,256,128]{2,1,0:T(8,128)S(1)}) custom-call(s32[256,128]{1,0:T(8,128)S(1)} %bitcast.10), custom_call_target="tpu_custom_call" | custom-call | flops 3000000000 | bytes 393216 | tf_op jit(solution)/shard_map/cell_rows/pallas_call | solution.py:526
  2.9 0.0 copy-start.1
  2.9 0.1 copy-done
  3.0 0.0 copy-done.2
  3.0 12.3 %to_cells.1 = (f32[12,32,8,128]{3,2,1,0:T(8,128)S(1)}, s32[1,32,8,128]{3,2,1,0:T(8,128)S(1)}) custom-call(s32[32,8,128]{2,1,0:T(8,128)S(1)} %bitcast.9, f32[12,32,8,128]{3,2,1,0:T(8,128)S(1)} %bitcast.8, s32[256,128]{1,0:T(8,128)S(1)} %get-tuple-element.29.key_ref, s32[1,256,128]{2,1,0:T(8,128)S(1)} %get-tuple-element.30.rows_ref), custom_call_target="tpu_custom_call" | custom-call | flops 10000000 | bytes 7208960 | tf_op jit(solution)/shard_map/to_cells/pallas_call | solution.py:526
  15.2 0.0 copy-done.1
  15.2 0.7 %deposit.1 = (f32[4,17,2,8,128]{4,3,2,1,0:T(8,128)S(1)}, f32[4,17,2,8,128]{4,3,2,1,0:T(8,128)S(1)}, f32[592,128]{1,0:T(8,128)S(1)}, f32[624,128]{1,0:T(8,128)S(1)}) custom-call(f32[12,32,8,128]{3,2,1,0:T(8,128)S(1)} %get-tuple-element.31.cells_ref, s32[1,32,8,128]{3,2,1,0:T(8,128)S(1)} %get-tuple-element.51.tag_ref, s32[16,8,256]{2,1,0:T(8,128)S(1)} %copy-done.1), custom_call_target="tpu_custom_call" | custom-call | bytes 3571712 | tf_op jit(solution)/shard_map/deposit/pallas_call | solution.py:526
  16.0 0.9 %collective-permute-start.1 = (f32[624,128]{1,0:T(8,128)S(1)}, f32[624,128]{1,0:T(8,128)S(1)}, u32[]{:S(2)}, u32[]{:S(2)}) collective-permute-start(f32[624,128]{1,0:T(8,128)S(1)} %get-tuple-element.62), channel_id=1, source_target_pairs={{1,2},{2,1},{5,6},{6,5},{9,10},{10,9},{13,14},{14,13},{17,18},{18,... | collective-permute-start | bytes 958472 | tf_op jit(solution)/shard_map/ppermute | solution.py:805
  16.9 5.9 %collective-permute-start = (f32[624,128]{1,0:T(8,128)S(1)}, f32[624,128]{1,0:T(8,128)S(1)}, u32[]{:S(2)}, u32[]{:S(2)}) collective-permute-start(f32[624,128]{1,0:T(8,128)S(1)} %get-tuple-element.63), channel_id=1, source_target_pairs={{0,1},{2,3},{1,0},{3,2},{4,5},{6,7},{5,4},{7,6},{8,9},{10,11},{9,8... | collective-permute-start | bytes 958472 | tf_op jit(solution)/shard_map/ppermute | solution.py:805
  22.8 6.3 %particle_plan.1 = (s32[9,256,128]{2,1,0:T(8,128)S(1)}, s32[3,256,128]{2,1,0:T(8,128)S(1)}, s32[3840,128]{1,0:T(8,128)S(1)}) custom-call(s32[256,128]{1,0:T(8,128)S(1)} %bitcast.7), custom_call_target="tpu_custom_call" | custom-call | flops 10000000 | bytes 3670016 | tf_op jit(solution)/shard_map/particle_plan/pallas_call | solution.py:526
  29.1 0.1 add_convert_fusion.keep_ref
  29.1 0.0 collective-permute-done.1
  29.2 0.9 %collective-permute-done = f32[624,128]{1,0:T(8,128)S(1)} collective-permute-done((f32[624,128]{1,0:T(8,128)S(1)}, f32[624,128]{1,0:T(8,128)S(1)}, u32[]{:S(2)}, u32[]{:S(2)}) %collective-permute-start) | collective-permute-done | bytes 319520 | tf_op jit(solution)/shard_map/ppermute | solution.py:805
  30.1 1.1 %widen.1 = (f32[3,16,2,24,128]{4,3,2,1,0:T(8,128)S(1)}, f32[4,2,2,24,128]{4,3,2,1,0:T(8,128)S(1)}, f32[16,2,24,128]{3,2,1,0:T(8,128)S(1)}, f32[440,128]{1,0:T(8,128)S(1)}, f32[464,128]{1,0:T(8,128)S(1)}) custom-call(f32[2]{0:T(128)S(1)} %add_convert_fusion.keep_ref, f32[4,17,2,8,128]{4,3,2,1,0:T(8,128)S(1)} %get-tuple-element.33.grid_ref, ...), custom_call_target="tpu_custom_call" | custom-call | bytes 6180864 | tf_op jit(solution)/shard_map/widen/pallas_call | solution.py:526
  31.2 0.7 %collective-permute-start.3 = (f32[464,128]{1,0:T(8,128)S(1)}, f32[464,128]{1,0:T(8,128)S(1)}, u32[]{:S(2)}, u32[]{:S(2)}) collective-permute-start(f32[464,128]{1,0:T(8,128)S(1)} %get-tuple-element.66), channel_id=1, source_target_pairs={{4,8},{8,4},{5,9},{9,5},{6,10},{10,6},{7,11},{11,7},{20,24},{24,20... | collective-permute-start | bytes 712712 | tf_op jit(solution)/shard_map/ppermute | solution.py:805
  31.9 2.9 %collective-permute-start.2 = (f32[464,128]{1,0:T(8,128)S(1)}, f32[464,128]{1,0:T(8,128)S(1)}, u32[]{:S(2)}, u32[]{:S(2)}) collective-permute-start(f32[464,128]{1,0:T(8,128)S(1)} %get-tuple-element.67), channel_id=1, source_target_pairs={{0,4},{8,12},{4,0},{12,8},{1,5},{9,13},{5,1},{13,9},{2,6},{10,14},... | collective-permute-start | bytes 712712 | tf_op jit(solution)/shard_map/ppermute | solution.py:805
  34.8 0.0 collective-permute-done.3
  34.8 1.1 %collective-permute-done.2 = f32[464,128]{1,0:T(8,128)S(1)} collective-permute-done((f32[464,128]{1,0:T(8,128)S(1)}, f32[464,128]{1,0:T(8,128)S(1)}, u32[]{:S(2)}, u32[]{:S(2)}) %collective-permute-start.2) | collective-permute-done | bytes 237600 | tf_op jit(solution)/shard_map/ppermute | solution.py:805
  35.9 0.1 broadcast_select_fusion.2
  36.0 1.8 %krylov.1 = (f32[3,25,2,24,128]{4,3,2,1,0:T(8,128)S(1)}, f32[25,2,24,128]{3,2,1,0:T(8,128)S(1)}, f32[25,2,24,128]{3,2,1,0:T(8,128)S(1)}, f32[25,2,24,128]{3,2,1,...) custom-call(f32[2]{0:T(128)S(1)} %add_convert_fusion.keep_ref, ...), custom_call_target="tpu_custom_call" | custom-call | bytes 6750208 | tf_op jit(solution)/shard_map/krylov/pallas_call | solution.py:526
  37.8 0.1 collective-permute-start.6
  37.9 4.3 %collective-permute-start.5 = (f32[16,128]{1,0:T(8,128)S(1)}, f32[16,128]{1,0:T(8,128)S(1)}, u32[]{:S(2)}, u32[]{:S(2)}) collective-permute-start(f32[16,128]{1,0:T(8,128)S(1)} %get-tuple-element.43), channel_id=1, source_target_pairs={{0,8},{4,12},{8,0},{12,4},{1,9},{5,13},{9,1},{13,5},{2,10},{6,14},... | collective-permute-start | bytes 24584 | tf_op jit(solution)/shard_map/ppermute | solution.py:816
  42.2 0.0 collective-permute-start.4
  42.2 1.5 %interpolate.2.first_ref = f32[6,32,8,128]{3,2,1,0:T(8,128)S(1)} custom-call(s32[1,32,8,128]{3,2,1,0:T(8,128)S(1)} %get-tuple-element.51.tag_ref, f32[25,2,24,128]{3,2,1,0:T(8,128)S(1)} %get-tuple-element.44.fluid_ref, f32[3,25,2,24,128]{4,3,2,1,0:T(8,128)S(1)} %get-tuple-element.45.refs_0_, f32[25,2,24,128]{3,2,1,0:T(8,128)S(1)} %get-tuple-element.46.refs_1_.k0_ref), custom_call_target="tpu_custom_call" | custom-call | flops 10000000 | bytes 7331840 | tf_op jit(solution)/shard_map/interpolate/pallas_call | solution.py:526
  43.7 0.0 collective-permute-done.6
  43.7 0.1 collective-permute-done.5
  43.8 0.0 collective-permute-done.4
  43.8 1.4 %collective-permute-start.9 = (f32[16,128]{1,0:T(8,128)S(1)}, f32[16,128]{1,0:T(8,128)S(1)}, u32[]{:S(2)}, u32[]{:S(2)}) collective-permute-start(f32[16,128]{1,0:T(8,128)S(1)} %add_add_fusion.1), channel_id=1, source_target_pairs={{0,3},{1,2},{2,1},{3,0},{4,7},{5,6},{6,5},{7,4},{8,11},{9,10},{10,... | collective-permute-start | bytes 24584 | tf_op jit(solution)/shard_map/ppermute | solution.py:816
  45.3 1.9 %collective-permute-start.8 = (f32[16,128]{1,0:T(8,128)S(1)}, f32[16,128]{1,0:T(8,128)S(1)}, u32[]{:S(2)}, u32[]{:S(2)}) collective-permute-start(f32[16,128]{1,0:T(8,128)S(1)} %add_add_fusion.1), channel_id=1, source_target_pairs={{0,2},{1,3},{2,0},{3,1},{4,6},{5,7},{6,4},{7,5},{8,10},{9,11},{10,... | collective-permute-start | bytes 24584 | tf_op jit(solution)/shard_map/ppermute | solution.py:816
  47.1 1.2 %collective-permute-start.7 = (f32[16,128]{1,0:T(8,128)S(1)}, f32[16,128]{1,0:T(8,128)S(1)}, u32[]{:S(2)}, u32[]{:S(2)}) collective-permute-start(f32[16,128]{1,0:T(8,128)S(1)} %add_add_fusion.1), channel_id=1, source_target_pairs={{0,1},{1,0},{2,3},{3,2},{4,5},{5,4},{6,7},{7,6},{8,9},{9,8},{10,11... | collective-permute-start | bytes 24584 | tf_op jit(solution)/shard_map/ppermute | solution.py:816
  48.3 2.4 %interpolate.3.second_ref = f32[6,32,8,128]{3,2,1,0:T(8,128)S(1)} custom-call(s32[1,32,8,128]{3,2,1,0:T(8,128)S(1)} %get-tuple-element.51.tag_ref, f32[25,2,24,128]{3,2,1,0:T(8,128)S(1)} %get-tuple-element.44.fluid_ref, f32[25,2,24,128]{3,2,1,0:T(8,128)S(1)} %get-tuple-element.48.refs_0_.k1_ref, f32[25,2,24,128]{3,2,1,0:T(8,128)S(1)} %get-tuple-element.49.refs_1_.k2_ref), custom_call_target="tpu_custom_call" | custom-call | flops 10000000 | bytes 6103040 | tf_op jit(solution)/shard_map/interpolate/pallas_call | solution.py:526
  50.7 0.0 collective-permute-done.9
  50.7 0.0 collective-permute-done.8
  50.8 0.0 collective-permute-done.7
  50.8 3.4 %finish.1 = (f32[16,8,256]{2,1,0:T(8,128)}, f32[3,32,8,128]{3,2,1,0:T(8,128)}) custom-call(f32[16,128]{1,0:T(8,128)S(1)} %add_add_fusion.sums_ref, f32[25,2,24,128]{3,2,1,0:T(8,128)S(1)} %get-tuple-element.46.refs_1_.k0_ref, f32[25,2,24,128]{3,2,1,0:T(8,128)S(1)} %get-tuple-element.48.refs_0_.k1_ref, ...), custom_call_target="tpu_custom_call" | custom-call | bytes 7487488 | tf_op jit(solution)/shard_map/finish/pallas_call | solution.py:526
  (5 shorter events, 0.1 us)
Async XLA Ops:
  0.6 0.9 %copy-start.3 = (s32[1,32768]{1,0:T(1,128)S(1)}, s32[1,32768]{1,0:T(1,128)}, u32[]{:S(2)}) copy-start(s32[1,32768]{1,0:T(1,128)} %param.4) | copy-start | bytes 393220
  1.5 1.4 %copy-start = (f32[1,12,32768]{2,0,1:T(1,128)S(1)}, f32[1,12,32768]{2,0,1:T(1,128)}, u32[]{:S(2)}) copy-start(f32[1,12,32768]{2,0,1:T(1,128)} %param.6) | copy-start | bytes 4718596
  1.6 1.4 %copy-start.2 = (s32[1,32768]{1,0:T(1,128)S(1)}, s32[1,32768]{1,0:T(1,128)}, u32[]{:S(2)}) copy-start(s32[1,32768]{1,0:T(1,128)} %param.5) | copy-start | bytes 393220
  2.9 12.4 %copy-start.1 = (s32[16,8,256]{2,1,0:T(8,128)S(1)}, s32[16,8,256]{2,1,0:T(8,128)}, u32[]{:S(2)}) copy-start(s32[16,8,256]{2,1,0:T(8,128)} %flag_ref.3) | copy-start | bytes 393220
  16.0 13.1 %collective-permute-start.1 = (f32[624,128]{1,0:T(8,128)S(1)}, f32[624,128]{1,0:T(8,128)S(1)}, u32[]{:S(2)}, u32[]{:S(2)}) collective-permute-start(f32[624,128]{1,0:T(8,128)S(1)} %get-tuple-element.62), channel_id=1, source_target_pairs={{1,2},{2,1},{5,6},{6,5},{9,10},{10,9},{13,14},{14,13},{17,18},{18,... | collective-permute-start | bytes 958472 | tf_op jit(solution)/shard_map/ppermute | solution.py:805
  16.9 13.1 %collective-permute-start = (f32[624,128]{1,0:T(8,128)S(1)}, f32[624,128]{1,0:T(8,128)S(1)}, u32[]{:S(2)}, u32[]{:S(2)}) collective-permute-start(f32[624,128]{1,0:T(8,128)S(1)} %get-tuple-element.63), channel_id=1, source_target_pairs={{0,1},{2,3},{1,0},{3,2},{4,5},{6,7},{5,4},{7,6},{8,9},{10,11},{9,8... | collective-permute-start | bytes 958472 | tf_op jit(solution)/shard_map/ppermute | solution.py:805
  31.2 3.6 %collective-permute-start.3 = (f32[464,128]{1,0:T(8,128)S(1)}, f32[464,128]{1,0:T(8,128)S(1)}, u32[]{:S(2)}, u32[]{:S(2)}) collective-permute-start(f32[464,128]{1,0:T(8,128)S(1)} %get-tuple-element.66), channel_id=1, source_target_pairs={{4,8},{8,4},{5,9},{9,5},{6,10},{10,6},{7,11},{11,7},{20,24},{24,20... | collective-permute-start | bytes 712712 | tf_op jit(solution)/shard_map/ppermute | solution.py:805
  31.9 4.0 %collective-permute-start.2 = (f32[464,128]{1,0:T(8,128)S(1)}, f32[464,128]{1,0:T(8,128)S(1)}, u32[]{:S(2)}, u32[]{:S(2)}) collective-permute-start(f32[464,128]{1,0:T(8,128)S(1)} %get-tuple-element.67), channel_id=1, source_target_pairs={{0,4},{8,12},{4,0},{12,8},{1,5},{9,13},{5,1},{13,9},{2,6},{10,14},... | collective-permute-start | bytes 712712 | tf_op jit(solution)/shard_map/ppermute | solution.py:805
  37.8 5.9 %collective-permute-start.6 = (f32[16,128]{1,0:T(8,128)S(1)}, f32[16,128]{1,0:T(8,128)S(1)}, u32[]{:S(2)}, u32[]{:S(2)}) collective-permute-start(f32[16,128]{1,0:T(8,128)S(1)} %get-tuple-element.43), channel_id=1, source_target_pairs={{0,12},{4,8},{8,4},{12,0},{1,13},{5,9},{9,5},{13,1},{2,14},{6,10},... | collective-permute-start | bytes 24584 | tf_op jit(solution)/shard_map/ppermute | solution.py:816
  37.9 5.9 %collective-permute-start.5 = (f32[16,128]{1,0:T(8,128)S(1)}, f32[16,128]{1,0:T(8,128)S(1)}, u32[]{:S(2)}, u32[]{:S(2)}) collective-permute-start(f32[16,128]{1,0:T(8,128)S(1)} %get-tuple-element.43), channel_id=1, source_target_pairs={{0,8},{4,12},{8,0},{12,4},{1,9},{5,13},{9,1},{13,5},{2,10},{6,14},... | collective-permute-start | bytes 24584 | tf_op jit(solution)/shard_map/ppermute | solution.py:816
  42.2 1.6 %collective-permute-start.4 = (f32[16,128]{1,0:T(8,128)S(1)}, f32[16,128]{1,0:T(8,128)S(1)}, u32[]{:S(2)}, u32[]{:S(2)}) collective-permute-start(f32[16,128]{1,0:T(8,128)S(1)} %get-tuple-element.43), channel_id=1, source_target_pairs={{0,4},{4,0},{8,12},{12,8},{1,5},{5,1},{9,13},{13,9},{2,6},{6,2},{1... | collective-permute-start | bytes 24584 | tf_op jit(solution)/shard_map/ppermute | solution.py:816
  43.8 6.9 %collective-permute-start.9 = (f32[16,128]{1,0:T(8,128)S(1)}, f32[16,128]{1,0:T(8,128)S(1)}, u32[]{:S(2)}, u32[]{:S(2)}) collective-permute-start(f32[16,128]{1,0:T(8,128)S(1)} %add_add_fusion.1), channel_id=1, source_target_pairs={{0,3},{1,2},{2,1},{3,0},{4,7},{5,6},{6,5},{7,4},{8,11},{9,10},{10,... | collective-permute-start | bytes 24584 | tf_op jit(solution)/shard_map/ppermute | solution.py:816
  45.3 5.5 %collective-permute-start.8 = (f32[16,128]{1,0:T(8,128)S(1)}, f32[16,128]{1,0:T(8,128)S(1)}, u32[]{:S(2)}, u32[]{:S(2)}) collective-permute-start(f32[16,128]{1,0:T(8,128)S(1)} %add_add_fusion.1), channel_id=1, source_target_pairs={{0,2},{1,3},{2,0},{3,1},{4,6},{5,7},{6,4},{7,5},{8,10},{9,11},{10,... | collective-permute-start | bytes 24584 | tf_op jit(solution)/shard_map/ppermute | solution.py:816
  47.1 3.7 %collective-permute-start.7 = (f32[16,128]{1,0:T(8,128)S(1)}, f32[16,128]{1,0:T(8,128)S(1)}, u32[]{:S(2)}, u32[]{:S(2)}) collective-permute-start(f32[16,128]{1,0:T(8,128)S(1)} %add_add_fusion.1), channel_id=1, source_target_pairs={{0,1},{1,0},{2,3},{3,2},{4,5},{5,4},{6,7},{7,6},{8,9},{9,8},{10,11... | collective-permute-start | bytes 24584 | tf_op jit(solution)/shard_map/ppermute | solution.py:816

commit v11 on v10

--- a/solution.py
+++ b/solution.py
@@ -12,7 +12,7 @@
 CX, CY, CELLS = 16, 8, 32768
 TILES = CELLS // 1024
 LANE_RUNS, SUB_RUNS, SWAPS = 9, 3, 30 * 16
-GROUP = 3
+GROUP = 4
 
 
 def take(x, index, axis):

time: 54.3 us -> 53.6 us (0.987)
  Pallas kernels: 30.8 us -> 30 us
    pallas_call x9, Pallas kernels: 30.8 us -> 30 us  [kernel_call(): pl.pallas_call(body, out_shape=outs, **{} if in_specs is None else dict(i...]
where the time goes in v11:
time: 53.6 us; the launch traced here: 53.4 us
  Pallas kernels  30 us (56%)
  starting transfers between devices  19.2 us (36%)
  waiting for transfers between devices  2.16 us (4%)
  local copies, waits for them, and re-layouts  0.98 us (2%)
  between operations  0.79 us (1%)
    pallas_call x9, Pallas kernels, kernel_call(): pl.pallas_call(body, out_shape=outs, **{} if in_specs is None else dict(i...  30 us
    ppermute x4, starting transfers between devices, neighbours(): arrived.append(lax.ppermute(slab, axis, pairs + [(b, a) for a, b in pairs]))  10.3 us
    ppermute x6, starting transfers between devices, summed(): parts.append(lax.ppermute(sums, axis, swaps))  8.84 us
    ppermute x4, waiting for transfers between devices, neighbours(): arrived.append(lax.ppermute(slab, axis, pairs + [(b, a) for a, b in pairs]))  2.04 us
  transfers between devices with their start and end apart: 10, of which 3 were waited for; matrix products, arithmetic and copies ran while one was open for 0% of the time, Pallas kernels for 19%

profile of v11, /device:TPU:0, one launch (start us, length us, event | category | flops | bytes accessed | tf_op | source)
XLA Modules:
  0.0 53.4 jit_solution(2952492356990680125)
XLA Ops:
  0.6 0.0 copy-start.3
  0.7 0.9 %copy-done.3 = s32[1,32768]{1,0:T(1,128)S(1)} copy-done((s32[1,32768]{1,0:T(1,128)S(1)}, s32[1,32768]{1,0:T(1,128)}, u32[]{:S(2)}) %copy-start.3) | copy-done | bytes 131096
  1.5 0.0 copy-start
  1.6 0.0 copy-start.2
  1.6 1.3 %cell_rows.1 = (s32[256,128]{1,0:T(8,128)S(1)}, s32[1,256,128]{2,1,0:T(8,128)S(1)}) custom-call(s32[256,128]{1,0:T(8,128)S(1)} %bitcast.10), custom_call_target="tpu_custom_call" | custom-call | flops 3000000000 | bytes 393216 | tf_op jit(solution)/shard_map/cell_rows/pallas_call | solution.py:526
  2.9 0.0 copy-start.1
  2.9 0.1 copy-done
  3.0 0.0 copy-done.2
  3.0 11.5 %to_cells.1 = (f32[12,32,8,128]{3,2,1,0:T(8,128)S(1)}, s32[1,32,8,128]{3,2,1,0:T(8,128)S(1)}) custom-call(s32[32,8,128]{2,1,0:T(8,128)S(1)} %bitcast.9, f32[12,32,8,128]{3,2,1,0:T(8,128)S(1)} %bitcast.8, s32[256,128]{1,0:T(8,128)S(1)} %get-tuple-element.29.key_ref, s32[1,256,128]{2,1,0:T(8,128)S(1)} %get-tuple-element.30.rows_ref), custom_call_target="tpu_custom_call" | custom-call | flops 10000000 | bytes 7208960 | tf_op jit(solution)/shard_map/to_cells/pallas_call | solution.py:526
  14.4 0.0 copy-done.1
  14.5 0.7 %deposit.1 = (f32[4,17,2,8,128]{4,3,2,1,0:T(8,128)S(1)}, f32[4,17,2,8,128]{4,3,2,1,0:T(8,128)S(1)}, f32[592,128]{1,0:T(8,128)S(1)}, f32[624,128]{1,0:T(8,128)S(1)}) custom-call(f32[12,32,8,128]{3,2,1,0:T(8,128)S(1)} %get-tuple-element.31.cells_ref, s32[1,32,8,128]{3,2,1,0:T(8,128)S(1)} %get-tuple-element.51.tag_ref, s32[16,8,256]{2,1,0:T(8,128)S(1)} %copy-done.1), custom_call_target="tpu_custom_call" | custom-call | bytes 3571712 | tf_op jit(solution)/shard_map/deposit/pallas_call | solution.py:526
  15.3 0.9 %collective-permute-start.1 = (f32[624,128]{1,0:T(8,128)S(1)}, f32[624,128]{1,0:T(8,128)S(1)}, u32[]{:S(2)}, u32[]{:S(2)}) collective-permute-start(f32[624,128]{1,0:T(8,128)S(1)} %get-tuple-element.62), channel_id=1, source_target_pairs={{1,2},{2,1},{5,6},{6,5},{9,10},{10,9},{13,14},{14,13},{17,18},{18,... | collective-permute-start | bytes 958472 | tf_op jit(solution)/shard_map/ppermute | solution.py:805
  16.1 5.9 %collective-permute-start = (f32[624,128]{1,0:T(8,128)S(1)}, f32[624,128]{1,0:T(8,128)S(1)}, u32[]{:S(2)}, u32[]{:S(2)}) collective-permute-start(f32[624,128]{1,0:T(8,128)S(1)} %get-tuple-element.63), channel_id=1, source_target_pairs={{0,1},{2,3},{1,0},{3,2},{4,5},{6,7},{5,4},{7,6},{8,9},{10,11},{9,8... | collective-permute-start | bytes 958472 | tf_op jit(solution)/shard_map/ppermute | solution.py:805
  22.0 6.3 %particle_plan.1 = (s32[9,256,128]{2,1,0:T(8,128)S(1)}, s32[3,256,128]{2,1,0:T(8,128)S(1)}, s32[3840,128]{1,0:T(8,128)S(1)}) custom-call(s32[256,128]{1,0:T(8,128)S(1)} %bitcast.7), custom_call_target="tpu_custom_call" | custom-call | flops 10000000 | bytes 3670016 | tf_op jit(solution)/shard_map/particle_plan/pallas_call | solution.py:526
  28.3 0.1 add_convert_fusion.keep_ref
  28.4 0.0 collective-permute-done.1
  28.4 0.9 %collective-permute-done = f32[624,128]{1,0:T(8,128)S(1)} collective-permute-done((f32[624,128]{1,0:T(8,128)S(1)}, f32[624,128]{1,0:T(8,128)S(1)}, u32[]{:S(2)}, u32[]{:S(2)}) %collective-permute-start) | collective-permute-done | bytes 319520 | tf_op jit(solution)/shard_map/ppermute | solution.py:805
  29.3 1.1 %widen.1 = (f32[3,16,2,24,128]{4,3,2,1,0:T(8,128)S(1)}, f32[4,2,2,24,128]{4,3,2,1,0:T(8,128)S(1)}, f32[16,2,24,128]{3,2,1,0:T(8,128)S(1)}, f32[440,128]{1,0:T(8,128)S(1)}, f32[464,128]{1,0:T(8,128)S(1)}) custom-call(f32[2]{0:T(128)S(1)} %add_convert_fusion.keep_ref, f32[4,17,2,8,128]{4,3,2,1,0:T(8,128)S(1)} %get-tuple-element.33.grid_ref, ...), custom_call_target="tpu_custom_call" | custom-call | bytes 6180864 | tf_op jit(solution)/shard_map/widen/pallas_call | solution.py:526
  30.4 0.7 %collective-permute-start.3 = (f32[464,128]{1,0:T(8,128)S(1)}, f32[464,128]{1,0:T(8,128)S(1)}, u32[]{:S(2)}, u32[]{:S(2)}) collective-permute-start(f32[464,128]{1,0:T(8,128)S(1)} %get-tuple-element.66), channel_id=1, source_target_pairs={{4,8},{8,4},{5,9},{9,5},{6,10},{10,6},{7,11},{11,7},{20,24},{24,20... | collective-permute-start | bytes 712712 | tf_op jit(solution)/shard_map/ppermute | solution.py:805
  31.1 2.9 %collective-permute-start.2 = (f32[464,128]{1,0:T(8,128)S(1)}, f32[464,128]{1,0:T(8,128)S(1)}, u32[]{:S(2)}, u32[]{:S(2)}) collective-permute-start(f32[464,128]{1,0:T(8,128)S(1)} %get-tuple-element.67), channel_id=1, source_target_pairs={{0,4},{8,12},{4,0},{12,8},{1,5},{9,13},{5,1},{13,9},{2,6},{10,14},... | collective-permute-start | bytes 712712 | tf_op jit(solution)/shard_map/ppermute | solution.py:805
  34.0 0.0 collective-permute-done.3
  34.0 1.1 %collective-permute-done.2 = f32[464,128]{1,0:T(8,128)S(1)} collective-permute-done((f32[464,128]{1,0:T(8,128)S(1)}, f32[464,128]{1,0:T(8,128)S(1)}, u32[]{:S(2)}, u32[]{:S(2)}) %collective-permute-start.2) | collective-permute-done | bytes 237600 | tf_op jit(solution)/shard_map/ppermute | solution.py:805
  35.1 0.1 broadcast_select_fusion.2
  35.2 1.8 %krylov.1 = (f32[3,25,2,24,128]{4,3,2,1,0:T(8,128)S(1)}, f32[25,2,24,128]{3,2,1,0:T(8,128)S(1)}, f32[25,2,24,128]{3,2,1,0:T(8,128)S(1)}, f32[25,2,24,128]{3,2,1,...) custom-call(f32[2]{0:T(128)S(1)} %add_convert_fusion.keep_ref, ...), custom_call_target="tpu_custom_call" | custom-call | bytes 6750208 | tf_op jit(solution)/shard_map/krylov/pallas_call | solution.py:526
  37.0 0.1 collective-permute-start.6
  37.1 4.3 %collective-permute-start.5 = (f32[16,128]{1,0:T(8,128)S(1)}, f32[16,128]{1,0:T(8,128)S(1)}, u32[]{:S(2)}, u32[]{:S(2)}) collective-permute-start(f32[16,128]{1,0:T(8,128)S(1)} %get-tuple-element.43), channel_id=1, source_target_pairs={{0,8},{4,12},{8,0},{12,4},{1,9},{5,13},{9,1},{13,5},{2,10},{6,14},... | collective-permute-start | bytes 24584 | tf_op jit(solution)/shard_map/ppermute | solution.py:816
  41.4 0.0 collective-permute-start.4
  41.4 1.5 %interpolate.2.first_ref = f32[6,32,8,128]{3,2,1,0:T(8,128)S(1)} custom-call(s32[1,32,8,128]{3,2,1,0:T(8,128)S(1)} %get-tuple-element.51.tag_ref, f32[25,2,24,128]{3,2,1,0:T(8,128)S(1)} %get-tuple-element.44.fluid_ref, f32[3,25,2,24,128]{4,3,2,1,0:T(8,128)S(1)} %get-tuple-element.45.refs_0_, f32[25,2,24,128]{3,2,1,0:T(8,128)S(1)} %get-tuple-element.46.refs_1_.k0_ref), custom_call_target="tpu_custom_call" | custom-call | flops 10000000 | bytes 7331840 | tf_op jit(solution)/shard_map/interpolate/pallas_call | solution.py:526
  42.9 0.0 collective-permute-done.6
  42.9 0.1 collective-permute-done.5
  43.0 0.0 collective-permute-done.4
  43.1 1.4 %collective-permute-start.9 = (f32[16,128]{1,0:T(8,128)S(1)}, f32[16,128]{1,0:T(8,128)S(1)}, u32[]{:S(2)}, u32[]{:S(2)}) collective-permute-start(f32[16,128]{1,0:T(8,128)S(1)} %add_add_fusion.1), channel_id=1, source_target_pairs={{0,3},{1,2},{2,1},{3,0},{4,7},{5,6},{6,5},{7,4},{8,11},{9,10},{10,... | collective-permute-start | bytes 24584 | tf_op jit(solution)/shard_map/ppermute | solution.py:816
  44.5 1.9 %collective-permute-start.8 = (f32[16,128]{1,0:T(8,128)S(1)}, f32[16,128]{1,0:T(8,128)S(1)}, u32[]{:S(2)}, u32[]{:S(2)}) collective-permute-start(f32[16,128]{1,0:T(8,128)S(1)} %add_add_fusion.1), channel_id=1, source_target_pairs={{0,2},{1,3},{2,0},{3,1},{4,6},{5,7},{6,4},{7,5},{8,10},{9,11},{10,... | collective-permute-start | bytes 24584 | tf_op jit(solution)/shard_map/ppermute | solution.py:816
  46.3 1.2 %collective-permute-start.7 = (f32[16,128]{1,0:T(8,128)S(1)}, f32[16,128]{1,0:T(8,128)S(1)}, u32[]{:S(2)}, u32[]{:S(2)}) collective-permute-start(f32[16,128]{1,0:T(8,128)S(1)} %add_add_fusion.1), channel_id=1, source_target_pairs={{0,1},{1,0},{2,3},{3,2},{4,5},{5,4},{6,7},{7,6},{8,9},{9,8},{10,11... | collective-permute-start | bytes 24584 | tf_op jit(solution)/shard_map/ppermute | solution.py:816
  47.5 2.4 %interpolate.3.second_ref = f32[6,32,8,128]{3,2,1,0:T(8,128)S(1)} custom-call(s32[1,32,8,128]{3,2,1,0:T(8,128)S(1)} %get-tuple-element.51.tag_ref, f32[25,2,24,128]{3,2,1,0:T(8,128)S(1)} %get-tuple-element.44.fluid_ref, f32[25,2,24,128]{3,2,1,0:T(8,128)S(1)} %get-tuple-element.48.refs_0_.k1_ref, f32[25,2,24,128]{3,2,1,0:T(8,128)S(1)} %get-tuple-element.49.refs_1_.k2_ref), custom_call_target="tpu_custom_call" | custom-call | flops 10000000 | bytes 6103040 | tf_op jit(solution)/shard_map/interpolate/pallas_call | solution.py:526
  49.9 0.0 collective-permute-done.9
  50.0 0.0 collective-permute-done.8
  50.0 0.0 collective-permute-done.7
  50.0 3.4 %finish.1 = (f32[16,8,256]{2,1,0:T(8,128)}, f32[3,32,8,128]{3,2,1,0:T(8,128)}) custom-call(f32[16,128]{1,0:T(8,128)S(1)} %add_add_fusion.sums_ref, f32[25,2,24,128]{3,2,1,0:T(8,128)S(1)} %get-tuple-element.46.refs_1_.k0_ref, f32[25,2,24,128]{3,2,1,0:T(8,128)S(1)} %get-tuple-element.48.refs_0_.k1_ref, ...), custom_call_target="tpu_custom_call" | custom-call | bytes 7487488 | tf_op jit(solution)/shard_map/finish/pallas_call | solution.py:526
  (5 shorter events, 0.1 us)
Async XLA Ops:
  0.6 0.9 %copy-start.3 = (s32[1,32768]{1,0:T(1,128)S(1)}, s32[1,32768]{1,0:T(1,128)}, u32[]{:S(2)}) copy-start(s32[1,32768]{1,0:T(1,128)} %param.4) | copy-start | bytes 393220
  1.5 1.4 %copy-start = (f32[1,12,32768]{2,0,1:T(1,128)S(1)}, f32[1,12,32768]{2,0,1:T(1,128)}, u32[]{:S(2)}) copy-start(f32[1,12,32768]{2,0,1:T(1,128)} %param.6) | copy-start | bytes 4718596
  1.6 1.4 %copy-start.2 = (s32[1,32768]{1,0:T(1,128)S(1)}, s32[1,32768]{1,0:T(1,128)}, u32[]{:S(2)}) copy-start(s32[1,32768]{1,0:T(1,128)} %param.5) | copy-start | bytes 393220
  2.9 11.6 %copy-start.1 = (s32[16,8,256]{2,1,0:T(8,128)S(1)}, s32[16,8,256]{2,1,0:T(8,128)}, u32[]{:S(2)}) copy-start(s32[16,8,256]{2,1,0:T(8,128)} %flag_ref.3) | copy-start | bytes 393220
  15.3 13.1 %collective-permute-start.1 = (f32[624,128]{1,0:T(8,128)S(1)}, f32[624,128]{1,0:T(8,128)S(1)}, u32[]{:S(2)}, u32[]{:S(2)}) collective-permute-start(f32[624,128]{1,0:T(8,128)S(1)} %get-tuple-element.62), channel_id=1, source_target_pairs={{1,2},{2,1},{5,6},{6,5},{9,10},{10,9},{13,14},{14,13},{17,18},{18,... | collective-permute-start | bytes 958472 | tf_op jit(solution)/shard_map/ppermute | solution.py:805
  16.1 13.1 %collective-permute-start = (f32[624,128]{1,0:T(8,128)S(1)}, f32[624,128]{1,0:T(8,128)S(1)}, u32[]{:S(2)}, u32[]{:S(2)}) collective-permute-start(f32[624,128]{1,0:T(8,128)S(1)} %get-tuple-element.63), channel_id=1, source_target_pairs={{0,1},{2,3},{1,0},{3,2},{4,5},{6,7},{5,4},{7,6},{8,9},{10,11},{9,8... | collective-permute-start | bytes 958472 | tf_op jit(solution)/shard_map/ppermute | solution.py:805
  30.4 3.6 %collective-permute-start.3 = (f32[464,128]{1,0:T(8,128)S(1)}, f32[464,128]{1,0:T(8,128)S(1)}, u32[]{:S(2)}, u32[]{:S(2)}) collective-permute-start(f32[464,128]{1,0:T(8,128)S(1)} %get-tuple-element.66), channel_id=1, source_target_pairs={{4,8},{8,4},{5,9},{9,5},{6,10},{10,6},{7,11},{11,7},{20,24},{24,20... | collective-permute-start | bytes 712712 | tf_op jit(solution)/shard_map/ppermute | solution.py:805
  31.1 4.0 %collective-permute-start.2 = (f32[464,128]{1,0:T(8,128)S(1)}, f32[464,128]{1,0:T(8,128)S(1)}, u32[]{:S(2)}, u32[]{:S(2)}) collective-permute-start(f32[464,128]{1,0:T(8,128)S(1)} %get-tuple-element.67), channel_id=1, source_target_pairs={{0,4},{8,12},{4,0},{12,8},{1,5},{9,13},{5,1},{13,9},{2,6},{10,14},... | collective-permute-start | bytes 712712 | tf_op jit(solution)/shard_map/ppermute | solution.py:805
  37.0 5.9 %collective-permute-start.6 = (f32[16,128]{1,0:T(8,128)S(1)}, f32[16,128]{1,0:T(8,128)S(1)}, u32[]{:S(2)}, u32[]{:S(2)}) collective-permute-start(f32[16,128]{1,0:T(8,128)S(1)} %get-tuple-element.43), channel_id=1, source_target_pairs={{0,12},{4,8},{8,4},{12,0},{1,13},{5,9},{9,5},{13,1},{2,14},{6,10},... | collective-permute-start | bytes 24584 | tf_op jit(solution)/shard_map/ppermute | solution.py:816
  37.1 5.9 %collective-permute-start.5 = (f32[16,128]{1,0:T(8,128)S(1)}, f32[16,128]{1,0:T(8,128)S(1)}, u32[]{:S(2)}, u32[]{:S(2)}) collective-permute-start(f32[16,128]{1,0:T(8,128)S(1)} %get-tuple-element.43), channel_id=1, source_target_pairs={{0,8},{4,12},{8,0},{12,4},{1,9},{5,13},{9,1},{13,5},{2,10},{6,14},... | collective-permute-start | bytes 24584 | tf_op jit(solution)/shard_map/ppermute | solution.py:816
  41.4 1.6 %collective-permute-start.4 = (f32[16,128]{1,0:T(8,128)S(1)}, f32[16,128]{1,0:T(8,128)S(1)}, u32[]{:S(2)}, u32[]{:S(2)}) collective-permute-start(f32[16,128]{1,0:T(8,128)S(1)} %get-tuple-element.43), channel_id=1, source_target_pairs={{0,4},{4,0},{8,12},{12,8},{1,5},{5,1},{9,13},{13,9},{2,6},{6,2},{1... | collective-permute-start | bytes 24584 | tf_op jit(solution)/shard_map/ppermute | solution.py:816
  43.1 6.9 %collective-permute-start.9 = (f32[16,128]{1,0:T(8,128)S(1)}, f32[16,128]{1,0:T(8,128)S(1)}, u32[]{:S(2)}, u32[]{:S(2)}) collective-permute-start(f32[16,128]{1,0:T(8,128)S(1)} %add_add_fusion.1), channel_id=1, source_target_pairs={{0,3},{1,2},{2,1},{3,0},{4,7},{5,6},{6,5},{7,4},{8,11},{9,10},{10,... | collective-permute-start | bytes 24584 | tf_op jit(solution)/shard_map/ppermute | solution.py:816
  44.5 5.5 %collective-permute-start.8 = (f32[16,128]{1,0:T(8,128)S(1)}, f32[16,128]{1,0:T(8,128)S(1)}, u32[]{:S(2)}, u32[]{:S(2)}) collective-permute-start(f32[16,128]{1,0:T(8,128)S(1)} %add_add_fusion.1), channel_id=1, source_target_pairs={{0,2},{1,3},{2,0},{3,1},{4,6},{5,7},{6,4},{7,5},{8,10},{9,11},{10,... | collective-permute-start | bytes 24584 | tf_op jit(solution)/shard_map/ppermute | solution.py:816
  46.3 3.7 %collective-permute-start.7 = (f32[16,128]{1,0:T(8,128)S(1)}, f32[16,128]{1,0:T(8,128)S(1)}, u32[]{:S(2)}, u32[]{:S(2)}) collective-permute-start(f32[16,128]{1,0:T(8,128)S(1)} %add_add_fusion.1), channel_id=1, source_target_pairs={{0,1},{1,0},{2,3},{3,2},{4,5},{5,4},{6,7},{7,6},{8,9},{9,8},{10,11... | collective-permute-start | bytes 24584 | tf_op jit(solution)/shard_map/ppermute | solution.py:816
